TPU v7x, 128 devices: a whole 4x4x4 slice. The times are simulated.
128 devices in a mesh: shot: 4 (over x), gx: 4 (over y_lo, core), gy: 8 (over y_hi, z).
Axes of the slice: x: 4, y: 4 (y_hi: 2, y_lo: 2; y = y_hi * 2 + y_lo), z: 4, core: 2. Of those that a mesh axis runs over, the one named last changes fastest.
Arguments:
- velocity: float32 [256, 512, 128], P(('shot', 'gx'), 'gy'), may hold values from 1.5 to 4.5
- density: float32 [256, 512, 128], P(('shot', 'gx'), 'gy'), may hold values from 1 to 3
- offsets: int32 [4, 2], replicated, may hold values from 0 to 256, as said below
- pressure: float32 [4, 128, 256, 128], P('shot', 'gx', 'gy'), may hold values from -6 to 6
- vel_x: float32 [4, 128, 256, 128], P('shot', 'gx', 'gy'), may hold values from -0.6 to 0.6
- vel_y: float32 [4, 128, 256, 128], P('shot', 'gx', 'gy'), may hold values from -0.6 to 0.6
- vel_z: float32 [4, 128, 256, 128], P('shot', 'gx', 'gy'), may hold values from -0.6 to 0.6
- source_cells: int32 [4, 3], replicated, may hold values from 0 to 255, as said below
- wavelet: float32 [4, 4], replicated, may hold values from -120 to 120
Outputs:
- pressure_out: float32 [4, 128, 256, 128], P('shot', 'gx', 'gy')
- vel_x_out: float32 [4, 128, 256, 128], P('shot', 'gx', 'gy')
- vel_y_out: float32 [4, 128, 256, 128], P('shot', 'gx', 'gy')
- vel_z_out: float32 [4, 128, 256, 128], P('shot', 'gx', 'gy')
Inputs may be any that keep to these rules, and one draw needn't show every extreme that they name: `offsets`: every aperture lies inside the model: x corner at most 128, y corner at most 256; one shot's x corner and another's y corner are at those ends. `source_cells`: every source cell lies inside its aperture: x below 128, y below 256, depth below 128; some shots' sources lie on the far ends of x, y and depth.
All inputs are finite; a program needn't handle non-finite values.
Results may differ from a plain program's by a relative error of at most 0.0003.
Values sent between devices are 32-bit elements; how exact they have to be, the bound alone decides.
No kernel may reach another device: no remote copies, remote signals or barrier semaphores. Data moves between devices by JAX's collectives and lax.ppermute only.
A program may use at most 128 MiB of HBM per device.

v0:
```python
import jax
import jax.numpy as jnp
from jax import lax
from jax.sharding import PartitionSpec as P

CX = 32
CY = 32
STEPS = 4


coefs = (1225.0 / 1024.0, -245.0 / 3072.0, 49.0 / 5120.0, -5.0 / 7168.0)
time_step = 0.09


def with_halo(block, sides, width):
    for axis, dim in sides:
        count = lax.axis_size(axis)
        forward = [(i, i + 1) for i in range(count - 1)]
        backward = [(target, source) for source, target in forward]
        low = lax.ppermute(
            lax.slice_in_dim(block, block.shape[dim] - width, None, axis=dim), axis, forward
        )
        high = lax.ppermute(lax.slice_in_dim(block, 0, width, axis=dim), axis, backward)
        block = jnp.concatenate([low, block, high], axis=dim)
    return block


def stencil(padded, axis, count):
    total = None
    for reach in range(1, 5):
        upper = lax.slice_in_dim(padded, 3 + reach, 3 + reach + count, axis=axis)
        lower = lax.slice_in_dim(padded, 4 - reach, 4 - reach + count, axis=axis)
        term = coefs[reach - 1] * (upper - lower)
        total = term if total is None else total + term
    return total


def pad_axis(field, axis, before, after):
    widths = [(0, 0), (0, 0), (0, 0)]
    widths[axis] = (before, after)
    return jnp.pad(field, widths)


def place_window(carry, pieces, wanted, axis):
    length = pieces[0].shape[axis]
    inside = (wanted >= 0) & (wanted < length)
    touches = jnp.any(inside)

    def insert(totals):
        clipped = jnp.clip(wanted, 0, length - 1)
        shape = [1, 1, 1]
        shape[axis] = wanted.shape[0]
        mask = inside.reshape(shape)
        return tuple(
            (
                total + jnp.where(mask, jnp.take(piece, clipped, axis=axis), jnp.float32(0.0))
                for total, piece in zip(totals, pieces)
            )
        )

    return lax.cond(touches, insert, lambda totals: totals, carry)


def move_rows(fields, wanted):
    empty = jnp.zeros((wanted.shape[0], fields[0].shape[1], fields[0].shape[2]), jnp.float32)

    def fold(carry, pieces, start):
        return place_window(carry, pieces, wanted, 0)

    return fold(
        (empty, empty),
        (
            lax.all_gather(fields[0], ("shot", "gx"), axis=0, tiled=True),
            lax.all_gather(fields[1], ("shot", "gx"), axis=0, tiled=True),
        ),
        jnp.int32(0),
    )


def move_columns(fields, wanted):
    empty = jnp.zeros((fields[0].shape[0], wanted.shape[0], fields[0].shape[2]), jnp.float32)

    def fold(carry, pieces, start):
        return place_window(carry, pieces, wanted, 1)

    return fold(
        (empty, empty),
        (
            lax.all_gather(fields[0], "gy", axis=1, tiled=True),
            lax.all_gather(fields[1], "gy", axis=1, tiled=True),
        ),
        jnp.int32(0),
    )


def shards(velocity, density, offsets, pressure, vel_x, vel_y, vel_z, source_cells, wavelet):
    shot_index = lax.axis_index("shot")
    column_x = lax.axis_index("gx")
    column_y = lax.axis_index("gy")
    corner = lax.dynamic_index_in_dim(offsets, shot_index, 0, keepdims=False)
    wanted_x = corner[0] + column_x * CX + jnp.arange(CX, dtype=jnp.int32)
    wanted_y = corner[1] + column_y * CY + jnp.arange(CY, dtype=jnp.int32)
    moved = move_rows((velocity, density), wanted_x)
    moved = move_columns(moved, wanted_y)
    speed, rho = moved
    buoyancy = 1.0 / rho
    modulus = rho * speed * speed
    depth_cells = speed.shape[2]
    source = lax.dynamic_index_in_dim(source_cells, shot_index, 0, keepdims=False)
    amplitude = lax.dynamic_index_in_dim(wavelet, shot_index, 0, keepdims=False)
    across = column_x * CX + jnp.arange(CX, dtype=jnp.int32)
    along = column_y * CY + jnp.arange(CY, dtype=jnp.int32)
    depth = jnp.arange(depth_cells, dtype=jnp.int32)
    hit = (
        (across == source[0])[:, None, None]
        & (along == source[1])[None, :, None]
        & (depth == source[2])[None, None, :]
    )
    inject = jnp.where(hit, jnp.float32(1.0), jnp.float32(0.0))
    pres = pressure[0]
    flow_x = vel_x[0]
    flow_y = vel_y[0]
    flow_z = vel_z[0]
    for step in range(STEPS):
        rim = with_halo(pres, (("gx", 0), ("gy", 1)), 4)
        grad_x = stencil(rim[1:, 4:-4, :], 0, CX)
        grad_y = stencil(rim[4:-4, 1:, :], 1, CY)
        grad_z = stencil(pad_axis(pres, 2, 3, 4), 2, depth_cells)
        flow_x = flow_x - time_step * buoyancy * grad_x
        flow_y = flow_y - time_step * buoyancy * grad_y
        flow_z = flow_z - time_step * buoyancy * grad_z
        rim_x = with_halo(flow_x, (("gx", 0),), 4)
        rim_y = with_halo(flow_y, (("gy", 1),), 4)
        spread = (
            stencil(rim_x[:-1], 0, CX)
            + stencil(rim_y[:, :-1], 1, CY)
            + stencil(pad_axis(flow_z, 2, 4, 3), 2, depth_cells)
        )
        pres = pres - time_step * modulus * spread + time_step * amplitude[step] * inject
    return (pres[None], flow_x[None], flow_y[None], flow_z[None])


def solution(mesh):
    return jax.shard_map(
        shards,
        mesh=mesh,
        in_specs=(
            P(("shot", "gx"), "gy", None),
            P(("shot", "gx"), "gy", None),
            P(),
            P("shot", "gx", "gy", None),
            P("shot", "gx", "gy", None),
            P("shot", "gx", "gy", None),
            P("shot", "gx", "gy", None),
            P(),
            P(),
        ),
        out_specs=(
            P("shot", "gx", "gy", None),
            P("shot", "gx", "gy", None),
            P("shot", "gx", "gy", None),
            P("shot", "gx", "gy", None),
        ),
        check_vma=False,
    )
```

profile of v0, /device:TPU:16, one launch (start us, length us, event | category | flops | bytes accessed | tf_op | source)
XLA Modules:
  0.0 495.8 jit_solution(5492061064784160796)
XLA Ops:
  11.9 52.0 %all-gather.5.cloned.1.call-done = f32[256,64,128]{2,1,0:T(8,128)} async-done(((f32[16,64,128]{2,1,0:T(8,128)}), f32[256,64,128]{2,1,0:T(8,128)}) %all-gather.5.cloned.1.call-update) | async-done | bytes 8388624 | tf_op jit(solution)/shard_map/all_gather | solution.py:73
  64.0 54.7 %all-gather.7.cloned.1.call-done = f32[256,64,128]{2,1,0:T(8,128)} async-done(((f32[16,64,128]{2,1,0:T(8,128)}), f32[256,64,128]{2,1,0:T(8,128)}) %all-gather.7.cloned.1.call-update) | async-done | bytes 8388624 | tf_op jit(solution)/shard_map/all_gather | solution.py:74
  118.7 9.7 %conditional.2 = (f32[32,64,128]{2,1,0:T(8,128)}, f32[32,64,128]{2,1,0:T(8,128)}) conditional(s32[]{:T(128)} %convert_element_type.17, () %tuple.27, (pred[32]{0:T(512)(128)(4,1)S(1)}, s32[32]{0:T(128)S(1)}, f32[256,64,128]{2,1,0:T(8,128)}, f32[256,64,128]{2,1,0:T(8,128)}) %tuple.28), branch_computations={%region_2.3_spmd, %region_3.5_spmd} | conditional | flops 1049824 | bytes 8393456 | solution.py:61
  118.7 4.0 gather_fusion
  122.8 4.0 gather_fusion.1
  144.5 4.9 collective-permute-start.4
  153.8 6.3 %collective-permute-done.5 = f32[40,4,128]{2,1,0:T(4,128)S(1)} collective-permute-done((f32[40,4,128]{2,1,0:T(4,128)S(1)}, f32[40,4,128]{2,1,0:T(4,128)S(1)}, u32[]{:S(2)}, u32[]{:S(2)}) %collective-permute-start.5) | collective-permute-done | bytes 81952 | tf_op jit(solution)/shard_map/ppermute | solution.py:20
  160.2 77.7 %all-gather.11.cloned.1.call-done = f32[32,512,128]{2,0,1:T(8,128)} async-done(((f32[32,64,128]{2,0,1:T(8,128)}), f32[32,512,128]{2,0,1:T(8,128)}) %all-gather.11.cloned.1.call-update) | async-done | bytes 8388624 | tf_op jit(solution)/shard_map/all_gather | solution.py:90
  237.9 107.2 %all-gather.9.cloned.1.call-done = f32[32,512,128]{2,0,1:T(8,128)} async-done(((f32[32,64,128]{2,0,1:T(8,128)}), f32[32,512,128]{2,0,1:T(8,128)}) %all-gather.9.cloned.1.call-update) | async-done | bytes 8388624 | tf_op jit(solution)/shard_map/all_gather | solution.py:89
  345.1 9.7 %conditional.3 = (f32[32,32,128]{2,1,0:T(8,128)S(1)}, f32[32,32,128]{2,1,0:T(8,128)}, f32[32,32,128]{2,1,0:T(8,128)}) conditional(s32[]{:T(128)} %convert_element_type.16, () %tuple.26, (pred[32]{0:T(512)(128)(4,1)S(1)}, s32[32]{0:T(128)S(1)}, f32[32,512,128]{2,0,1:T(8,128)}, f32[32,512,128]{2,0,1:T(8,128)}) %tuple.29), branch_computations={%region_4.6_spmd, %region_5.8_spmd} | conditional | flops 656608 | bytes 6820600 | solution.py:61
  345.2 4.0 gather_fusion.2
  349.1 4.0 gather_fusion.3
  358.6 7.4 %collective-permute-start.7 = (f32[32,4,128]{2,1,0:T(4,128)S(1)}, f32[32,4,128]{2,1,0:T(4,128)S(1)}, u32[]{:S(2)}, u32[]{:S(2)}) collective-permute-start(f32[32,4,128]{2,1,0:T(4,128)S(1)} %get-tuple-element.97), channel_id=1, source_target_pairs={{1,0},{2,1},{3,2},{4,3},{5,4},{6,5},{7,6},{9,8},{10,9},{11,10},{12... | collective-permute-start | bytes 196616 | tf_op jit(solution)/shard_map/ppermute | solution.py:23
  379.3 5.5 %collective-permute-start.9 = (f32[4,32,128]{2,1,0:T(8,128)S(1)}, f32[4,32,128]{2,1,0:T(8,128)S(1)}, u32[]{:S(2)}, u32[]{:S(2)}) collective-permute-start(f32[4,32,128]{2,1,0:T(8,128)S(1)} %get-tuple-element.95), channel_id=1, source_target_pairs={{0,8},{8,16},{16,24},{1,9},{9,17},{17,25},{2,10},{10,18},{18,26},{... | collective-permute-start | bytes 196616 | tf_op jit(solution)/shard_map/ppermute | solution.py:20
  387.7 3.9 collective-permute-start.13
  400.7 7.5 %collective-permute-start.15 = (f32[32,4,128]{2,1,0:T(4,128)S(1)}, f32[32,4,128]{2,1,0:T(4,128)S(1)}, u32[]{:S(2)}, u32[]{:S(2)}) collective-permute-start(f32[32,4,128]{2,1,0:T(4,128)S(1)} %get-tuple-element.91), channel_id=1, source_target_pairs={{1,0},{2,1},{3,2},{4,3},{5,4},{6,5},{7,6},{9,8},{10,9},{11,10},{12... | collective-permute-start | bytes 196616 | tf_op jit(solution)/shard_map/ppermute | solution.py:23
  413.4 4.1 collective-permute-start.17
  418.4 7.6 %collective-permute-start.20 = (f32[40,4,128]{2,1,0:T(4,128)S(1)}, f32[40,4,128]{2,1,0:T(4,128)S(1)}, u32[]{:S(2)}, u32[]{:S(2)}) collective-permute-start(f32[40,4,128]{2,1,0:T(4,128)S(1)} %get-tuple-element.68), channel_id=1, source_target_pairs={{1,0},{2,1},{3,2},{4,3},{5,4},{6,5},{7,6},{9,8},{10,9},{11,10},{12... | collective-permute-start | bytes 245768 | tf_op jit(solution)/shard_map/ppermute | solution.py:23
  428.2 4.7 collective-permute-start.18
  439.0 7.5 %collective-permute-start.23 = (f32[32,4,128]{2,1,0:T(4,128)S(1)}, f32[32,4,128]{2,1,0:T(4,128)S(1)}, u32[]{:S(2)}, u32[]{:S(2)}) collective-permute-start(f32[32,4,128]{2,1,0:T(4,128)S(1)} %get-tuple-element.85), channel_id=1, source_target_pairs={{1,0},{2,1},{3,2},{4,3},{5,4},{6,5},{7,6},{9,8},{10,9},{11,10},{12... | collective-permute-start | bytes 196616 | tf_op jit(solution)/shard_map/ppermute | solution.py:23
  451.7 3.8 collective-permute-start.25
  456.4 7.6 %collective-permute-start.28 = (f32[40,4,128]{2,1,0:T(4,128)S(1)}, f32[40,4,128]{2,1,0:T(4,128)S(1)}, u32[]{:S(2)}, u32[]{:S(2)}) collective-permute-start(f32[40,4,128]{2,1,0:T(4,128)S(1)} %get-tuple-element.64), channel_id=1, source_target_pairs={{1,0},{2,1},{3,2},{4,3},{5,4},{6,5},{7,6},{9,8},{10,9},{11,10},{12... | collective-permute-start | bytes 245768 | tf_op jit(solution)/shard_map/ppermute | solution.py:23
  466.2 6.6 %collective-permute-start.26 = (f32[4,32,128]{2,1,0:T(8,128)S(1)}, f32[4,32,128]{2,1,0:T(8,128)S(1)}, u32[]{:S(2)}, u32[]{:S(2)}) collective-permute-start(f32[4,32,128]{2,1,0:T(8,128)S(1)} %get-tuple-element.80), channel_id=1, source_target_pairs={{0,8},{8,16},{16,24},{1,9},{9,17},{17,25},{2,10},{10,18},{18,26},{... | collective-permute-start | bytes 196616 | tf_op jit(solution)/shard_map/ppermute | solution.py:20
  477.3 7.5 %collective-permute-start.31 = (f32[32,4,128]{2,1,0:T(4,128)S(1)}, f32[32,4,128]{2,1,0:T(4,128)S(1)}, u32[]{:S(2)}, u32[]{:S(2)}) collective-permute-start(f32[32,4,128]{2,1,0:T(4,128)S(1)} %get-tuple-element.79), channel_id=1, source_target_pairs={{1,0},{2,1},{3,2},{4,3},{5,4},{6,5},{7,6},{9,8},{10,9},{11,10},{12... | collective-permute-start | bytes 196616 | tf_op jit(solution)/shard_map/ppermute | solution.py:23
  (122 shorter events, 83.6 us)
Async XLA Ops:
  7.2 56.8 %all-gather.5.cloned.1.call-start = ((), (), s32[]{:S(2)}) async-start(), calls=%async_computation | async-start | bytes 8912896 | tf_op jit(solution)/shard_map/all_gather | solution.py:73
  7.9 110.8 %all-gather.7.cloned.1.call-start = ((), (), s32[]{:S(2)}) async-start(), calls=%async_computation.1 | async-start | bytes 8912896 | tf_op jit(solution)/shard_map/all_gather | solution.py:74
  8.7 229.2 %all-gather.11.cloned.1.call-start = ((), (), s32[]{:S(2)}) async-start(), calls=%async_computation.3 | async-start | bytes 9437184 | tf_op jit(solution)/shard_map/all_gather | solution.py:90
  131.2 213.9 %all-gather.9.cloned.1.call-start = ((), (), s32[]{:S(2)}) async-start(), calls=%async_computation.2 | async-start | bytes 9437184 | tf_op jit(solution)/shard_map/all_gather | solution.py:89
  134.1 10.3 %collective-permute-start = (f32[4,32,128]{2,1,0:T(8,128)S(1)}, f32[4,32,128]{2,1,0:T(8,128)S(1)}, u32[]{:S(2)}, u32[]{:S(2)}) collective-permute-start(f32[4,32,128]{2,1,0:T(8,128)S(1)} %get-tuple-element.100), channel_id=1, source_target_pairs={{8,0},{16,8},{24,16},{9,1},{17,9},{25,17},{10,2},{18,10},{26,18},{... | collective-permute-start | bytes 196616 | tf_op jit(solution)/shard_map/ppermute | solution.py:23
  149.4 10.7 %collective-permute-start.5 = (f32[40,4,128]{2,1,0:T(4,128)S(1)}, f32[40,4,128]{2,1,0:T(4,128)S(1)}, u32[]{:S(2)}, u32[]{:S(2)}) collective-permute-start(f32[40,4,128]{2,1,0:T(4,128)S(1)} %get-tuple-element.77), channel_id=1, source_target_pairs={{0,1},{1,2},{2,3},{3,4},{4,5},{5,6},{6,7},{8,9},{9,10},{10,11},{11... | collective-permute-start | bytes 245768 | tf_op jit(solution)/shard_map/ppermute | solution.py:20
  356.5 15.0 %collective-permute-start.6 = (f32[32,4,128]{2,1,0:T(4,128)S(1)}, f32[32,4,128]{2,1,0:T(4,128)S(1)}, u32[]{:S(2)}, u32[]{:S(2)}) collective-permute-start(f32[32,4,128]{2,1,0:T(4,128)S(1)} %get-tuple-element.96), channel_id=1, source_target_pairs={{0,1},{1,2},{2,3},{3,4},{4,5},{5,6},{6,7},{8,9},{9,10},{10,11},{11... | collective-permute-start | bytes 196616 | tf_op jit(solution)/shard_map/ppermute | solution.py:20
  358.6 12.9 %collective-permute-start.7 = (f32[32,4,128]{2,1,0:T(4,128)S(1)}, f32[32,4,128]{2,1,0:T(4,128)S(1)}, u32[]{:S(2)}, u32[]{:S(2)}) collective-permute-start(f32[32,4,128]{2,1,0:T(4,128)S(1)} %get-tuple-element.97), channel_id=1, source_target_pairs={{1,0},{2,1},{3,2},{4,3},{5,4},{6,5},{7,6},{9,8},{10,9},{11,10},{12... | collective-permute-start | bytes 196616 | tf_op jit(solution)/shard_map/ppermute | solution.py:23
  385.7 11.0 %collective-permute-start.12 = (f32[40,4,128]{2,1,0:T(4,128)S(1)}, f32[40,4,128]{2,1,0:T(4,128)S(1)}, u32[]{:S(2)}, u32[]{:S(2)}) collective-permute-start(f32[40,4,128]{2,1,0:T(4,128)S(1)} %get-tuple-element.72), channel_id=1, source_target_pairs={{1,0},{2,1},{3,2},{4,3},{5,4},{6,5},{7,6},{9,8},{10,9},{11,10},{12... | collective-permute-start | bytes 245768 | tf_op jit(solution)/shard_map/ppermute | solution.py:23
  387.7 9.9 %collective-permute-start.13 = (f32[40,4,128]{2,1,0:T(4,128)S(1)}, f32[40,4,128]{2,1,0:T(4,128)S(1)}, u32[]{:S(2)}, u32[]{:S(2)}) collective-permute-start(f32[40,4,128]{2,1,0:T(4,128)S(1)} %get-tuple-element.73), channel_id=1, source_target_pairs={{0,1},{1,2},{2,3},{3,4},{4,5},{5,6},{6,7},{8,9},{9,10},{10,11},{11... | collective-permute-start | bytes 245768 | tf_op jit(solution)/shard_map/ppermute | solution.py:20
  391.9 16.9 %collective-permute-start.10 = (f32[4,32,128]{2,1,0:T(8,128)S(1)}, f32[4,32,128]{2,1,0:T(8,128)S(1)}, u32[]{:S(2)}, u32[]{:S(2)}) collective-permute-start(f32[4,32,128]{2,1,0:T(8,128)S(1)} %get-tuple-element.92), channel_id=1, source_target_pairs={{0,8},{8,16},{16,24},{1,9},{9,17},{17,25},{2,10},{10,18},{18,26},{... | collective-permute-start | bytes 196616 | tf_op jit(solution)/shard_map/ppermute | solution.py:20
  395.4 13.4 %collective-permute-start.11 = (f32[4,32,128]{2,1,0:T(8,128)S(1)}, f32[4,32,128]{2,1,0:T(8,128)S(1)}, u32[]{:S(2)}, u32[]{:S(2)}) collective-permute-start(f32[4,32,128]{2,1,0:T(8,128)S(1)} %get-tuple-element.93), channel_id=1, source_target_pairs={{8,0},{16,8},{24,16},{9,1},{17,9},{25,17},{10,2},{18,10},{26,18},{... | collective-permute-start | bytes 196616 | tf_op jit(solution)/shard_map/ppermute | solution.py:23
  398.8 10.1 %collective-permute-start.14 = (f32[32,4,128]{2,1,0:T(4,128)S(1)}, f32[32,4,128]{2,1,0:T(4,128)S(1)}, u32[]{:S(2)}, u32[]{:S(2)}) collective-permute-start(f32[32,4,128]{2,1,0:T(4,128)S(1)} %get-tuple-element.90), channel_id=1, source_target_pairs={{0,1},{1,2},{2,3},{3,4},{4,5},{5,6},{6,7},{8,9},{9,10},{10,11},{11... | collective-permute-start | bytes 196616 | tf_op jit(solution)/shard_map/ppermute | solution.py:20
  418.4 16.0 %collective-permute-start.20 = (f32[40,4,128]{2,1,0:T(4,128)S(1)}, f32[40,4,128]{2,1,0:T(4,128)S(1)}, u32[]{:S(2)}, u32[]{:S(2)}) collective-permute-start(f32[40,4,128]{2,1,0:T(4,128)S(1)} %get-tuple-element.68), channel_id=1, source_target_pairs={{1,0},{2,1},{3,2},{4,3},{5,4},{6,5},{7,6},{9,8},{10,9},{11,10},{12... | collective-permute-start | bytes 245768 | tf_op jit(solution)/shard_map/ppermute | solution.py:23
  426.0 9.9 %collective-permute-start.21 = (f32[40,4,128]{2,1,0:T(4,128)S(1)}, f32[40,4,128]{2,1,0:T(4,128)S(1)}, u32[]{:S(2)}, u32[]{:S(2)}) collective-permute-start(f32[40,4,128]{2,1,0:T(4,128)S(1)} %get-tuple-element.69), channel_id=1, source_target_pairs={{0,1},{1,2},{2,3},{3,4},{4,5},{5,6},{6,7},{8,9},{9,10},{10,11},{11... | collective-permute-start | bytes 245768 | tf_op jit(solution)/shard_map/ppermute | solution.py:20
  428.2 19.1 %collective-permute-start.18 = (f32[4,32,128]{2,1,0:T(8,128)S(1)}, f32[4,32,128]{2,1,0:T(8,128)S(1)}, u32[]{:S(2)}, u32[]{:S(2)}) collective-permute-start(f32[4,32,128]{2,1,0:T(8,128)S(1)} %get-tuple-element.86), channel_id=1, source_target_pairs={{0,8},{8,16},{16,24},{1,9},{9,17},{17,25},{2,10},{10,18},{18,26},{... | collective-permute-start | bytes 196616 | tf_op jit(solution)/shard_map/ppermute | solution.py:20
  432.9 14.3 %collective-permute-start.19 = (f32[4,32,128]{2,1,0:T(8,128)S(1)}, f32[4,32,128]{2,1,0:T(8,128)S(1)}, u32[]{:S(2)}, u32[]{:S(2)}) collective-permute-start(f32[4,32,128]{2,1,0:T(8,128)S(1)} %get-tuple-element.87), channel_id=1, source_target_pairs={{8,0},{16,8},{24,16},{9,1},{17,9},{25,17},{10,2},{18,10},{26,18},{... | collective-permute-start | bytes 196616 | tf_op jit(solution)/shard_map/ppermute | solution.py:23
  437.1 10.2 %collective-permute-start.22 = (f32[32,4,128]{2,1,0:T(4,128)S(1)}, f32[32,4,128]{2,1,0:T(4,128)S(1)}, u32[]{:S(2)}, u32[]{:S(2)}) collective-permute-start(f32[32,4,128]{2,1,0:T(4,128)S(1)} %get-tuple-element.84), channel_id=1, source_target_pairs={{0,1},{1,2},{2,3},{3,4},{4,5},{5,6},{6,7},{8,9},{9,10},{10,11},{11... | collective-permute-start | bytes 196616 | tf_op jit(solution)/shard_map/ppermute | solution.py:20
  456.4 17.7 %collective-permute-start.28 = (f32[40,4,128]{2,1,0:T(4,128)S(1)}, f32[40,4,128]{2,1,0:T(4,128)S(1)}, u32[]{:S(2)}, u32[]{:S(2)}) collective-permute-start(f32[40,4,128]{2,1,0:T(4,128)S(1)} %get-tuple-element.64), channel_id=1, source_target_pairs={{1,0},{2,1},{3,2},{4,3},{5,4},{6,5},{7,6},{9,8},{10,9},{11,10},{12... | collective-permute-start | bytes 245768 | tf_op jit(solution)/shard_map/ppermute | solution.py:23
  464.0 10.1 %collective-permute-start.29 = (f32[40,4,128]{2,1,0:T(4,128)S(1)}, f32[40,4,128]{2,1,0:T(4,128)S(1)}, u32[]{:S(2)}, u32[]{:S(2)}) collective-permute-start(f32[40,4,128]{2,1,0:T(4,128)S(1)} %get-tuple-element.65), channel_id=1, source_target_pairs={{0,1},{1,2},{2,3},{3,4},{4,5},{5,6},{6,7},{8,9},{9,10},{10,11},{11... | collective-permute-start | bytes 245768 | tf_op jit(solution)/shard_map/ppermute | solution.py:20
  466.2 19.2 %collective-permute-start.26 = (f32[4,32,128]{2,1,0:T(8,128)S(1)}, f32[4,32,128]{2,1,0:T(8,128)S(1)}, u32[]{:S(2)}, u32[]{:S(2)}) collective-permute-start(f32[4,32,128]{2,1,0:T(8,128)S(1)} %get-tuple-element.80), channel_id=1, source_target_pairs={{0,8},{8,16},{16,24},{1,9},{9,17},{17,25},{2,10},{10,18},{18,26},{... | collective-permute-start | bytes 196616 | tf_op jit(solution)/shard_map/ppermute | solution.py:20
  472.8 12.7 %collective-permute-start.27 = (f32[4,32,128]{2,1,0:T(8,128)S(1)}, f32[4,32,128]{2,1,0:T(8,128)S(1)}, u32[]{:S(2)}, u32[]{:S(2)}) collective-permute-start(f32[4,32,128]{2,1,0:T(8,128)S(1)} %get-tuple-element.81), channel_id=1, source_target_pairs={{8,0},{16,8},{24,16},{9,1},{17,9},{25,17},{10,2},{18,10},{26,18},{... | collective-permute-start | bytes 196616 | tf_op jit(solution)/shard_map/ppermute | solution.py:23
  475.3 10.1 %collective-permute-start.30 = (f32[32,4,128]{2,1,0:T(4,128)S(1)}, f32[32,4,128]{2,1,0:T(4,128)S(1)}, u32[]{:S(2)}, u32[]{:S(2)}) collective-permute-start(f32[32,4,128]{2,1,0:T(4,128)S(1)} %get-tuple-element.78), channel_id=1, source_target_pairs={{0,1},{1,2},{2,3},{3,4},{4,5},{5,6},{6,7},{8,9},{9,10},{10,11},{11... | collective-permute-start | bytes 196616 | tf_op jit(solution)/shard_map/ppermute | solution.py:20
  477.3 9.4 %collective-permute-start.31 = (f32[32,4,128]{2,1,0:T(4,128)S(1)}, f32[32,4,128]{2,1,0:T(4,128)S(1)}, u32[]{:S(2)}, u32[]{:S(2)}) collective-permute-start(f32[32,4,128]{2,1,0:T(4,128)S(1)} %get-tuple-element.79), channel_id=1, source_target_pairs={{1,0},{2,1},{3,2},{4,3},{5,4},{6,5},{7,6},{9,8},{10,9},{11,10},{12... | collective-permute-start | bytes 196616 | tf_op jit(solution)/shard_map/ppermute | solution.py:23
  (17 other events, 279.6 us)
Sparse Core Ops, SparseCore 0:
  9.7 54.1 all-gather.4
  65.7 52.9 all-gather.6
  131.3 106.5 all-gather.10
  240.1 104.9 all-gather.8
where the time goes:
time: 505 us; the launch traced here: 496 us
  waiting for transfers between devices  314 us (62%)
  starting transfers between devices  113 us (22%)
  local copies, waits for them, and re-layouts  25 us (5%)
  other arithmetic  24.4 us (5%)
  between operations  19.6 us (4%)
    all_gather x1, waiting for transfers between devices, move_columns(): lax.all_gather(fields[0], 'gy', axis=1, tiled=True)  107 us
    all_gather x1, waiting for transfers between devices, move_columns(): lax.all_gather(fields[1], 'gy', axis=1, tiled=True)  77.7 us
    ppermute x16, starting transfers between devices, with_halo(): lax.ppermute(lax.slice_in_dim(block, 0, width, axis=dim), axis, backward)  62.5 us
    all_gather x1, waiting for transfers between devices, move_rows(): lax.all_gather(fields[1], ('shot', 'gx'), axis=0, tiled=True)  54.7 us
    all_gather x1, waiting for transfers between devices, move_rows(): lax.all_gather(fields[0], ('shot', 'gx'), axis=0, tiled=True)  52 us
    ppermute x16, starting transfers between devices, with_halo(): lax.ppermute(lax.slice_in_dim(block, block.shape[dim] - width, None, axis...  50 us
    gather x4, local copies, waits for them, and re-layouts, insert(): jnp.take(piece, clipped, axis=axis)  16 us
    ppermute x16, waiting for transfers between devices, with_halo(): lax.ppermute(lax.slice_in_dim(block, block.shape[dim] - width, None, axis...  11.3 us
  transfers between devices with their start and end apart: 36, of which 15 were waited for; matrix products, arithmetic and copies ran while one was open for 3% of the time, Pallas kernels for 0%

commit v1 on v0

v1 whole, which is shorter than its diff:
```python
import functools

import jax
import jax.numpy as jnp
import numpy as np
from jax import lax
from jax.experimental import pallas as pl
from jax.experimental.pallas import tpu as pltpu
from jax.sharding import PartitionSpec as P

CX = 32
CY = 32
STEPS = 4
HALO = 7
WIDE = 40
PAD = 48
LINE = 80
DEVICES = ("shot", "gx", "gy")

coefs = (1225.0 / 1024.0, -245.0 / 3072.0, 49.0 / 5120.0, -5.0 / 7168.0)
time_step = 0.09

f32 = jnp.float32
bf16 = jnp.bfloat16


def depth_matrices():
    out = []
    for lead in (0, 1):
        full = np.zeros((128, 128), np.float32)
        for reach in range(1, 5):
            for k in range(128):
                up, down = k + reach - lead, k - reach + 1 - lead
                if up < 128:
                    full[up, k] += np.float32(coefs[reach - 1])
                if down >= 0:
                    full[down, k] -= np.float32(coefs[reach - 1])
        high = full.astype(jnp.bfloat16)
        low = (full - high.astype(np.float32)).astype(jnp.bfloat16)
        out.append(np.concatenate([high, high, low], axis=0))
    return out


def depth_difference(values, mat_ref):
    high = values.astype(bf16)
    low = (values - high.astype(f32)).astype(bf16)
    main = jnp.dot(
        jnp.concatenate([high, low], axis=1), mat_ref[0:256, :], preferred_element_type=f32
    )
    return main + jnp.dot(high, mat_ref[256:384, :], preferred_element_type=f32)


def forward(taps, at):
    total = None
    for reach in range(1, 5):
        term = coefs[reach - 1] * (taps[at + 3 + reach] - taps[at + 4 - reach])
        total = term if total is None else total + term
    return total


def backward(taps, at):
    total = None
    for reach in range(1, 5):
        term = coefs[reach - 1] * (taps[at + 3 + reach] - taps[at + 4 - reach])
        total = term if total is None else total + term
    return total


def every(ref, start, step):
    return ref[pl.ds(start, 8, stride=step), :]


def put_every(ref, start, step, value):
    ref[pl.ds(start, 8, stride=step), :] = value


def send_faces(info, field, x_pair, y_pair, base, count):
    odd_x, odd_y = info[8], info[9]
    for which, ref in enumerate(x_pair):
        high = (odd_x == 0) if which == 0 else (odd_x == 1)
        start = pl.multiple_of(jnp.where(high, (CX - count[0]) * CY, 0), 32)
        rows = max(count)
        if count[0] != count[1]:
            start = pl.multiple_of(jnp.where(high, (CX - count[0]) * CY, 0), 32)
        ref[base * 32 : (base + rows) * 32, :] = field[pl.ds(start, rows * 32), :]
    for which, ref in enumerate(y_pair):
        high = (odd_y == 0) if which == 0 else (odd_y == 1)
        start = jnp.where(high, CY - count[0], 0)
        for c in range(max(count)):
            for part in range(4):
                at = (base + c) * 32 + part * 8
                ref[at : at + 8, :] = every(field, part * 8 * CY + start + c, CY)


def pack_kernel(info, vel, den, pres, flow_x, flow_y, deal, gx_a, gx_b, gy_a, gy_b):
    for row in range(16):
        for cls in range(8):
            at = (row * 8 + cls) * 16
            deal[at : at + 8, :] = every(vel, row * 64 + cls, 8)
            deal[at + 8 : at + 16, :] = every(den, row * 64 + cls, 8)
    send_faces(info, pres, (gx_a, gx_b), (gy_a, gy_b), 0, (HALO, HALO))
    send_faces(info, flow_x, (gx_a, gx_b), (), HALO, (4, 4))
    send_faces(info, flow_y, (), (gy_a, gy_b), HALO, (4, 4))


def cut_kernel(info, corners, dealt, out, rho_lines, vel_lines):
    row_class, col_class = info[3], info[2]
    for t in range(16):
        for part in range(8):
            src = (t * 8 + part) * 16
            dst = t * LINE + 8 + part * 8
            vel_lines[dst : dst + 8, :] = dealt[src : src + 8, :]
            rho_lines[dst : dst + 8, :] = dealt[src + 8 : src + 16, :]

    def block(index, carry):
        shot = index // 4
        corner_x = corners[shot * 2] + (index % 4) * CX
        corner_y = corners[shot * 2 + 1]
        wide_row = lax.shift_right_arithmetic(corner_x - 4 - row_class + 15, 4)
        row = lax.shift_right_arithmetic(corner_x - row_class + 15, 4)
        for h in range(8):
            base = (index * 8 + h) * 24
            wide_col = lax.shift_right_arithmetic(corner_y + h * CY - 4 - col_class + 7, 3)
            col = lax.shift_right_arithmetic(corner_y + h * CY - col_class + 7, 3)
            for k in range(3):
                line = jnp.clip(wide_row + k, 0, 15)
                out[pl.ds(base + 5 * k, 5), :] = rho_lines[
                    pl.ds(line * LINE + 8 + wide_col, 5), :
                ]
            for k in range(2):
                out[pl.ds(base + 16 + 4 * k, 4), :] = vel_lines[
                    pl.ds((row + k) * LINE + 8 + col, 4), :
                ]
        return carry

    lax.fori_loop(0, 16, block, 0)


def unpack_model(info, corners, window, buoy, modu, rho, vel):
    shot, g, h = info[0], info[1], info[2]
    corner_x = corners[shot * 2] + g * CX
    corner_y = corners[shot * 2 + 1] + h * CY
    turn = lax.rem(8 - lax.rem(corner_y + 4, 8), 8)
    wide_turn = turn
    turn = lax.rem(8 - lax.rem(corner_y, 8), 8)
    sub = lax.broadcasted_iota(jnp.int32, (8, 128), 0)
    for w in range(WIDE):
        cls = lax.rem(corner_x + 12 + w, 16)
        row_in = (g * CX + w - 4 >= 0) & (g * CX + w - 4 < 4 * CX)
        for n in range(5):
            got = every(window, cls * 192 + 5 * (w // 16) + n, 24)
            got = pltpu.roll(got, wide_turn, 0)
            at = w * WIDE + n * 8
            rho[at : at + 8, :] = got
            col = sub + (h * CY + n * 8 - 4)
            inside = (col >= 0) & (col < 8 * CY) & row_in
            buoy[at : at + 8, :] = jnp.where(inside, time_step * (1.0 / got), 0.0)
    for w in range(CX):
        cls = lax.rem(corner_x + w, 16)
        for n in range(4):
            got = every(window, cls * 192 + 16 + 4 * (w // 16) + n, 24)
            at = w * CY + n * 8
            vel[at : at + 8, :] = pltpu.roll(got, turn, 0)
    for w in range(CX):
        for j in range(4):
            speed = every(vel, w * CY + j, 4)
            dens = every(rho, (w + 4) * WIDE + 4 + j, 4)
            put_every(modu, w * CY + j, 4, time_step * (dens * speed * speed))


def receive_faces(info, x_pair, y_pair, padded):
    odd_x, odd_y, end_x, end_y = info[8], info[9], info[10], info[11]
    for which, ref in enumerate(x_pair):
        high = (odd_x == 0) if which == 0 else (odd_x == 1)
        start = jnp.where(high, CX, -HALO)
        for i in range(HALO):
            value = ref[i * 32 : (i + 1) * 32, :]
            if which == 1:
                value = jnp.where(end_x == 1, 0.0, value)
            padded[pl.ds(pl.multiple_of((start + i + 8) * PAD + 8, 8), 32), :] = value
    for which, ref in enumerate(y_pair):
        high = (odd_y == 0) if which == 0 else (odd_y == 1)
        start = jnp.where(high, CY, -HALO)
        for c in range(HALO):
            for part in range(4):
                value = ref[c * 32 + part * 8 : c * 32 + part * 8 + 8, :]
                if which == 1:
                    value = jnp.where(end_y == 1, 0.0, value)
                put_every(padded, (part * 8 + 8) * PAD + start + c + 8, PAD, value)


def step_kernel(step, *refs):
    first, last = step == 0, step == STEPS - 1
    info, corners, amps, mat_f, mat_b, pres, gx_a, gx_b, gy_a, gy_b = refs[:10]
    rest = list(refs[10:])
    if first:
        window, in_x, in_y, in_z = rest[:4]
        rest = rest[4:]
        new_p, wide_x, wide_y, new_z, out_a, out_b, out_c, out_d, buoy, modu = rest[:10]
        rest = rest[10:]
        padded, rho, vel = rest
        unpack_model(info, corners, window, buoy, modu, rho, vel)
        wide_x[4 * CY : 36 * CY, :] = in_x[...]

        def spread_y(x, carry):
            for j in range(4):
                put_every(wide_y, x * WIDE + 4 + j, 4, every(in_y, x * CY + j, 4))
            return carry

        lax.fori_loop(0, CX, spread_y, 0)
        odd_x, odd_y, end_x, end_y = info[8], info[9], info[10], info[11]
        for which, ref in enumerate((gx_a, gx_b)):
            high = (odd_x == 0) if which == 0 else (odd_x == 1)
            value = ref[HALO * 32 : (HALO + 4) * 32, :]
            if which == 1:
                value = jnp.where(end_x == 1, 0.0, value)
            wide_x[pl.ds(pl.multiple_of(jnp.where(high, 36 * CY, 0), 32), 4 * CY), :] = value
        for which, ref in enumerate((gy_a, gy_b)):
            high = (odd_y == 0) if which == 0 else (odd_y == 1)
            start = jnp.where(high, 36, 0)
            for c in range(4):
                for part in range(4):
                    at = (HALO + c) * 32 + part * 8
                    value = ref[at : at + 8, :]
                    if which == 1:
                        value = jnp.where(end_y == 1, 0.0, value)
                    put_every(wide_y, part * 8 * WIDE + start + c, WIDE, value)
        old_x, old_y, old_z = wide_x, wide_y, in_z
    else:
        old_x, old_y, old_z, buoy, modu = rest[:5]
        rest = rest[5:]
        if last:
            new_p, out_x, out_y, new_z = rest[:4]
            padded, wide_x, wide_y = rest[4:]
        else:
            new_p, wide_x, wide_y, new_z, out_a, out_b, out_c, out_d = rest[:8]
            padded = rest[8]

    def spread_p(x, carry):
        padded[pl.ds(pl.multiple_of((x + 8) * PAD + 8, 8), 32), :] = pres[
            pl.ds(pl.multiple_of(x * CY, 32), 32), :
        ]
        return carry

    lax.fori_loop(0, CX, spread_p, 0)
    receive_faces(info, (gx_a, gx_b), (gy_a, gy_b), padded)

    def update_x(chunk, carry):
        x0 = chunk * 4 - 4
        for j in range(4):
            taps = [every(padded, (x0 + d + 8) * PAD + 8 + j, 4) for d in range(-3, 8)]
            for i in range(4):
                at = (x0 + i + 4) * CY + j
                value = every(old_x, at, 4) - every(buoy, (x0 + i + 4) * WIDE + 4 + j, 4) * forward(taps, i)
                put_every(wide_x, at, 4, value)
        return carry

    lax.fori_loop(0, 10, update_x, 0)

    def update_y(x, carry):
        taps = [every(padded, (x + 8) * PAD + 4 + d, 5) for d in range(-3, 9)]
        for j in range(5):
            at = x * WIDE + j
            value = every(old_y, at, 5) - every(buoy, (x + 4) * WIDE + j, 5) * forward(taps, j)
            put_every(wide_y, at, 5, value)
        return carry

    lax.fori_loop(0, CX, update_y, 0)

    def update_p(chunk, carry):
        x0 = chunk * 4
        old = [every(pres, (x0 + i) * CY + j, 4) for i in range(4) for j in range(4)]
        grad = depth_difference(jnp.concatenate(old, axis=0), mat_f)
        flow = []
        for i in range(4):
            for j in range(4):
                n = i * 4 + j
                at = (x0 + i) * CY + j
                value = every(old_z, at, 4) - every(
                    buoy, (x0 + i + 4) * WIDE + 4 + j, 4
                ) * grad[n * 8 : n * 8 + 8, :]
                put_every(new_z, at, 4, value)
                flow.append(value)
        part_z = depth_difference(jnp.concatenate(flow, axis=0), mat_b)
        part_x = {}
        for j in range(4):
            taps = [every(wide_x, (x0 + d + 4) * CY + j, 4) for d in range(-4, 7)]
            for i in range(4):
                part_x[i, j] = backward(taps, i)
        for i in range(4):
            taps = [every(wide_y, (x0 + i) * WIDE + 4 + d, 4) for d in range(-4, 7)]
            for j in range(4):
                n = i * 4 + j
                total = part_x[i, j] + backward(taps, j) + part_z[n * 8 : n * 8 + 8, :]
                at = (x0 + i) * CY + j
                put_every(new_p, at, 4, old[n] - every(modu, at, 4) * total)
        return carry

    lax.fori_loop(0, 8, update_p, 0)

    shot = info[0]
    src_x = info[4] - info[1] * CX
    src_y = info[5] - info[2] * CY

    @pl.when((src_x >= 0) & (src_x < CX) & (src_y >= 0) & (src_y < CY))
    def _():
        at = src_x * CY + src_y
        lane = lax.broadcasted_iota(jnp.int32, (1, 128), 1)
        kick = time_step * amps[shot * STEPS + step]
        new_p[pl.ds(at, 1), :] = new_p[pl.ds(at, 1), :] + jnp.where(lane == info[6], kick, 0.0)

    if last:
        out_x[...] = wide_x[4 * CY : 36 * CY, :]

        def trim_y(x, carry):
            for j in range(4):
                put_every(out_y, x * CY + j, 4, every(wide_y, x * WIDE + 4 + j, 4))
            return carry

        lax.fori_loop(0, CX, trim_y, 0)
    else:
        send_faces(info, new_p, (out_a, out_b), (out_c, out_d), 0, (HALO, HALO))


def shape(rows, dtype=f32):
    return jax.ShapeDtypeStruct((rows, 128), dtype)


def call(kernel, outs, args, scratch, smem, name):
    specs = [pl.BlockSpec(memory_space=pltpu.SMEM)] * smem + [
        pl.BlockSpec(memory_space=pltpu.VMEM)
    ] * (len(args) - smem)
    return pl.pallas_call(
        kernel,
        out_shape=outs,
        in_specs=specs,
        out_specs=[pl.BlockSpec(memory_space=pltpu.VMEM)] * len(outs),
        scratch_shapes=scratch,
        compiler_params=pltpu.CompilerParams(vmem_limit_bytes=40 * 1024 * 1024),
        name=name,
    )(*args)


x_swaps = ([(0, 1), (1, 0), (2, 3), (3, 2)], [(1, 2), (2, 1), (0, 3), (3, 0)])
y_swaps = (
    [(i, i ^ 1) for i in range(8)],
    [(1, 2), (2, 1), (3, 4), (4, 3), (5, 6), (6, 5), (7, 0), (0, 7)],
)


def exchange(faces):
    return [
        lax.ppermute(faces[0], "gx", x_swaps[0]),
        lax.ppermute(faces[1], "gx", x_swaps[1]),
        lax.ppermute(faces[2], "gy", y_swaps[0]),
        lax.ppermute(faces[3], "gy", y_swaps[1]),
    ]


def shards(velocity, density, offsets, pressure, vel_x, vel_y, vel_z, source_cells, wavelet):
    s, g, h = (lax.axis_index(axis) for axis in DEVICES)
    cell = lax.dynamic_index_in_dim(source_cells, s, 0, keepdims=False)
    zero = jnp.int32(0)
    info = jnp.stack(
        [
            s, g, h, s * 4 + g,
            cell[0], cell[1], cell[2], zero,
            g % 2, h % 2,
            ((g == 0) | (g == 3)).astype(jnp.int32),
            ((h == 0) | (h == 7)).astype(jnp.int32),
        ]
    ).astype(jnp.int32)
    corners = offsets.reshape(-1)
    amps = wavelet.reshape(-1)
    mat_f, mat_b = (jnp.asarray(m) for m in depth_matrices())

    vel = velocity.reshape(16 * 64, 128)
    den = density.reshape(16 * 64, 128)
    pres = pressure.reshape(CX * CY, 128)
    flow_x = vel_x.reshape(CX * CY, 128)
    flow_y = vel_y.reshape(CX * CY, 128)
    flow_z = vel_z.reshape(CX * CY, 128)

    face = shape((HALO + 4) * 32)
    deal, *faces = call(
        pack_kernel, [shape(128 * 16)] + [face] * 4, [info, vel, den, pres, flow_x, flow_y], [], 1, "pack"
    )
    faces = exchange(faces)
    dealt = lax.all_to_all(deal.reshape(128, 16, 128), DEVICES, 0, 0, tiled=True)
    (cut,) = call(
        cut_kernel,
        [shape(128 * 24)],
        [info, corners, dealt.reshape(128 * 16, 128)],
        [pltpu.VMEM((16 * LINE, 128), f32), pltpu.VMEM((16 * LINE, 128), f32)],
        2,
        "cut",
    )
    window = lax.all_to_all(cut.reshape(128, 24, 128), DEVICES, 0, 0, tiled=True)
    window = window.reshape(128 * 24, 128)

    block = shape(CX * CY)
    wide = shape(WIDE * CY)
    face = shape(HALO * 32)
    padded = pltpu.VMEM((PAD * PAD, 128), f32)
    for step in range(STEPS):
        head = [info, corners, amps, mat_f, mat_b, pres] + list(faces)
        kernel = functools.partial(step_kernel, step)
        name = f"step{step}"
        if step == 0:
            pres, flow_x, flow_y, flow_z, *faces, buoy, modu = call(
                kernel,
                [block, wide, wide, block] + [face] * 4 + [shape(WIDE * WIDE), block],
                head + [window, flow_x, flow_y, flow_z],
                [padded, pltpu.VMEM((WIDE * WIDE, 128), f32), pltpu.VMEM((CX * CY, 128), f32)],
                3,
                name,
            )
        elif step < STEPS - 1:
            pres, flow_x, flow_y, flow_z, *faces = call(
                kernel,
                [block, wide, wide, block] + [face] * 4,
                head + [flow_x, flow_y, flow_z, buoy, modu],
                [padded],
                3,
                name,
            )
        else:
            pres, flow_x, flow_y, flow_z = call(
                kernel,
                [block] * 4,
                head + [flow_x, flow_y, flow_z, buoy, modu],
                [padded] + [pltpu.VMEM((WIDE * CY, 128), f32)] * 2,
                3,
                name,
            )
        if step < STEPS - 1:
            faces = exchange(faces)
    return tuple(a.reshape(1, CX, CY, 128) for a in (pres, flow_x, flow_y, flow_z))


def solution(mesh):
    return jax.shard_map(
        shards,
        mesh=mesh,
        in_specs=(
            P(("shot", "gx"), "gy", None),
            P(("shot", "gx"), "gy", None),
            P(),
            P("shot", "gx", "gy", None),
            P("shot", "gx", "gy", None),
            P("shot", "gx", "gy", None),
            P("shot", "gx", "gy", None),
            P(),
            P(),
        ),
        out_specs=(
            P("shot", "gx", "gy", None),
            P("shot", "gx", "gy", None),
            P("shot", "gx", "gy", None),
            P("shot", "gx", "gy", None),
        ),
        check_vma=False,
    )
```

time: 505 us -> 136 us (0.27); the launches traced: 496 us -> 133 us
  waiting for transfers between devices: 314 us -> 60.1 us
  starting transfers between devices: 113 us -> 33.8 us
  Pallas kernels: 0 us -> 25.8 us
  other arithmetic: 24.4 us -> 0 us
  between operations: 19.6 us -> 0.84 us
  local copies, waits for them, and re-layouts: 25 us -> 12.5 us
    all_gather x4 -> x0, waiting for transfers between devices: 292 us -> none  [the longest x1 107 us: move_columns(): lax.all_gather(fields[0], 'gy', axis=1, tiled=True)]
    ppermute x32 -> x16, starting transfers between devices: 113 us -> 16.5 us  [the longest x4 8.09 us: exchange(): lax.ppermute(faces[3], 'gy', y_swaps[1])]
    pallas_call x0 -> x6, Pallas kernels: none -> 25.8 us  [call(): pl.pallas_call(kernel, out_shape=outs, in_specs=specs, out_specs=[pl.Bloc...]
    ppermute x32 -> x16, waiting for transfers between devices: 21 us -> 43.3 us  [the longest x4 22 us: exchange(): lax.ppermute(faces[1], 'gx', x_swaps[1])]
    all_to_all x0 -> x2, starting transfers between devices: none -> 17.3 us  [the longest x1 10.3 us: shards(): lax.all_to_all(deal.reshape(128, 16, 128), DEVICES, 0, 0, tiled=True)]
    all_to_all x0 -> x2, waiting for transfers between devices: none -> 16.9 us  [the longest x1 16.9 us: shards(): lax.all_to_all(deal.reshape(128, 16, 128), DEVICES, 0, 0, tiled=True)]
    gather x4 -> x0, local copies, waits for them, and re-layouts: 16 us -> none  [insert(): jnp.take(piece, clipped, axis=axis)]
    unnamed x10 -> x37, local copies, waits for them, and re-layouts: 0.03 us -> 9.7 us
  transfers between devices with their start and end apart: 36 -> 18, of which waited for: 15 -> 13; matrix products, arithmetic and copies ran while one was open for 3% -> 0% of each run, Pallas kernels for 0% -> 0%
where the time goes in v1:
time: 136 us; the launch traced here: 133 us
  waiting for transfers between devices  60.1 us (44%)
  starting transfers between devices  33.8 us (25%)
  Pallas kernels  25.8 us (19%)
  local copies, waits for them, and re-layouts  12.5 us (9%)
    pallas_call x6, Pallas kernels, call(): pl.pallas_call(kernel, out_shape=outs, in_specs=specs, out_specs=[pl.Bloc...  25.8 us
    ppermute x4, waiting for transfers between devices, exchange(): lax.ppermute(faces[1], 'gx', x_swaps[1])  22 us
    all_to_all x1, waiting for transfers between devices, shards(): lax.all_to_all(deal.reshape(128, 16, 128), DEVICES, 0, 0, tiled=True)  16.9 us
    ppermute x4, waiting for transfers between devices, exchange(): lax.ppermute(faces[3], 'gy', y_swaps[1])  16.3 us
    all_to_all x1, starting transfers between devices, shards(): lax.all_to_all(deal.reshape(128, 16, 128), DEVICES, 0, 0, tiled=True)  10.3 us
    unnamed x37, local copies, waits for them, and re-layouts  9.7 us
    ppermute x4, starting transfers between devices, exchange(): lax.ppermute(faces[3], 'gy', y_swaps[1])  8.09 us
    all_to_all x1, starting transfers between devices, shards(): lax.all_to_all(cut.reshape(128, 24, 128), DEVICES, 0, 0, tiled=True)  6.93 us
  transfers between devices with their start and end apart: 18, of which 13 were waited for; matrix products, arithmetic and copies ran while one was open for 0% of the time, Pallas kernels for 0%

profile of v1, /device:TPU:16, one launch (start us, length us, event | category | flops | bytes accessed | tf_op | source)
XLA Modules:
  0.0 133.1 jit_solution(17600858993588686598)
XLA Ops:
  2.0 2.0 %stack.43.info.refs_0_ = s32[12]{0:T(128)S(1)} concatenate(s32[1]{0:T(128)} %bitcast, s32[1]{0:T(128)} %bitcast.1, s32[1]{0:T(128)} %bitcast.2, s32[1]{0:T(128)} %bitcast.3, s32[1]{0:T(128)} %bitcast.4, s32[1]{0:T(128)} %bitcast.5, s32[1]{0:T(128)} %bitcast.6, s32[1]{0:T(128)} %constant.41.clone.1, s32[1]{0:T(128)} %bitcast.7, s32[1]{0:T(128)} %bitcast.8, s32[1]{0:T(128)} %bitcast.9, ...), dimensions={0} | concatenate | bytes 96 | tf_op jit(solution)/shard_map/stack | solution.py:364
  9.2 2.0 %pack.1 = (f32[2048,128]{1,0:T(8,128)}, f32[352,128]{1,0:T(8,128)S(1)}, f32[352,128]{1,0:T(8,128)S(1)}, f32[352,128]{1,0:T(8,128)S(1)}, f32[352,128]{1,0:T(8,128)S(1)}) custom-call(s32[12]{0:T(128)S(1)} %stack.43.info.refs_0_, f32[1024,128]{1,0:T(8,128)S(1)} %bitcast.33, f32[1024,128]{1,0:T(8,128)S(1)} %bitcast.34, f32[1024,128]{1,0:T(8,128)S(1)} %bitcast.27, ...), custom_call_target="tpu_custom_call" | custom-call | tf_op jit(solution)/shard_map/pack/pallas_call | solution.py:333
  13.8 10.3 %all-to-all-start = ((f32[128,16,128]{2,1,0:T(8,128)}), f32[128,16,128]{2,1,0:T(8,128)S(1)}, u32[]{:S(2)}, u32[]{:S(2)}) async-start(f32[128,16,128]{2,1,0:T(8,128)} %bitcast.16), calls=%async_computation | async-start | bytes 2097152 | tf_op jit(solution)/shard_map/all_to_all | solution.py:389
  24.4 16.9 %all-to-all-done = f32[128,16,128]{2,1,0:T(8,128)S(1)} async-done(((f32[128,16,128]{2,1,0:T(8,128)}), f32[128,16,128]{2,1,0:T(8,128)S(1)}, u32[]{:S(2)}, u32[]{:S(2)}) %all-to-all-start) | async-done | bytes 1048608 | tf_op jit(solution)/shard_map/all_to_all | solution.py:389
  41.3 2.6 %cut.1 = f32[3072,128]{1,0:T(8,128)} custom-call(s32[12]{0:T(128)S(1)} %stack.43.info.refs_0_, s32[8]{0:T(128)S(1)} %reshape.59.corners.refs_1_, f32[2048,128]{1,0:T(8,128)S(1)} %bitcast.26), custom_call_target="tpu_custom_call" | custom-call | tf_op jit(solution)/shard_map/cut/pallas_call | solution.py:333
  43.9 6.9 %all-to-all-start.1 = ((f32[128,24,128]{2,1,0:T(8,128)}), f32[128,24,128]{2,1,0:T(8,128)S(1)}, u32[]{:S(2)}, u32[]{:S(2)}) async-start(f32[128,24,128]{2,1,0:T(8,128)} %bitcast.18), calls=%async_computation.1 | async-start | bytes 3145728 | tf_op jit(solution)/shard_map/all_to_all | solution.py:398
  52.3 1.7 %collective-permute-start.2 = (f32[352,128]{1,0:T(8,128)}, f32[352,128]{1,0:T(8,128)}, u32[]{:S(2)}, u32[]{:S(2)}) collective-permute-start(f32[352,128]{1,0:T(8,128)} %copy-done.13), channel_id=1, source_target_pairs={{0,1},{1,0},{2,3},{3,2},{4,5},{5,4},{6,7},{7,6},{8,9},{9,8},{10,11... | collective-permute-start | bytes 540680 | tf_op jit(solution)/shard_map/ppermute | solution.py:355
  54.0 2.5 %collective-permute-start.3 = (f32[352,128]{1,0:T(8,128)}, f32[352,128]{1,0:T(8,128)}, u32[]{:S(2)}, u32[]{:S(2)}) collective-permute-start(f32[352,128]{1,0:T(8,128)} %copy-done.12), channel_id=1, source_target_pairs={{1,2},{2,1},{3,4},{4,3},{5,6},{6,5},{7,0},{0,7},{9,10},{10,9},{11,... | collective-permute-start | bytes 540680 | tf_op jit(solution)/shard_map/ppermute | solution.py:356
  56.6 16.2 %collective-permute-done.1.refs_7_ = f32[352,128]{1,0:T(8,128)} collective-permute-done((f32[352,128]{1,0:T(8,128)}, f32[352,128]{1,0:T(8,128)}, u32[]{:S(2)}, u32[]{:S(2)}) %collective-permute-start.1) | collective-permute-done | bytes 180256 | tf_op jit(solution)/shard_map/ppermute | solution.py:354
  73.8 5.5 %collective-permute-done.3.refs_9_ = f32[352,128]{1,0:T(8,128)} collective-permute-done((f32[352,128]{1,0:T(8,128)}, f32[352,128]{1,0:T(8,128)}, u32[]{:S(2)}, u32[]{:S(2)}) %collective-permute-start.3) | collective-permute-done | bytes 180256 | tf_op jit(solution)/shard_map/ppermute | solution.py:356
  80.3 5.9 %step0.1 = (f32[1024,128]{1,0:T(8,128)S(1)}, f32[1280,128]{1,0:T(8,128)S(1)}, f32[1280,128]{1,0:T(8,128)S(1)}, f32[1024,128]{1,0:T(8,128)S(1)}, f32[224,128]{1,0...) custom-call(s32[12]{0:T(128)S(1)} %stack.43.info.refs_0_, ...), custom_call_target="tpu_custom_call" | custom-call | tf_op jit(solution)/shard_map/step0/pallas_call | solution.py:333
  86.4 2.3 %collective-permute-start.5 = (f32[224,128]{1,0:T(8,128)S(1)}, f32[224,128]{1,0:T(8,128)S(1)}, u32[]{:S(2)}, u32[]{:S(2)}) collective-permute-start(f32[224,128]{1,0:T(8,128)S(1)} %get-tuple-element.46), channel_id=1, source_target_pairs={{8,16},{16,8},{0,24},{24,0},{9,17},{17,9},{1,25},{25,1},{10,18},{1... | collective-permute-start | bytes 344072 | tf_op jit(solution)/shard_map/ppermute | solution.py:354
  89.4 2.8 %collective-permute-done.5.refs_7_ = f32[224,128]{1,0:T(8,128)S(1)} collective-permute-done((f32[224,128]{1,0:T(8,128)S(1)}, f32[224,128]{1,0:T(8,128)S(1)}, u32[]{:S(2)}, u32[]{:S(2)}) %collective-permute-start.5) | collective-permute-done | bytes 114720 | tf_op jit(solution)/shard_map/ppermute | solution.py:354
  93.8 3.6 %collective-permute-done.7.refs_9_ = f32[224,128]{1,0:T(8,128)S(1)} collective-permute-done((f32[224,128]{1,0:T(8,128)S(1)}, f32[224,128]{1,0:T(8,128)S(1)}, u32[]{:S(2)}, u32[]{:S(2)}) %collective-permute-start.7) | collective-permute-done | bytes 114720 | tf_op jit(solution)/shard_map/ppermute | solution.py:356
  97.4 4.6 %step1.1 = (f32[1024,128]{1,0:T(8,128)S(1)}, f32[1280,128]{1,0:T(8,128)S(1)}, f32[1280,128]{1,0:T(8,128)S(1)}, f32[1024,128]{1,0:T(8,128)S(1)}, f32[224,128]{1,0...) custom-call(s32[12]{0:T(128)S(1)} %stack.43.info.refs_0_, ...), custom_call_target="tpu_custom_call" | custom-call | tf_op jit(solution)/shard_map/step1/pallas_call | solution.py:333
  102.6 2.6 %collective-permute-start.11 = (f32[224,128]{1,0:T(8,128)S(1)}, f32[224,128]{1,0:T(8,128)S(1)}, u32[]{:S(2)}, u32[]{:S(2)}) collective-permute-start(f32[224,128]{1,0:T(8,128)S(1)} %get-tuple-element.58), channel_id=1, source_target_pairs={{1,2},{2,1},{3,4},{4,3},{5,6},{6,5},{7,0},{0,7},{9,10},{10,9},{11,... | collective-permute-start | bytes 344072 | tf_op jit(solution)/shard_map/ppermute | solution.py:356
  105.2 2.0 %collective-permute-done.9.refs_7_ = f32[224,128]{1,0:T(8,128)S(1)} collective-permute-done((f32[224,128]{1,0:T(8,128)S(1)}, f32[224,128]{1,0:T(8,128)S(1)}, u32[]{:S(2)}, u32[]{:S(2)}) %collective-permute-start.9) | collective-permute-done | bytes 114720 | tf_op jit(solution)/shard_map/ppermute | solution.py:354
  107.7 3.6 %collective-permute-done.11.refs_9_ = f32[224,128]{1,0:T(8,128)S(1)} collective-permute-done((f32[224,128]{1,0:T(8,128)S(1)}, f32[224,128]{1,0:T(8,128)S(1)}, u32[]{:S(2)}, u32[]{:S(2)}) %collective-permute-start.11) | collective-permute-done | bytes 114720 | tf_op jit(solution)/shard_map/ppermute | solution.py:356
  111.3 4.6 %step2.1 = (f32[1024,128]{1,0:T(8,128)S(1)}, f32[1280,128]{1,0:T(8,128)S(1)}, f32[1280,128]{1,0:T(8,128)S(1)}, f32[1024,128]{1,0:T(8,128)S(1)}, f32[224,128]{1,0...) custom-call(s32[12]{0:T(128)S(1)} %stack.43.info.refs_0_, ...), custom_call_target="tpu_custom_call" | custom-call | tf_op jit(solution)/shard_map/step2/pallas_call | solution.py:333
  116.1 2.3 %collective-permute-start.13 = (f32[224,128]{1,0:T(8,128)S(1)}, f32[224,128]{1,0:T(8,128)S(1)}, u32[]{:S(2)}, u32[]{:S(2)}) collective-permute-start(f32[224,128]{1,0:T(8,128)S(1)} %get-tuple-element.64), channel_id=1, source_target_pairs={{8,16},{16,8},{0,24},{24,0},{9,17},{17,9},{1,25},{25,1},{10,18},{1... | collective-permute-start | bytes 344072 | tf_op jit(solution)/shard_map/ppermute | solution.py:354
  118.3 2.3 %collective-permute-start.15 = (f32[224,128]{1,0:T(8,128)S(1)}, f32[224,128]{1,0:T(8,128)S(1)}, u32[]{:S(2)}, u32[]{:S(2)}) collective-permute-start(f32[224,128]{1,0:T(8,128)S(1)} %get-tuple-element.66), channel_id=1, source_target_pairs={{1,2},{2,1},{3,4},{4,3},{5,6},{6,5},{7,0},{0,7},{9,10},{10,9},{11,... | collective-permute-start | bytes 344072 | tf_op jit(solution)/shard_map/ppermute | solution.py:356
  121.7 1.7 %collective-permute-done.14.refs_8_ = f32[224,128]{1,0:T(8,128)S(1)} collective-permute-done((f32[224,128]{1,0:T(8,128)S(1)}, f32[224,128]{1,0:T(8,128)S(1)}, u32[]{:S(2)}, u32[]{:S(2)}) %collective-permute-start.14) | collective-permute-done | bytes 114720 | tf_op jit(solution)/shard_map/ppermute | solution.py:355
  123.5 3.6 %collective-permute-done.15.refs_9_ = f32[224,128]{1,0:T(8,128)S(1)} collective-permute-done((f32[224,128]{1,0:T(8,128)S(1)}, f32[224,128]{1,0:T(8,128)S(1)}, u32[]{:S(2)}, u32[]{:S(2)}) %collective-permute-start.15) | collective-permute-done | bytes 114720 | tf_op jit(solution)/shard_map/ppermute | solution.py:356
  127.1 6.0 %step3.1 = (f32[1024,128]{1,0:T(8,128)}, f32[1024,128]{1,0:T(8,128)}, f32[1024,128]{1,0:T(8,128)}, f32[1024,128]{1,0:T(8,128)}) custom-call(s32[12]{0:T(128)S(1)} %stack.43.info.refs_0_, s32[8]{0:T(128)S(1)} %reshape.59.corners.refs_1_, f32[16]{0:T(128)S(1)} %reshape.60.refs_2_, bf16[384,128]{1,0:T(8,128)(2,1)S(1)} %copy-done.8, ...), custom_call_target="tpu_custom_call" | custom-call | tf_op jit(solution)/shard_map/step3/pallas_call | solution.py:333
  (60 shorter events, 17.7 us)
Async XLA Ops:
  13.8 27.4 %all-to-all-start = ((f32[128,16,128]{2,1,0:T(8,128)}), f32[128,16,128]{2,1,0:T(8,128)S(1)}, u32[]{:S(2)}, u32[]{:S(2)}) async-start(f32[128,16,128]{2,1,0:T(8,128)} %bitcast.16), calls=%async_computation | async-start | bytes 2097152 | tf_op jit(solution)/shard_map/all_to_all | solution.py:389
  43.9 12.6 %copy-start.16 = (f32[4,4]{1,0:T(4,128)S(1)}, f32[4,4]{1,0:T(4,128)}, u32[]{:S(2)}) copy-start(f32[4,4]{1,0:T(4,128)} %param.19) | copy-start | bytes 196
  43.9 35.4 %copy-start.2 = (f32[1,32,32,128]{3,2,1,0:T(8,128)S(1)}, f32[1,32,32,128]{3,2,1,0:T(8,128)}, u32[]{:S(2)}) copy-start(f32[1,32,32,128]{3,2,1,0:T(8,128)} %param.14) | copy-start | bytes 1572868
  43.9 35.4 %copy-start.4 = (f32[1,32,32,128]{3,2,1,0:T(8,128)S(1)}, f32[1,32,32,128]{3,2,1,0:T(8,128)}, u32[]{:S(2)}) copy-start(f32[1,32,32,128]{3,2,1,0:T(8,128)} %param.15) | copy-start | bytes 1572868
  43.9 35.4 %copy-start.6 = (f32[1,32,32,128]{3,2,1,0:T(8,128)S(1)}, f32[1,32,32,128]{3,2,1,0:T(8,128)}, u32[]{:S(2)}) copy-start(f32[1,32,32,128]{3,2,1,0:T(8,128)} %param.16) | copy-start | bytes 1572868
  43.9 35.4 %copy-start.7 = (bf16[384,128]{1,0:T(8,128)(2,1)S(1)}, bf16[384,128]{1,0:T(8,128)(2,1)}, u32[]{:S(2)}) copy-start(bf16[384,128]{1,0:T(8,128)(2,1)} %constant.47.clone.refs_4_) | copy-start | bytes 294916
  43.9 35.4 %copy-start.8 = (bf16[384,128]{1,0:T(8,128)(2,1)S(1)}, bf16[384,128]{1,0:T(8,128)(2,1)}, u32[]{:S(2)}) copy-start(bf16[384,128]{1,0:T(8,128)(2,1)} %constant.46.clone.refs_3_) | copy-start | bytes 294916
  43.9 35.3 %all-to-all-start.1 = ((f32[128,24,128]{2,1,0:T(8,128)}), f32[128,24,128]{2,1,0:T(8,128)S(1)}, u32[]{:S(2)}, u32[]{:S(2)}) async-start(f32[128,24,128]{2,1,0:T(8,128)} %bitcast.18), calls=%async_computation.1 | async-start | bytes 3145728 | tf_op jit(solution)/shard_map/all_to_all | solution.py:398
  50.9 5.7 %collective-permute-start = (f32[352,128]{1,0:T(8,128)}, f32[352,128]{1,0:T(8,128)S(1)}, u32[]{:S(2)}, u32[]{:S(2)}) collective-permute-start(f32[352,128]{1,0:T(8,128)} %copy-done.15), channel_id=1, source_target_pairs={{0,8},{8,0},{16,24},{24,16},{1,9},{9,1},{17,25},{25,17},{2,10},{10... | collective-permute-start | bytes 540680 | tf_op jit(solution)/shard_map/ppermute | solution.py:353
  51.1 21.7 %collective-permute-start.1 = (f32[352,128]{1,0:T(8,128)}, f32[352,128]{1,0:T(8,128)}, u32[]{:S(2)}, u32[]{:S(2)}) collective-permute-start(f32[352,128]{1,0:T(8,128)} %copy-done.14), channel_id=1, source_target_pairs={{8,16},{16,8},{0,24},{24,0},{9,17},{17,9},{1,25},{25,1},{10,18},{1... | collective-permute-start | bytes 540680 | tf_op jit(solution)/shard_map/ppermute | solution.py:354
  52.3 21.5 %collective-permute-start.2 = (f32[352,128]{1,0:T(8,128)}, f32[352,128]{1,0:T(8,128)}, u32[]{:S(2)}, u32[]{:S(2)}) collective-permute-start(f32[352,128]{1,0:T(8,128)} %copy-done.13), channel_id=1, source_target_pairs={{0,1},{1,0},{2,3},{3,2},{4,5},{5,4},{6,7},{7,6},{8,9},{9,8},{10,11... | collective-permute-start | bytes 540680 | tf_op jit(solution)/shard_map/ppermute | solution.py:355
  54.0 25.2 %collective-permute-start.3 = (f32[352,128]{1,0:T(8,128)}, f32[352,128]{1,0:T(8,128)}, u32[]{:S(2)}, u32[]{:S(2)}) collective-permute-start(f32[352,128]{1,0:T(8,128)} %copy-done.12), channel_id=1, source_target_pairs={{1,2},{2,1},{3,4},{4,3},{5,6},{6,5},{7,0},{0,7},{9,10},{10,9},{11,... | collective-permute-start | bytes 540680 | tf_op jit(solution)/shard_map/ppermute | solution.py:356
  86.3 3.1 %collective-permute-start.4 = (f32[224,128]{1,0:T(8,128)S(1)}, f32[224,128]{1,0:T(8,128)S(1)}, u32[]{:S(2)}, u32[]{:S(2)}) collective-permute-start(f32[224,128]{1,0:T(8,128)S(1)} %get-tuple-element.45), channel_id=1, source_target_pairs={{0,8},{8,0},{16,24},{24,16},{1,9},{9,1},{17,25},{25,17},{2,10},{10... | collective-permute-start | bytes 344072 | tf_op jit(solution)/shard_map/ppermute | solution.py:353
  86.4 5.8 %collective-permute-start.5 = (f32[224,128]{1,0:T(8,128)S(1)}, f32[224,128]{1,0:T(8,128)S(1)}, u32[]{:S(2)}, u32[]{:S(2)}) collective-permute-start(f32[224,128]{1,0:T(8,128)S(1)} %get-tuple-element.46), channel_id=1, source_target_pairs={{8,16},{16,8},{0,24},{24,0},{9,17},{17,9},{1,25},{25,1},{10,18},{1... | collective-permute-start | bytes 344072 | tf_op jit(solution)/shard_map/ppermute | solution.py:354
  88.7 5.1 %collective-permute-start.6 = (f32[224,128]{1,0:T(8,128)S(1)}, f32[224,128]{1,0:T(8,128)S(1)}, u32[]{:S(2)}, u32[]{:S(2)}) collective-permute-start(f32[224,128]{1,0:T(8,128)S(1)} %get-tuple-element.47), channel_id=1, source_target_pairs={{0,1},{1,0},{2,3},{3,2},{4,5},{5,4},{6,7},{7,6},{8,9},{9,8},{10,11... | collective-permute-start | bytes 344072 | tf_op jit(solution)/shard_map/ppermute | solution.py:355
  88.7 8.7 %collective-permute-start.7 = (f32[224,128]{1,0:T(8,128)S(1)}, f32[224,128]{1,0:T(8,128)S(1)}, u32[]{:S(2)}, u32[]{:S(2)}) collective-permute-start(f32[224,128]{1,0:T(8,128)S(1)} %get-tuple-element.48), channel_id=1, source_target_pairs={{1,2},{2,1},{3,4},{4,3},{5,6},{6,5},{7,0},{0,7},{9,10},{10,9},{11,... | collective-permute-start | bytes 344072 | tf_op jit(solution)/shard_map/ppermute | solution.py:356
  102.1 3.1 %collective-permute-start.8 = (f32[224,128]{1,0:T(8,128)S(1)}, f32[224,128]{1,0:T(8,128)S(1)}, u32[]{:S(2)}, u32[]{:S(2)}) collective-permute-start(f32[224,128]{1,0:T(8,128)S(1)} %get-tuple-element.55), channel_id=1, source_target_pairs={{0,8},{8,0},{16,24},{24,16},{1,9},{9,1},{17,25},{25,17},{2,10},{10... | collective-permute-start | bytes 344072 | tf_op jit(solution)/shard_map/ppermute | solution.py:353
  102.2 5.0 %collective-permute-start.9 = (f32[224,128]{1,0:T(8,128)S(1)}, f32[224,128]{1,0:T(8,128)S(1)}, u32[]{:S(2)}, u32[]{:S(2)}) collective-permute-start(f32[224,128]{1,0:T(8,128)S(1)} %get-tuple-element.56), channel_id=1, source_target_pairs={{8,16},{16,8},{0,24},{24,0},{9,17},{17,9},{1,25},{25,1},{10,18},{1... | collective-permute-start | bytes 344072 | tf_op jit(solution)/shard_map/ppermute | solution.py:354
  102.6 5.1 %collective-permute-start.10 = (f32[224,128]{1,0:T(8,128)S(1)}, f32[224,128]{1,0:T(8,128)S(1)}, u32[]{:S(2)}, u32[]{:S(2)}) collective-permute-start(f32[224,128]{1,0:T(8,128)S(1)} %get-tuple-element.57), channel_id=1, source_target_pairs={{0,1},{1,0},{2,3},{3,2},{4,5},{5,4},{6,7},{7,6},{8,9},{9,8},{10,11... | collective-permute-start | bytes 344072 | tf_op jit(solution)/shard_map/ppermute | solution.py:355
  102.6 8.7 %collective-permute-start.11 = (f32[224,128]{1,0:T(8,128)S(1)}, f32[224,128]{1,0:T(8,128)S(1)}, u32[]{:S(2)}, u32[]{:S(2)}) collective-permute-start(f32[224,128]{1,0:T(8,128)S(1)} %get-tuple-element.58), channel_id=1, source_target_pairs={{1,2},{2,1},{3,4},{4,3},{5,6},{6,5},{7,0},{0,7},{9,10},{10,9},{11,... | collective-permute-start | bytes 344072 | tf_op jit(solution)/shard_map/ppermute | solution.py:356
  116.0 4.7 %collective-permute-start.12 = (f32[224,128]{1,0:T(8,128)S(1)}, f32[224,128]{1,0:T(8,128)S(1)}, u32[]{:S(2)}, u32[]{:S(2)}) collective-permute-start(f32[224,128]{1,0:T(8,128)S(1)} %get-tuple-element.63), channel_id=1, source_target_pairs={{0,8},{8,0},{16,24},{24,16},{1,9},{9,1},{17,25},{25,17},{2,10},{10... | collective-permute-start | bytes 344072 | tf_op jit(solution)/shard_map/ppermute | solution.py:353
  116.1 5.7 %collective-permute-start.13 = (f32[224,128]{1,0:T(8,128)S(1)}, f32[224,128]{1,0:T(8,128)S(1)}, u32[]{:S(2)}, u32[]{:S(2)}) collective-permute-start(f32[224,128]{1,0:T(8,128)S(1)} %get-tuple-element.64), channel_id=1, source_target_pairs={{8,16},{16,8},{0,24},{24,0},{9,17},{17,9},{1,25},{25,1},{10,18},{1... | collective-permute-start | bytes 344072 | tf_op jit(solution)/shard_map/ppermute | solution.py:354
  118.3 5.1 %collective-permute-start.14 = (f32[224,128]{1,0:T(8,128)S(1)}, f32[224,128]{1,0:T(8,128)S(1)}, u32[]{:S(2)}, u32[]{:S(2)}) collective-permute-start(f32[224,128]{1,0:T(8,128)S(1)} %get-tuple-element.65), channel_id=1, source_target_pairs={{0,1},{1,0},{2,3},{3,2},{4,5},{5,4},{6,7},{7,6},{8,9},{9,8},{10,11... | collective-permute-start | bytes 344072 | tf_op jit(solution)/shard_map/ppermute | solution.py:355
  118.3 8.7 %collective-permute-start.15 = (f32[224,128]{1,0:T(8,128)S(1)}, f32[224,128]{1,0:T(8,128)S(1)}, u32[]{:S(2)}, u32[]{:S(2)}) collective-permute-start(f32[224,128]{1,0:T(8,128)S(1)} %get-tuple-element.66), channel_id=1, source_target_pairs={{1,2},{2,1},{3,4},{4,3},{5,6},{6,5},{7,0},{0,7},{9,10},{10,9},{11,... | collective-permute-start | bytes 344072 | tf_op jit(solution)/shard_map/ppermute | solution.py:356
  (12 other events, 20.0 us)

commit v2 on v1

v2 whole, which is shorter than its diff:
```python
import functools

import jax
import jax.numpy as jnp
import numpy as np
from jax import lax
from jax.experimental import pallas as pl
from jax.experimental.pallas import tpu as pltpu
from jax.sharding import PartitionSpec as P

CX = 32
CY = 32
STEPS = 4
HALO = 7
WIDE = 40
PAD = 48
LINE = 80
STRIP = 24
DEVICES = ("shot", "gx", "gy")

coefs = (1225.0 / 1024.0, -245.0 / 3072.0, 49.0 / 5120.0, -5.0 / 7168.0)
time_step = 0.09

f32 = jnp.float32
bf16 = jnp.bfloat16


def depth_matrices():
    out = []
    for lead in (0, 1):
        full = np.zeros((128, 128), np.float32)
        for reach in range(1, 5):
            for k in range(128):
                up, down = k + reach - lead, k - reach + 1 - lead
                if up < 128:
                    full[up, k] += np.float32(coefs[reach - 1])
                if down >= 0:
                    full[down, k] -= np.float32(coefs[reach - 1])
        high = full.astype(jnp.bfloat16)
        low = (full - high.astype(np.float32)).astype(jnp.bfloat16)
        out.append(np.concatenate([high, high, low], axis=0))
    return out


def depth_difference(values, mat_ref):
    high = values.astype(bf16)
    low = (values - high.astype(f32)).astype(bf16)
    main = jnp.dot(
        jnp.concatenate([high, low], axis=1), mat_ref[0:256, :], preferred_element_type=f32
    )
    return main + jnp.dot(high, mat_ref[256:384, :], preferred_element_type=f32)


def forward(taps, at):
    total = None
    for reach in range(1, 5):
        term = coefs[reach - 1] * (taps[at + 3 + reach] - taps[at + 4 - reach])
        total = term if total is None else total + term
    return total


def backward(taps, at):
    total = None
    for reach in range(1, 5):
        term = coefs[reach - 1] * (taps[at + 3 + reach] - taps[at + 4 - reach])
        total = term if total is None else total + term
    return total


def every(ref, start, step):
    return ref[pl.ds(start, 8, stride=step), :]


def put_every(ref, start, step, value):
    ref[pl.ds(start, 8, stride=step), :] = value


def place():
    return tuple(lax.axis_index(axis) for axis in DEVICES)


def odd(index):
    return lax.rem(index, 2) == 1


def send_faces(field, x_pair, y_pair, base, rows):
    s, g, h = place()
    for which, ref in enumerate(x_pair):
        low = odd(g) if which == 0 else jnp.logical_not(odd(g))
        start = pl.multiple_of(jnp.where(low, 0, (CX - rows) * CY), 32)
        ref[base * 32 : (base + rows) * 32, :] = field[pl.ds(start, rows * 32), :]
    for which, ref in enumerate(y_pair):
        low = odd(h) if which == 0 else jnp.logical_not(odd(h))
        start = jnp.where(low, 0, CY - rows)
        for c in range(rows):
            for part in range(4):
                at = (base + c) * 32 + part * 8
                ref[at : at + 8, :] = every(field, part * 8 * CY + start + c, CY)


def received(pair, which, end, at):
    value = pair[which][at : at + 8, :]
    return jnp.where(end, 0.0, value) if which == 1 else value


def pack_kernel(vel, den, deal, vel_in, den_in, out, in_sem, out_sem):
    pulls = []
    for part in range(4):
        rows = pl.ds(part * 256, 256)
        pulls.append(
            [
                pltpu.make_async_copy(src.at[rows], dst.at[rows], in_sem.at[part * 2 + i])
                for i, (src, dst) in enumerate(((vel, vel_in), (den, den_in)))
            ]
        )
        for pull in pulls[-1]:
            pull.start()
    pushes = []
    for part in range(4):
        for pull in pulls[part]:
            pull.wait()
        for row in range(part * 4, part * 4 + 4):
            for cls in range(8):
                at = (row * 8 + cls) * 16
                out[at : at + 8, :] = every(vel_in, row * 64 + cls, 8)
                out[at + 8 : at + 16, :] = every(den_in, row * 64 + cls, 8)
        rows = pl.ds(part * 512, 512)
        pushes.append(pltpu.make_async_copy(out.at[rows], deal.at[rows], out_sem.at[part]))
        pushes[-1].start()
    for push in pushes:
        push.wait()


def face_kernel(pres, flow_x, flow_y, gx_a, gx_b, gy_a, gy_b, pres_in, x_in, y_in, sem):
    pulls = [
        pltpu.make_async_copy(src, dst, sem.at[i])
        for i, (src, dst) in enumerate(((pres, pres_in), (flow_x, x_in), (flow_y, y_in)))
    ]
    for pull in pulls:
        pull.start()
    for pull in pulls:
        pull.wait()
    send_faces(pres_in, (gx_a, gx_b), (gy_a, gy_b), 0, HALO)
    send_faces(x_in, (gx_a, gx_b), (), HALO, 4)
    send_faces(y_in, (), (gy_a, gy_b), HALO, 4)


def cut_kernel(corners, dealt, out, rho_lines, vel_lines, cuts, sem):
    s, g, col_class = place()
    row_class = s * 4 + g
    for t in range(16):
        for part in range(8):
            src = (t * 8 + part) * 16
            dst = t * LINE + 8 + part * 8
            vel_lines[dst : dst + 8, :] = dealt[src : src + 8, :]
            rho_lines[dst : dst + 8, :] = dealt[src + 8 : src + 16, :]

    pushes = []
    for shot in range(4):
        corner_y = corners[shot, 1]

        def block(part, carry):
            corner_x = corners[shot, 0] + part * CX
            wide_row = lax.shift_right_arithmetic(corner_x - 4 - row_class + 15, 4)
            row = lax.shift_right_arithmetic(corner_x - row_class + 15, 4)
            for h in range(8):
                base = (shot * 32 + part * 8 + h) * 24
                wide_col = lax.shift_right_arithmetic(corner_y + h * CY - 4 - col_class + 7, 3)
                col = lax.shift_right_arithmetic(corner_y + h * CY - col_class + 7, 3)
                for k in range(3):
                    line = jnp.clip(wide_row + k, 0, 15)
                    cuts[pl.ds(base + 5 * k, 5), :] = rho_lines[
                        pl.ds(line * LINE + 8 + wide_col, 5), :
                    ]
                for k in range(2):
                    cuts[pl.ds(base + 16 + 4 * k, 4), :] = vel_lines[
                        pl.ds((row + k) * LINE + 8 + col, 4), :
                    ]
            return carry

        lax.fori_loop(0, 4, block, 0)
        rows = pl.ds(shot * 768, 768)
        pushes.append(pltpu.make_async_copy(cuts.at[rows], out.at[rows], sem.at[shot]))
        pushes[-1].start()
    for push in pushes:
        push.wait()


def unpack_model(corners, window, buoy, modu, rho, vel):
    s, g, h = place()
    corner_x = corners[s, 0] + g * CX
    corner_y = corners[s, 1] + h * CY
    wide_turn = lax.rem(8 - lax.rem(corner_y + 4, 8), 8)
    turn = lax.rem(8 - lax.rem(corner_y, 8), 8)
    sub = lax.broadcasted_iota(jnp.int32, (8, 128), 0)
    for w in range(WIDE):
        cls = lax.rem(corner_x + 12 + w, 16)
        row_in = (g * CX + w - 4 >= 0) & (g * CX + w - 4 < 4 * CX)
        for n in range(5):
            got = every(window, cls * 192 + 5 * (w // 16) + n, 24)
            got = pltpu.roll(got, wide_turn, 0)
            at = w * WIDE + n * 8
            rho[at : at + 8, :] = got
            col = sub + (h * CY + n * 8 - 4)
            inside = (col >= 0) & (col < 8 * CY) & row_in
            buoy[at : at + 8, :] = jnp.where(inside, time_step * (1.0 / got), 0.0)
    for w in range(CX):
        cls = lax.rem(corner_x + w, 16)
        for n in range(4):
            got = every(window, cls * 192 + 16 + 4 * (w // 16) + n, 24)
            speed = pltpu.roll(got, turn, 0)
            at = w * CY + n * 8
            dens = rho[(w + 4) * WIDE + 4 + n * 8 : (w + 4) * WIDE + 12 + n * 8, :]
            modu[at : at + 8, :] = time_step * (dens * speed * speed)


def buoy_at(buoy, x, y, rows=8):
    return buoy[pl.ds((x + 4) * WIDE + 4 + y, rows), :]


def grad0_kernel(
    mat_f, pres, gx_a, gx_b, gy_a, gy_b, in_x, in_y, grad_x, grad_y, grad_z, wide_x, wide_y, padded
):
    s, g, h = place()
    end_x = (g == 0) | (g == 3)
    end_y = (h == 0) | (h == 7)
    for x in range(CX):
        at = (x + 8) * PAD + 8
        padded[at : at + 32, :] = pres[x * CY : (x + 1) * CY, :]
        wide_y[x * WIDE + 4 : x * WIDE + 36, :] = in_y[x * CY : (x + 1) * CY, :]
    wide_x[4 * CY : 36 * CY, :] = in_x[...]
    x_pair, y_pair = (gx_a, gx_b), (gy_a, gy_b)
    for which in range(2):
        low = odd(g) if which == 0 else jnp.logical_not(odd(g))
        start = jnp.where(low, -HALO, CX)
        for i in range(HALO):
            for part in range(4):
                at = pl.multiple_of((start + i + 8) * PAD + 8 + part * 8, 8)
                padded[pl.ds(at, 8), :] = received(x_pair, which, end_x, i * 32 + part * 8)
        start = jnp.where(low, 0, 36)
        for i in range(4):
            for part in range(4):
                at = pl.multiple_of((start + i) * CY + part * 8, 8)
                wide_x[pl.ds(at, 8), :] = received(x_pair, which, end_x, (HALO + i) * 32 + part * 8)
        low = odd(h) if which == 0 else jnp.logical_not(odd(h))
        start = jnp.where(low, -HALO, CY)
        for c in range(HALO):
            for part in range(4):
                at = (part * 8 + 8) * PAD + start + c + 8
                put_every(padded, at, PAD, received(y_pair, which, end_y, c * 32 + part * 8))
        start = jnp.where(low, 0, 36)
        for c in range(4):
            for part in range(4):
                value = received(y_pair, which, end_y, (HALO + c) * 32 + part * 8)
                put_every(wide_y, part * 8 * WIDE + start + c, WIDE, value)

    def along_x(chunk, carry):
        x0 = chunk * 4 - 4
        for n in range(4):
            taps = [
                padded[pl.ds(pl.multiple_of((x0 + d + 8) * PAD + 8 + n * 8, 8), 8), :]
                for d in range(-3, 8)
            ]
            for i in range(4):
                at = pl.multiple_of((x0 + i + 4) * CY + n * 8, 8)
                grad_x[pl.ds(at, 8), :] = forward(taps, i)
        return carry

    lax.fori_loop(0, 10, along_x, 0)

    def along_y(x, carry):
        taps = [every(padded, (x + 8) * PAD + 4 + d, 5) for d in range(-3, 9)]
        for j in range(5):
            put_every(grad_y, x * WIDE + j, 5, forward(taps, j))
        return carry

    lax.fori_loop(0, CX, along_y, 0)
    for chunk in range(8):
        rows = slice(chunk * 128, (chunk + 1) * 128)
        grad_z[rows, :] = depth_difference(pres[rows, :], mat_f)


def kick_source(step, cells, amps, field):
    s, g, h = place()
    x = cells[s, 0] - g * CX
    y = cells[s, 1] - h * CY

    @pl.when((x >= 0) & (x < CX) & (y >= 0) & (y < CY))
    def _():
        at = x * CY + y
        lane = lax.broadcasted_iota(jnp.int32, (1, 128), 1)
        kick = time_step * amps[s, step]
        field[pl.ds(at, 1), :] = field[pl.ds(at, 1), :] + jnp.where(lane == cells[s, 2], kick, 0.0)


def step0_kernel(
    corners, cells, amps, mat_b, window, pres, in_x, in_y, in_z, grad_x, grad_y, grad_z,
    new_p, wide_x, wide_y, new_z, buoy, modu, gx_a, gx_b, gy_a, gy_b, rho, vel, spread,
):
    unpack_model(corners, window, buoy, modu, rho, vel)

    def flow(x, carry):
        for n in range(4):
            at = pl.multiple_of(x * CY + n * 8, 8)
            value = in_z[pl.ds(at, 8), :] - buoy_at(buoy, x, n * 8) * grad_z[pl.ds(at, 8), :]
            new_z[pl.ds(at, 8), :] = value
        for n in range(5):
            at = pl.multiple_of(x * WIDE + n * 8, 8)
            wide_y[pl.ds(at, 8), :] = (
                in_y[pl.ds(at, 8), :] - buoy_at(buoy, x, n * 8 - 4) * grad_y[pl.ds(at, 8), :]
            )
        return carry

    lax.fori_loop(0, CX, flow, 0, unroll=4)

    def flow_x(x, carry):
        for n in range(4):
            at = pl.multiple_of(x * CY + n * 8, 8)
            wide_x[pl.ds(at, 8), :] = (
                in_x[pl.ds(at, 8), :] - buoy_at(buoy, x - 4, n * 8) * grad_x[pl.ds(at, 8), :]
            )
        return carry

    lax.fori_loop(0, WIDE, flow_x, 0, unroll=4)
    for chunk in range(8):
        rows = slice(chunk * 128, (chunk + 1) * 128)
        spread[rows, :] = depth_difference(new_z[rows, :], mat_b)

    def update(chunk, carry):
        x0 = chunk * 4
        part_x = {}
        for j in range(4):
            taps = [every(wide_x, (x0 + d + 4) * CY + j, 4) for d in range(-4, 7)]
            for i in range(4):
                part_x[i, j] = backward(taps, i)
        for i in range(4):
            taps = [every(wide_y, (x0 + i) * WIDE + 4 + d, 4) for d in range(-4, 7)]
            for j in range(4):
                at = (x0 + i) * CY + j
                total = part_x[i, j] + backward(taps, j) + every(spread, at, 4)
                put_every(new_p, at, 4, every(pres, at, 4) - every(modu, at, 4) * total)
        return carry

    lax.fori_loop(0, 8, update, 0)
    kick_source(0, cells, amps, new_p)
    send_faces(new_p, (gx_a, gx_b), (gy_a, gy_b), 0, HALO)


def inner_kernel(mat_f, mat_b, pres, in_x, in_y, in_z, buoy, wide_x, wide_y, new_z, spread):
    for chunk in range(8):
        rows = slice(chunk * 128, (chunk + 1) * 128)
        grad = depth_difference(pres[rows, :], mat_f)
        light = jnp.concatenate(
            [buoy_at(buoy, x, 0, 32) for x in range(chunk * 4, chunk * 4 + 4)], axis=0
        )
        new_z[rows, :] = in_z[rows, :] - light * grad

    def along_x(chunk, carry):
        x0 = chunk * 4 + 4
        for n in range(4):
            taps = [
                pres[pl.ds(pl.multiple_of((x0 + d) * CY + n * 8, 8), 8), :] for d in range(-3, 8)
            ]
            for i in range(4):
                at = pl.multiple_of((x0 + i + 4) * CY + n * 8, 8)
                wide_x[pl.ds(at, 8), :] = in_x[pl.ds(at, 8), :] - buoy_at(
                    buoy, x0 + i, n * 8
                ) * forward(taps, i)
        return carry

    lax.fori_loop(0, 6, along_x, 0)

    def along_y(x, carry):
        taps = [every(pres, x * CY + 4 + d, 3) for d in range(-3, 7)]
        for j in range(3):
            at = x * WIDE + 8 + j
            light = every(buoy, (x + 4) * WIDE + 8 + j, 3)
            put_every(wide_y, at, 3, every(in_y, at, 3) - light * forward(taps, j))
        return carry

    lax.fori_loop(0, CX, along_y, 0, unroll=4)
    wide_x[0 : 8 * CY, :] = in_x[0 : 8 * CY, :]
    wide_x[32 * CY : 40 * CY, :] = in_x[32 * CY : 40 * CY, :]
    for x in range(CX):
        wide_y[x * WIDE : x * WIDE + 8, :] = in_y[x * WIDE : x * WIDE + 8, :]
        wide_y[x * WIDE + 32 : x * WIDE + 40, :] = in_y[x * WIDE + 32 : x * WIDE + 40, :]
    for chunk in range(8):
        rows = slice(chunk * 128, (chunk + 1) * 128)
        spread[rows, :] = depth_difference(new_z[rows, :], mat_b)

    def across(chunk, carry):
        x0 = chunk * 4 + 8
        for n in range(4):
            taps = [
                wide_x[pl.ds(pl.multiple_of((x0 + d + 4) * CY + n * 8, 8), 8), :]
                for d in range(-4, 7)
            ]
            for i in range(4):
                at = pl.multiple_of((x0 + i) * CY + n * 8, 8)
                spread[pl.ds(at, 8), :] = spread[pl.ds(at, 8), :] + backward(taps, i)
        return carry

    lax.fori_loop(0, 4, across, 0)

    def along(x, carry):
        taps = [every(wide_y, x * WIDE + 12 + d, 2) for d in range(-4, 5)]
        for j in range(2):
            at = x * CY + 8 + j
            put_every(spread, at, 2, every(spread, at, 2) + backward(taps, j))
        return carry

    lax.fori_loop(0, CX, along, 0, unroll=4)


def edge_kernel(step, *refs):
    cells, amps, pres, gx_a, gx_b, gy_a, gy_b, in_x, in_y, buoy, modu, spread = refs[:12]
    last = step == STEPS - 1
    if last:
        new_p, out_x, out_y, low_x, high_x, low_y, high_y, wide_x, wide_y = refs[12:]
    else:
        new_p, wide_x, wide_y, to_a, to_b, to_c, to_d, low_x, high_x, low_y, high_y = refs[12:]
    wide_x[8 * CY : 32 * CY, :] = in_x[8 * CY : 32 * CY, :]
    for x in range(CX):
        wide_y[x * WIDE + 8 : x * WIDE + 32, :] = in_y[x * WIDE + 8 : x * WIDE + 32, :]
    s, g, h = place()
    end_x = (g == 0) | (g == 3)
    end_y = (h == 0) | (h == 7)
    x_pair, y_pair = (gx_a, gx_b), (gy_a, gy_b)
    low_x[8 * CY : 16 * CY, :] = pres[0 : 8 * CY, :]
    high_x[0 : 8 * CY, :] = pres[24 * CY : 32 * CY, :]
    for x in range(CX):
        low_y[x * STRIP + 8 : x * STRIP + 16, :] = pres[x * CY : x * CY + 8, :]
        high_y[x * STRIP : x * STRIP + 8, :] = pres[x * CY + 24 : x * CY + 32, :]

    def place_x(which, ref, start):
        for i in range(HALO):
            for part in range(4):
                at = (start + i) * CY + part * 8
                ref[at : at + 8, :] = received(x_pair, which, end_x, i * 32 + part * 8)

    def place_y(which, ref, start):
        for c in range(HALO):
            for part in range(4):
                value = received(y_pair, which, end_y, c * 32 + part * 8)
                put_every(ref, part * 8 * STRIP + start + c, STRIP, value)

    for where, put, low, high in ((g, place_x, low_x, high_x), (h, place_y, low_y, high_y)):

        @pl.when(odd(where))
        def _():
            put(0, low, 1)
            put(1, high, 8)

        @pl.when(jnp.logical_not(odd(where)))
        def _():
            put(1, low, 1)
            put(0, high, 8)

    for strip, first in ((low_x, -4), (high_x, 28)):
        for half in range(2):
            for n in range(4):
                taps = [
                    strip[(half * 4 + 4 + d) * CY + n * 8 : (half * 4 + 4 + d) * CY + n * 8 + 8, :]
                    for d in range(-3, 8)
                ]
                for i in range(4):
                    x = first + half * 4 + i
                    at = (x + 4) * CY + n * 8
                    wide_x[at : at + 8, :] = in_x[at : at + 8, :] - buoy_at(
                        buoy, x, n * 8
                    ) * forward(taps, i)

    def rows(x0, with_x):
        part_x = {}
        if with_x:
            for n in range(4):
                taps = [
                    wide_x[pl.ds(pl.multiple_of((x0 + d + 4) * CY + n * 8, 8), 8), :]
                    for d in range(-4, 7)
                ]
                for i in range(4):
                    part_x[i, n] = backward(taps, i)
        for i in range(4):
            x = x0 + i
            for strip, col in ((low_y, 0), (high_y, 32)):
                taps = [strip[pl.ds(x * STRIP + 4 + d, 8), :] for d in range(-3, 5)]
                at = pl.multiple_of(x * WIDE + col, 8)
                wide_y[pl.ds(at, 8), :] = in_y[pl.ds(at, 8), :] - buoy_at(
                    buoy, x, col - 4
                ) * forward(taps, 0)
            for n in range(4):
                at = pl.multiple_of(x * CY + n * 8, 8)
                total = spread[pl.ds(at, 8), :]
                if n in (0, 3):
                    taps = [wide_y[pl.ds(x * WIDE + 4 + n * 8 + d, 8), :] for d in range(-4, 4)]
                    total = total + backward(taps, 0)
                if with_x:
                    total = total + part_x[i, n]
                new_p[pl.ds(at, 8), :] = pres[pl.ds(at, 8), :] - modu[pl.ds(at, 8), :] * total

    for first, count, with_x in ((0, 2, True), (8, 4, False), (24, 2, True)):

        def some(chunk, carry):
            rows(first + chunk * 4, with_x)
            return carry

        lax.fori_loop(0, count, some, 0)

    kick_source(step, cells, amps, new_p)
    if last:
        out_x[...] = wide_x[4 * CY : 36 * CY, :]
        for x in range(CX):
            out_y[x * CY : (x + 1) * CY, :] = wide_y[x * WIDE + 4 : x * WIDE + 36, :]
    else:
        send_faces(new_p, (to_a, to_b), (to_c, to_d), 0, HALO)


def shape(rows, dtype=f32):
    return jax.ShapeDtypeStruct((rows, 128), dtype)


def vmem(rows):
    return pltpu.VMEM((rows, 128), f32)


def call(kernel, outs, args, scratch, name, smem=0, inputs=pltpu.VMEM, outputs=pltpu.VMEM, cost=None):
    specs = [pl.BlockSpec(memory_space=pltpu.SMEM)] * smem + [
        pl.BlockSpec(memory_space=inputs)
    ] * (len(args) - smem)
    return pl.pallas_call(
        kernel,
        out_shape=outs,
        in_specs=specs,
        out_specs=[pl.BlockSpec(memory_space=outputs)] * len(outs),
        scratch_shapes=scratch,
        cost_estimate=cost,
        compiler_params=pltpu.CompilerParams(vmem_limit_bytes=24 * 1024 * 1024),
        name=name,
    )(*args)


x_swaps = ([(0, 1), (1, 0), (2, 3), (3, 2)], [(1, 2), (2, 1), (0, 3), (3, 0)])
y_swaps = (
    [(i, i ^ 1) for i in range(8)],
    [(1, 2), (2, 1), (3, 4), (4, 3), (5, 6), (6, 5), (7, 0), (0, 7)],
)


def exchange(faces):
    return [
        lax.ppermute(faces[0], "gx", x_swaps[0]),
        lax.ppermute(faces[1], "gx", x_swaps[1]),
        lax.ppermute(faces[2], "gy", y_swaps[0]),
        lax.ppermute(faces[3], "gy", y_swaps[1]),
    ]


def shards(velocity, density, offsets, pressure, vel_x, vel_y, vel_z, source_cells, wavelet):
    mat_f, mat_b = (jnp.asarray(m) for m in depth_matrices())
    vel = velocity.reshape(16 * 64, 128)
    den = density.reshape(16 * 64, 128)
    pres = pressure.reshape(CX * CY, 128)
    flow_x = vel_x.reshape(CX * CY, 128)
    flow_y = vel_y.reshape(CX * CY, 128)
    flow_z = vel_z.reshape(CX * CY, 128)
    block = shape(CX * CY)
    wide = shape(WIDE * CY)
    face = shape(HALO * 32)
    cost = pl.CostEstimate(flops=20_000_000, bytes_accessed=8_000_000, transcendentals=0)

    (deal,) = call(
        pack_kernel,
        [shape(128 * 16)],
        [vel, den],
        [vmem(1024), vmem(1024), vmem(2048), pltpu.SemaphoreType.DMA((8,)), pltpu.SemaphoreType.DMA((4,))],
        "pack",
        inputs=pl.ANY,
        outputs=pl.ANY,
    )
    dealt = lax.all_to_all(deal.reshape(128, 16, 128), DEVICES, 0, 0, tiled=True)
    faces = call(
        face_kernel,
        [shape((HALO + 4) * 32)] * 4,
        [pres, flow_x, flow_y],
        [vmem(1024)] * 3 + [pltpu.SemaphoreType.DMA((3,))],
        "first_faces",
        inputs=pl.ANY,
        cost=cost,
    )
    faces = exchange(faces)
    (cut,) = call(
        cut_kernel,
        [shape(128 * 24)],
        [offsets, dealt.reshape(128 * 16, 128)],
        [vmem(16 * LINE), vmem(16 * LINE), vmem(128 * 24), pltpu.SemaphoreType.DMA((4,))],
        "cut",
        smem=1,
        outputs=pl.ANY,
    )
    window = lax.all_to_all(cut.reshape(128, 24, 128), DEVICES, 0, 0, tiled=True)
    window = window.reshape(128 * 24, 128)
    grad_x, grad_y, grad_z, flow_x, flow_y = call(
        grad0_kernel,
        [wide, wide, block, wide, wide],
        [mat_f, pres] + list(faces) + [flow_x, flow_y],
        [vmem(PAD * PAD)],
        "step0_gradients",
        cost=cost,
    )
    pres, flow_x, flow_y, flow_z, buoy, modu, *faces = call(
        step0_kernel,
        [block, wide, wide, block, shape(WIDE * WIDE), block] + [face] * 4,
        [offsets, source_cells, wavelet, mat_b, window, pres, flow_x, flow_y, flow_z]
        + [grad_x, grad_y, grad_z],
        [vmem(WIDE * WIDE), vmem(CX * CY), vmem(CX * CY)],
        "step0",
        smem=3,
    )
    for step in range(1, STEPS):
        last = step == STEPS - 1
        faces = exchange(faces)
        flow_x, flow_y, flow_z, spread = call(
            inner_kernel,
            [wide, wide, block, block],
            [mat_f, mat_b, pres, flow_x, flow_y, flow_z, buoy],
            [],
            f"inner{step}",
            cost=cost,
        )
        pres, flow_x, flow_y, *faces = call(
            functools.partial(edge_kernel, step),
            [block, block, block] if last else [block, wide, wide] + [face] * 4,
            [source_cells, wavelet, pres, *faces, flow_x, flow_y, buoy, modu, spread],
            [vmem(16 * CY), vmem(16 * CY), vmem(CX * STRIP), vmem(CX * STRIP)]
            + ([vmem(WIDE * CY)] * 2 if last else []),
            f"edge{step}",
            smem=2,
        )
    return tuple(a.reshape(1, CX, CY, 128) for a in (pres, flow_x, flow_y, flow_z))


def solution(mesh):
    return jax.shard_map(
        shards,
        mesh=mesh,
        in_specs=(
            P(("shot", "gx"), "gy", None),
            P(("shot", "gx"), "gy", None),
            P(),
            P("shot", "gx", "gy", None),
            P("shot", "gx", "gy", None),
            P("shot", "gx", "gy", None),
            P("shot", "gx", "gy", None),
            P(),
            P(),
        ),
        out_specs=(
            P("shot", "gx", "gy", None),
            P("shot", "gx", "gy", None),
            P("shot", "gx", "gy", None),
            P("shot", "gx", "gy", None),
        ),
        check_vma=False,
    )
```

time: 136 us -> 125 us (0.919)
  the two profiles are of different devices: /device:TPU:16 before, /device:TPU:1 now
where the time goes in v2:
time: 125 us; the launch traced here: 124 us
  waiting for transfers between devices  54.2 us (43%)
  starting transfers between devices  35.7 us (29%)
  Pallas kernels  20.5 us (16%)
  local copies, waits for them, and re-layouts  12.8 us (10%)
    pallas_call x11, Pallas kernels, call(): pl.pallas_call(kernel, out_shape=outs, in_specs=specs, out_specs=[pl.Bloc...  20.5 us
    all_to_all x1, waiting for transfers between devices, shards(): lax.all_to_all(deal.reshape(128, 16, 128), DEVICES, 0, 0, tiled=True)  18.8 us
    ppermute x4, waiting for transfers between devices, exchange(): lax.ppermute(faces[1], 'gx', x_swaps[1])  17.9 us
    ppermute x4, waiting for transfers between devices, exchange(): lax.ppermute(faces[3], 'gy', y_swaps[1])  17.3 us
    unnamed x43, local copies, waits for them, and re-layouts  12.8 us
    all_to_all x1, starting transfers between devices, shards(): lax.all_to_all(deal.reshape(128, 16, 128), DEVICES, 0, 0, tiled=True)  11.5 us
    ppermute x4, starting transfers between devices, exchange(): lax.ppermute(faces[3], 'gy', y_swaps[1])  11.2 us
    all_to_all x1, starting transfers between devices, shards(): lax.all_to_all(cut.reshape(128, 24, 128), DEVICES, 0, 0, tiled=True)  4.97 us
  transfers between devices with their start and end apart: 18, of which 8 were waited for; matrix products, arithmetic and copies ran while one was open for 0% of the time, Pallas kernels for 6%

profile of v2, /device:TPU:1, one launch (start us, length us, event | category | flops | bytes accessed | tf_op | source)
XLA Modules:
  0.0 124.2 jit_solution(7136050091577882460)
XLA Ops:
  2.7 2.5 %pack.1 = f32[2048,128]{1,0:T(8,128)} custom-call(f32[1024,128]{1,0:T(8,128)S(1)} %bitcast.24, f32[1024,128]{1,0:T(8,128)S(1)} %bitcast.25), custom_call_target="tpu_custom_call" | custom-call | tf_op jit(solution)/shard_map/pack/pallas_call | solution.py:530
  5.2 11.5 %all-to-all-start = ((f32[128,16,128]{2,1,0:T(8,128)}), f32[128,16,128]{2,1,0:T(8,128)S(1)}, u32[]{:S(2)}, u32[]{:S(2)}) async-start(f32[128,16,128]{2,1,0:T(8,128)} %bitcast.2), calls=%async_computation | async-start | bytes 2097152 | tf_op jit(solution)/shard_map/all_to_all | solution.py:580
  16.8 18.8 %all-to-all-done = f32[128,16,128]{2,1,0:T(8,128)S(1)} async-done(((f32[128,16,128]{2,1,0:T(8,128)}), f32[128,16,128]{2,1,0:T(8,128)S(1)}, u32[]{:S(2)}, u32[]{:S(2)}) %all-to-all-start) | async-done | bytes 1048608 | tf_op jit(solution)/shard_map/all_to_all | solution.py:580
  35.6 2.2 %cut.1 = f32[3072,128]{1,0:T(8,128)} custom-call(s32[4,2]{1,0:T(4,128)S(1)} %copy.16.corners, f32[2048,128]{1,0:T(8,128)S(1)} %bitcast.18), custom_call_target="tpu_custom_call" | custom-call | tf_op jit(solution)/shard_map/cut/pallas_call | solution.py:530
  37.9 5.0 %all-to-all-start.1 = ((f32[128,24,128]{2,1,0:T(8,128)}), f32[128,24,128]{2,1,0:T(8,128)S(1)}, u32[]{:S(2)}, u32[]{:S(2)}) async-start(f32[128,24,128]{2,1,0:T(8,128)} %bitcast.4), calls=%async_computation.1 | async-start | bytes 3145728 | tf_op jit(solution)/shard_map/all_to_all | solution.py:600
  45.2 1.5 %collective-permute-start.2 = (f32[352,128]{1,0:T(8,128)S(1)}, f32[352,128]{1,0:T(8,128)S(1)}, u32[]{:S(2)}, u32[]{:S(2)}) collective-permute-start(f32[352,128]{1,0:T(8,128)S(1)} %get-tuple-element.54), channel_id=1, source_target_pairs={{0,1},{1,0},{2,3},{3,2},{4,5},{5,4},{6,7},{7,6},{8,9},{9,8},{10,11... | collective-permute-start | bytes 540680 | tf_op jit(solution)/shard_map/ppermute | solution.py:553
  46.7 4.3 %collective-permute-start.3 = (f32[352,128]{1,0:T(8,128)S(1)}, f32[352,128]{1,0:T(8,128)S(1)}, u32[]{:S(2)}, u32[]{:S(2)}) collective-permute-start(f32[352,128]{1,0:T(8,128)S(1)} %get-tuple-element.55), channel_id=1, source_target_pairs={{1,2},{2,1},{3,4},{4,3},{5,6},{6,5},{7,0},{0,7},{9,10},{10,9},{11,... | collective-permute-start | bytes 540680 | tf_op jit(solution)/shard_map/ppermute | solution.py:554
  51.0 15.1 %collective-permute-done.1.gx_b = f32[352,128]{1,0:T(8,128)S(1)} collective-permute-done((f32[352,128]{1,0:T(8,128)S(1)}, f32[352,128]{1,0:T(8,128)S(1)}, u32[]{:S(2)}, u32[]{:S(2)}) %collective-permute-start.1) | collective-permute-done | bytes 180256 | tf_op jit(solution)/shard_map/ppermute | solution.py:552
  66.3 7.1 %collective-permute-done.3.gy_b = f32[352,128]{1,0:T(8,128)S(1)} collective-permute-done((f32[352,128]{1,0:T(8,128)S(1)}, f32[352,128]{1,0:T(8,128)S(1)}, u32[]{:S(2)}, u32[]{:S(2)}) %collective-permute-start.3) | collective-permute-done | bytes 180256 | tf_op jit(solution)/shard_map/ppermute | solution.py:554
  73.4 1.4 %step0_gradients.1 = (f32[1280,128]{1,0:T(8,128)S(1)}, f32[1280,128]{1,0:T(8,128)S(1)}, f32[1024,128]{1,0:T(8,128)S(1)}, f32[1280,128]{1,0:T(8,128)S(1)}, f32[1280,128]{1,0:T(8,128)S(1)}) custom-call(bf16[384,128]{1,0:T(8,128)(2,1)S(1)} %copy-done.3, f32[1024,128]{1,0:T(8,128)S(1)} %bitcast.16, f32[352,128]{1,0:T(8,128)S(1)} %collective-permute-done.gx_a, ...), custom_call_target="tpu_custom_call" | custom-call | flops 20000000 | bytes 8000000 | tf_op jit(solution)/shard_map/step0_gradients/pallas_call | solution.py:530
  85.3 2.5 %step0.1 = (f32[1024,128]{1,0:T(8,128)S(1)}, f32[1280,128]{1,0:T(8,128)S(1)}, f32[1280,128]{1,0:T(8,128)S(1)}, f32[1024,128]{1,0:T(8,128)S(1)}, f32[1600,128]{1,...) custom-call(s32[4,2]{1,0:T(4,128)S(1)} %copy.16.corners, ...), custom_call_target="tpu_custom_call" | custom-call | tf_op jit(solution)/shard_map/step0/pallas_call | solution.py:530
  90.0 1.5 %inner1.1 = (f32[1280,128]{1,0:T(8,128)S(1)}, f32[1280,128]{1,0:T(8,128)S(1)}, f32[1024,128]{1,0:T(8,128)S(1)}, f32[1024,128]{1,0:T(8,128)S(1)}) custom-call(bf16[384,128]{1,0:T(8,128)(2,1)S(1)} %copy-done.3, bf16[384,128]{1,0:T(8,128)(2,1)S(1)} %copy-done.4, f32[1024,128]{1,0:T(8,128)S(1)} %get-tuple-element.61.pres.refs_2_, ...), custom_call_target="tpu_custom_call" | custom-call | flops 20000000 | bytes 8000000 | tf_op jit(solution)/shard_map/inner1/pallas_call | solution.py:530
  91.6 2.8 %collective-permute-done.5.refs_4_ = f32[224,128]{1,0:T(8,128)S(1)} collective-permute-done((f32[224,128]{1,0:T(8,128)S(1)}, f32[224,128]{1,0:T(8,128)S(1)}, u32[]{:S(2)}, u32[]{:S(2)}) %collective-permute-start.5) | collective-permute-done | bytes 114720 | tf_op jit(solution)/shard_map/ppermute | solution.py:552
  94.4 2.7 %collective-permute-done.7.refs_6_ = f32[224,128]{1,0:T(8,128)S(1)} collective-permute-done((f32[224,128]{1,0:T(8,128)S(1)}, f32[224,128]{1,0:T(8,128)S(1)}, u32[]{:S(2)}, u32[]{:S(2)}) %collective-permute-start.7) | collective-permute-done | bytes 114720 | tf_op jit(solution)/shard_map/ppermute | solution.py:554
  97.2 1.8 %edge1.1 = (f32[1024,128]{1,0:T(8,128)S(1)}, f32[1280,128]{1,0:T(8,128)S(1)}, f32[1280,128]{1,0:T(8,128)S(1)}, f32[224,128]{1,0:T(8,128)S(1)}, f32[224,128]{1,0:...) custom-call(s32[4,3]{1,0:T(4,128)S(1)} %copy-done.18, f32[4,4]{1,0:T(4,128)S(1)} %copy-done.19, ...), custom_call_target="tpu_custom_call" | custom-call | tf_op jit(solution)/shard_map/edge1/pallas_call | solution.py:530
  98.9 1.3 %collective-permute-start.8 = (f32[224,128]{1,0:T(8,128)S(1)}, f32[224,128]{1,0:T(8,128)S(1)}, u32[]{:S(2)}, u32[]{:S(2)}) collective-permute-start(f32[224,128]{1,0:T(8,128)S(1)} %get-tuple-element.75), channel_id=1, source_target_pairs={{0,8},{8,0},{16,24},{24,16},{1,9},{9,1},{17,25},{25,17},{2,10},{10... | collective-permute-start | bytes 344072 | tf_op jit(solution)/shard_map/ppermute | solution.py:551
  101.3 3.1 %collective-permute-start.11 = (f32[224,128]{1,0:T(8,128)S(1)}, f32[224,128]{1,0:T(8,128)S(1)}, u32[]{:S(2)}, u32[]{:S(2)}) collective-permute-start(f32[224,128]{1,0:T(8,128)S(1)} %get-tuple-element.78), channel_id=1, source_target_pairs={{1,2},{2,1},{3,4},{4,3},{5,6},{6,5},{7,0},{0,7},{9,10},{10,9},{11,... | collective-permute-start | bytes 344072 | tf_op jit(solution)/shard_map/ppermute | solution.py:554
  104.4 1.5 %inner2.1 = (f32[1280,128]{1,0:T(8,128)S(1)}, f32[1280,128]{1,0:T(8,128)S(1)}, f32[1024,128]{1,0:T(8,128)S(1)}, f32[1024,128]{1,0:T(8,128)S(1)}) custom-call(bf16[384,128]{1,0:T(8,128)(2,1)S(1)} %copy-done.3, bf16[384,128]{1,0:T(8,128)(2,1)S(1)} %copy-done.4, f32[1024,128]{1,0:T(8,128)S(1)} %get-tuple-element.74.pres.refs_2_, ...), custom_call_target="tpu_custom_call" | custom-call | flops 20000000 | bytes 8000000 | tf_op jit(solution)/shard_map/inner2/pallas_call | solution.py:530
  106.0 4.1 %collective-permute-done.11.refs_6_ = f32[224,128]{1,0:T(8,128)S(1)} collective-permute-done((f32[224,128]{1,0:T(8,128)S(1)}, f32[224,128]{1,0:T(8,128)S(1)}, u32[]{:S(2)}, u32[]{:S(2)}) %collective-permute-start.11) | collective-permute-done | bytes 114720 | tf_op jit(solution)/shard_map/ppermute | solution.py:554
  110.1 1.7 %edge2.1 = (f32[1024,128]{1,0:T(8,128)S(1)}, f32[1280,128]{1,0:T(8,128)S(1)}, f32[1280,128]{1,0:T(8,128)S(1)}, f32[224,128]{1,0:T(8,128)S(1)}, f32[224,128]{1,0:...) custom-call(s32[4,3]{1,0:T(4,128)S(1)} %copy-done.18, f32[4,4]{1,0:T(4,128)S(1)} %copy-done.19, ...), custom_call_target="tpu_custom_call" | custom-call | tf_op jit(solution)/shard_map/edge2/pallas_call | solution.py:530
  112.7 3.0 %collective-permute-start.15 = (f32[224,128]{1,0:T(8,128)S(1)}, f32[224,128]{1,0:T(8,128)S(1)}, u32[]{:S(2)}, u32[]{:S(2)}) collective-permute-start(f32[224,128]{1,0:T(8,128)S(1)} %get-tuple-element.89), channel_id=1, source_target_pairs={{1,2},{2,1},{3,4},{4,3},{5,6},{6,5},{7,0},{0,7},{9,10},{10,9},{11,... | collective-permute-start | bytes 344072 | tf_op jit(solution)/shard_map/ppermute | solution.py:554
  115.7 2.3 %inner3.1 = (f32[1280,128]{1,0:T(8,128)S(1)}, f32[1280,128]{1,0:T(8,128)S(1)}, f32[1024,128]{1,0:T(8,128)}, f32[1024,128]{1,0:T(8,128)S(1)}) custom-call(bf16[384,128]{1,0:T(8,128)(2,1)S(1)} %copy-done.3, bf16[384,128]{1,0:T(8,128)(2,1)S(1)} %copy-done.4, f32[1024,128]{1,0:T(8,128)S(1)} %get-tuple-element.85.pres.refs_2_, ...), custom_call_target="tpu_custom_call" | custom-call | flops 20000000 | bytes 8000000 | tf_op jit(solution)/shard_map/inner3/pallas_call | solution.py:530
  118.1 3.4 %collective-permute-done.15.refs_6_ = f32[224,128]{1,0:T(8,128)S(1)} collective-permute-done((f32[224,128]{1,0:T(8,128)S(1)}, f32[224,128]{1,0:T(8,128)S(1)}, u32[]{:S(2)}, u32[]{:S(2)}) %collective-permute-start.15) | collective-permute-done | bytes 114720 | tf_op jit(solution)/shard_map/ppermute | solution.py:554
  121.4 2.7 %edge3.1 = (f32[1024,128]{1,0:T(8,128)}, f32[1024,128]{1,0:T(8,128)}, f32[1024,128]{1,0:T(8,128)}) custom-call(s32[4,3]{1,0:T(4,128)S(1)} %copy-done.18, f32[4,4]{1,0:T(4,128)S(1)} %copy-done.19, f32[1024,128]{1,0:T(8,128)S(1)} %get-tuple-element.85.pres.refs_2_, f32[224,128]{1,0:T(8,128)S(1)} %collective-permute-done.12.refs_3_, ...), custom_call_target="tpu_custom_call" | custom-call | tf_op jit(solution)/shard_map/edge3/pallas_call | solution.py:530
  (66 shorter events, 19.5 us)
Async XLA Ops:
  5.2 11.5 %copy-start.20 = (s32[4,2]{0,1:T(2,128)S(1)}, s32[4,2]{0,1:T(2,128)}, u32[]{:S(2)}) copy-start(s32[4,2]{0,1:T(2,128)} %param.13) | copy-start | bytes 100
  5.2 30.4 %all-to-all-start = ((f32[128,16,128]{2,1,0:T(8,128)}), f32[128,16,128]{2,1,0:T(8,128)S(1)}, u32[]{:S(2)}, u32[]{:S(2)}) async-start(f32[128,16,128]{2,1,0:T(8,128)} %bitcast.2), calls=%async_computation | async-start | bytes 2097152 | tf_op jit(solution)/shard_map/all_to_all | solution.py:580
  37.8 5.0 %copy-start = (f32[1,32,32,128]{3,2,1,0:T(8,128)S(1)}, f32[1,32,32,128]{3,2,1,0:T(8,128)}, u32[]{:S(2)}) copy-start(f32[1,32,32,128]{3,2,1,0:T(8,128)} %param.14) | copy-start | bytes 1572868
  37.9 41.0 %all-to-all-start.1 = ((f32[128,24,128]{2,1,0:T(8,128)}), f32[128,24,128]{2,1,0:T(8,128)S(1)}, u32[]{:S(2)}, u32[]{:S(2)}) async-start(f32[128,24,128]{2,1,0:T(8,128)} %bitcast.4), calls=%async_computation.1 | async-start | bytes 3145728 | tf_op jit(solution)/shard_map/all_to_all | solution.py:600
  42.8 30.5 %copy-start.3 = (bf16[384,128]{1,0:T(8,128)(2,1)S(1)}, bf16[384,128]{1,0:T(8,128)(2,1)}, u32[]{:S(2)}) copy-start(bf16[384,128]{1,0:T(8,128)(2,1)} %constant.4.clone.mat_f) | copy-start | bytes 294916
  43.3 35.6 %copy-start.4 = (bf16[384,128]{1,0:T(8,128)(2,1)S(1)}, bf16[384,128]{1,0:T(8,128)(2,1)}, u32[]{:S(2)}) copy-start(bf16[384,128]{1,0:T(8,128)(2,1)} %constant.5.clone.mat_b) | copy-start | bytes 294916
  43.3 35.6 %copy-start.18 = (s32[4,3]{1,0:T(4,128)S(1)}, s32[4,3]{1,0:T(4,128)}, u32[]{:S(2)}) copy-start(s32[4,3]{1,0:T(4,128)} %refs_0_.5) | copy-start | bytes 148
  43.3 35.6 %copy-start.19 = (f32[4,4]{1,0:T(4,128)S(1)}, f32[4,4]{1,0:T(4,128)}, u32[]{:S(2)}) copy-start(f32[4,4]{1,0:T(4,128)} %refs_1_.5) | copy-start | bytes 196
  43.3 7.7 %collective-permute-start = (f32[352,128]{1,0:T(8,128)S(1)}, f32[352,128]{1,0:T(8,128)S(1)}, u32[]{:S(2)}, u32[]{:S(2)}) collective-permute-start(f32[352,128]{1,0:T(8,128)S(1)} %get-tuple-element.52), channel_id=1, source_target_pairs={{0,8},{8,0},{16,24},{24,16},{1,9},{9,1},{17,25},{25,17},{2,10},{10... | collective-permute-start | bytes 540680 | tf_op jit(solution)/shard_map/ppermute | solution.py:551
  44.6 21.5 %collective-permute-start.1 = (f32[352,128]{1,0:T(8,128)S(1)}, f32[352,128]{1,0:T(8,128)S(1)}, u32[]{:S(2)}, u32[]{:S(2)}) collective-permute-start(f32[352,128]{1,0:T(8,128)S(1)} %get-tuple-element.53), channel_id=1, source_target_pairs={{8,16},{16,8},{0,24},{24,0},{9,17},{17,9},{1,25},{25,1},{10,18},{1... | collective-permute-start | bytes 540680 | tf_op jit(solution)/shard_map/ppermute | solution.py:552
  45.2 21.0 %collective-permute-start.2 = (f32[352,128]{1,0:T(8,128)S(1)}, f32[352,128]{1,0:T(8,128)S(1)}, u32[]{:S(2)}, u32[]{:S(2)}) collective-permute-start(f32[352,128]{1,0:T(8,128)S(1)} %get-tuple-element.54), channel_id=1, source_target_pairs={{0,1},{1,0},{2,3},{3,2},{4,5},{5,4},{6,7},{7,6},{8,9},{9,8},{10,11... | collective-permute-start | bytes 540680 | tf_op jit(solution)/shard_map/ppermute | solution.py:553
  46.7 26.7 %collective-permute-start.3 = (f32[352,128]{1,0:T(8,128)S(1)}, f32[352,128]{1,0:T(8,128)S(1)}, u32[]{:S(2)}, u32[]{:S(2)}) collective-permute-start(f32[352,128]{1,0:T(8,128)S(1)} %get-tuple-element.55), channel_id=1, source_target_pairs={{1,2},{2,1},{3,4},{4,3},{5,6},{6,5},{7,0},{0,7},{9,10},{10,9},{11,... | collective-permute-start | bytes 540680 | tf_op jit(solution)/shard_map/ppermute | solution.py:554
  87.8 3.8 %collective-permute-start.4 = (f32[224,128]{1,0:T(8,128)S(1)}, f32[224,128]{1,0:T(8,128)S(1)}, u32[]{:S(2)}, u32[]{:S(2)}) collective-permute-start(f32[224,128]{1,0:T(8,128)S(1)} %get-tuple-element.62), channel_id=1, source_target_pairs={{0,8},{8,0},{16,24},{24,16},{1,9},{9,1},{17,25},{25,17},{2,10},{10... | collective-permute-start | bytes 344072 | tf_op jit(solution)/shard_map/ppermute | solution.py:551
  88.9 5.6 %collective-permute-start.5 = (f32[224,128]{1,0:T(8,128)S(1)}, f32[224,128]{1,0:T(8,128)S(1)}, u32[]{:S(2)}, u32[]{:S(2)}) collective-permute-start(f32[224,128]{1,0:T(8,128)S(1)} %get-tuple-element.63), channel_id=1, source_target_pairs={{8,16},{16,8},{0,24},{24,0},{9,17},{17,9},{1,25},{25,1},{10,18},{1... | collective-permute-start | bytes 344072 | tf_op jit(solution)/shard_map/ppermute | solution.py:552
  89.3 5.2 %collective-permute-start.6 = (f32[224,128]{1,0:T(8,128)S(1)}, f32[224,128]{1,0:T(8,128)S(1)}, u32[]{:S(2)}, u32[]{:S(2)}) collective-permute-start(f32[224,128]{1,0:T(8,128)S(1)} %get-tuple-element.64), channel_id=1, source_target_pairs={{0,1},{1,0},{2,3},{3,2},{4,5},{5,4},{6,7},{7,6},{8,9},{9,8},{10,11... | collective-permute-start | bytes 344072 | tf_op jit(solution)/shard_map/ppermute | solution.py:553
  89.3 7.9 %collective-permute-start.7 = (f32[224,128]{1,0:T(8,128)S(1)}, f32[224,128]{1,0:T(8,128)S(1)}, u32[]{:S(2)}, u32[]{:S(2)}) collective-permute-start(f32[224,128]{1,0:T(8,128)S(1)} %get-tuple-element.65), channel_id=1, source_target_pairs={{1,2},{2,1},{3,4},{4,3},{5,6},{6,5},{7,0},{0,7},{9,10},{10,9},{11,... | collective-permute-start | bytes 344072 | tf_op jit(solution)/shard_map/ppermute | solution.py:554
  98.9 7.0 %collective-permute-start.8 = (f32[224,128]{1,0:T(8,128)S(1)}, f32[224,128]{1,0:T(8,128)S(1)}, u32[]{:S(2)}, u32[]{:S(2)}) collective-permute-start(f32[224,128]{1,0:T(8,128)S(1)} %get-tuple-element.75), channel_id=1, source_target_pairs={{0,8},{8,0},{16,24},{24,16},{1,9},{9,1},{17,25},{25,17},{2,10},{10... | collective-permute-start | bytes 344072 | tf_op jit(solution)/shard_map/ppermute | solution.py:551
  100.3 5.7 %collective-permute-start.9 = (f32[224,128]{1,0:T(8,128)S(1)}, f32[224,128]{1,0:T(8,128)S(1)}, u32[]{:S(2)}, u32[]{:S(2)}) collective-permute-start(f32[224,128]{1,0:T(8,128)S(1)} %get-tuple-element.76), channel_id=1, source_target_pairs={{8,16},{16,8},{0,24},{24,0},{9,17},{17,9},{1,25},{25,1},{10,18},{1... | collective-permute-start | bytes 344072 | tf_op jit(solution)/shard_map/ppermute | solution.py:552
  101.3 4.6 %collective-permute-start.10 = (f32[224,128]{1,0:T(8,128)S(1)}, f32[224,128]{1,0:T(8,128)S(1)}, u32[]{:S(2)}, u32[]{:S(2)}) collective-permute-start(f32[224,128]{1,0:T(8,128)S(1)} %get-tuple-element.77), channel_id=1, source_target_pairs={{0,1},{1,0},{2,3},{3,2},{4,5},{5,4},{6,7},{7,6},{8,9},{9,8},{10,11... | collective-permute-start | bytes 344072 | tf_op jit(solution)/shard_map/ppermute | solution.py:553
  101.3 8.8 %collective-permute-start.11 = (f32[224,128]{1,0:T(8,128)S(1)}, f32[224,128]{1,0:T(8,128)S(1)}, u32[]{:S(2)}, u32[]{:S(2)}) collective-permute-start(f32[224,128]{1,0:T(8,128)S(1)} %get-tuple-element.78), channel_id=1, source_target_pairs={{1,2},{2,1},{3,4},{4,3},{5,6},{6,5},{7,0},{0,7},{9,10},{10,9},{11,... | collective-permute-start | bytes 344072 | tf_op jit(solution)/shard_map/ppermute | solution.py:554
  111.8 6.3 %collective-permute-start.12 = (f32[224,128]{1,0:T(8,128)S(1)}, f32[224,128]{1,0:T(8,128)S(1)}, u32[]{:S(2)}, u32[]{:S(2)}) collective-permute-start(f32[224,128]{1,0:T(8,128)S(1)} %get-tuple-element.86), channel_id=1, source_target_pairs={{0,8},{8,0},{16,24},{24,16},{1,9},{9,1},{17,25},{25,17},{2,10},{10... | collective-permute-start | bytes 344072 | tf_op jit(solution)/shard_map/ppermute | solution.py:551
  112.7 5.4 %collective-permute-start.13 = (f32[224,128]{1,0:T(8,128)S(1)}, f32[224,128]{1,0:T(8,128)S(1)}, u32[]{:S(2)}, u32[]{:S(2)}) collective-permute-start(f32[224,128]{1,0:T(8,128)S(1)} %get-tuple-element.87), channel_id=1, source_target_pairs={{8,16},{16,8},{0,24},{24,0},{9,17},{17,9},{1,25},{25,1},{10,18},{1... | collective-permute-start | bytes 344072 | tf_op jit(solution)/shard_map/ppermute | solution.py:552
  112.7 5.4 %collective-permute-start.14 = (f32[224,128]{1,0:T(8,128)S(1)}, f32[224,128]{1,0:T(8,128)S(1)}, u32[]{:S(2)}, u32[]{:S(2)}) collective-permute-start(f32[224,128]{1,0:T(8,128)S(1)} %get-tuple-element.88), channel_id=1, source_target_pairs={{0,1},{1,0},{2,3},{3,2},{4,5},{5,4},{6,7},{7,6},{8,9},{9,8},{10,11... | collective-permute-start | bytes 344072 | tf_op jit(solution)/shard_map/ppermute | solution.py:553
  112.7 8.7 %collective-permute-start.15 = (f32[224,128]{1,0:T(8,128)S(1)}, f32[224,128]{1,0:T(8,128)S(1)}, u32[]{:S(2)}, u32[]{:S(2)}) collective-permute-start(f32[224,128]{1,0:T(8,128)S(1)} %get-tuple-element.89), channel_id=1, source_target_pairs={{1,2},{2,1},{3,4},{4,3},{5,6},{6,5},{7,0},{0,7},{9,10},{10,9},{11,... | collective-permute-start | bytes 344072 | tf_op jit(solution)/shard_map/ppermute | solution.py:554
  (15 other events, 22.7 us)

commit v3 on v2

--- a/solution.py
+++ b/solution.py
@@ -145,7 +145,8 @@
     send_faces(y_in, (), (gy_a, gy_b), HALO, 4)
 
 
-def cut_kernel(corners, dealt, out, rho_lines, vel_lines, cuts, sem):
+def cut_kernel(corners, dealt, *refs):
+    out, rho_lines, vel_lines, cuts, sem = refs[-5:]
     s, g, col_class = place()
     row_class = s * 4 + g
     for t in range(16):
@@ -186,7 +187,7 @@
         push.wait()
 
 
-def unpack_model(corners, window, buoy, modu, rho, vel):
+def unpack_model(corners, window, buoy, modu, rho):
     s, g, h = place()
     corner_x = corners[s, 0] + g * CX
     corner_y = corners[s, 1] + h * CY
@@ -218,9 +219,18 @@
     return buoy[pl.ds((x + 4) * WIDE + 4 + y, rows), :]
 
 
-def grad0_kernel(
-    mat_f, pres, gx_a, gx_b, gy_a, gy_b, in_x, in_y, grad_x, grad_y, grad_z, wide_x, wide_y, padded
-):
+def pull_all(pairs, sem):
+    pulls = [pltpu.make_async_copy(src, dst, sem.at[i]) for i, (src, dst) in enumerate(pairs)]
+    for pull in pulls:
+        pull.start()
+    return pulls
+
+
+def grad0_kernel(mat_f, pres_from, gx_a, gx_b, gy_a, gy_b, x_from, y_from, *refs):
+    outs, scratch = refs[:5], refs[5:]
+    grad_x, grad_y, grad_z, wide_x, wide_y, padded, pres, in_x, in_y, in_sem, out_sem = scratch
+    for pull in pull_all(((pres_from, pres), (x_from, in_x), (y_from, in_y)), in_sem):
+        pull.wait()
     s, g, h = place()
     end_x = (g == 0) | (g == 3)
     end_y = (h == 0) | (h == 7)
@@ -278,14 +288,16 @@
     for chunk in range(8):
         rows = slice(chunk * 128, (chunk + 1) * 128)
         grad_z[rows, :] = depth_difference(pres[rows, :], mat_f)
-
-
-def kick_source(step, cells, amps, field):
+    for push in pull_all(zip(scratch[:5], outs), out_sem):
+        push.wait()
+
+
+def kick_source(step, cells, amps, field, first=0, end=CX):
     s, g, h = place()
     x = cells[s, 0] - g * CX
     y = cells[s, 1] - h * CY
 
-    @pl.when((x >= 0) & (x < CX) & (y >= 0) & (y < CY))
+    @pl.when((x >= first) & (x < end) & (y >= 0) & (y < CY))
     def _():
         at = x * CY + y
         lane = lax.broadcasted_iota(jnp.int32, (1, 128), 1)
@@ -293,11 +305,14 @@
         field[pl.ds(at, 1), :] = field[pl.ds(at, 1), :] + jnp.where(lane == cells[s, 2], kick, 0.0)
 
 
-def step0_kernel(
-    corners, cells, amps, mat_b, window, pres, in_x, in_y, in_z, grad_x, grad_y, grad_z,
-    new_p, wide_x, wide_y, new_z, buoy, modu, gx_a, gx_b, gy_a, gy_b, rho, vel, spread,
-):
-    unpack_model(corners, window, buoy, modu, rho, vel)
+def step0_kernel(corners, cells, amps, mat_b, window, *refs):
+    sources, outs, scratch = refs[:7], refs[7:17], refs[17:]
+    new_p, wide_x, wide_y, new_z, buoy, modu, gx_a, gx_b, gy_a, gy_b = outs
+    pres, in_x, in_y, in_z, grad_x, grad_y, grad_z, rho, spread, sem = scratch
+    pulls = pull_all(zip(sources, scratch[:7]), sem)
+    unpack_model(corners, window, buoy, modu, rho)
+    for pull in pulls:
+        pull.wait()
 
     def flow(x, carry):
         for n in range(4):
@@ -416,7 +431,13 @@
     cells, amps, pres, gx_a, gx_b, gy_a, gy_b, in_x, in_y, buoy, modu, spread = refs[:12]
     last = step == STEPS - 1
     if last:
-        new_p, out_x, out_y, low_x, high_x, low_y, high_y, wide_x, wide_y = refs[12:]
+        p_to, x_to, y_to, low_x, high_x, low_y, high_y, wide_x, wide_y, new_p, out_y, sem = refs[12:]
+        pushes = []
+
+        def push(src, dst, rows):
+            pushes.append(pltpu.make_async_copy(src, dst.at[rows], sem.at[len(pushes)]))
+            pushes[-1].start()
+
     else:
         new_p, wide_x, wide_y, to_a, to_b, to_c, to_d, low_x, high_x, low_y, high_y = refs[12:]
     wide_x[8 * CY : 32 * CY, :] = in_x[8 * CY : 32 * CY, :]
@@ -469,6 +490,9 @@
                     wide_x[at : at + 8, :] = in_x[at : at + 8, :] - buoy_at(
                         buoy, x, n * 8
                     ) * forward(taps, i)
+
+    if last:
+        push(wide_x.at[pl.ds(4 * CY, CX * CY)], x_to, pl.ds(0, CX * CY))
 
     def rows(x0, with_x):
         part_x = {}
@@ -505,13 +529,18 @@
             return carry
 
         lax.fori_loop(0, count, some, 0)
-
-    kick_source(step, cells, amps, new_p)
+        if last:
+            kick_source(step, cells, amps, new_p, first, first + count * 4)
+            for x in range(first, first + count * 4):
+                out_y[x * CY : (x + 1) * CY, :] = wide_y[x * WIDE + 4 : x * WIDE + 36, :]
+            part = pl.ds(first * CY, count * 4 * CY)
+            push(new_p.at[part], p_to, part)
+            push(out_y.at[part], y_to, part)
     if last:
-        out_x[...] = wide_x[4 * CY : 36 * CY, :]
-        for x in range(CX):
-            out_y[x * CY : (x + 1) * CY, :] = wide_y[x * WIDE + 4 : x * WIDE + 36, :]
+        for copy in pushes:
+            copy.wait()
     else:
+        kick_source(step, cells, amps, new_p)
         send_faces(new_p, (to_a, to_b), (to_c, to_d), 0, HALO)
 
 
@@ -523,10 +552,19 @@
     return pltpu.VMEM((rows, 128), f32)
 
 
-def call(kernel, outs, args, scratch, name, smem=0, inputs=pltpu.VMEM, outputs=pltpu.VMEM, cost=None):
-    specs = [pl.BlockSpec(memory_space=pltpu.SMEM)] * smem + [
-        pl.BlockSpec(memory_space=inputs)
-    ] * (len(args) - smem)
+def call(kernel, outs, args, scratch, name, smem=0, hbm=(), loose=(), to_hbm=False, cost=None):
+    spaces = [
+        pltpu.SMEM if i < smem else pltpu.HBM if i in hbm else pl.ANY if i in loose else pltpu.VMEM
+        for i in range(len(args))
+    ]
+    if to_hbm:
+        outs = [pltpu.HBM(out.shape, out.dtype) for out in outs]
+    outputs = pltpu.HBM if to_hbm else pltpu.VMEM
+    specs = [pl.BlockSpec(memory_space=space) for space in spaces]
+    args = [
+        pltpu.with_memory_space_constraint(arg, pltpu.HBM) if i in hbm else arg
+        for i, arg in enumerate(args)
+    ]
     return pl.pallas_call(
         kernel,
         out_shape=outs,
@@ -547,12 +585,11 @@
 
 
 def exchange(faces):
-    return [
-        lax.ppermute(faces[0], "gx", x_swaps[0]),
-        lax.ppermute(faces[1], "gx", x_swaps[1]),
-        lax.ppermute(faces[2], "gy", y_swaps[0]),
-        lax.ppermute(faces[3], "gy", y_swaps[1]),
-    ]
+    gy_b = lax.ppermute(faces[3], "gy", y_swaps[1])
+    gy_a = lax.ppermute(faces[2], "gy", y_swaps[0])
+    gx_b = lax.ppermute(faces[1], "gx", x_swaps[1])
+    gx_a = lax.ppermute(faces[0], "gx", x_swaps[0])
+    return [gx_a, gx_b, gy_a, gy_b]
 
 
 def shards(velocity, density, offsets, pressure, vel_x, vel_y, vel_z, source_cells, wavelet):
@@ -568,53 +605,61 @@
     face = shape(HALO * 32)
     cost = pl.CostEstimate(flops=20_000_000, bytes_accessed=8_000_000, transcendentals=0)
 
+    dma = pltpu.SemaphoreType.DMA
     (deal,) = call(
         pack_kernel,
         [shape(128 * 16)],
         [vel, den],
-        [vmem(1024), vmem(1024), vmem(2048), pltpu.SemaphoreType.DMA((8,)), pltpu.SemaphoreType.DMA((4,))],
+        [vmem(1024), vmem(1024), vmem(2048), dma((8,)), dma((4,))],
         "pack",
-        inputs=pl.ANY,
-        outputs=pl.ANY,
+        hbm=(0, 1),
+        to_hbm=True,
     )
     dealt = lax.all_to_all(deal.reshape(128, 16, 128), DEVICES, 0, 0, tiled=True)
     faces = call(
         face_kernel,
         [shape((HALO + 4) * 32)] * 4,
         [pres, flow_x, flow_y],
-        [vmem(1024)] * 3 + [pltpu.SemaphoreType.DMA((3,))],
+        [vmem(1024)] * 3 + [dma((3,))],
         "first_faces",
-        inputs=pl.ANY,
+        hbm=(0, 1, 2),
         cost=cost,
     )
     faces = exchange(faces)
     (cut,) = call(
         cut_kernel,
         [shape(128 * 24)],
-        [offsets, dealt.reshape(128 * 16, 128)],
-        [vmem(16 * LINE), vmem(16 * LINE), vmem(128 * 24), pltpu.SemaphoreType.DMA((4,))],
+        [offsets, dealt.reshape(128 * 16, 128), *faces],
+        [vmem(16 * LINE), vmem(16 * LINE), vmem(128 * 24), dma((4,))],
         "cut",
         smem=1,
-        outputs=pl.ANY,
+        loose=(2, 3, 4, 5),
+        to_hbm=True,
     )
     window = lax.all_to_all(cut.reshape(128, 24, 128), DEVICES, 0, 0, tiled=True)
     window = window.reshape(128 * 24, 128)
     grad_x, grad_y, grad_z, flow_x, flow_y = call(
         grad0_kernel,
         [wide, wide, block, wide, wide],
-        [mat_f, pres] + list(faces) + [flow_x, flow_y],
-        [vmem(PAD * PAD)],
+        [mat_f, pres, *faces, flow_x, flow_y],
+        [vmem(WIDE * CY)] * 2 + [vmem(CX * CY)] + [vmem(WIDE * CY)] * 2
+        + [vmem(PAD * PAD)] + [vmem(CX * CY)] * 3 + [dma((3,)), dma((5,))],
         "step0_gradients",
+        hbm=(1, 6, 7),
+        to_hbm=True,
         cost=cost,
     )
     pres, flow_x, flow_y, flow_z, buoy, modu, *faces = call(
         step0_kernel,
         [block, wide, wide, block, shape(WIDE * WIDE), block] + [face] * 4,
-        [offsets, source_cells, wavelet, mat_b, window, pres, flow_x, flow_y, flow_z]
-        + [grad_x, grad_y, grad_z],
-        [vmem(WIDE * WIDE), vmem(CX * CY), vmem(CX * CY)],
+        [offsets, source_cells, wavelet, mat_b, window]
+        + [pres, flow_x, flow_y, flow_z, grad_x, grad_y, grad_z],
+        [vmem(CX * CY), vmem(WIDE * CY), vmem(WIDE * CY), vmem(CX * CY)]
+        + [vmem(WIDE * CY), vmem(WIDE * CY), vmem(CX * CY)]
+        + [vmem(WIDE * WIDE), vmem(CX * CY), dma((7,))],
         "step0",
         smem=3,
+        hbm=range(5, 12),
     )
     for step in range(1, STEPS):
         last = step == STEPS - 1
@@ -632,9 +677,10 @@
             [block, block, block] if last else [block, wide, wide] + [face] * 4,
             [source_cells, wavelet, pres, *faces, flow_x, flow_y, buoy, modu, spread],
             [vmem(16 * CY), vmem(16 * CY), vmem(CX * STRIP), vmem(CX * STRIP)]
-            + ([vmem(WIDE * CY)] * 2 if last else []),
+            + ([vmem(WIDE * CY)] * 2 + [vmem(CX * CY)] * 2 + [dma((7,))] if last else []),
             f"edge{step}",
             smem=2,
+            to_hbm=last,
         )
     return tuple(a.reshape(1, CX, CY, 128) for a in (pres, flow_x, flow_y, flow_z))
 

time: 125 us -> 112 us (0.90)
  local copies, waits for them, and re-layouts: 12.8 us -> 0.12 us
  waiting for transfers between devices: 54.2 us -> 47 us
  Pallas kernels: 20.5 us -> 25.4 us
  starting transfers between devices: 35.7 us -> 38.4 us
    all_to_all x1, waiting for transfers between devices: 0.01 us -> 20 us  [shards(): lax.all_to_all(cut.reshape(128, 24, 128), DEVICES, 0, 0, tiled=True)]
    all_to_all x1, waiting for transfers between devices: 18.8 us -> 0.01 us  [shards(): lax.all_to_all(deal.reshape(128, 16, 128), DEVICES, 0, 0, tiled=True)]
    unnamed x43 -> x11, local copies, waits for them, and re-layouts: 12.8 us -> 0.12 us
    ppermute x16, waiting for transfers between devices: 35.4 us -> 26.9 us  [the longest x4 16.8 us: exchange(): gy_b = lax.ppermute(faces[3], 'gy', y_swaps[1])]
    pallas_call x11, Pallas kernels: 20.5 us -> 25.4 us  [call(): pl.pallas_call(kernel, out_shape=outs, in_specs=specs, out_specs=[pl.Bloc...]
    ppermute x16, starting transfers between devices: 19.3 us -> 21.9 us  [the longest x4 12.4 us: exchange(): gy_b = lax.ppermute(faces[3], 'gy', y_swaps[1])]
  transfers between devices with their start and end apart: 18 -> 18, of which waited for: 8 -> 10; matrix products, arithmetic and copies ran while one was open for 0% -> 0% of each run, Pallas kernels for 6% -> 10%
where the time goes in v3:
time: 112 us
  waiting for transfers between devices  47 us (42%)
  starting transfers between devices  38.4 us (34%)
  Pallas kernels  25.4 us (23%)
    pallas_call x11, Pallas kernels, call(): pl.pallas_call(kernel, out_shape=outs, in_specs=specs, out_specs=[pl.Bloc...  25.4 us
    all_to_all x1, waiting for transfers between devices, shards(): lax.all_to_all(cut.reshape(128, 24, 128), DEVICES, 0, 0, tiled=True)  20 us
    ppermute x4, waiting for transfers between devices, exchange(): gy_b = lax.ppermute(faces[3], 'gy', y_swaps[1])  16.8 us
    ppermute x4, starting transfers between devices, exchange(): gy_b = lax.ppermute(faces[3], 'gy', y_swaps[1])  12.4 us
    all_to_all x1, starting transfers between devices, shards(): lax.all_to_all(deal.reshape(128, 16, 128), DEVICES, 0, 0, tiled=True)  11.5 us
    ppermute x4, waiting for transfers between devices, exchange(): gx_b = lax.ppermute(faces[1], 'gx', x_swaps[1])  9.16 us
    ppermute x4, starting transfers between devices, exchange(): gx_a = lax.ppermute(faces[0], 'gx', x_swaps[0])  5.38 us
    all_to_all x1, starting transfers between devices, shards(): lax.all_to_all(cut.reshape(128, 24, 128), DEVICES, 0, 0, tiled=True)  5.03 us
  transfers between devices with their start and end apart: 18, of which 10 were waited for; matrix products, arithmetic and copies ran while one was open for 0% of the time, Pallas kernels for 10%

profile of v3, /device:TPU:1, one launch (start us, length us, event | category | flops | bytes accessed | tf_op | source)
XLA Modules:
  0.0 111.7 jit_solution(18205368962821012474)
XLA Ops:
  0.6 2.2 %pack.1 = f32[2048,128]{1,0:T(8,128)} custom-call(f32[1024,128]{1,0:T(8,128)} %bitcast.26, f32[1024,128]{1,0:T(8,128)} %bitcast.27), custom_call_target="tpu_custom_call" | custom-call | tf_op jit(solution)/shard_map/pack/pallas_call | solution.py:568
  2.8 11.5 %all-to-all-start = ((f32[128,16,128]{2,1,0:T(8,128)}), f32[128,16,128]{2,1,0:T(8,128)S(1)}, u32[]{:S(2)}, u32[]{:S(2)}) async-start(f32[128,16,128]{2,1,0:T(8,128)} %bitcast.20), calls=%async_computation | async-start | bytes 2097152 | tf_op jit(solution)/shard_map/all_to_all | solution.py:618
  14.3 1.6 %first_faces.1 = (f32[352,128]{1,0:T(8,128)S(1)}, f32[352,128]{1,0:T(8,128)S(1)}, f32[352,128]{1,0:T(8,128)S(1)}, f32[352,128]{1,0:T(8,128)S(1)}) custom-call(f32[1024,128]{1,0:T(8,128)} %bitcast.17, f32[1024,128]{1,0:T(8,128)} %bitcast.21, f32[1024,128]{1,0:T(8,128)} %bitcast.23), custom_call_target="tpu_custom_call" | custom-call | flops 20000000 | bytes 8000000 | tf_op jit(solution)/shard_map/first_faces/pallas_call | solution.py:568
  19.2 4.3 %collective-permute-start.3 = (f32[352,128]{1,0:T(8,128)S(1)}, f32[352,128]{1,0:T(8,128)S(1)}, u32[]{:S(2)}, u32[]{:S(2)}) collective-permute-start(f32[352,128]{1,0:T(8,128)S(1)} %get-tuple-element.55), channel_id=1, source_target_pairs={{1,2},{2,1},{3,4},{4,3},{5,6},{6,5},{7,0},{0,7},{9,10},{10,9},{11,... | collective-permute-start | bytes 540680 | tf_op jit(solution)/shard_map/ppermute | solution.py:588
  23.6 8.3 %collective-permute-done.1.refs_1_.gx_b = f32[352,128]{1,0:T(8,128)S(1)} collective-permute-done((f32[352,128]{1,0:T(8,128)S(1)}, f32[352,128]{1,0:T(8,128)S(1)}, u32[]{:S(2)}, u32[]{:S(2)}) %collective-permute-start.1) | collective-permute-done | bytes 180256 | tf_op jit(solution)/shard_map/ppermute | solution.py:590
  32.8 6.8 %collective-permute-done.3.refs_3_.gy_b = f32[352,128]{1,0:T(8,128)S(1)} collective-permute-done((f32[352,128]{1,0:T(8,128)S(1)}, f32[352,128]{1,0:T(8,128)S(1)}, u32[]{:S(2)}, u32[]{:S(2)}) %collective-permute-start.3) | collective-permute-done | bytes 180256 | tf_op jit(solution)/shard_map/ppermute | solution.py:588
  39.5 2.2 %cut.1 = f32[3072,128]{1,0:T(8,128)} custom-call(s32[4,2]{1,0:T(4,128)S(1)} %copy.16.corners, f32[2048,128]{1,0:T(8,128)S(1)} %bitcast.15, f32[352,128]{1,0:T(8,128)S(1)} %collective-permute-done.refs_0_.gx_a, f32[352,128]{1,0:T(8,128)S(1)} %collective-permute-done.1.refs_1_.gx_b, f32[352,128]{1,0:T(8,128)S(1)} %collective-permute-done.2.refs_2_.gy_a, ...), custom_call_target="tpu_custom_call" | custom-call | tf_op jit(solution)/shard_map/cut/pallas_call | solution.py:568
  41.7 5.0 %all-to-all-start.1 = ((f32[128,24,128]{2,1,0:T(8,128)}), f32[128,24,128]{2,1,0:T(8,128)S(1)}, u32[]{:S(2)}, u32[]{:S(2)}) async-start(f32[128,24,128]{2,1,0:T(8,128)} %bitcast.16), calls=%async_computation.1 | async-start | bytes 3145728 | tf_op jit(solution)/shard_map/all_to_all | solution.py:639
  46.8 4.3 %step0_gradients.1 = (f32[1280,128]{1,0:T(8,128)}, f32[1280,128]{1,0:T(8,128)}, f32[1024,128]{1,0:T(8,128)}, f32[1280,128]{1,0:T(8,128)}, f32[1280,128]{1,0:T(8,128)}) custom-call(bf16[384,128]{1,0:T(8,128)(2,1)S(1)} %copy-done, f32[1024,128]{1,0:T(8,128)} %bitcast.18, f32[352,128]{1,0:T(8,128)S(1)} %collective-permute-done.refs_0_.gx_a, ...), custom_call_target="tpu_custom_call" | custom-call | flops 20000000 | bytes 8000000 | tf_op jit(solution)/shard_map/step0_gradients/pallas_call | solution.py:568
  51.1 20.0 %all-to-all-done.1 = f32[128,24,128]{2,1,0:T(8,128)S(1)} async-done(((f32[128,24,128]{2,1,0:T(8,128)}), f32[128,24,128]{2,1,0:T(8,128)S(1)}, u32[]{:S(2)}, u32[]{:S(2)}) %all-to-all-start.1) | async-done | bytes 1572896 | tf_op jit(solution)/shard_map/all_to_all | solution.py:639
  71.2 4.3 %step0.1 = (f32[1024,128]{1,0:T(8,128)S(1)}, f32[1280,128]{1,0:T(8,128)S(1)}, f32[1280,128]{1,0:T(8,128)S(1)}, f32[1024,128]{1,0:T(8,128)S(1)}, f32[1600,128]{1,...) custom-call(s32[4,2]{1,0:T(4,128)S(1)} %copy.16.corners, ...), custom_call_target="tpu_custom_call" | custom-call | tf_op jit(solution)/shard_map/step0/pallas_call | solution.py:568
  75.5 1.5 %collective-permute-start.4 = (f32[224,128]{1,0:T(8,128)S(1)}, f32[224,128]{1,0:T(8,128)S(1)}, u32[]{:S(2)}, u32[]{:S(2)}) collective-permute-start(f32[224,128]{1,0:T(8,128)S(1)} %get-tuple-element.62), channel_id=1, source_target_pairs={{0,8},{8,0},{16,24},{24,16},{1,9},{9,1},{17,25},{25,17},{2,10},{10... | collective-permute-start | bytes 344072 | tf_op jit(solution)/shard_map/ppermute | solution.py:591
  77.5 2.5 %collective-permute-start.7 = (f32[224,128]{1,0:T(8,128)S(1)}, f32[224,128]{1,0:T(8,128)S(1)}, u32[]{:S(2)}, u32[]{:S(2)}) collective-permute-start(f32[224,128]{1,0:T(8,128)S(1)} %get-tuple-element.65), channel_id=1, source_target_pairs={{1,2},{2,1},{3,4},{4,3},{5,6},{6,5},{7,0},{0,7},{9,10},{10,9},{11,... | collective-permute-start | bytes 344072 | tf_op jit(solution)/shard_map/ppermute | solution.py:588
  80.1 1.5 %inner1.1 = (f32[1280,128]{1,0:T(8,128)S(1)}, f32[1280,128]{1,0:T(8,128)S(1)}, f32[1024,128]{1,0:T(8,128)S(1)}, f32[1024,128]{1,0:T(8,128)S(1)}) custom-call(bf16[384,128]{1,0:T(8,128)(2,1)S(1)} %copy-done, bf16[384,128]{1,0:T(8,128)(2,1)S(1)} %copy-done.1, f32[1024,128]{1,0:T(8,128)S(1)} %get-tuple-element.61.pres.refs_2_, ...), custom_call_target="tpu_custom_call" | custom-call | flops 20000000 | bytes 8000000 | tf_op jit(solution)/shard_map/inner1/pallas_call | solution.py:568
  82.4 3.0 %collective-permute-done.7.refs_6_ = f32[224,128]{1,0:T(8,128)S(1)} collective-permute-done((f32[224,128]{1,0:T(8,128)S(1)}, f32[224,128]{1,0:T(8,128)S(1)}, u32[]{:S(2)}, u32[]{:S(2)}) %collective-permute-start.7) | collective-permute-done | bytes 114720 | tf_op jit(solution)/shard_map/ppermute | solution.py:588
  85.4 1.6 %edge1.1 = (f32[1024,128]{1,0:T(8,128)S(1)}, f32[1280,128]{1,0:T(8,128)S(1)}, f32[1280,128]{1,0:T(8,128)S(1)}, f32[224,128]{1,0:T(8,128)S(1)}, f32[224,128]{1,0:...) custom-call(s32[4,3]{1,0:T(4,128)S(1)} %copy-done.2, f32[4,4]{1,0:T(4,128)S(1)} %copy-done.3, ...), custom_call_target="tpu_custom_call" | custom-call | tf_op jit(solution)/shard_map/edge1/pallas_call | solution.py:568
  89.8 2.5 %collective-permute-start.11 = (f32[224,128]{1,0:T(8,128)S(1)}, f32[224,128]{1,0:T(8,128)S(1)}, u32[]{:S(2)}, u32[]{:S(2)}) collective-permute-start(f32[224,128]{1,0:T(8,128)S(1)} %get-tuple-element.78), channel_id=1, source_target_pairs={{1,2},{2,1},{3,4},{4,3},{5,6},{6,5},{7,0},{0,7},{9,10},{10,9},{11,... | collective-permute-start | bytes 344072 | tf_op jit(solution)/shard_map/ppermute | solution.py:588
  92.3 1.5 %inner2.1 = (f32[1280,128]{1,0:T(8,128)S(1)}, f32[1280,128]{1,0:T(8,128)S(1)}, f32[1024,128]{1,0:T(8,128)S(1)}, f32[1024,128]{1,0:T(8,128)S(1)}) custom-call(bf16[384,128]{1,0:T(8,128)(2,1)S(1)} %copy-done, bf16[384,128]{1,0:T(8,128)(2,1)S(1)} %copy-done.1, f32[1024,128]{1,0:T(8,128)S(1)} %get-tuple-element.74.pres.refs_2_, ...), custom_call_target="tpu_custom_call" | custom-call | flops 20000000 | bytes 8000000 | tf_op jit(solution)/shard_map/inner2/pallas_call | solution.py:568
  94.1 3.6 %collective-permute-done.11.refs_6_ = f32[224,128]{1,0:T(8,128)S(1)} collective-permute-done((f32[224,128]{1,0:T(8,128)S(1)}, f32[224,128]{1,0:T(8,128)S(1)}, u32[]{:S(2)}, u32[]{:S(2)}) %collective-permute-start.11) | collective-permute-done | bytes 114720 | tf_op jit(solution)/shard_map/ppermute | solution.py:588
  97.7 1.6 %edge2.1 = (f32[1024,128]{1,0:T(8,128)S(1)}, f32[1280,128]{1,0:T(8,128)S(1)}, f32[1280,128]{1,0:T(8,128)S(1)}, f32[224,128]{1,0:T(8,128)S(1)}, f32[224,128]{1,0:...) custom-call(s32[4,3]{1,0:T(4,128)S(1)} %copy-done.2, f32[4,4]{1,0:T(4,128)S(1)} %copy-done.3, ...), custom_call_target="tpu_custom_call" | custom-call | tf_op jit(solution)/shard_map/edge2/pallas_call | solution.py:568
  100.7 3.1 %collective-permute-start.15 = (f32[224,128]{1,0:T(8,128)S(1)}, f32[224,128]{1,0:T(8,128)S(1)}, u32[]{:S(2)}, u32[]{:S(2)}) collective-permute-start(f32[224,128]{1,0:T(8,128)S(1)} %get-tuple-element.89), channel_id=1, source_target_pairs={{1,2},{2,1},{3,4},{4,3},{5,6},{6,5},{7,0},{0,7},{9,10},{10,9},{11,... | collective-permute-start | bytes 344072 | tf_op jit(solution)/shard_map/ppermute | solution.py:588
  103.8 2.3 %inner3.1 = (f32[1280,128]{1,0:T(8,128)S(1)}, f32[1280,128]{1,0:T(8,128)S(1)}, f32[1024,128]{1,0:T(8,128)}, f32[1024,128]{1,0:T(8,128)S(1)}) custom-call(bf16[384,128]{1,0:T(8,128)(2,1)S(1)} %copy-done, bf16[384,128]{1,0:T(8,128)(2,1)S(1)} %copy-done.1, f32[1024,128]{1,0:T(8,128)S(1)} %get-tuple-element.85.pres.refs_2_, ...), custom_call_target="tpu_custom_call" | custom-call | flops 20000000 | bytes 8000000 | tf_op jit(solution)/shard_map/inner3/pallas_call | solution.py:568
  106.1 3.4 %collective-permute-done.15.refs_6_ = f32[224,128]{1,0:T(8,128)S(1)} collective-permute-done((f32[224,128]{1,0:T(8,128)S(1)}, f32[224,128]{1,0:T(8,128)S(1)}, u32[]{:S(2)}, u32[]{:S(2)}) %collective-permute-start.15) | collective-permute-done | bytes 114720 | tf_op jit(solution)/shard_map/ppermute | solution.py:588
  109.5 2.3 %edge3.1 = (f32[1024,128]{1,0:T(8,128)}, f32[1024,128]{1,0:T(8,128)}, f32[1024,128]{1,0:T(8,128)}) custom-call(s32[4,3]{1,0:T(4,128)S(1)} %copy-done.2, f32[4,4]{1,0:T(4,128)S(1)} %copy-done.3, f32[1024,128]{1,0:T(8,128)S(1)} %get-tuple-element.85.pres.refs_2_, f32[224,128]{1,0:T(8,128)S(1)} %collective-permute-done.12.refs_3_, ...), custom_call_target="tpu_custom_call" | custom-call | tf_op jit(solution)/shard_map/edge3/pallas_call | solution.py:568
  (34 shorter events, 10.0 us)
Async XLA Ops:
  2.8 20.7 %copy-start.4 = (s32[4,2]{0,1:T(2,128)S(1)}, s32[4,2]{0,1:T(2,128)}, u32[]{:S(2)}) copy-start(s32[4,2]{0,1:T(2,128)} %param.13) | copy-start | bytes 100
  2.8 36.7 %all-to-all-start = ((f32[128,16,128]{2,1,0:T(8,128)}), f32[128,16,128]{2,1,0:T(8,128)S(1)}, u32[]{:S(2)}, u32[]{:S(2)}) async-start(f32[128,16,128]{2,1,0:T(8,128)} %bitcast.20), calls=%async_computation | async-start | bytes 2097152 | tf_op jit(solution)/shard_map/all_to_all | solution.py:618
  16.0 7.6 %collective-permute-start = (f32[352,128]{1,0:T(8,128)S(1)}, f32[352,128]{1,0:T(8,128)S(1)}, u32[]{:S(2)}, u32[]{:S(2)}) collective-permute-start(f32[352,128]{1,0:T(8,128)S(1)} %get-tuple-element.52), channel_id=1, source_target_pairs={{0,8},{8,0},{16,24},{24,16},{1,9},{9,1},{17,25},{25,17},{2,10},{10... | collective-permute-start | bytes 540680 | tf_op jit(solution)/shard_map/ppermute | solution.py:591
  17.1 14.8 %collective-permute-start.1 = (f32[352,128]{1,0:T(8,128)S(1)}, f32[352,128]{1,0:T(8,128)S(1)}, u32[]{:S(2)}, u32[]{:S(2)}) collective-permute-start(f32[352,128]{1,0:T(8,128)S(1)} %get-tuple-element.53), channel_id=1, source_target_pairs={{8,16},{16,8},{0,24},{24,0},{9,17},{17,9},{1,25},{25,1},{10,18},{1... | collective-permute-start | bytes 540680 | tf_op jit(solution)/shard_map/ppermute | solution.py:590
  17.8 14.9 %collective-permute-start.2 = (f32[352,128]{1,0:T(8,128)S(1)}, f32[352,128]{1,0:T(8,128)S(1)}, u32[]{:S(2)}, u32[]{:S(2)}) collective-permute-start(f32[352,128]{1,0:T(8,128)S(1)} %get-tuple-element.54), channel_id=1, source_target_pairs={{0,1},{1,0},{2,3},{3,2},{4,5},{5,4},{6,7},{7,6},{8,9},{9,8},{10,11... | collective-permute-start | bytes 540680 | tf_op jit(solution)/shard_map/ppermute | solution.py:589
  19.2 20.3 %collective-permute-start.3 = (f32[352,128]{1,0:T(8,128)S(1)}, f32[352,128]{1,0:T(8,128)S(1)}, u32[]{:S(2)}, u32[]{:S(2)}) collective-permute-start(f32[352,128]{1,0:T(8,128)S(1)} %get-tuple-element.55), channel_id=1, source_target_pairs={{1,2},{2,1},{3,4},{4,3},{5,6},{6,5},{7,0},{0,7},{9,10},{10,9},{11,... | collective-permute-start | bytes 540680 | tf_op jit(solution)/shard_map/ppermute | solution.py:588
  41.7 5.1 %copy-start = (bf16[384,128]{1,0:T(8,128)(2,1)S(1)}, bf16[384,128]{1,0:T(8,128)(2,1)}, u32[]{:S(2)}) copy-start(bf16[384,128]{1,0:T(8,128)(2,1)} %constant.4.clone.mat_f) | copy-start | bytes 294916
  41.7 29.5 %all-to-all-start.1 = ((f32[128,24,128]{2,1,0:T(8,128)}), f32[128,24,128]{2,1,0:T(8,128)S(1)}, u32[]{:S(2)}, u32[]{:S(2)}) async-start(f32[128,24,128]{2,1,0:T(8,128)} %bitcast.16), calls=%async_computation.1 | async-start | bytes 3145728 | tf_op jit(solution)/shard_map/all_to_all | solution.py:639
  46.7 24.4 %copy-start.1 = (bf16[384,128]{1,0:T(8,128)(2,1)S(1)}, bf16[384,128]{1,0:T(8,128)(2,1)}, u32[]{:S(2)}) copy-start(bf16[384,128]{1,0:T(8,128)(2,1)} %constant.5.clone.mat_b) | copy-start | bytes 294916
  46.8 24.4 %copy-start.2 = (s32[4,3]{1,0:T(4,128)S(1)}, s32[4,3]{1,0:T(4,128)}, u32[]{:S(2)}) copy-start(s32[4,3]{1,0:T(4,128)} %refs_0_.5) | copy-start | bytes 148
  46.8 24.4 %copy-start.3 = (f32[4,4]{1,0:T(4,128)S(1)}, f32[4,4]{1,0:T(4,128)}, u32[]{:S(2)}) copy-start(f32[4,4]{1,0:T(4,128)} %refs_1_.5) | copy-start | bytes 196
  75.5 6.2 %collective-permute-start.4 = (f32[224,128]{1,0:T(8,128)S(1)}, f32[224,128]{1,0:T(8,128)S(1)}, u32[]{:S(2)}, u32[]{:S(2)}) collective-permute-start(f32[224,128]{1,0:T(8,128)S(1)} %get-tuple-element.62), channel_id=1, source_target_pairs={{0,8},{8,0},{16,24},{24,16},{1,9},{9,1},{17,25},{25,17},{2,10},{10... | collective-permute-start | bytes 344072 | tf_op jit(solution)/shard_map/ppermute | solution.py:591
  77.0 5.4 %collective-permute-start.5 = (f32[224,128]{1,0:T(8,128)S(1)}, f32[224,128]{1,0:T(8,128)S(1)}, u32[]{:S(2)}, u32[]{:S(2)}) collective-permute-start(f32[224,128]{1,0:T(8,128)S(1)} %get-tuple-element.63), channel_id=1, source_target_pairs={{8,16},{16,8},{0,24},{24,0},{9,17},{17,9},{1,25},{25,1},{10,18},{1... | collective-permute-start | bytes 344072 | tf_op jit(solution)/shard_map/ppermute | solution.py:590
  77.0 5.4 %collective-permute-start.6 = (f32[224,128]{1,0:T(8,128)S(1)}, f32[224,128]{1,0:T(8,128)S(1)}, u32[]{:S(2)}, u32[]{:S(2)}) collective-permute-start(f32[224,128]{1,0:T(8,128)S(1)} %get-tuple-element.64), channel_id=1, source_target_pairs={{0,1},{1,0},{2,3},{3,2},{4,5},{5,4},{6,7},{7,6},{8,9},{9,8},{10,11... | collective-permute-start | bytes 344072 | tf_op jit(solution)/shard_map/ppermute | solution.py:589
  77.5 7.9 %collective-permute-start.7 = (f32[224,128]{1,0:T(8,128)S(1)}, f32[224,128]{1,0:T(8,128)S(1)}, u32[]{:S(2)}, u32[]{:S(2)}) collective-permute-start(f32[224,128]{1,0:T(8,128)S(1)} %get-tuple-element.65), channel_id=1, source_target_pairs={{1,2},{2,1},{3,4},{4,3},{5,6},{6,5},{7,0},{0,7},{9,10},{10,9},{11,... | collective-permute-start | bytes 344072 | tf_op jit(solution)/shard_map/ppermute | solution.py:588
  87.0 6.8 %collective-permute-start.8 = (f32[224,128]{1,0:T(8,128)S(1)}, f32[224,128]{1,0:T(8,128)S(1)}, u32[]{:S(2)}, u32[]{:S(2)}) collective-permute-start(f32[224,128]{1,0:T(8,128)S(1)} %get-tuple-element.75), channel_id=1, source_target_pairs={{0,8},{8,0},{16,24},{24,16},{1,9},{9,1},{17,25},{25,17},{2,10},{10... | collective-permute-start | bytes 344072 | tf_op jit(solution)/shard_map/ppermute | solution.py:591
  88.4 5.6 %collective-permute-start.9 = (f32[224,128]{1,0:T(8,128)S(1)}, f32[224,128]{1,0:T(8,128)S(1)}, u32[]{:S(2)}, u32[]{:S(2)}) collective-permute-start(f32[224,128]{1,0:T(8,128)S(1)} %get-tuple-element.76), channel_id=1, source_target_pairs={{8,16},{16,8},{0,24},{24,0},{9,17},{17,9},{1,25},{25,1},{10,18},{1... | collective-permute-start | bytes 344072 | tf_op jit(solution)/shard_map/ppermute | solution.py:590
  89.8 4.3 %collective-permute-start.10 = (f32[224,128]{1,0:T(8,128)S(1)}, f32[224,128]{1,0:T(8,128)S(1)}, u32[]{:S(2)}, u32[]{:S(2)}) collective-permute-start(f32[224,128]{1,0:T(8,128)S(1)} %get-tuple-element.77), channel_id=1, source_target_pairs={{0,1},{1,0},{2,3},{3,2},{4,5},{5,4},{6,7},{7,6},{8,9},{9,8},{10,11... | collective-permute-start | bytes 344072 | tf_op jit(solution)/shard_map/ppermute | solution.py:589
  89.8 7.9 %collective-permute-start.11 = (f32[224,128]{1,0:T(8,128)S(1)}, f32[224,128]{1,0:T(8,128)S(1)}, u32[]{:S(2)}, u32[]{:S(2)}) collective-permute-start(f32[224,128]{1,0:T(8,128)S(1)} %get-tuple-element.78), channel_id=1, source_target_pairs={{1,2},{2,1},{3,4},{4,3},{5,6},{6,5},{7,0},{0,7},{9,10},{10,9},{11,... | collective-permute-start | bytes 344072 | tf_op jit(solution)/shard_map/ppermute | solution.py:588
  99.4 6.7 %collective-permute-start.12 = (f32[224,128]{1,0:T(8,128)S(1)}, f32[224,128]{1,0:T(8,128)S(1)}, u32[]{:S(2)}, u32[]{:S(2)}) collective-permute-start(f32[224,128]{1,0:T(8,128)S(1)} %get-tuple-element.86), channel_id=1, source_target_pairs={{0,8},{8,0},{16,24},{24,16},{1,9},{9,1},{17,25},{25,17},{2,10},{10... | collective-permute-start | bytes 344072 | tf_op jit(solution)/shard_map/ppermute | solution.py:591
  100.7 5.4 %collective-permute-start.13 = (f32[224,128]{1,0:T(8,128)S(1)}, f32[224,128]{1,0:T(8,128)S(1)}, u32[]{:S(2)}, u32[]{:S(2)}) collective-permute-start(f32[224,128]{1,0:T(8,128)S(1)} %get-tuple-element.87), channel_id=1, source_target_pairs={{8,16},{16,8},{0,24},{24,0},{9,17},{17,9},{1,25},{25,1},{10,18},{1... | collective-permute-start | bytes 344072 | tf_op jit(solution)/shard_map/ppermute | solution.py:590
  100.7 5.4 %collective-permute-start.14 = (f32[224,128]{1,0:T(8,128)S(1)}, f32[224,128]{1,0:T(8,128)S(1)}, u32[]{:S(2)}, u32[]{:S(2)}) collective-permute-start(f32[224,128]{1,0:T(8,128)S(1)} %get-tuple-element.88), channel_id=1, source_target_pairs={{0,1},{1,0},{2,3},{3,2},{4,5},{5,4},{6,7},{7,6},{8,9},{9,8},{10,11... | collective-permute-start | bytes 344072 | tf_op jit(solution)/shard_map/ppermute | solution.py:589
  100.7 8.8 %collective-permute-start.15 = (f32[224,128]{1,0:T(8,128)S(1)}, f32[224,128]{1,0:T(8,128)S(1)}, u32[]{:S(2)}, u32[]{:S(2)}) collective-permute-start(f32[224,128]{1,0:T(8,128)S(1)} %get-tuple-element.89), channel_id=1, source_target_pairs={{1,2},{2,1},{3,4},{4,3},{5,6},{6,5},{7,0},{0,7},{9,10},{10,9},{11,... | collective-permute-start | bytes 344072 | tf_op jit(solution)/shard_map/ppermute | solution.py:588

commit v4 on v3

--- a/solution.py
+++ b/solution.py
@@ -103,7 +103,15 @@
     return jnp.where(end, 0.0, value) if which == 1 else value
 
 
-def pack_kernel(vel, den, deal, vel_in, den_in, out, in_sem, out_sem):
+def pull_all(pairs, sem):
+    pulls = [pltpu.make_async_copy(src, dst, sem.at[i]) for i, (src, dst) in enumerate(pairs)]
+    for pull in pulls:
+        pull.start()
+    return pulls
+
+
+def pack_kernel(vel, den, pres, flow_x, flow_y, deal, gy_b, gy_a, gx_b, gx_a, *scratch):
+    vel_in, den_in, pres_in, x_in, y_in, out, in_sem, field_sem, out_sem = scratch
     pulls = []
     for part in range(4):
         rows = pl.ds(part * 256, 256)
@@ -115,6 +123,7 @@
         )
         for pull in pulls[-1]:
             pull.start()
+    fields = pull_all(((pres, pres_in), (flow_x, x_in), (flow_y, y_in)), field_sem)
     pushes = []
     for part in range(4):
         for pull in pulls[part]:
@@ -127,22 +136,13 @@
         rows = pl.ds(part * 512, 512)
         pushes.append(pltpu.make_async_copy(out.at[rows], deal.at[rows], out_sem.at[part]))
         pushes[-1].start()
-    for push in pushes:
-        push.wait()
-
-
-def face_kernel(pres, flow_x, flow_y, gx_a, gx_b, gy_a, gy_b, pres_in, x_in, y_in, sem):
-    pulls = [
-        pltpu.make_async_copy(src, dst, sem.at[i])
-        for i, (src, dst) in enumerate(((pres, pres_in), (flow_x, x_in), (flow_y, y_in)))
-    ]
-    for pull in pulls:
-        pull.start()
-    for pull in pulls:
+    for pull in fields:
         pull.wait()
     send_faces(pres_in, (gx_a, gx_b), (gy_a, gy_b), 0, HALO)
     send_faces(x_in, (gx_a, gx_b), (), HALO, 4)
     send_faces(y_in, (), (gy_a, gy_b), HALO, 4)
+    for push in pushes:
+        push.wait()
 
 
 def cut_kernel(corners, dealt, *refs):
@@ -219,16 +219,21 @@
     return buoy[pl.ds((x + 4) * WIDE + 4 + y, rows), :]
 
 
-def pull_all(pairs, sem):
-    pulls = [pltpu.make_async_copy(src, dst, sem.at[i]) for i, (src, dst) in enumerate(pairs)]
-    for pull in pulls:
-        pull.start()
-    return pulls
-
-
-def grad0_kernel(mat_f, pres_from, gx_a, gx_b, gy_a, gy_b, x_from, y_from, *refs):
-    outs, scratch = refs[:5], refs[5:]
-    grad_x, grad_y, grad_z, wide_x, wide_y, padded, pres, in_x, in_y, in_sem, out_sem = scratch
+def depth_kernel(mat_f, pres_from, grad_to, pres, grad_z, sem):
+    pull = pltpu.make_async_copy(pres_from, pres, sem.at[0])
+    pull.start()
+    pull.wait()
+    for chunk in range(8):
+        rows = slice(chunk * 128, (chunk + 1) * 128)
+        grad_z[rows, :] = depth_difference(pres[rows, :], mat_f)
+    push = pltpu.make_async_copy(grad_z, grad_to, sem.at[1])
+    push.start()
+    push.wait()
+
+
+def grad0_kernel(pres_from, gy_b, gy_a, gx_b, gx_a, x_from, y_from, *refs):
+    outs, scratch = refs[:4], refs[4:]
+    grad_x, grad_y, wide_x, wide_y, padded, pres, in_x, in_y, in_sem, out_sem = scratch
     for pull in pull_all(((pres_from, pres), (x_from, in_x), (y_from, in_y)), in_sem):
         pull.wait()
     s, g, h = place()
@@ -285,10 +290,7 @@
         return carry
 
     lax.fori_loop(0, CX, along_y, 0)
-    for chunk in range(8):
-        rows = slice(chunk * 128, (chunk + 1) * 128)
-        grad_z[rows, :] = depth_difference(pres[rows, :], mat_f)
-    for push in pull_all(zip(scratch[:5], outs), out_sem):
+    for push in pull_all(zip(scratch[:4], outs), out_sem):
         push.wait()
 
 
@@ -307,26 +309,11 @@
 
 def step0_kernel(corners, cells, amps, mat_b, window, *refs):
     sources, outs, scratch = refs[:7], refs[7:17], refs[17:]
-    new_p, wide_x, wide_y, new_z, buoy, modu, gx_a, gx_b, gy_a, gy_b = outs
+    new_p, wide_x, wide_y, new_z, buoy, modu, gy_b, gy_a, gx_b, gx_a = outs
     pres, in_x, in_y, in_z, grad_x, grad_y, grad_z, rho, spread, sem = scratch
-    pulls = pull_all(zip(sources, scratch[:7]), sem)
+    order = (4, 1, 5, 2, 6, 3, 0)
+    pulls = pull_all([(sources[i], scratch[i]) for i in order], sem)
     unpack_model(corners, window, buoy, modu, rho)
-    for pull in pulls:
-        pull.wait()
-
-    def flow(x, carry):
-        for n in range(4):
-            at = pl.multiple_of(x * CY + n * 8, 8)
-            value = in_z[pl.ds(at, 8), :] - buoy_at(buoy, x, n * 8) * grad_z[pl.ds(at, 8), :]
-            new_z[pl.ds(at, 8), :] = value
-        for n in range(5):
-            at = pl.multiple_of(x * WIDE + n * 8, 8)
-            wide_y[pl.ds(at, 8), :] = (
-                in_y[pl.ds(at, 8), :] - buoy_at(buoy, x, n * 8 - 4) * grad_y[pl.ds(at, 8), :]
-            )
-        return carry
-
-    lax.fori_loop(0, CX, flow, 0, unroll=4)
 
     def flow_x(x, carry):
         for n in range(4):
@@ -336,10 +323,30 @@
             )
         return carry
 
-    lax.fori_loop(0, WIDE, flow_x, 0, unroll=4)
+    def flow_y(x, carry):
+        for n in range(5):
+            at = pl.multiple_of(x * WIDE + n * 8, 8)
+            wide_y[pl.ds(at, 8), :] = (
+                in_y[pl.ds(at, 8), :] - buoy_at(buoy, x, n * 8 - 4) * grad_y[pl.ds(at, 8), :]
+            )
+        return carry
+
+    def flow_z(x, carry):
+        for n in range(4):
+            at = pl.multiple_of(x * CY + n * 8, 8)
+            new_z[pl.ds(at, 8), :] = (
+                in_z[pl.ds(at, 8), :] - buoy_at(buoy, x, n * 8) * grad_z[pl.ds(at, 8), :]
+            )
+        return carry
+
+    for i, (some, count) in enumerate(((flow_x, WIDE), (flow_y, CX), (flow_z, CX))):
+        pulls[2 * i].wait()
+        pulls[2 * i + 1].wait()
+        lax.fori_loop(0, count, some, 0, unroll=4)
     for chunk in range(8):
         rows = slice(chunk * 128, (chunk + 1) * 128)
         spread[rows, :] = depth_difference(new_z[rows, :], mat_b)
+    pulls[6].wait()
 
     def update(chunk, carry):
         x0 = chunk * 4
@@ -428,7 +435,7 @@
 
 
 def edge_kernel(step, *refs):
-    cells, amps, pres, gx_a, gx_b, gy_a, gy_b, in_x, in_y, buoy, modu, spread = refs[:12]
+    cells, amps, pres, gy_b, gy_a, gx_b, gx_a, in_x, in_y, buoy, modu, spread = refs[:12]
     last = step == STEPS - 1
     if last:
         p_to, x_to, y_to, low_x, high_x, low_y, high_y, wide_x, wide_y, new_p, out_y, sem = refs[12:]
@@ -439,7 +446,7 @@
             pushes[-1].start()
 
     else:
-        new_p, wide_x, wide_y, to_a, to_b, to_c, to_d, low_x, high_x, low_y, high_y = refs[12:]
+        new_p, wide_x, wide_y, to_d, to_c, to_b, to_a, low_x, high_x, low_y, high_y = refs[12:]
     wide_x[8 * CY : 32 * CY, :] = in_x[8 * CY : 32 * CY, :]
     for x in range(CX):
         wide_y[x * WIDE + 8 : x * WIDE + 32, :] = in_y[x * WIDE + 8 : x * WIDE + 32, :]
@@ -552,14 +559,14 @@
     return pltpu.VMEM((rows, 128), f32)
 
 
-def call(kernel, outs, args, scratch, name, smem=0, hbm=(), loose=(), to_hbm=False, cost=None):
+def call(kernel, outs, args, scratch, name, smem=0, hbm=(), loose=(), to_hbm=(), cost=None):
     spaces = [
         pltpu.SMEM if i < smem else pltpu.HBM if i in hbm else pl.ANY if i in loose else pltpu.VMEM
         for i in range(len(args))
     ]
-    if to_hbm:
-        outs = [pltpu.HBM(out.shape, out.dtype) for out in outs]
-    outputs = pltpu.HBM if to_hbm else pltpu.VMEM
+    to_hbm = range(len(outs)) if to_hbm is True else to_hbm
+    outs = [pltpu.HBM(o.shape, o.dtype) if i in to_hbm else o for i, o in enumerate(outs)]
+    places = [pltpu.HBM if i in to_hbm else pltpu.VMEM for i in range(len(outs))]
     specs = [pl.BlockSpec(memory_space=space) for space in spaces]
     args = [
         pltpu.with_memory_space_constraint(arg, pltpu.HBM) if i in hbm else arg
@@ -569,7 +576,7 @@
         kernel,
         out_shape=outs,
         in_specs=specs,
-        out_specs=[pl.BlockSpec(memory_space=outputs)] * len(outs),
+        out_specs=[pl.BlockSpec(memory_space=place) for place in places],
         scratch_shapes=scratch,
         cost_estimate=cost,
         compiler_params=pltpu.CompilerParams(vmem_limit_bytes=24 * 1024 * 1024),
@@ -585,11 +592,12 @@
 
 
 def exchange(faces):
-    gy_b = lax.ppermute(faces[3], "gy", y_swaps[1])
-    gy_a = lax.ppermute(faces[2], "gy", y_swaps[0])
-    gx_b = lax.ppermute(faces[1], "gx", x_swaps[1])
-    gx_a = lax.ppermute(faces[0], "gx", x_swaps[0])
-    return [gx_a, gx_b, gy_a, gy_b]
+    return [
+        lax.ppermute(faces[0], "gy", y_swaps[1]),
+        lax.ppermute(faces[1], "gy", y_swaps[0]),
+        lax.ppermute(faces[2], "gx", x_swaps[1]),
+        lax.ppermute(faces[3], "gx", x_swaps[0]),
+    ]
 
 
 def shards(velocity, density, offsets, pressure, vel_x, vel_y, vel_z, source_cells, wavelet):
@@ -604,50 +612,52 @@
     wide = shape(WIDE * CY)
     face = shape(HALO * 32)
     cost = pl.CostEstimate(flops=20_000_000, bytes_accessed=8_000_000, transcendentals=0)
+    long = pl.CostEstimate(flops=10**12, bytes_accessed=8_000_000, transcendentals=0)
 
     dma = pltpu.SemaphoreType.DMA
-    (deal,) = call(
+    deal, *faces = call(
         pack_kernel,
-        [shape(128 * 16)],
-        [vel, den],
-        [vmem(1024), vmem(1024), vmem(2048), dma((8,)), dma((4,))],
+        [shape(128 * 16)] + [shape((HALO + 4) * 32)] * 4,
+        [vel, den, pres, flow_x, flow_y],
+        [vmem(1024)] * 5 + [vmem(2048), dma((8,)), dma((3,)), dma((4,))],
         "pack",
-        hbm=(0, 1),
-        to_hbm=True,
-    )
-    dealt = lax.all_to_all(deal.reshape(128, 16, 128), DEVICES, 0, 0, tiled=True)
-    faces = call(
-        face_kernel,
-        [shape((HALO + 4) * 32)] * 4,
-        [pres, flow_x, flow_y],
-        [vmem(1024)] * 3 + [dma((3,))],
-        "first_faces",
-        hbm=(0, 1, 2),
-        cost=cost,
+        hbm=range(5),
+        to_hbm=(0,),
     )
     faces = exchange(faces)
+    dealt = lax.all_to_all(deal.reshape(128, 16, 128), DEVICES, 0, 0, tiled=True)
+    (grad_z,) = call(
+        depth_kernel,
+        [block],
+        [mat_f, pres],
+        [vmem(CX * CY), vmem(CX * CY), dma((2,))],
+        "step0_depth",
+        hbm=(1,),
+        to_hbm=True,
+        cost=long,
+    )
     (cut,) = call(
         cut_kernel,
         [shape(128 * 24)],
-        [offsets, dealt.reshape(128 * 16, 128), *faces],
+        [offsets, dealt.reshape(128 * 16, 128), grad_z],
         [vmem(16 * LINE), vmem(16 * LINE), vmem(128 * 24), dma((4,))],
         "cut",
         smem=1,
-        loose=(2, 3, 4, 5),
+        loose=(2,),
         to_hbm=True,
     )
     window = lax.all_to_all(cut.reshape(128, 24, 128), DEVICES, 0, 0, tiled=True)
     window = window.reshape(128 * 24, 128)
-    grad_x, grad_y, grad_z, flow_x, flow_y = call(
+    grad_x, grad_y, flow_x, flow_y = call(
         grad0_kernel,
-        [wide, wide, block, wide, wide],
-        [mat_f, pres, *faces, flow_x, flow_y],
-        [vmem(WIDE * CY)] * 2 + [vmem(CX * CY)] + [vmem(WIDE * CY)] * 2
-        + [vmem(PAD * PAD)] + [vmem(CX * CY)] * 3 + [dma((3,)), dma((5,))],
+        [wide, wide, wide, wide],
+        [pres, *faces, flow_x, flow_y],
+        [vmem(WIDE * CY)] * 4
+        + [vmem(PAD * PAD)] + [vmem(CX * CY)] * 3 + [dma((3,)), dma((4,))],
         "step0_gradients",
-        hbm=(1, 6, 7),
+        hbm=(0, 5, 6),
         to_hbm=True,
-        cost=cost,
+        cost=long,
     )
     pres, flow_x, flow_y, flow_z, buoy, modu, *faces = call(
         step0_kernel,
@@ -680,7 +690,7 @@
             + ([vmem(WIDE * CY)] * 2 + [vmem(CX * CY)] * 2 + [dma((7,))] if last else []),
             f"edge{step}",
             smem=2,
-            to_hbm=last,
+            to_hbm=last or (),
         )
     return tuple(a.reshape(1, CX, CY, 128) for a in (pres, flow_x, flow_y, flow_z))
 

time: 112 us -> 108 us (0.964)
  the two profiles are of different devices: /device:TPU:1 before, /device:TPU:16 now
where the time goes in v4:
time: 108 us; the launch traced here: 106 us
  starting transfers between devices  38.2 us (35%)
  waiting for transfers between devices  36.8 us (34%)
  Pallas kernels  29 us (27%)
  local copies, waits for them, and re-layouts  1.18 us (1%)
    pallas_call x11, Pallas kernels, call(): pl.pallas_call(kernel, out_shape=outs, in_specs=specs, out_specs=[pl.Bloc...  29 us
    all_to_all x1, waiting for transfers between devices, shards(): lax.all_to_all(cut.reshape(128, 24, 128), DEVICES, 0, 0, tiled=True)  17.1 us
    ppermute x4, starting transfers between devices, exchange(): lax.ppermute(faces[0], 'gy', y_swaps[1])  11.5 us
    all_to_all x1, starting transfers between devices, shards(): lax.all_to_all(deal.reshape(128, 16, 128), DEVICES, 0, 0, tiled=True)  10.8 us
    ppermute x4, waiting for transfers between devices, exchange(): lax.ppermute(faces[0], 'gy', y_swaps[1])  10.8 us
    all_to_all x1, waiting for transfers between devices, shards(): lax.all_to_all(deal.reshape(128, 16, 128), DEVICES, 0, 0, tiled=True)  8.9 us
    all_to_all x1, starting transfers between devices, shards(): lax.all_to_all(cut.reshape(128, 24, 128), DEVICES, 0, 0, tiled=True)  8.75 us
    ppermute x4, starting transfers between devices, exchange(): lax.ppermute(faces[2], 'gx', x_swaps[1])  3.71 us
  transfers between devices with their start and end apart: 18, of which 5 were waited for; matrix products, arithmetic and copies ran while one was open for 0% of the time, Pallas kernels for 15%

profile of v4, /device:TPU:16, one launch (start us, length us, event | category | flops | bytes accessed | tf_op | source)
XLA Modules:
  0.0 106.1 jit_solution(14780012753856309632)
XLA Ops:
  0.6 3.3 %pack.1 = (f32[2048,128]{1,0:T(8,128)}, f32[352,128]{1,0:T(8,128)}, f32[352,128]{1,0:T(8,128)}, f32[352,128]{1,0:T(8,128)}, f32[352,128]{1,0:T(8,128)}) custom-call(f32[1024,128]{1,0:T(8,128)} %bitcast.20, f32[1024,128]{1,0:T(8,128)} %bitcast.21, f32[1024,128]{1,0:T(8,128)} %bitcast.15, f32[1024,128]{1,0:T(8,128)} %bitcast.22, f32[1024,128]{1,0:T(8,128)} %bitcast.24), custom_call_target="tpu_custom_call" | custom-call | tf_op jit(solution)/shard_map/pack/pallas_call | solution.py:575
  4.0 10.8 %all-to-all-start = ((f32[128,16,128]{2,1,0:T(8,128)}), f32[128,16,128]{2,1,0:T(8,128)}, u32[]{:S(2)}, u32[]{:S(2)}) async-start(f32[128,16,128]{2,1,0:T(8,128)} %bitcast.19), calls=%async_computation | async-start | bytes 2097152 | tf_op jit(solution)/shard_map/all_to_all | solution.py:628
  14.8 3.4 %collective-permute-start = (f32[352,128]{1,0:T(8,128)}, f32[352,128]{1,0:T(8,128)}, u32[]{:S(2)}, u32[]{:S(2)}) collective-permute-start(f32[352,128]{1,0:T(8,128)} %get-tuple-element.53), channel_id=1, source_target_pairs={{1,2},{2,1},{3,4},{4,3},{5,6},{6,5},{7,0},{0,7},{9,10},{10,9},{11,... | collective-permute-start | bytes 540680 | tf_op jit(solution)/shard_map/ppermute | solution.py:596
  18.3 1.5 %collective-permute-start.2 = (f32[352,128]{1,0:T(8,128)}, f32[352,128]{1,0:T(8,128)}, u32[]{:S(2)}, u32[]{:S(2)}) collective-permute-start(f32[352,128]{1,0:T(8,128)} %get-tuple-element.55), channel_id=1, source_target_pairs={{8,16},{16,8},{0,24},{24,0},{9,17},{17,9},{1,25},{25,1},{10,18},{1... | collective-permute-start | bytes 540680 | tf_op jit(solution)/shard_map/ppermute | solution.py:598
  20.5 2.2 %step0_depth.1.refs_0_.refs_6_ = f32[1024,128]{1,0:T(8,128)} custom-call(bf16[384,128]{1,0:T(8,128)(2,1)S(1)} %copy-done.2, f32[1024,128]{1,0:T(8,128)} %bitcast.16), custom_call_target="tpu_custom_call" | custom-call | flops 999999995904 | bytes 8000000 | tf_op jit(solution)/shard_map/step0_depth/pallas_call | solution.py:575
  22.8 8.9 %all-to-all-done = f32[128,16,128]{2,1,0:T(8,128)} async-done(((f32[128,16,128]{2,1,0:T(8,128)}), f32[128,16,128]{2,1,0:T(8,128)}, u32[]{:S(2)}, u32[]{:S(2)}) %all-to-all-start) | async-done | bytes 1048608 | tf_op jit(solution)/shard_map/all_to_all | solution.py:628
  32.7 2.8 %cut.1 = f32[3072,128]{1,0:T(8,128)} custom-call(s32[4,2]{1,0:T(4,128)S(1)} %copy.16.corners, f32[2048,128]{1,0:T(8,128)} %bitcast.6.dealt, f32[1024,128]{1,0:T(8,128)S(1)} %copy-done), custom_call_target="tpu_custom_call" | custom-call | tf_op jit(solution)/shard_map/cut/pallas_call | solution.py:575
  35.6 8.7 %all-to-all-start.1 = ((f32[128,24,128]{2,1,0:T(8,128)}), f32[128,24,128]{2,1,0:T(8,128)}, u32[]{:S(2)}, u32[]{:S(2)}) async-start(f32[128,24,128]{2,1,0:T(8,128)} %bitcast.14), calls=%async_computation.1 | async-start | bytes 3145728 | tf_op jit(solution)/shard_map/all_to_all | solution.py:649
  44.4 5.1 %step0_gradients.1 = (f32[1280,128]{1,0:T(8,128)}, f32[1280,128]{1,0:T(8,128)}, f32[1280,128]{1,0:T(8,128)}, f32[1280,128]{1,0:T(8,128)}) custom-call(f32[1024,128]{1,0:T(8,128)} %bitcast.17, f32[352,128]{1,0:T(8,128)} %collective-permute-done.gy_b, f32[352,128]{1,0:T(8,128)} %collective-permute-done.1.gy_a, f32[352,128]{1,0:T(8,128)} %collective-permute-done.2.gx_b, ...), custom_call_target="tpu_custom_call" | custom-call | flops 999999995904 | bytes 8000000 | tf_op jit(solution)/shard_map/step0_gradients/pallas_call | solution.py:575
  49.5 17.1 %all-to-all-done.1 = f32[128,24,128]{2,1,0:T(8,128)} async-done(((f32[128,24,128]{2,1,0:T(8,128)}), f32[128,24,128]{2,1,0:T(8,128)}, u32[]{:S(2)}, u32[]{:S(2)}) %all-to-all-start.1) | async-done | bytes 1572896 | tf_op jit(solution)/shard_map/all_to_all | solution.py:649
  66.7 4.7 %step0.1 = (f32[1024,128]{1,0:T(8,128)S(1)}, f32[1280,128]{1,0:T(8,128)S(1)}, f32[1280,128]{1,0:T(8,128)S(1)}, f32[1024,128]{1,0:T(8,128)S(1)}, f32[1600,128]{1,...) custom-call(s32[4,2]{1,0:T(4,128)S(1)} %copy-done.7, ...), custom_call_target="tpu_custom_call" | custom-call | tf_op jit(solution)/shard_map/step0/pallas_call | solution.py:575
  71.4 2.9 %collective-permute-start.4 = (f32[224,128]{1,0:T(8,128)S(1)}, f32[224,128]{1,0:T(8,128)S(1)}, u32[]{:S(2)}, u32[]{:S(2)}) collective-permute-start(f32[224,128]{1,0:T(8,128)S(1)} %get-tuple-element.62), channel_id=1, source_target_pairs={{1,2},{2,1},{3,4},{4,3},{5,6},{6,5},{7,0},{0,7},{9,10},{10,9},{11,... | collective-permute-start | bytes 344072 | tf_op jit(solution)/shard_map/ppermute | solution.py:596
  74.4 1.4 %collective-permute-start.7 = (f32[224,128]{1,0:T(8,128)S(1)}, f32[224,128]{1,0:T(8,128)S(1)}, u32[]{:S(2)}, u32[]{:S(2)}) collective-permute-start(f32[224,128]{1,0:T(8,128)S(1)} %get-tuple-element.65), channel_id=1, source_target_pairs={{0,8},{8,0},{16,24},{24,16},{1,9},{9,1},{17,25},{25,17},{2,10},{10... | collective-permute-start | bytes 344072 | tf_op jit(solution)/shard_map/ppermute | solution.py:599
  75.8 1.5 %inner1.1 = (f32[1280,128]{1,0:T(8,128)S(1)}, f32[1280,128]{1,0:T(8,128)S(1)}, f32[1024,128]{1,0:T(8,128)S(1)}, f32[1024,128]{1,0:T(8,128)S(1)}) custom-call(bf16[384,128]{1,0:T(8,128)(2,1)S(1)} %copy-done.3, bf16[384,128]{1,0:T(8,128)(2,1)S(1)} %copy-done.1, f32[1024,128]{1,0:T(8,128)S(1)} %get-tuple-element.61.pres.refs_2_, ...), custom_call_target="tpu_custom_call" | custom-call | flops 20000000 | bytes 8000000 | tf_op jit(solution)/shard_map/inner1/pallas_call | solution.py:575
  77.3 3.8 %collective-permute-done.4.refs_3_ = f32[224,128]{1,0:T(8,128)S(1)} collective-permute-done((f32[224,128]{1,0:T(8,128)S(1)}, f32[224,128]{1,0:T(8,128)S(1)}, u32[]{:S(2)}, u32[]{:S(2)}) %collective-permute-start.4) | collective-permute-done | bytes 114720 | tf_op jit(solution)/shard_map/ppermute | solution.py:596
  81.1 1.6 %edge1.1 = (f32[1024,128]{1,0:T(8,128)S(1)}, f32[1280,128]{1,0:T(8,128)S(1)}, f32[1280,128]{1,0:T(8,128)S(1)}, f32[224,128]{1,0:T(8,128)S(1)}, f32[224,128]{1,0:...) custom-call(s32[4,3]{1,0:T(4,128)S(1)} %copy-done.4, f32[4,4]{1,0:T(4,128)S(1)} %copy-done.5, ...), custom_call_target="tpu_custom_call" | custom-call | tf_op jit(solution)/shard_map/edge1/pallas_call | solution.py:575
  82.7 2.7 %collective-permute-start.8 = (f32[224,128]{1,0:T(8,128)S(1)}, f32[224,128]{1,0:T(8,128)S(1)}, u32[]{:S(2)}, u32[]{:S(2)}) collective-permute-start(f32[224,128]{1,0:T(8,128)S(1)} %get-tuple-element.75), channel_id=1, source_target_pairs={{1,2},{2,1},{3,4},{4,3},{5,6},{6,5},{7,0},{0,7},{9,10},{10,9},{11,... | collective-permute-start | bytes 344072 | tf_op jit(solution)/shard_map/ppermute | solution.py:596
  87.1 1.5 %inner2.1 = (f32[1280,128]{1,0:T(8,128)S(1)}, f32[1280,128]{1,0:T(8,128)S(1)}, f32[1024,128]{1,0:T(8,128)S(1)}, f32[1024,128]{1,0:T(8,128)S(1)}) custom-call(bf16[384,128]{1,0:T(8,128)(2,1)S(1)} %copy-done.3, bf16[384,128]{1,0:T(8,128)(2,1)S(1)} %copy-done.1, f32[1024,128]{1,0:T(8,128)S(1)} %get-tuple-element.74.pres.refs_2_, ...), custom_call_target="tpu_custom_call" | custom-call | flops 20000000 | bytes 8000000 | tf_op jit(solution)/shard_map/inner2/pallas_call | solution.py:575
  88.6 3.9 %collective-permute-done.8.refs_3_ = f32[224,128]{1,0:T(8,128)S(1)} collective-permute-done((f32[224,128]{1,0:T(8,128)S(1)}, f32[224,128]{1,0:T(8,128)S(1)}, u32[]{:S(2)}, u32[]{:S(2)}) %collective-permute-start.8) | collective-permute-done | bytes 114720 | tf_op jit(solution)/shard_map/ppermute | solution.py:596
  92.5 1.6 %edge2.1 = (f32[1024,128]{1,0:T(8,128)S(1)}, f32[1280,128]{1,0:T(8,128)S(1)}, f32[1280,128]{1,0:T(8,128)S(1)}, f32[224,128]{1,0:T(8,128)S(1)}, f32[224,128]{1,0:...) custom-call(s32[4,3]{1,0:T(4,128)S(1)} %copy-done.4, f32[4,4]{1,0:T(4,128)S(1)} %copy-done.5, ...), custom_call_target="tpu_custom_call" | custom-call | tf_op jit(solution)/shard_map/edge2/pallas_call | solution.py:575
  94.1 2.5 %collective-permute-start.12 = (f32[224,128]{1,0:T(8,128)S(1)}, f32[224,128]{1,0:T(8,128)S(1)}, u32[]{:S(2)}, u32[]{:S(2)}) collective-permute-start(f32[224,128]{1,0:T(8,128)S(1)} %get-tuple-element.86), channel_id=1, source_target_pairs={{1,2},{2,1},{3,4},{4,3},{5,6},{6,5},{7,0},{0,7},{9,10},{10,9},{11,... | collective-permute-start | bytes 344072 | tf_op jit(solution)/shard_map/ppermute | solution.py:596
  98.4 2.3 %inner3.1 = (f32[1280,128]{1,0:T(8,128)S(1)}, f32[1280,128]{1,0:T(8,128)S(1)}, f32[1024,128]{1,0:T(8,128)}, f32[1024,128]{1,0:T(8,128)S(1)}) custom-call(bf16[384,128]{1,0:T(8,128)(2,1)S(1)} %copy-done.3, bf16[384,128]{1,0:T(8,128)(2,1)S(1)} %copy-done.1, f32[1024,128]{1,0:T(8,128)S(1)} %get-tuple-element.85.pres.refs_2_, ...), custom_call_target="tpu_custom_call" | custom-call | flops 20000000 | bytes 8000000 | tf_op jit(solution)/shard_map/inner3/pallas_call | solution.py:575
  100.7 3.1 %collective-permute-done.12.refs_3_ = f32[224,128]{1,0:T(8,128)S(1)} collective-permute-done((f32[224,128]{1,0:T(8,128)S(1)}, f32[224,128]{1,0:T(8,128)S(1)}, u32[]{:S(2)}, u32[]{:S(2)}) %collective-permute-start.12) | collective-permute-done | bytes 114720 | tf_op jit(solution)/shard_map/ppermute | solution.py:596
  103.8 2.3 %edge3.1 = (f32[1024,128]{1,0:T(8,128)}, f32[1024,128]{1,0:T(8,128)}, f32[1024,128]{1,0:T(8,128)}) custom-call(s32[4,3]{1,0:T(4,128)S(1)} %copy-done.4, f32[4,4]{1,0:T(4,128)S(1)} %copy-done.5, f32[1024,128]{1,0:T(8,128)S(1)} %get-tuple-element.85.pres.refs_2_, f32[224,128]{1,0:T(8,128)S(1)} %collective-permute-done.12.refs_3_, ...), custom_call_target="tpu_custom_call" | custom-call | tf_op jit(solution)/shard_map/edge3/pallas_call | solution.py:575
  (42 shorter events, 5.5 us)
Async XLA Ops:
  4.0 16.5 %copy-start.2 = (bf16[384,128]{1,0:T(8,128)(2,1)S(1)}, bf16[384,128]{1,0:T(8,128)(2,1)}, u32[]{:S(2)}) copy-start(bf16[384,128]{1,0:T(8,128)(2,1)} %constant.4.clone.mat_f) | copy-start | bytes 294916
  4.0 27.7 %all-to-all-start = ((f32[128,16,128]{2,1,0:T(8,128)}), f32[128,16,128]{2,1,0:T(8,128)}, u32[]{:S(2)}, u32[]{:S(2)}) async-start(f32[128,16,128]{2,1,0:T(8,128)} %bitcast.19), calls=%async_computation | async-start | bytes 2097152 | tf_op jit(solution)/shard_map/all_to_all | solution.py:628
  14.8 29.6 %collective-permute-start = (f32[352,128]{1,0:T(8,128)}, f32[352,128]{1,0:T(8,128)}, u32[]{:S(2)}, u32[]{:S(2)}) collective-permute-start(f32[352,128]{1,0:T(8,128)} %get-tuple-element.53), channel_id=1, source_target_pairs={{1,2},{2,1},{3,4},{4,3},{5,6},{6,5},{7,0},{0,7},{9,10},{10,9},{11,... | collective-permute-start | bytes 540680 | tf_op jit(solution)/shard_map/ppermute | solution.py:596
  18.2 26.2 %collective-permute-start.1 = (f32[352,128]{1,0:T(8,128)}, f32[352,128]{1,0:T(8,128)}, u32[]{:S(2)}, u32[]{:S(2)}) collective-permute-start(f32[352,128]{1,0:T(8,128)} %get-tuple-element.54), channel_id=1, source_target_pairs={{0,1},{1,0},{2,3},{3,2},{4,5},{5,4},{6,7},{7,6},{8,9},{9,8},{10,11... | collective-permute-start | bytes 540680 | tf_op jit(solution)/shard_map/ppermute | solution.py:597
  18.3 26.1 %collective-permute-start.2 = (f32[352,128]{1,0:T(8,128)}, f32[352,128]{1,0:T(8,128)}, u32[]{:S(2)}, u32[]{:S(2)}) collective-permute-start(f32[352,128]{1,0:T(8,128)} %get-tuple-element.55), channel_id=1, source_target_pairs={{8,16},{16,8},{0,24},{24,0},{9,17},{17,9},{1,25},{25,1},{10,18},{1... | collective-permute-start | bytes 540680 | tf_op jit(solution)/shard_map/ppermute | solution.py:598
  19.8 24.6 %collective-permute-start.3 = (f32[352,128]{1,0:T(8,128)}, f32[352,128]{1,0:T(8,128)}, u32[]{:S(2)}, u32[]{:S(2)}) collective-permute-start(f32[352,128]{1,0:T(8,128)} %get-tuple-element.56), channel_id=1, source_target_pairs={{0,8},{8,0},{16,24},{24,16},{1,9},{9,1},{17,25},{25,17},{2,10},{10... | collective-permute-start | bytes 540680 | tf_op jit(solution)/shard_map/ppermute | solution.py:599
  22.8 12.8 %copy-start.6 = (s32[4,2]{1,0:T(4,128)}, s32[4,2]{1,0:T(4,128)S(1)}, u32[]{:S(2)}) copy-start(s32[4,2]{1,0:T(4,128)S(1)} %copy.16.corners) | copy-start | bytes 100
  35.6 31.1 %all-to-all-start.1 = ((f32[128,24,128]{2,1,0:T(8,128)}), f32[128,24,128]{2,1,0:T(8,128)}, u32[]{:S(2)}, u32[]{:S(2)}) async-start(f32[128,24,128]{2,1,0:T(8,128)} %bitcast.14), calls=%async_computation.1 | async-start | bytes 3145728 | tf_op jit(solution)/shard_map/all_to_all | solution.py:649
  44.4 22.3 %copy-start.1 = (bf16[384,128]{1,0:T(8,128)(2,1)S(1)}, bf16[384,128]{1,0:T(8,128)(2,1)}, u32[]{:S(2)}) copy-start(bf16[384,128]{1,0:T(8,128)(2,1)} %constant.5.clone.mat_b) | copy-start | bytes 294916
  44.4 22.3 %copy-start.4 = (s32[4,3]{1,0:T(4,128)S(1)}, s32[4,3]{1,0:T(4,128)}, u32[]{:S(2)}) copy-start(s32[4,3]{1,0:T(4,128)} %refs_0_.5) | copy-start | bytes 148
  44.4 22.3 %copy-start.5 = (f32[4,4]{1,0:T(4,128)S(1)}, f32[4,4]{1,0:T(4,128)}, u32[]{:S(2)}) copy-start(f32[4,4]{1,0:T(4,128)} %refs_1_.5) | copy-start | bytes 196
  44.4 22.2 %copy-start.7 = (s32[4,2]{1,0:T(4,128)S(1)}, s32[4,2]{1,0:T(4,128)}, u32[]{:S(2)}) copy-start(s32[4,2]{1,0:T(4,128)} %copy-done.6) | copy-start | bytes 100
  71.4 9.6 %collective-permute-start.4 = (f32[224,128]{1,0:T(8,128)S(1)}, f32[224,128]{1,0:T(8,128)S(1)}, u32[]{:S(2)}, u32[]{:S(2)}) collective-permute-start(f32[224,128]{1,0:T(8,128)S(1)} %get-tuple-element.62), channel_id=1, source_target_pairs={{1,2},{2,1},{3,4},{4,3},{5,6},{6,5},{7,0},{0,7},{9,10},{10,9},{11,... | collective-permute-start | bytes 344072 | tf_op jit(solution)/shard_map/ppermute | solution.py:596
  74.3 6.8 %collective-permute-start.5 = (f32[224,128]{1,0:T(8,128)S(1)}, f32[224,128]{1,0:T(8,128)S(1)}, u32[]{:S(2)}, u32[]{:S(2)}) collective-permute-start(f32[224,128]{1,0:T(8,128)S(1)} %get-tuple-element.63), channel_id=1, source_target_pairs={{0,1},{1,0},{2,3},{3,2},{4,5},{5,4},{6,7},{7,6},{8,9},{9,8},{10,11... | collective-permute-start | bytes 344072 | tf_op jit(solution)/shard_map/ppermute | solution.py:597
  74.3 6.8 %collective-permute-start.6 = (f32[224,128]{1,0:T(8,128)S(1)}, f32[224,128]{1,0:T(8,128)S(1)}, u32[]{:S(2)}, u32[]{:S(2)}) collective-permute-start(f32[224,128]{1,0:T(8,128)S(1)} %get-tuple-element.64), channel_id=1, source_target_pairs={{8,16},{16,8},{0,24},{24,0},{9,17},{17,9},{1,25},{25,1},{10,18},{1... | collective-permute-start | bytes 344072 | tf_op jit(solution)/shard_map/ppermute | solution.py:598
  74.4 6.7 %collective-permute-start.7 = (f32[224,128]{1,0:T(8,128)S(1)}, f32[224,128]{1,0:T(8,128)S(1)}, u32[]{:S(2)}, u32[]{:S(2)}) collective-permute-start(f32[224,128]{1,0:T(8,128)S(1)} %get-tuple-element.65), channel_id=1, source_target_pairs={{0,8},{8,0},{16,24},{24,16},{1,9},{9,1},{17,25},{25,17},{2,10},{10... | collective-permute-start | bytes 344072 | tf_op jit(solution)/shard_map/ppermute | solution.py:599
  82.7 9.7 %collective-permute-start.8 = (f32[224,128]{1,0:T(8,128)S(1)}, f32[224,128]{1,0:T(8,128)S(1)}, u32[]{:S(2)}, u32[]{:S(2)}) collective-permute-start(f32[224,128]{1,0:T(8,128)S(1)} %get-tuple-element.75), channel_id=1, source_target_pairs={{1,2},{2,1},{3,4},{4,3},{5,6},{6,5},{7,0},{0,7},{9,10},{10,9},{11,... | collective-permute-start | bytes 344072 | tf_op jit(solution)/shard_map/ppermute | solution.py:596
  85.4 7.0 %collective-permute-start.9 = (f32[224,128]{1,0:T(8,128)S(1)}, f32[224,128]{1,0:T(8,128)S(1)}, u32[]{:S(2)}, u32[]{:S(2)}) collective-permute-start(f32[224,128]{1,0:T(8,128)S(1)} %get-tuple-element.76), channel_id=1, source_target_pairs={{0,1},{1,0},{2,3},{3,2},{4,5},{5,4},{6,7},{7,6},{8,9},{9,8},{10,11... | collective-permute-start | bytes 344072 | tf_op jit(solution)/shard_map/ppermute | solution.py:597
  85.5 7.0 %collective-permute-start.10 = (f32[224,128]{1,0:T(8,128)S(1)}, f32[224,128]{1,0:T(8,128)S(1)}, u32[]{:S(2)}, u32[]{:S(2)}) collective-permute-start(f32[224,128]{1,0:T(8,128)S(1)} %get-tuple-element.77), channel_id=1, source_target_pairs={{8,16},{16,8},{0,24},{24,0},{9,17},{17,9},{1,25},{25,1},{10,18},{1... | collective-permute-start | bytes 344072 | tf_op jit(solution)/shard_map/ppermute | solution.py:598
  86.5 5.9 %collective-permute-start.11 = (f32[224,128]{1,0:T(8,128)S(1)}, f32[224,128]{1,0:T(8,128)S(1)}, u32[]{:S(2)}, u32[]{:S(2)}) collective-permute-start(f32[224,128]{1,0:T(8,128)S(1)} %get-tuple-element.78), channel_id=1, source_target_pairs={{0,8},{8,0},{16,24},{24,16},{1,9},{9,1},{17,25},{25,17},{2,10},{10... | collective-permute-start | bytes 344072 | tf_op jit(solution)/shard_map/ppermute | solution.py:599
  94.1 9.7 %collective-permute-start.12 = (f32[224,128]{1,0:T(8,128)S(1)}, f32[224,128]{1,0:T(8,128)S(1)}, u32[]{:S(2)}, u32[]{:S(2)}) collective-permute-start(f32[224,128]{1,0:T(8,128)S(1)} %get-tuple-element.86), channel_id=1, source_target_pairs={{1,2},{2,1},{3,4},{4,3},{5,6},{6,5},{7,0},{0,7},{9,10},{10,9},{11,... | collective-permute-start | bytes 344072 | tf_op jit(solution)/shard_map/ppermute | solution.py:596
  96.6 7.2 %collective-permute-start.13 = (f32[224,128]{1,0:T(8,128)S(1)}, f32[224,128]{1,0:T(8,128)S(1)}, u32[]{:S(2)}, u32[]{:S(2)}) collective-permute-start(f32[224,128]{1,0:T(8,128)S(1)} %get-tuple-element.87), channel_id=1, source_target_pairs={{0,1},{1,0},{2,3},{3,2},{4,5},{5,4},{6,7},{7,6},{8,9},{9,8},{10,11... | collective-permute-start | bytes 344072 | tf_op jit(solution)/shard_map/ppermute | solution.py:597
  96.6 7.2 %collective-permute-start.14 = (f32[224,128]{1,0:T(8,128)S(1)}, f32[224,128]{1,0:T(8,128)S(1)}, u32[]{:S(2)}, u32[]{:S(2)}) collective-permute-start(f32[224,128]{1,0:T(8,128)S(1)} %get-tuple-element.88), channel_id=1, source_target_pairs={{8,16},{16,8},{0,24},{24,0},{9,17},{17,9},{1,25},{25,1},{10,18},{1... | collective-permute-start | bytes 344072 | tf_op jit(solution)/shard_map/ppermute | solution.py:598
  97.6 6.2 %collective-permute-start.15 = (f32[224,128]{1,0:T(8,128)S(1)}, f32[224,128]{1,0:T(8,128)S(1)}, u32[]{:S(2)}, u32[]{:S(2)}) collective-permute-start(f32[224,128]{1,0:T(8,128)S(1)} %get-tuple-element.89), channel_id=1, source_target_pairs={{0,8},{8,0},{16,24},{24,16},{1,9},{9,1},{17,25},{25,17},{2,10},{10... | collective-permute-start | bytes 344072 | tf_op jit(solution)/shard_map/ppermute | solution.py:599
  (3 other events, 12.4 us)

commit v5 on v4

--- a/solution.py
+++ b/solution.py
@@ -584,19 +584,29 @@
     )(*args)
 
 
-x_swaps = ([(0, 1), (1, 0), (2, 3), (3, 2)], [(1, 2), (2, 1), (0, 3), (3, 0)])
-y_swaps = (
-    [(i, i ^ 1) for i in range(8)],
-    [(1, 2), (2, 1), (3, 4), (4, 3), (5, 6), (6, 5), (7, 0), (0, 7)],
-)
+GX, GY = 4, 8
+
+
+def partners(match):
+    out = []
+    for g in range(GX):
+        for h in range(GY):
+            to_g, to_h = match(g, h)
+            out.append((g * GY + h, to_g * GY + to_h))
+    return out
+
+
+gx_near = partners(lambda g, h: (g ^ 1, h))
+gx_far = partners(lambda g, h: (g, h ^ 1) if g in (0, GX - 1) else (3 - g, h))
+gy_near = partners(lambda g, h: (g, h ^ 1))
+gy_far = partners(lambda g, h: (g ^ 1, h) if h in (0, GY - 1) else (g, ((h + 1) ^ 1) - 1))
 
 
 def exchange(faces):
+    plane = ("gx", "gy")
     return [
-        lax.ppermute(faces[0], "gy", y_swaps[1]),
-        lax.ppermute(faces[1], "gy", y_swaps[0]),
-        lax.ppermute(faces[2], "gx", x_swaps[1]),
-        lax.ppermute(faces[3], "gx", x_swaps[0]),
+        lax.ppermute(face, plane, pairs)
+        for face, pairs in zip(faces, (gy_far, gy_near, gx_far, gx_near))
     ]
 
 
@@ -612,7 +622,7 @@
     wide = shape(WIDE * CY)
     face = shape(HALO * 32)
     cost = pl.CostEstimate(flops=20_000_000, bytes_accessed=8_000_000, transcendentals=0)
-    long = pl.CostEstimate(flops=10**12, bytes_accessed=8_000_000, transcendentals=0)
+    long = pl.CostEstimate(flops=3 * 10**10, bytes_accessed=8_000_000, transcendentals=0)
 
     dma = pltpu.SemaphoreType.DMA
     deal, *faces = call(
@@ -643,7 +653,7 @@
         [vmem(16 * LINE), vmem(16 * LINE), vmem(128 * 24), dma((4,))],
         "cut",
         smem=1,
-        loose=(2,),
+        hbm=(2,),
         to_hbm=True,
     )
     window = lax.all_to_all(cut.reshape(128, 24, 128), DEVICES, 0, 0, tiled=True)

time: 108 us -> 100 us (0.926); the launches traced: 106 us -> 99.6 us
  Pallas kernels: 29 us -> 25.5 us
  starting transfers between devices: 38.2 us -> 37 us
    pallas_call x11, Pallas kernels: 29 us -> 25.5 us  [call(): pl.pallas_call(kernel, out_shape=outs, in_specs=specs, out_specs=[pl.Bloc...]
    ppermute x16, waiting for transfers between devices: 10.8 us -> 8.2 us  [exchange(): lax.ppermute(face, plane, pairs)]
    all_to_all x1, starting transfers between devices: 8.75 us -> 6.62 us  [shards(): lax.all_to_all(cut.reshape(128, 24, 128), DEVICES, 0, 0, tiled=True)]
    all_to_all x1, waiting for transfers between devices: 17.1 us -> 18.7 us  [shards(): lax.all_to_all(cut.reshape(128, 24, 128), DEVICES, 0, 0, tiled=True)]
    ppermute x16, starting transfers between devices: 18.6 us -> 20.1 us  [exchange(): lax.ppermute(face, plane, pairs)]
  transfers between devices with their start and end apart: 18 -> 18, of which waited for: 5 -> 6; matrix products, arithmetic and copies ran while one was open for 0% -> 0% of each run, Pallas kernels for 15% -> 14%
where the time goes in v5:
time: 100 us; the launch traced here: 99.6 us
  starting transfers between devices  37 us (37%)
  waiting for transfers between devices  36.1 us (36%)
  Pallas kernels  25.5 us (26%)
    pallas_call x11, Pallas kernels, call(): pl.pallas_call(kernel, out_shape=outs, in_specs=specs, out_specs=[pl.Bloc...  25.5 us
    ppermute x16, starting transfers between devices, exchange(): lax.ppermute(face, plane, pairs)  20.1 us
    all_to_all x1, waiting for transfers between devices, shards(): lax.all_to_all(cut.reshape(128, 24, 128), DEVICES, 0, 0, tiled=True)  18.7 us
    all_to_all x1, starting transfers between devices, shards(): lax.all_to_all(deal.reshape(128, 16, 128), DEVICES, 0, 0, tiled=True)  10.3 us
    all_to_all x1, waiting for transfers between devices, shards(): lax.all_to_all(deal.reshape(128, 16, 128), DEVICES, 0, 0, tiled=True)  9.25 us
    ppermute x16, waiting for transfers between devices, exchange(): lax.ppermute(face, plane, pairs)  8.2 us
    all_to_all x1, starting transfers between devices, shards(): lax.all_to_all(cut.reshape(128, 24, 128), DEVICES, 0, 0, tiled=True)  6.62 us
  transfers between devices with their start and end apart: 18, of which 6 were waited for; matrix products, arithmetic and copies ran while one was open for 0% of the time, Pallas kernels for 14%

profile of v5, /device:TPU:16, one launch (start us, length us, event | category | flops | bytes accessed | tf_op | source)
XLA Modules:
  0.0 99.6 jit_solution(4313943276813713260)
XLA Ops:
  0.6 2.5 %pack.1 = (f32[2048,128]{1,0:T(8,128)}, f32[352,128]{1,0:T(8,128)S(1)}, f32[352,128]{1,0:T(8,128)S(1)}, f32[352,128]{1,0:T(8,128)S(1)}, f32[352,128]{1,0:T(8,128)S(1)}) custom-call(f32[1024,128]{1,0:T(8,128)} %bitcast.22, f32[1024,128]{1,0:T(8,128)} %bitcast.23, f32[1024,128]{1,0:T(8,128)} %bitcast.17, f32[1024,128]{1,0:T(8,128)} %bitcast.24, ...), custom_call_target="tpu_custom_call" | custom-call | tf_op jit(solution)/shard_map/pack/pallas_call | solution.py:575
  3.1 10.3 %all-to-all-start = ((f32[128,16,128]{2,1,0:T(8,128)}), f32[128,16,128]{2,1,0:T(8,128)S(1)}, u32[]{:S(2)}, u32[]{:S(2)}) async-start(f32[128,16,128]{2,1,0:T(8,128)} %bitcast.21), calls=%async_computation | async-start | bytes 2097152 | tf_op jit(solution)/shard_map/all_to_all | solution.py:638
  13.5 3.4 %collective-permute-start = (f32[352,128]{1,0:T(8,128)S(1)}, f32[352,128]{1,0:T(8,128)S(1)}, u32[]{:S(2)}, u32[]{:S(2)}) collective-permute-start(f32[352,128]{1,0:T(8,128)S(1)} %get-tuple-element.53), channel_id=1, source_target_pairs={{0,8},{1,2},{2,1},{3,4},{4,3},{5,6},{6,5},{7,15},{8,0},{9,10},{10,... | collective-permute-start | bytes 540680 | tf_op jit(solution)/shard_map/ppermute | solution.py:608
  17.0 1.9 %collective-permute-start.2 = (f32[352,128]{1,0:T(8,128)S(1)}, f32[352,128]{1,0:T(8,128)S(1)}, u32[]{:S(2)}, u32[]{:S(2)}) collective-permute-start(f32[352,128]{1,0:T(8,128)S(1)} %get-tuple-element.55), channel_id=1, source_target_pairs={{0,1},{1,0},{2,3},{3,2},{4,5},{5,4},{6,7},{7,6},{8,16},{9,17},{10,... | collective-permute-start | bytes 540680 | tf_op jit(solution)/shard_map/ppermute | solution.py:608
  19.2 2.2 %step0_depth.1.refs_0_.refs_6_ = f32[1024,128]{1,0:T(8,128)} custom-call(bf16[384,128]{1,0:T(8,128)(2,1)S(1)} %copy-done.1, f32[1024,128]{1,0:T(8,128)} %bitcast.18), custom_call_target="tpu_custom_call" | custom-call | flops 30000001024 | bytes 8000000 | tf_op jit(solution)/shard_map/step0_depth/pallas_call | solution.py:575
  21.5 9.3 %all-to-all-done = f32[128,16,128]{2,1,0:T(8,128)S(1)} async-done(((f32[128,16,128]{2,1,0:T(8,128)}), f32[128,16,128]{2,1,0:T(8,128)S(1)}, u32[]{:S(2)}, u32[]{:S(2)}) %all-to-all-start) | async-done | bytes 1048608 | tf_op jit(solution)/shard_map/all_to_all | solution.py:638
  30.7 2.2 %cut.1 = f32[3072,128]{1,0:T(8,128)} custom-call(s32[4,2]{1,0:T(4,128)S(1)} %copy.16.corners, f32[2048,128]{1,0:T(8,128)S(1)} %bitcast.15, f32[1024,128]{1,0:T(8,128)} %step0_depth.1.refs_0_.refs_6_), custom_call_target="tpu_custom_call" | custom-call | tf_op jit(solution)/shard_map/cut/pallas_call | solution.py:575
  32.9 6.6 %all-to-all-start.1 = ((f32[128,24,128]{2,1,0:T(8,128)}), f32[128,24,128]{2,1,0:T(8,128)S(1)}, u32[]{:S(2)}, u32[]{:S(2)}) async-start(f32[128,24,128]{2,1,0:T(8,128)} %bitcast.16), calls=%async_computation.1 | async-start | bytes 3145728 | tf_op jit(solution)/shard_map/all_to_all | solution.py:659
  39.6 3.9 %step0_gradients.1 = (f32[1280,128]{1,0:T(8,128)}, f32[1280,128]{1,0:T(8,128)}, f32[1280,128]{1,0:T(8,128)}, f32[1280,128]{1,0:T(8,128)}) custom-call(f32[1024,128]{1,0:T(8,128)} %bitcast.19, f32[352,128]{1,0:T(8,128)S(1)} %collective-permute-done.gy_b, f32[352,128]{1,0:T(8,128)S(1)} %collective-permute-done.1.gy_a, ...), custom_call_target="tpu_custom_call" | custom-call | flops 30000001024 | bytes 8000000 | tf_op jit(solution)/shard_map/step0_gradients/pallas_call | solution.py:575
  43.5 18.7 %all-to-all-done.1 = f32[128,24,128]{2,1,0:T(8,128)S(1)} async-done(((f32[128,24,128]{2,1,0:T(8,128)}), f32[128,24,128]{2,1,0:T(8,128)S(1)}, u32[]{:S(2)}, u32[]{:S(2)}) %all-to-all-start.1) | async-done | bytes 1572896 | tf_op jit(solution)/shard_map/all_to_all | solution.py:659
  62.2 3.9 %step0.1 = (f32[1024,128]{1,0:T(8,128)S(1)}, f32[1280,128]{1,0:T(8,128)S(1)}, f32[1280,128]{1,0:T(8,128)S(1)}, f32[1024,128]{1,0:T(8,128)S(1)}, f32[1600,128]{1,...) custom-call(s32[4,2]{1,0:T(4,128)S(1)} %copy.16.corners, ...), custom_call_target="tpu_custom_call" | custom-call | tf_op jit(solution)/shard_map/step0/pallas_call | solution.py:575
  66.1 2.9 %collective-permute-start.4 = (f32[224,128]{1,0:T(8,128)S(1)}, f32[224,128]{1,0:T(8,128)S(1)}, u32[]{:S(2)}, u32[]{:S(2)}) collective-permute-start(f32[224,128]{1,0:T(8,128)S(1)} %get-tuple-element.62), channel_id=1, source_target_pairs={{0,8},{1,2},{2,1},{3,4},{4,3},{5,6},{6,5},{7,15},{8,0},{9,10},{10,... | collective-permute-start | bytes 344072 | tf_op jit(solution)/shard_map/ppermute | solution.py:608
  69.0 2.0 %collective-permute-start.6 = (f32[224,128]{1,0:T(8,128)S(1)}, f32[224,128]{1,0:T(8,128)S(1)}, u32[]{:S(2)}, u32[]{:S(2)}) collective-permute-start(f32[224,128]{1,0:T(8,128)S(1)} %get-tuple-element.64), channel_id=1, source_target_pairs={{0,1},{1,0},{2,3},{3,2},{4,5},{5,4},{6,7},{7,6},{8,16},{9,17},{10,... | collective-permute-start | bytes 344072 | tf_op jit(solution)/shard_map/ppermute | solution.py:608
  72.5 3.2 %collective-permute-done.4.refs_3_ = f32[224,128]{1,0:T(8,128)S(1)} collective-permute-done((f32[224,128]{1,0:T(8,128)S(1)}, f32[224,128]{1,0:T(8,128)S(1)}, u32[]{:S(2)}, u32[]{:S(2)}) %collective-permute-start.4) | collective-permute-done | bytes 114720 | tf_op jit(solution)/shard_map/ppermute | solution.py:608
  75.7 1.6 %edge1.1 = (f32[1024,128]{1,0:T(8,128)S(1)}, f32[1280,128]{1,0:T(8,128)S(1)}, f32[1280,128]{1,0:T(8,128)S(1)}, f32[224,128]{1,0:T(8,128)S(1)}, f32[224,128]{1,0:...) custom-call(s32[4,3]{1,0:T(4,128)S(1)} %copy-done.2, f32[4,4]{1,0:T(4,128)S(1)} %copy-done.3, ...), custom_call_target="tpu_custom_call" | custom-call | tf_op jit(solution)/shard_map/edge1/pallas_call | solution.py:575
  77.4 2.7 %collective-permute-start.8 = (f32[224,128]{1,0:T(8,128)S(1)}, f32[224,128]{1,0:T(8,128)S(1)}, u32[]{:S(2)}, u32[]{:S(2)}) collective-permute-start(f32[224,128]{1,0:T(8,128)S(1)} %get-tuple-element.75), channel_id=1, source_target_pairs={{0,8},{1,2},{2,1},{3,4},{4,3},{5,6},{6,5},{7,15},{8,0},{9,10},{10,... | collective-permute-start | bytes 344072 | tf_op jit(solution)/shard_map/ppermute | solution.py:608
  80.1 2.0 %collective-permute-start.10 = (f32[224,128]{1,0:T(8,128)S(1)}, f32[224,128]{1,0:T(8,128)S(1)}, u32[]{:S(2)}, u32[]{:S(2)}) collective-permute-start(f32[224,128]{1,0:T(8,128)S(1)} %get-tuple-element.77), channel_id=1, source_target_pairs={{0,1},{1,0},{2,3},{3,2},{4,5},{5,4},{6,7},{7,6},{8,16},{9,17},{10,... | collective-permute-start | bytes 344072 | tf_op jit(solution)/shard_map/ppermute | solution.py:608
  83.6 3.3 %collective-permute-done.8.refs_3_ = f32[224,128]{1,0:T(8,128)S(1)} collective-permute-done((f32[224,128]{1,0:T(8,128)S(1)}, f32[224,128]{1,0:T(8,128)S(1)}, u32[]{:S(2)}, u32[]{:S(2)}) %collective-permute-start.8) | collective-permute-done | bytes 114720 | tf_op jit(solution)/shard_map/ppermute | solution.py:608
  86.9 1.6 %edge2.1 = (f32[1024,128]{1,0:T(8,128)S(1)}, f32[1280,128]{1,0:T(8,128)S(1)}, f32[1280,128]{1,0:T(8,128)S(1)}, f32[224,128]{1,0:T(8,128)S(1)}, f32[224,128]{1,0:...) custom-call(s32[4,3]{1,0:T(4,128)S(1)} %copy-done.2, f32[4,4]{1,0:T(4,128)S(1)} %copy-done.3, ...), custom_call_target="tpu_custom_call" | custom-call | tf_op jit(solution)/shard_map/edge2/pallas_call | solution.py:575
  88.6 2.7 %collective-permute-start.12 = (f32[224,128]{1,0:T(8,128)S(1)}, f32[224,128]{1,0:T(8,128)S(1)}, u32[]{:S(2)}, u32[]{:S(2)}) collective-permute-start(f32[224,128]{1,0:T(8,128)S(1)} %get-tuple-element.86), channel_id=1, source_target_pairs={{0,8},{1,2},{2,1},{3,4},{4,3},{5,6},{6,5},{7,15},{8,0},{9,10},{10,... | collective-permute-start | bytes 344072 | tf_op jit(solution)/shard_map/ppermute | solution.py:608
  91.3 2.0 %collective-permute-start.14 = (f32[224,128]{1,0:T(8,128)S(1)}, f32[224,128]{1,0:T(8,128)S(1)}, u32[]{:S(2)}, u32[]{:S(2)}) collective-permute-start(f32[224,128]{1,0:T(8,128)S(1)} %get-tuple-element.88), channel_id=1, source_target_pairs={{0,1},{1,0},{2,3},{3,2},{4,5},{5,4},{6,7},{7,6},{8,16},{9,17},{10,... | collective-permute-start | bytes 344072 | tf_op jit(solution)/shard_map/ppermute | solution.py:608
  93.3 2.3 %inner3.1 = (f32[1280,128]{1,0:T(8,128)S(1)}, f32[1280,128]{1,0:T(8,128)S(1)}, f32[1024,128]{1,0:T(8,128)}, f32[1024,128]{1,0:T(8,128)S(1)}) custom-call(bf16[384,128]{1,0:T(8,128)(2,1)S(1)} %copy-done.1, bf16[384,128]{1,0:T(8,128)(2,1)S(1)} %copy-done, f32[1024,128]{1,0:T(8,128)S(1)} %get-tuple-element.85.pres.refs_2_, ...), custom_call_target="tpu_custom_call" | custom-call | flops 20000000 | bytes 8000000 | tf_op jit(solution)/shard_map/inner3/pallas_call | solution.py:575
  95.6 1.6 %collective-permute-done.12.refs_3_ = f32[224,128]{1,0:T(8,128)S(1)} collective-permute-done((f32[224,128]{1,0:T(8,128)S(1)}, f32[224,128]{1,0:T(8,128)S(1)}, u32[]{:S(2)}, u32[]{:S(2)}) %collective-permute-start.12) | collective-permute-done | bytes 114720 | tf_op jit(solution)/shard_map/ppermute | solution.py:608
  97.3 2.3 %edge3.1 = (f32[1024,128]{1,0:T(8,128)}, f32[1024,128]{1,0:T(8,128)}, f32[1024,128]{1,0:T(8,128)}) custom-call(s32[4,3]{1,0:T(4,128)S(1)} %copy-done.2, f32[4,4]{1,0:T(4,128)S(1)} %copy-done.3, f32[1024,128]{1,0:T(8,128)S(1)} %get-tuple-element.85.pres.refs_2_, f32[224,128]{1,0:T(8,128)S(1)} %collective-permute-done.12.refs_3_, ...), custom_call_target="tpu_custom_call" | custom-call | tf_op jit(solution)/shard_map/edge3/pallas_call | solution.py:575
  (34 shorter events, 3.6 us)
Async XLA Ops:
  3.1 16.0 %copy-start.1 = (bf16[384,128]{1,0:T(8,128)(2,1)S(1)}, bf16[384,128]{1,0:T(8,128)(2,1)}, u32[]{:S(2)}) copy-start(bf16[384,128]{1,0:T(8,128)(2,1)} %constant.4.clone.mat_f) | copy-start | bytes 294916
  3.1 27.6 %all-to-all-start = ((f32[128,16,128]{2,1,0:T(8,128)}), f32[128,16,128]{2,1,0:T(8,128)S(1)}, u32[]{:S(2)}, u32[]{:S(2)}) async-start(f32[128,16,128]{2,1,0:T(8,128)} %bitcast.21), calls=%async_computation | async-start | bytes 2097152 | tf_op jit(solution)/shard_map/all_to_all | solution.py:638
  13.5 26.1 %collective-permute-start = (f32[352,128]{1,0:T(8,128)S(1)}, f32[352,128]{1,0:T(8,128)S(1)}, u32[]{:S(2)}, u32[]{:S(2)}) collective-permute-start(f32[352,128]{1,0:T(8,128)S(1)} %get-tuple-element.53), channel_id=1, source_target_pairs={{0,8},{1,2},{2,1},{3,4},{4,3},{5,6},{6,5},{7,15},{8,0},{9,10},{10,... | collective-permute-start | bytes 540680 | tf_op jit(solution)/shard_map/ppermute | solution.py:608
  16.9 22.7 %collective-permute-start.1 = (f32[352,128]{1,0:T(8,128)S(1)}, f32[352,128]{1,0:T(8,128)S(1)}, u32[]{:S(2)}, u32[]{:S(2)}) collective-permute-start(f32[352,128]{1,0:T(8,128)S(1)} %get-tuple-element.54), channel_id=1, source_target_pairs={{0,1},{1,0},{2,3},{3,2},{4,5},{5,4},{6,7},{7,6},{8,9},{9,8},{10,11... | collective-permute-start | bytes 540680 | tf_op jit(solution)/shard_map/ppermute | solution.py:608
  17.0 22.6 %collective-permute-start.2 = (f32[352,128]{1,0:T(8,128)S(1)}, f32[352,128]{1,0:T(8,128)S(1)}, u32[]{:S(2)}, u32[]{:S(2)}) collective-permute-start(f32[352,128]{1,0:T(8,128)S(1)} %get-tuple-element.55), channel_id=1, source_target_pairs={{0,1},{1,0},{2,3},{3,2},{4,5},{5,4},{6,7},{7,6},{8,16},{9,17},{10,... | collective-permute-start | bytes 540680 | tf_op jit(solution)/shard_map/ppermute | solution.py:608
  18.9 2.5 %copy-start.4 = (s32[4,2]{0,1:T(2,128)S(1)}, s32[4,2]{0,1:T(2,128)}, u32[]{:S(2)}) copy-start(s32[4,2]{0,1:T(2,128)} %param.13) | copy-start | bytes 100
  18.9 20.7 %collective-permute-start.3 = (f32[352,128]{1,0:T(8,128)S(1)}, f32[352,128]{1,0:T(8,128)S(1)}, u32[]{:S(2)}, u32[]{:S(2)}) collective-permute-start(f32[352,128]{1,0:T(8,128)S(1)} %get-tuple-element.56), channel_id=1, source_target_pairs={{0,8},{1,9},{2,10},{3,11},{4,12},{5,13},{6,14},{7,15},{8,0},{9,1},... | collective-permute-start | bytes 540680 | tf_op jit(solution)/shard_map/ppermute | solution.py:608
  32.9 29.3 %all-to-all-start.1 = ((f32[128,24,128]{2,1,0:T(8,128)}), f32[128,24,128]{2,1,0:T(8,128)S(1)}, u32[]{:S(2)}, u32[]{:S(2)}) async-start(f32[128,24,128]{2,1,0:T(8,128)} %bitcast.16), calls=%async_computation.1 | async-start | bytes 3145728 | tf_op jit(solution)/shard_map/all_to_all | solution.py:659
  39.5 22.6 %copy-start = (bf16[384,128]{1,0:T(8,128)(2,1)S(1)}, bf16[384,128]{1,0:T(8,128)(2,1)}, u32[]{:S(2)}) copy-start(bf16[384,128]{1,0:T(8,128)(2,1)} %constant.5.clone.mat_b) | copy-start | bytes 294916
  39.6 22.6 %copy-start.2 = (s32[4,3]{1,0:T(4,128)S(1)}, s32[4,3]{1,0:T(4,128)}, u32[]{:S(2)}) copy-start(s32[4,3]{1,0:T(4,128)} %refs_0_.5) | copy-start | bytes 148
  39.6 22.6 %copy-start.3 = (f32[4,4]{1,0:T(4,128)S(1)}, f32[4,4]{1,0:T(4,128)}, u32[]{:S(2)}) copy-start(f32[4,4]{1,0:T(4,128)} %refs_1_.5) | copy-start | bytes 196
  66.1 9.6 %collective-permute-start.4 = (f32[224,128]{1,0:T(8,128)S(1)}, f32[224,128]{1,0:T(8,128)S(1)}, u32[]{:S(2)}, u32[]{:S(2)}) collective-permute-start(f32[224,128]{1,0:T(8,128)S(1)} %get-tuple-element.62), channel_id=1, source_target_pairs={{0,8},{1,2},{2,1},{3,4},{4,3},{5,6},{6,5},{7,15},{8,0},{9,10},{10,... | collective-permute-start | bytes 344072 | tf_op jit(solution)/shard_map/ppermute | solution.py:608
  69.0 6.8 %collective-permute-start.5 = (f32[224,128]{1,0:T(8,128)S(1)}, f32[224,128]{1,0:T(8,128)S(1)}, u32[]{:S(2)}, u32[]{:S(2)}) collective-permute-start(f32[224,128]{1,0:T(8,128)S(1)} %get-tuple-element.63), channel_id=1, source_target_pairs={{0,1},{1,0},{2,3},{3,2},{4,5},{5,4},{6,7},{7,6},{8,9},{9,8},{10,11... | collective-permute-start | bytes 344072 | tf_op jit(solution)/shard_map/ppermute | solution.py:608
  69.0 6.8 %collective-permute-start.6 = (f32[224,128]{1,0:T(8,128)S(1)}, f32[224,128]{1,0:T(8,128)S(1)}, u32[]{:S(2)}, u32[]{:S(2)}) collective-permute-start(f32[224,128]{1,0:T(8,128)S(1)} %get-tuple-element.64), channel_id=1, source_target_pairs={{0,1},{1,0},{2,3},{3,2},{4,5},{5,4},{6,7},{7,6},{8,16},{9,17},{10,... | collective-permute-start | bytes 344072 | tf_op jit(solution)/shard_map/ppermute | solution.py:608
  71.0 4.8 %collective-permute-start.7 = (f32[224,128]{1,0:T(8,128)S(1)}, f32[224,128]{1,0:T(8,128)S(1)}, u32[]{:S(2)}, u32[]{:S(2)}) collective-permute-start(f32[224,128]{1,0:T(8,128)S(1)} %get-tuple-element.65), channel_id=1, source_target_pairs={{0,8},{1,9},{2,10},{3,11},{4,12},{5,13},{6,14},{7,15},{8,0},{9,1},... | collective-permute-start | bytes 344072 | tf_op jit(solution)/shard_map/ppermute | solution.py:608
  77.4 9.5 %collective-permute-start.8 = (f32[224,128]{1,0:T(8,128)S(1)}, f32[224,128]{1,0:T(8,128)S(1)}, u32[]{:S(2)}, u32[]{:S(2)}) collective-permute-start(f32[224,128]{1,0:T(8,128)S(1)} %get-tuple-element.75), channel_id=1, source_target_pairs={{0,8},{1,2},{2,1},{3,4},{4,3},{5,6},{6,5},{7,15},{8,0},{9,10},{10,... | collective-permute-start | bytes 344072 | tf_op jit(solution)/shard_map/ppermute | solution.py:608
  80.1 6.8 %collective-permute-start.9 = (f32[224,128]{1,0:T(8,128)S(1)}, f32[224,128]{1,0:T(8,128)S(1)}, u32[]{:S(2)}, u32[]{:S(2)}) collective-permute-start(f32[224,128]{1,0:T(8,128)S(1)} %get-tuple-element.76), channel_id=1, source_target_pairs={{0,1},{1,0},{2,3},{3,2},{4,5},{5,4},{6,7},{7,6},{8,9},{9,8},{10,11... | collective-permute-start | bytes 344072 | tf_op jit(solution)/shard_map/ppermute | solution.py:608
  80.1 6.8 %collective-permute-start.10 = (f32[224,128]{1,0:T(8,128)S(1)}, f32[224,128]{1,0:T(8,128)S(1)}, u32[]{:S(2)}, u32[]{:S(2)}) collective-permute-start(f32[224,128]{1,0:T(8,128)S(1)} %get-tuple-element.77), channel_id=1, source_target_pairs={{0,1},{1,0},{2,3},{3,2},{4,5},{5,4},{6,7},{7,6},{8,16},{9,17},{10,... | collective-permute-start | bytes 344072 | tf_op jit(solution)/shard_map/ppermute | solution.py:608
  82.1 4.8 %collective-permute-start.11 = (f32[224,128]{1,0:T(8,128)S(1)}, f32[224,128]{1,0:T(8,128)S(1)}, u32[]{:S(2)}, u32[]{:S(2)}) collective-permute-start(f32[224,128]{1,0:T(8,128)S(1)} %get-tuple-element.78), channel_id=1, source_target_pairs={{0,8},{1,9},{2,10},{3,11},{4,12},{5,13},{6,14},{7,15},{8,0},{9,1},... | collective-permute-start | bytes 344072 | tf_op jit(solution)/shard_map/ppermute | solution.py:608
  88.6 8.7 %collective-permute-start.12 = (f32[224,128]{1,0:T(8,128)S(1)}, f32[224,128]{1,0:T(8,128)S(1)}, u32[]{:S(2)}, u32[]{:S(2)}) collective-permute-start(f32[224,128]{1,0:T(8,128)S(1)} %get-tuple-element.86), channel_id=1, source_target_pairs={{0,8},{1,2},{2,1},{3,4},{4,3},{5,6},{6,5},{7,15},{8,0},{9,10},{10,... | collective-permute-start | bytes 344072 | tf_op jit(solution)/shard_map/ppermute | solution.py:608
  91.3 5.9 %collective-permute-start.13 = (f32[224,128]{1,0:T(8,128)S(1)}, f32[224,128]{1,0:T(8,128)S(1)}, u32[]{:S(2)}, u32[]{:S(2)}) collective-permute-start(f32[224,128]{1,0:T(8,128)S(1)} %get-tuple-element.87), channel_id=1, source_target_pairs={{0,1},{1,0},{2,3},{3,2},{4,5},{5,4},{6,7},{7,6},{8,9},{9,8},{10,11... | collective-permute-start | bytes 344072 | tf_op jit(solution)/shard_map/ppermute | solution.py:608
  91.3 6.0 %collective-permute-start.14 = (f32[224,128]{1,0:T(8,128)S(1)}, f32[224,128]{1,0:T(8,128)S(1)}, u32[]{:S(2)}, u32[]{:S(2)}) collective-permute-start(f32[224,128]{1,0:T(8,128)S(1)} %get-tuple-element.88), channel_id=1, source_target_pairs={{0,1},{1,0},{2,3},{3,2},{4,5},{5,4},{6,7},{7,6},{8,16},{9,17},{10,... | collective-permute-start | bytes 344072 | tf_op jit(solution)/shard_map/ppermute | solution.py:608
  93.3 4.0 %collective-permute-start.15 = (f32[224,128]{1,0:T(8,128)S(1)}, f32[224,128]{1,0:T(8,128)S(1)}, u32[]{:S(2)}, u32[]{:S(2)}) collective-permute-start(f32[224,128]{1,0:T(8,128)S(1)} %get-tuple-element.89), channel_id=1, source_target_pairs={{0,8},{1,9},{2,10},{3,11},{4,12},{5,13},{6,14},{7,15},{8,0},{9,1},... | collective-permute-start | bytes 344072 | tf_op jit(solution)/shard_map/ppermute | solution.py:608

commit v6 on v5

--- a/solution.py
+++ b/solution.py
@@ -15,6 +15,7 @@
 WIDE = 40
 PAD = 48
 LINE = 80
+MESSAGE = 22
 STRIP = 24
 DEVICES = ("shot", "gx", "gy")
 
@@ -110,8 +111,7 @@
     return pulls
 
 
-def pack_kernel(vel, den, pres, flow_x, flow_y, deal, gy_b, gy_a, gx_b, gx_a, *scratch):
-    vel_in, den_in, pres_in, x_in, y_in, out, in_sem, field_sem, out_sem = scratch
+def pack_kernel(vel, den, deal, vel_in, den_in, out, in_sem, out_sem):
     pulls = []
     for part in range(4):
         rows = pl.ds(part * 256, 256)
@@ -123,7 +123,6 @@
         )
         for pull in pulls[-1]:
             pull.start()
-    fields = pull_all(((pres, pres_in), (flow_x, x_in), (flow_y, y_in)), field_sem)
     pushes = []
     for part in range(4):
         for pull in pulls[part]:
@@ -136,17 +135,20 @@
         rows = pl.ds(part * 512, 512)
         pushes.append(pltpu.make_async_copy(out.at[rows], deal.at[rows], out_sem.at[part]))
         pushes[-1].start()
-    for pull in fields:
+    for push in pushes:
+        push.wait()
+
+
+def face_kernel(pres, flow_x, flow_y, _, gy_b, gy_a, gx_b, gx_a, pres_in, x_in, y_in, sem):
+    pulls = pull_all(((pres, pres_in), (flow_x, x_in), (flow_y, y_in)), sem)
+    for pull in pulls:
         pull.wait()
     send_faces(pres_in, (gx_a, gx_b), (gy_a, gy_b), 0, HALO)
     send_faces(x_in, (gx_a, gx_b), (), HALO, 4)
     send_faces(y_in, (), (gy_a, gy_b), HALO, 4)
-    for push in pushes:
-        push.wait()
-
-
-def cut_kernel(corners, dealt, *refs):
-    out, rho_lines, vel_lines, cuts, sem = refs[-5:]
+
+
+def cut_kernel(corners, dealt, _, out, rho_lines, vel_lines, cuts, sem):
     s, g, col_class = place()
     row_class = s * 4 + g
     for t in range(16):
@@ -155,33 +157,35 @@
             dst = t * LINE + 8 + part * 8
             vel_lines[dst : dst + 8, :] = dealt[src : src + 8, :]
             rho_lines[dst : dst + 8, :] = dealt[src + 8 : src + 16, :]
-
+    flat = out.reshape(128 * MESSAGE, 128)
     pushes = []
     for shot in range(4):
-        corner_y = corners[shot, 1]
+        col = lax.shift_right_arithmetic(corners[shot, 1] - col_class + 7, 3)
+        wide_col = lax.shift_right_arithmetic(corners[shot, 1] - 4 - col_class + 7, 3)
 
         def block(part, carry):
             corner_x = corners[shot, 0] + part * CX
-            wide_row = lax.shift_right_arithmetic(corner_x - 4 - row_class + 15, 4)
             row = lax.shift_right_arithmetic(corner_x - row_class + 15, 4)
+            low = lax.rem(row_class - corner_x + 4 + 1024, 16) < 4
+            rim = jnp.clip(jnp.where(low, row - 1, row + 2), 0, 15)
+            base = (shot * 32 + part * 8) * MESSAGE
+            line = row * LINE + 8
+            rim_line = rim * LINE + 8 + col
             for h in range(8):
-                base = (shot * 32 + part * 8 + h) * 24
-                wide_col = lax.shift_right_arithmetic(corner_y + h * CY - 4 - col_class + 7, 3)
-                col = lax.shift_right_arithmetic(corner_y + h * CY - col_class + 7, 3)
-                for k in range(3):
-                    line = jnp.clip(wide_row + k, 0, 15)
-                    cuts[pl.ds(base + 5 * k, 5), :] = rho_lines[
-                        pl.ds(line * LINE + 8 + wide_col, 5), :
+                to = base + h * MESSAGE
+                for k in range(2):
+                    cuts[pl.ds(to + 5 * k, 5), :] = rho_lines[
+                        pl.ds(line + wide_col + (k * LINE + 4 * h), 5), :
                     ]
-                for k in range(2):
-                    cuts[pl.ds(base + 16 + 4 * k, 4), :] = vel_lines[
-                        pl.ds((row + k) * LINE + 8 + col, 4), :
+                    cuts[pl.ds(to + 14 + 4 * k, 4), :] = vel_lines[
+                        pl.ds(line + col + (k * LINE + 4 * h), 4), :
                     ]
+                cuts[pl.ds(to + 10, 4), :] = rho_lines[pl.ds(rim_line + 4 * h, 4), :]
             return carry
 
         lax.fori_loop(0, 4, block, 0)
-        rows = pl.ds(shot * 768, 768)
-        pushes.append(pltpu.make_async_copy(cuts.at[rows], out.at[rows], sem.at[shot]))
+        rows = pl.ds(shot * 32 * MESSAGE, 32 * MESSAGE)
+        pushes.append(pltpu.make_async_copy(cuts.at[rows], flat.at[rows], sem.at[shot]))
         pushes[-1].start()
     for push in pushes:
         push.wait()
@@ -194,25 +198,35 @@
     wide_turn = lax.rem(8 - lax.rem(corner_y + 4, 8), 8)
     turn = lax.rem(8 - lax.rem(corner_y, 8), 8)
     sub = lax.broadcasted_iota(jnp.int32, (8, 128), 0)
-    for w in range(WIDE):
-        cls = lax.rem(corner_x + 12 + w, 16)
-        row_in = (g * CX + w - 4 >= 0) & (g * CX + w - 4 < 4 * CX)
-        for n in range(5):
-            got = every(window, cls * 192 + 5 * (w // 16) + n, 24)
-            got = pltpu.roll(got, wide_turn, 0)
-            at = w * WIDE + n * 8
-            rho[at : at + 8, :] = got
-            col = sub + (h * CY + n * 8 - 4)
-            inside = (col >= 0) & (col < 8 * CY) & row_in
-            buoy[at : at + 8, :] = jnp.where(inside, time_step * (1.0 / got), 0.0)
-    for w in range(CX):
-        cls = lax.rem(corner_x + w, 16)
-        for n in range(4):
-            got = every(window, cls * 192 + 16 + 4 * (w // 16) + n, 24)
-            speed = pltpu.roll(got, turn, 0)
-            at = w * CY + n * 8
-            dens = rho[(w + 4) * WIDE + 4 + n * 8 : (w + 4) * WIDE + 12 + n * 8, :]
-            modu[at : at + 8, :] = time_step * (dens * speed * speed)
+    flat = window.reshape(128 * MESSAGE, 128)
+    low_in = (h > 0) | (sub >= 4)
+    high_in = (h < 7) | (sub < 4)
+    for x in range(-4, CX + 3):
+        start = lax.rem(corner_x + 16 + x, 16) * (8 * MESSAGE)
+        base = (x + 4) * WIDE
+        if 0 <= x < CX:
+            for n in range(5):
+                got = pltpu.roll(every(flat, start + 5 * (x // 16) + n, MESSAGE), wide_turn, 0)
+                rho[base + n * 8 : base + n * 8 + 8, :] = got
+                light = time_step * (1.0 / got)
+                if n == 0:
+                    light = jnp.where(low_in, light, 0.0)
+                elif n == 4:
+                    light = jnp.where(high_in, light, 0.0)
+                buoy[base + n * 8 : base + n * 8 + 8, :] = light
+            for n in range(4):
+                got = every(flat, start + 14 + 4 * (x // 16) + n, MESSAGE)
+                speed = pltpu.roll(got, turn, 0)
+                at = x * CY + n * 8
+                dens = rho[base + 4 + n * 8 : base + 12 + n * 8, :]
+                modu[at : at + 8, :] = time_step * (dens * speed * speed)
+        else:
+            row_in = (g > 0) if x < 0 else (g < 3)
+            for n in range(4):
+                got = pltpu.roll(every(flat, start + 10 + n, MESSAGE), turn, 0)
+                buoy[base + 4 + n * 8 : base + 12 + n * 8, :] = jnp.where(
+                    row_in, time_step * (1.0 / got), 0.0
+                )
 
 
 def buoy_at(buoy, x, y, rows=8):
@@ -311,7 +325,7 @@
     sources, outs, scratch = refs[:7], refs[7:17], refs[17:]
     new_p, wide_x, wide_y, new_z, buoy, modu, gy_b, gy_a, gx_b, gx_a = outs
     pres, in_x, in_y, in_z, grad_x, grad_y, grad_z, rho, spread, sem = scratch
-    order = (4, 1, 5, 2, 6, 3, 0)
+    order = (6, 3, 4, 1, 0, 5, 2)
     pulls = pull_all([(sources[i], scratch[i]) for i in order], sem)
     unpack_model(corners, window, buoy, modu, rho)
 
@@ -339,14 +353,19 @@
             )
         return carry
 
-    for i, (some, count) in enumerate(((flow_x, WIDE), (flow_y, CX), (flow_z, CX))):
-        pulls[2 * i].wait()
-        pulls[2 * i + 1].wait()
-        lax.fori_loop(0, count, some, 0, unroll=4)
+    def wait(*which):
+        for i in which:
+            pulls[i].wait()
+
+    wait(0, 1)
+    lax.fori_loop(0, CX, flow_z, 0, unroll=4)
     for chunk in range(8):
         rows = slice(chunk * 128, (chunk + 1) * 128)
         spread[rows, :] = depth_difference(new_z[rows, :], mat_b)
-    pulls[6].wait()
+    wait(2, 3)
+    lax.fori_loop(0, WIDE, flow_x, 0, unroll=4)
+    wait(4, 5, 6)
+    lax.fori_loop(0, CX, flow_y, 0, unroll=4)
 
     def update(chunk, carry):
         x0 = chunk * 4
@@ -625,17 +644,26 @@
     long = pl.CostEstimate(flops=3 * 10**10, bytes_accessed=8_000_000, transcendentals=0)
 
     dma = pltpu.SemaphoreType.DMA
-    deal, *faces = call(
+    (deal,) = call(
         pack_kernel,
-        [shape(128 * 16)] + [shape((HALO + 4) * 32)] * 4,
-        [vel, den, pres, flow_x, flow_y],
-        [vmem(1024)] * 5 + [vmem(2048), dma((8,)), dma((3,)), dma((4,))],
+        [shape(128 * 16)],
+        [vel, den],
+        [vmem(1024)] * 2 + [vmem(2048), dma((8,)), dma((4,))],
         "pack",
-        hbm=range(5),
-        to_hbm=(0,),
+        hbm=range(2),
+        to_hbm=True,
+    )
+    dealt = lax.all_to_all(deal.reshape(128, 16, 128), DEVICES, 0, 0, tiled=True)
+    faces = call(
+        face_kernel,
+        [shape((HALO + 4) * 32)] * 4,
+        [pres, flow_x, flow_y, deal],
+        [vmem(1024)] * 3 + [dma((3,))],
+        "first_faces",
+        hbm=range(4),
+        cost=cost,
     )
     faces = exchange(faces)
-    dealt = lax.all_to_all(deal.reshape(128, 16, 128), DEVICES, 0, 0, tiled=True)
     (grad_z,) = call(
         depth_kernel,
         [block],
@@ -648,16 +676,15 @@
     )
     (cut,) = call(
         cut_kernel,
-        [shape(128 * 24)],
+        [jax.ShapeDtypeStruct((128, MESSAGE // 2, 2, 128), f32)],
         [offsets, dealt.reshape(128 * 16, 128), grad_z],
-        [vmem(16 * LINE), vmem(16 * LINE), vmem(128 * 24), dma((4,))],
+        [vmem(16 * LINE), vmem(16 * LINE), vmem(128 * MESSAGE), dma((4,))],
         "cut",
         smem=1,
         hbm=(2,),
         to_hbm=True,
     )
-    window = lax.all_to_all(cut.reshape(128, 24, 128), DEVICES, 0, 0, tiled=True)
-    window = window.reshape(128 * 24, 128)
+    window = lax.all_to_all(cut, DEVICES, 0, 0, tiled=True)
     grad_x, grad_y, flow_x, flow_y = call(
         grad0_kernel,
         [wide, wide, wide, wide],

time: 100 us -> 98.3 us (0.983)
  waiting for transfers between devices: 36.1 us -> 32.7 us
  Pallas kernels: 25.5 us -> 26.7 us
    all_to_all x1, waiting for transfers between devices: 9.25 us -> 7.57 us  [shards(): lax.all_to_all(deal.reshape(128, 16, 128), DEVICES, 0, 0, tiled=True)]
    all_to_all x1, waiting for transfers between devices: 18.7 us -> 17.3 us  [shards(): window = lax.all_to_all(cut, DEVICES, 0, 0, tiled=True)]
    pallas_call x11 -> x12, Pallas kernels: 25.5 us -> 26.7 us  [call(): pl.pallas_call(kernel, out_shape=outs, in_specs=specs, out_specs=[pl.Bloc...]
  transfers between devices with their start and end apart: 18 -> 18, of which waited for: 6 -> 6; matrix products, arithmetic and copies ran while one was open for 0% -> 0% of each run, Pallas kernels for 14% -> 15%
where the time goes in v6:
time: 98.3 us; the launch traced here: 98 us
  starting transfers between devices  37.6 us (38%)
  waiting for transfers between devices  32.7 us (33%)
  Pallas kernels  26.7 us (27%)
    pallas_call x12, Pallas kernels, call(): pl.pallas_call(kernel, out_shape=outs, in_specs=specs, out_specs=[pl.Bloc...  26.7 us
    ppermute x16, starting transfers between devices, exchange(): lax.ppermute(face, plane, pairs)  20.6 us
    all_to_all x1, waiting for transfers between devices, shards(): window = lax.all_to_all(cut, DEVICES, 0, 0, tiled=True)  17.3 us
    all_to_all x1, starting transfers between devices, shards(): lax.all_to_all(deal.reshape(128, 16, 128), DEVICES, 0, 0, tiled=True)  10.3 us
    ppermute x16, waiting for transfers between devices, exchange(): lax.ppermute(face, plane, pairs)  7.9 us
    all_to_all x1, waiting for transfers between devices, shards(): lax.all_to_all(deal.reshape(128, 16, 128), DEVICES, 0, 0, tiled=True)  7.57 us
    all_to_all x1, starting transfers between devices, shards(): window = lax.all_to_all(cut, DEVICES, 0, 0, tiled=True)  6.61 us
  transfers between devices with their start and end apart: 18, of which 6 were waited for; matrix products, arithmetic and copies ran while one was open for 0% of the time, Pallas kernels for 15%

profile of v6, /device:TPU:16, one launch (start us, length us, event | category | flops | bytes accessed | tf_op | source)
XLA Modules:
  0.0 98.0 jit_solution(17837132092578184494)
XLA Ops:
  0.6 2.2 %pack.1._ = f32[2048,128]{1,0:T(8,128)} custom-call(f32[1024,128]{1,0:T(8,128)} %bitcast.23, f32[1024,128]{1,0:T(8,128)} %bitcast.24), custom_call_target="tpu_custom_call" | custom-call | tf_op jit(solution)/shard_map/pack/pallas_call | solution.py:594
  2.8 10.3 %all-to-all-start = ((f32[128,16,128]{2,1,0:T(8,128)}), f32[128,16,128]{2,1,0:T(8,128)S(1)}, u32[]{:S(2)}, u32[]{:S(2)}) async-start(f32[128,16,128]{2,1,0:T(8,128)} %bitcast.13), calls=%async_computation | async-start | bytes 2097152 | tf_op jit(solution)/shard_map/all_to_all | solution.py:656
  13.2 1.7 %first_faces.1 = (f32[352,128]{1,0:T(8,128)S(1)}, f32[352,128]{1,0:T(8,128)S(1)}, f32[352,128]{1,0:T(8,128)S(1)}, f32[352,128]{1,0:T(8,128)S(1)}) custom-call(f32[1024,128]{1,0:T(8,128)} %bitcast.14, f32[1024,128]{1,0:T(8,128)} %bitcast.18, f32[1024,128]{1,0:T(8,128)} %bitcast.20, f32[2048,128]{1,0:T(8,128)} %pack.1._), custom_call_target="tpu_custom_call" | custom-call | flops 20000000 | bytes 8000000 | tf_op jit(solution)/shard_map/first_faces/pallas_call | solution.py:594
  14.8 3.4 %collective-permute-start = (f32[352,128]{1,0:T(8,128)S(1)}, f32[352,128]{1,0:T(8,128)S(1)}, u32[]{:S(2)}, u32[]{:S(2)}) collective-permute-start(f32[352,128]{1,0:T(8,128)S(1)} %get-tuple-element.51), channel_id=1, source_target_pairs={{0,8},{1,2},{2,1},{3,4},{4,3},{5,6},{6,5},{7,15},{8,0},{9,10},{10,... | collective-permute-start | bytes 540680 | tf_op jit(solution)/shard_map/ppermute | solution.py:627
  18.4 1.9 %collective-permute-start.2 = (f32[352,128]{1,0:T(8,128)S(1)}, f32[352,128]{1,0:T(8,128)S(1)}, u32[]{:S(2)}, u32[]{:S(2)}) collective-permute-start(f32[352,128]{1,0:T(8,128)S(1)} %get-tuple-element.53), channel_id=1, source_target_pairs={{0,1},{1,0},{2,3},{3,2},{4,5},{5,4},{6,7},{7,6},{8,16},{9,17},{10,... | collective-permute-start | bytes 540680 | tf_op jit(solution)/shard_map/ppermute | solution.py:627
  20.5 2.2 %step0_depth.1._.refs_6_ = f32[1024,128]{1,0:T(8,128)} custom-call(bf16[384,128]{1,0:T(8,128)(2,1)S(1)} %copy-done.1, f32[1024,128]{1,0:T(8,128)} %bitcast.15), custom_call_target="tpu_custom_call" | custom-call | flops 30000001024 | bytes 8000000 | tf_op jit(solution)/shard_map/step0_depth/pallas_call | solution.py:594
  22.8 7.6 %all-to-all-done = f32[128,16,128]{2,1,0:T(8,128)S(1)} async-done(((f32[128,16,128]{2,1,0:T(8,128)}), f32[128,16,128]{2,1,0:T(8,128)S(1)}, u32[]{:S(2)}, u32[]{:S(2)}) %all-to-all-start) | async-done | bytes 1048608 | tf_op jit(solution)/shard_map/all_to_all | solution.py:656
  30.4 1.9 %cut.1 = f32[128,11,2,128]{3,2,1,0:T(2,128)} custom-call(s32[4,2]{1,0:T(4,128)S(1)} %copy.16.corners, f32[2048,128]{1,0:T(8,128)S(1)} %bitcast.12, f32[1024,128]{1,0:T(8,128)} %step0_depth.1._.refs_6_), custom_call_target="tpu_custom_call" | custom-call | tf_op jit(solution)/shard_map/cut/pallas_call | solution.py:594
  32.3 6.6 %all-to-all-start.1 = ((f32[128,11,2,128]{3,2,1,0:T(2,128)}), f32[128,11,2,128]{3,2,1,0:T(2,128)S(1)}, u32[]{:S(2)}, u32[]{:S(2)}) async-start(f32[128,11,2,128]{3,2,1,0:T(2,128)} %cut.1), calls=%async_computation.1 | async-start | bytes 2883584 | tf_op jit(solution)/shard_map/all_to_all | solution.py:687
  39.0 3.9 %step0_gradients.1 = (f32[1280,128]{1,0:T(8,128)}, f32[1280,128]{1,0:T(8,128)}, f32[1280,128]{1,0:T(8,128)}, f32[1280,128]{1,0:T(8,128)}) custom-call(f32[1024,128]{1,0:T(8,128)} %bitcast.16, f32[352,128]{1,0:T(8,128)S(1)} %collective-permute-done.gy_b, f32[352,128]{1,0:T(8,128)S(1)} %collective-permute-done.1.gy_a, ...), custom_call_target="tpu_custom_call" | custom-call | flops 30000001024 | bytes 8000000 | tf_op jit(solution)/shard_map/step0_gradients/pallas_call | solution.py:594
  42.9 17.3 %all-to-all-done.1.window = f32[128,11,2,128]{3,2,1,0:T(2,128)S(1)} async-done(((f32[128,11,2,128]{3,2,1,0:T(2,128)}), f32[128,11,2,128]{3,2,1,0:T(2,128)S(1)}, u32[]{:S(2)}, u32[]{:S(2)}) %all-to-all-start.1) | async-done | bytes 1441824 | tf_op jit(solution)/shard_map/all_to_all | solution.py:687
  60.2 3.7 %step0.1 = (f32[1024,128]{1,0:T(8,128)S(1)}, f32[1280,128]{1,0:T(8,128)S(1)}, f32[1280,128]{1,0:T(8,128)S(1)}, f32[1024,128]{1,0:T(8,128)S(1)}, f32[1600,128]{1,...) custom-call(s32[4,2]{1,0:T(4,128)S(1)} %copy.16.corners, ...), custom_call_target="tpu_custom_call" | custom-call | tf_op jit(solution)/shard_map/step0/pallas_call | solution.py:594
  63.9 2.9 %collective-permute-start.4 = (f32[224,128]{1,0:T(8,128)S(1)}, f32[224,128]{1,0:T(8,128)S(1)}, u32[]{:S(2)}, u32[]{:S(2)}) collective-permute-start(f32[224,128]{1,0:T(8,128)S(1)} %get-tuple-element.60), channel_id=1, source_target_pairs={{0,8},{1,2},{2,1},{3,4},{4,3},{5,6},{6,5},{7,15},{8,0},{9,10},{10,... | collective-permute-start | bytes 344072 | tf_op jit(solution)/shard_map/ppermute | solution.py:627
  66.8 2.0 %collective-permute-start.6 = (f32[224,128]{1,0:T(8,128)S(1)}, f32[224,128]{1,0:T(8,128)S(1)}, u32[]{:S(2)}, u32[]{:S(2)}) collective-permute-start(f32[224,128]{1,0:T(8,128)S(1)} %get-tuple-element.62), channel_id=1, source_target_pairs={{0,1},{1,0},{2,3},{3,2},{4,5},{5,4},{6,7},{7,6},{8,16},{9,17},{10,... | collective-permute-start | bytes 344072 | tf_op jit(solution)/shard_map/ppermute | solution.py:627
  70.3 3.2 %collective-permute-done.4.refs_3_ = f32[224,128]{1,0:T(8,128)S(1)} collective-permute-done((f32[224,128]{1,0:T(8,128)S(1)}, f32[224,128]{1,0:T(8,128)S(1)}, u32[]{:S(2)}, u32[]{:S(2)}) %collective-permute-start.4) | collective-permute-done | bytes 114720 | tf_op jit(solution)/shard_map/ppermute | solution.py:627
  73.5 1.7 %edge1.1 = (f32[1024,128]{1,0:T(8,128)S(1)}, f32[1280,128]{1,0:T(8,128)S(1)}, f32[1280,128]{1,0:T(8,128)S(1)}, f32[224,128]{1,0:T(8,128)S(1)}, f32[224,128]{1,0:...) custom-call(s32[4,3]{1,0:T(4,128)S(1)} %copy-done.2, f32[4,4]{1,0:T(4,128)S(1)} %copy-done.3, ...), custom_call_target="tpu_custom_call" | custom-call | tf_op jit(solution)/shard_map/edge1/pallas_call | solution.py:594
  75.2 2.9 %collective-permute-start.8 = (f32[224,128]{1,0:T(8,128)S(1)}, f32[224,128]{1,0:T(8,128)S(1)}, u32[]{:S(2)}, u32[]{:S(2)}) collective-permute-start(f32[224,128]{1,0:T(8,128)S(1)} %get-tuple-element.73), channel_id=1, source_target_pairs={{0,8},{1,2},{2,1},{3,4},{4,3},{5,6},{6,5},{7,15},{8,0},{9,10},{10,... | collective-permute-start | bytes 344072 | tf_op jit(solution)/shard_map/ppermute | solution.py:627
  78.2 2.0 %collective-permute-start.10 = (f32[224,128]{1,0:T(8,128)S(1)}, f32[224,128]{1,0:T(8,128)S(1)}, u32[]{:S(2)}, u32[]{:S(2)}) collective-permute-start(f32[224,128]{1,0:T(8,128)S(1)} %get-tuple-element.75), channel_id=1, source_target_pairs={{0,1},{1,0},{2,3},{3,2},{4,5},{5,4},{6,7},{7,6},{8,16},{9,17},{10,... | collective-permute-start | bytes 344072 | tf_op jit(solution)/shard_map/ppermute | solution.py:627
  81.8 3.0 %collective-permute-done.8.refs_3_ = f32[224,128]{1,0:T(8,128)S(1)} collective-permute-done((f32[224,128]{1,0:T(8,128)S(1)}, f32[224,128]{1,0:T(8,128)S(1)}, u32[]{:S(2)}, u32[]{:S(2)}) %collective-permute-start.8) | collective-permute-done | bytes 114720 | tf_op jit(solution)/shard_map/ppermute | solution.py:627
  84.8 1.7 %edge2.1 = (f32[1024,128]{1,0:T(8,128)S(1)}, f32[1280,128]{1,0:T(8,128)S(1)}, f32[1280,128]{1,0:T(8,128)S(1)}, f32[224,128]{1,0:T(8,128)S(1)}, f32[224,128]{1,0:...) custom-call(s32[4,3]{1,0:T(4,128)S(1)} %copy-done.2, f32[4,4]{1,0:T(4,128)S(1)} %copy-done.3, ...), custom_call_target="tpu_custom_call" | custom-call | tf_op jit(solution)/shard_map/edge2/pallas_call | solution.py:594
  86.5 3.1 %collective-permute-start.12 = (f32[224,128]{1,0:T(8,128)S(1)}, f32[224,128]{1,0:T(8,128)S(1)}, u32[]{:S(2)}, u32[]{:S(2)}) collective-permute-start(f32[224,128]{1,0:T(8,128)S(1)} %get-tuple-element.84), channel_id=1, source_target_pairs={{0,8},{1,2},{2,1},{3,4},{4,3},{5,6},{6,5},{7,15},{8,0},{9,10},{10,... | collective-permute-start | bytes 344072 | tf_op jit(solution)/shard_map/ppermute | solution.py:627
  89.6 2.0 %collective-permute-start.14 = (f32[224,128]{1,0:T(8,128)S(1)}, f32[224,128]{1,0:T(8,128)S(1)}, u32[]{:S(2)}, u32[]{:S(2)}) collective-permute-start(f32[224,128]{1,0:T(8,128)S(1)} %get-tuple-element.86), channel_id=1, source_target_pairs={{0,1},{1,0},{2,3},{3,2},{4,5},{5,4},{6,7},{7,6},{8,16},{9,17},{10,... | collective-permute-start | bytes 344072 | tf_op jit(solution)/shard_map/ppermute | solution.py:627
  91.6 2.3 %inner3.1 = (f32[1280,128]{1,0:T(8,128)S(1)}, f32[1280,128]{1,0:T(8,128)S(1)}, f32[1024,128]{1,0:T(8,128)}, f32[1024,128]{1,0:T(8,128)S(1)}) custom-call(bf16[384,128]{1,0:T(8,128)(2,1)S(1)} %copy-done.1, bf16[384,128]{1,0:T(8,128)(2,1)S(1)} %copy-done, f32[1024,128]{1,0:T(8,128)S(1)} %get-tuple-element.83.pres.refs_2_, ...), custom_call_target="tpu_custom_call" | custom-call | flops 20000000 | bytes 8000000 | tf_op jit(solution)/shard_map/inner3/pallas_call | solution.py:594
  95.6 2.3 %edge3.1 = (f32[1024,128]{1,0:T(8,128)}, f32[1024,128]{1,0:T(8,128)}, f32[1024,128]{1,0:T(8,128)}) custom-call(s32[4,3]{1,0:T(4,128)S(1)} %copy-done.2, f32[4,4]{1,0:T(4,128)S(1)} %copy-done.3, f32[1024,128]{1,0:T(8,128)S(1)} %get-tuple-element.83.pres.refs_2_, f32[224,128]{1,0:T(8,128)S(1)} %collective-permute-done.12.refs_3_, ...), custom_call_target="tpu_custom_call" | custom-call | tf_op jit(solution)/shard_map/edge3/pallas_call | solution.py:594
  (35 shorter events, 5.3 us)
Async XLA Ops:
  2.8 27.6 %all-to-all-start = ((f32[128,16,128]{2,1,0:T(8,128)}), f32[128,16,128]{2,1,0:T(8,128)S(1)}, u32[]{:S(2)}, u32[]{:S(2)}) async-start(f32[128,16,128]{2,1,0:T(8,128)} %bitcast.13), calls=%async_computation | async-start | bytes 2097152 | tf_op jit(solution)/shard_map/all_to_all | solution.py:656
  13.2 7.3 %copy-start.1 = (bf16[384,128]{1,0:T(8,128)(2,1)S(1)}, bf16[384,128]{1,0:T(8,128)(2,1)}, u32[]{:S(2)}) copy-start(bf16[384,128]{1,0:T(8,128)(2,1)} %constant.4.clone.mat_f) | copy-start | bytes 294916
  14.8 24.1 %collective-permute-start = (f32[352,128]{1,0:T(8,128)S(1)}, f32[352,128]{1,0:T(8,128)S(1)}, u32[]{:S(2)}, u32[]{:S(2)}) collective-permute-start(f32[352,128]{1,0:T(8,128)S(1)} %get-tuple-element.51), channel_id=1, source_target_pairs={{0,8},{1,2},{2,1},{3,4},{4,3},{5,6},{6,5},{7,15},{8,0},{9,10},{10,... | collective-permute-start | bytes 540680 | tf_op jit(solution)/shard_map/ppermute | solution.py:627
  18.2 20.7 %collective-permute-start.1 = (f32[352,128]{1,0:T(8,128)S(1)}, f32[352,128]{1,0:T(8,128)S(1)}, u32[]{:S(2)}, u32[]{:S(2)}) collective-permute-start(f32[352,128]{1,0:T(8,128)S(1)} %get-tuple-element.52), channel_id=1, source_target_pairs={{0,1},{1,0},{2,3},{3,2},{4,5},{5,4},{6,7},{7,6},{8,9},{9,8},{10,11... | collective-permute-start | bytes 540680 | tf_op jit(solution)/shard_map/ppermute | solution.py:627
  18.4 20.6 %collective-permute-start.2 = (f32[352,128]{1,0:T(8,128)S(1)}, f32[352,128]{1,0:T(8,128)S(1)}, u32[]{:S(2)}, u32[]{:S(2)}) collective-permute-start(f32[352,128]{1,0:T(8,128)S(1)} %get-tuple-element.53), channel_id=1, source_target_pairs={{0,1},{1,0},{2,3},{3,2},{4,5},{5,4},{6,7},{7,6},{8,16},{9,17},{10,... | collective-permute-start | bytes 540680 | tf_op jit(solution)/shard_map/ppermute | solution.py:627
  20.3 2.5 %copy-start.4 = (s32[4,2]{0,1:T(2,128)S(1)}, s32[4,2]{0,1:T(2,128)}, u32[]{:S(2)}) copy-start(s32[4,2]{0,1:T(2,128)} %param.13) | copy-start | bytes 100
  20.3 18.7 %collective-permute-start.3 = (f32[352,128]{1,0:T(8,128)S(1)}, f32[352,128]{1,0:T(8,128)S(1)}, u32[]{:S(2)}, u32[]{:S(2)}) collective-permute-start(f32[352,128]{1,0:T(8,128)S(1)} %get-tuple-element.54), channel_id=1, source_target_pairs={{0,8},{1,9},{2,10},{3,11},{4,12},{5,13},{6,14},{7,15},{8,0},{9,1},... | collective-permute-start | bytes 540680 | tf_op jit(solution)/shard_map/ppermute | solution.py:627
  32.3 27.9 %all-to-all-start.1 = ((f32[128,11,2,128]{3,2,1,0:T(2,128)}), f32[128,11,2,128]{3,2,1,0:T(2,128)S(1)}, u32[]{:S(2)}, u32[]{:S(2)}) async-start(f32[128,11,2,128]{3,2,1,0:T(2,128)} %cut.1), calls=%async_computation.1 | async-start | bytes 2883584 | tf_op jit(solution)/shard_map/all_to_all | solution.py:687
  38.9 21.2 %copy-start = (bf16[384,128]{1,0:T(8,128)(2,1)S(1)}, bf16[384,128]{1,0:T(8,128)(2,1)}, u32[]{:S(2)}) copy-start(bf16[384,128]{1,0:T(8,128)(2,1)} %constant.5.clone.mat_b) | copy-start | bytes 294916
  38.9 21.2 %copy-start.2 = (s32[4,3]{1,0:T(4,128)S(1)}, s32[4,3]{1,0:T(4,128)}, u32[]{:S(2)}) copy-start(s32[4,3]{1,0:T(4,128)} %refs_0_.5) | copy-start | bytes 148
  39.0 21.2 %copy-start.3 = (f32[4,4]{1,0:T(4,128)S(1)}, f32[4,4]{1,0:T(4,128)}, u32[]{:S(2)}) copy-start(f32[4,4]{1,0:T(4,128)} %refs_1_.5) | copy-start | bytes 196
  63.9 9.6 %collective-permute-start.4 = (f32[224,128]{1,0:T(8,128)S(1)}, f32[224,128]{1,0:T(8,128)S(1)}, u32[]{:S(2)}, u32[]{:S(2)}) collective-permute-start(f32[224,128]{1,0:T(8,128)S(1)} %get-tuple-element.60), channel_id=1, source_target_pairs={{0,8},{1,2},{2,1},{3,4},{4,3},{5,6},{6,5},{7,15},{8,0},{9,10},{10,... | collective-permute-start | bytes 344072 | tf_op jit(solution)/shard_map/ppermute | solution.py:627
  66.8 6.7 %collective-permute-start.5 = (f32[224,128]{1,0:T(8,128)S(1)}, f32[224,128]{1,0:T(8,128)S(1)}, u32[]{:S(2)}, u32[]{:S(2)}) collective-permute-start(f32[224,128]{1,0:T(8,128)S(1)} %get-tuple-element.61), channel_id=1, source_target_pairs={{0,1},{1,0},{2,3},{3,2},{4,5},{5,4},{6,7},{7,6},{8,9},{9,8},{10,11... | collective-permute-start | bytes 344072 | tf_op jit(solution)/shard_map/ppermute | solution.py:627
  66.8 6.7 %collective-permute-start.6 = (f32[224,128]{1,0:T(8,128)S(1)}, f32[224,128]{1,0:T(8,128)S(1)}, u32[]{:S(2)}, u32[]{:S(2)}) collective-permute-start(f32[224,128]{1,0:T(8,128)S(1)} %get-tuple-element.62), channel_id=1, source_target_pairs={{0,1},{1,0},{2,3},{3,2},{4,5},{5,4},{6,7},{7,6},{8,16},{9,17},{10,... | collective-permute-start | bytes 344072 | tf_op jit(solution)/shard_map/ppermute | solution.py:627
  68.8 4.7 %collective-permute-start.7 = (f32[224,128]{1,0:T(8,128)S(1)}, f32[224,128]{1,0:T(8,128)S(1)}, u32[]{:S(2)}, u32[]{:S(2)}) collective-permute-start(f32[224,128]{1,0:T(8,128)S(1)} %get-tuple-element.63), channel_id=1, source_target_pairs={{0,8},{1,9},{2,10},{3,11},{4,12},{5,13},{6,14},{7,15},{8,0},{9,1},... | collective-permute-start | bytes 344072 | tf_op jit(solution)/shard_map/ppermute | solution.py:627
  75.2 9.6 %collective-permute-start.8 = (f32[224,128]{1,0:T(8,128)S(1)}, f32[224,128]{1,0:T(8,128)S(1)}, u32[]{:S(2)}, u32[]{:S(2)}) collective-permute-start(f32[224,128]{1,0:T(8,128)S(1)} %get-tuple-element.73), channel_id=1, source_target_pairs={{0,8},{1,2},{2,1},{3,4},{4,3},{5,6},{6,5},{7,15},{8,0},{9,10},{10,... | collective-permute-start | bytes 344072 | tf_op jit(solution)/shard_map/ppermute | solution.py:627
  78.2 6.6 %collective-permute-start.9 = (f32[224,128]{1,0:T(8,128)S(1)}, f32[224,128]{1,0:T(8,128)S(1)}, u32[]{:S(2)}, u32[]{:S(2)}) collective-permute-start(f32[224,128]{1,0:T(8,128)S(1)} %get-tuple-element.74), channel_id=1, source_target_pairs={{0,1},{1,0},{2,3},{3,2},{4,5},{5,4},{6,7},{7,6},{8,9},{9,8},{10,11... | collective-permute-start | bytes 344072 | tf_op jit(solution)/shard_map/ppermute | solution.py:627
  78.2 6.6 %collective-permute-start.10 = (f32[224,128]{1,0:T(8,128)S(1)}, f32[224,128]{1,0:T(8,128)S(1)}, u32[]{:S(2)}, u32[]{:S(2)}) collective-permute-start(f32[224,128]{1,0:T(8,128)S(1)} %get-tuple-element.75), channel_id=1, source_target_pairs={{0,1},{1,0},{2,3},{3,2},{4,5},{5,4},{6,7},{7,6},{8,16},{9,17},{10,... | collective-permute-start | bytes 344072 | tf_op jit(solution)/shard_map/ppermute | solution.py:627
  80.2 4.6 %collective-permute-start.11 = (f32[224,128]{1,0:T(8,128)S(1)}, f32[224,128]{1,0:T(8,128)S(1)}, u32[]{:S(2)}, u32[]{:S(2)}) collective-permute-start(f32[224,128]{1,0:T(8,128)S(1)} %get-tuple-element.76), channel_id=1, source_target_pairs={{0,8},{1,9},{2,10},{3,11},{4,12},{5,13},{6,14},{7,15},{8,0},{9,1},... | collective-permute-start | bytes 344072 | tf_op jit(solution)/shard_map/ppermute | solution.py:627
  86.5 8.6 %collective-permute-start.12 = (f32[224,128]{1,0:T(8,128)S(1)}, f32[224,128]{1,0:T(8,128)S(1)}, u32[]{:S(2)}, u32[]{:S(2)}) collective-permute-start(f32[224,128]{1,0:T(8,128)S(1)} %get-tuple-element.84), channel_id=1, source_target_pairs={{0,8},{1,2},{2,1},{3,4},{4,3},{5,6},{6,5},{7,15},{8,0},{9,10},{10,... | collective-permute-start | bytes 344072 | tf_op jit(solution)/shard_map/ppermute | solution.py:627
  89.6 5.6 %collective-permute-start.13 = (f32[224,128]{1,0:T(8,128)S(1)}, f32[224,128]{1,0:T(8,128)S(1)}, u32[]{:S(2)}, u32[]{:S(2)}) collective-permute-start(f32[224,128]{1,0:T(8,128)S(1)} %get-tuple-element.85), channel_id=1, source_target_pairs={{0,1},{1,0},{2,3},{3,2},{4,5},{5,4},{6,7},{7,6},{8,9},{9,8},{10,11... | collective-permute-start | bytes 344072 | tf_op jit(solution)/shard_map/ppermute | solution.py:627
  89.6 6.0 %collective-permute-start.14 = (f32[224,128]{1,0:T(8,128)S(1)}, f32[224,128]{1,0:T(8,128)S(1)}, u32[]{:S(2)}, u32[]{:S(2)}) collective-permute-start(f32[224,128]{1,0:T(8,128)S(1)} %get-tuple-element.86), channel_id=1, source_target_pairs={{0,1},{1,0},{2,3},{3,2},{4,5},{5,4},{6,7},{7,6},{8,16},{9,17},{10,... | collective-permute-start | bytes 344072 | tf_op jit(solution)/shard_map/ppermute | solution.py:627
  91.6 4.0 %collective-permute-start.15 = (f32[224,128]{1,0:T(8,128)S(1)}, f32[224,128]{1,0:T(8,128)S(1)}, u32[]{:S(2)}, u32[]{:S(2)}) collective-permute-start(f32[224,128]{1,0:T(8,128)S(1)} %get-tuple-element.87), channel_id=1, source_target_pairs={{0,8},{1,9},{2,10},{3,11},{4,12},{5,13},{6,14},{7,15},{8,0},{9,1},... | collective-permute-start | bytes 344072 | tf_op jit(solution)/shard_map/ppermute | solution.py:627

commit v7 on v6

--- a/solution.py
+++ b/solution.py
@@ -245,9 +245,9 @@
     push.wait()
 
 
-def grad0_kernel(pres_from, gy_b, gy_a, gx_b, gx_a, x_from, y_from, *refs):
-    outs, scratch = refs[:4], refs[4:]
-    grad_x, grad_y, wide_x, wide_y, padded, pres, in_x, in_y, in_sem, out_sem = scratch
+def grad0_kernel(cells, amps, pres_from, gy_b, gy_a, gx_b, gx_a, x_from, y_from, *refs):
+    outs, scratch = refs[:5], refs[5:]
+    grad_x, grad_y, wide_x, wide_y, pres, padded, in_x, in_y, in_sem, out_sem = scratch
     for pull in pull_all(((pres_from, pres), (x_from, in_x), (y_from, in_y)), in_sem):
         pull.wait()
     s, g, h = place()
@@ -304,16 +304,17 @@
         return carry
 
     lax.fori_loop(0, CX, along_y, 0)
-    for push in pull_all(zip(scratch[:4], outs), out_sem):
+    kick_source(0, cells, amps, pres)
+    for push in pull_all(zip(scratch[:5], outs), out_sem):
         push.wait()
 
 
-def kick_source(step, cells, amps, field, first=0, end=CX):
+def kick_source(step, cells, amps, field):
     s, g, h = place()
     x = cells[s, 0] - g * CX
     y = cells[s, 1] - h * CY
 
-    @pl.when((x >= first) & (x < end) & (y >= 0) & (y < CY))
+    @pl.when((x >= 0) & (x < CX) & (y >= 0) & (y < CY))
     def _():
         at = x * CY + y
         lane = lax.broadcasted_iota(jnp.int32, (1, 128), 1)
@@ -321,7 +322,7 @@
         field[pl.ds(at, 1), :] = field[pl.ds(at, 1), :] + jnp.where(lane == cells[s, 2], kick, 0.0)
 
 
-def step0_kernel(corners, cells, amps, mat_b, window, *refs):
+def step0_kernel(corners, mat_b, window, *refs):
     sources, outs, scratch = refs[:7], refs[7:17], refs[17:]
     new_p, wide_x, wide_y, new_z, buoy, modu, gy_b, gy_a, gx_b, gx_a = outs
     pres, in_x, in_y, in_z, grad_x, grad_y, grad_z, rho, spread, sem = scratch
@@ -329,46 +330,30 @@
     pulls = pull_all([(sources[i], scratch[i]) for i in order], sem)
     unpack_model(corners, window, buoy, modu, rho)
 
-    def flow_x(x, carry):
-        for n in range(4):
-            at = pl.multiple_of(x * CY + n * 8, 8)
-            wide_x[pl.ds(at, 8), :] = (
-                in_x[pl.ds(at, 8), :] - buoy_at(buoy, x - 4, n * 8) * grad_x[pl.ds(at, 8), :]
-            )
-        return carry
-
-    def flow_y(x, carry):
-        for n in range(5):
-            at = pl.multiple_of(x * WIDE + n * 8, 8)
-            wide_y[pl.ds(at, 8), :] = (
-                in_y[pl.ds(at, 8), :] - buoy_at(buoy, x, n * 8 - 4) * grad_y[pl.ds(at, 8), :]
-            )
-        return carry
-
-    def flow_z(x, carry):
-        for n in range(4):
-            at = pl.multiple_of(x * CY + n * 8, 8)
-            new_z[pl.ds(at, 8), :] = (
-                in_z[pl.ds(at, 8), :] - buoy_at(buoy, x, n * 8) * grad_z[pl.ds(at, 8), :]
-            )
-        return carry
-
     def wait(*which):
         for i in which:
             pulls[i].wait()
 
+    def tiles(count, per):
+        return [(x, n, (x * per + n) * 8) for x in range(count) for n in range(per)]
+
     wait(0, 1)
-    lax.fori_loop(0, CX, flow_z, 0, unroll=4)
+    for x, n, at in tiles(CX, 4):
+        new_z[at : at + 8, :] = in_z[at : at + 8, :] - buoy_at(buoy, x, n * 8) * grad_z[at : at + 8, :]
     for chunk in range(8):
         rows = slice(chunk * 128, (chunk + 1) * 128)
         spread[rows, :] = depth_difference(new_z[rows, :], mat_b)
     wait(2, 3)
-    lax.fori_loop(0, WIDE, flow_x, 0, unroll=4)
+    for x, n, at in tiles(WIDE, 4):
+        wide_x[at : at + 8, :] = (
+            in_x[at : at + 8, :] - buoy_at(buoy, x - 4, n * 8) * grad_x[at : at + 8, :]
+        )
     wait(4, 5, 6)
-    lax.fori_loop(0, CX, flow_y, 0, unroll=4)
-
-    def update(chunk, carry):
-        x0 = chunk * 4
+    for x, n, at in tiles(CX, 5):
+        wide_y[at : at + 8, :] = (
+            in_y[at : at + 8, :] - buoy_at(buoy, x, n * 8 - 4) * grad_y[at : at + 8, :]
+        )
+    for x0 in range(0, CX, 4):
         part_x = {}
         for j in range(4):
             taps = [every(wide_x, (x0 + d + 4) * CY + j, 4) for d in range(-4, 7)]
@@ -380,14 +365,13 @@
                 at = (x0 + i) * CY + j
                 total = part_x[i, j] + backward(taps, j) + every(spread, at, 4)
                 put_every(new_p, at, 4, every(pres, at, 4) - every(modu, at, 4) * total)
-        return carry
-
-    lax.fori_loop(0, 8, update, 0)
-    kick_source(0, cells, amps, new_p)
     send_faces(new_p, (gx_a, gx_b), (gy_a, gy_b), 0, HALO)
 
 
-def inner_kernel(mat_f, mat_b, pres, in_x, in_y, in_z, buoy, wide_x, wide_y, new_z, spread):
+def inner_kernel(step, cells, amps, mat_f, mat_b, pres, in_x, in_y, in_z, buoy, *outs):
+    wide_x, wide_y, new_z, spread, kicked = outs
+    kicked[...] = pres[...]
+    kick_source(step, cells, amps, kicked)
     for chunk in range(8):
         rows = slice(chunk * 128, (chunk + 1) * 128)
         grad = depth_difference(pres[rows, :], mat_f)
@@ -454,10 +438,10 @@
 
 
 def edge_kernel(step, *refs):
-    cells, amps, pres, gy_b, gy_a, gx_b, gx_a, in_x, in_y, buoy, modu, spread = refs[:12]
+    pres, gy_b, gy_a, gx_b, gx_a, in_x, in_y, buoy, modu, spread, kicked = refs[:11]
     last = step == STEPS - 1
     if last:
-        p_to, x_to, y_to, low_x, high_x, low_y, high_y, wide_x, wide_y, new_p, out_y, sem = refs[12:]
+        p_to, x_to, y_to, rim_x, rim_y, wide_x, wide_y, new_p, out_y, sem = refs[11:]
         pushes = []
 
         def push(src, dst, rows):
@@ -465,51 +449,36 @@
             pushes[-1].start()
 
     else:
-        new_p, wide_x, wide_y, to_d, to_c, to_b, to_a, low_x, high_x, low_y, high_y = refs[12:]
+        new_p, wide_x, wide_y, to_d, to_c, to_b, to_a, rim_x, rim_y = refs[11:]
+    s, g, h = place()
+    end_x = (g == 0) | (g == 3)
+    end_y = (h == 0) | (h == 7)
+    for which in range(2):
+        low = odd(g) if which == 0 else jnp.logical_not(odd(g))
+        start = jnp.where(low, 1, 24) * CY
+        for i in range(HALO):
+            for part in range(4):
+                at = pl.multiple_of(start + (i * CY + part * 8), 8)
+                rim_x[pl.ds(at, 8), :] = received((gx_a, gx_b), which, end_x, i * 32 + part * 8)
+        low = odd(h) if which == 0 else jnp.logical_not(odd(h))
+        start = jnp.where(low, 1, CX * STRIP + 8)
+        for c in range(HALO):
+            for part in range(4):
+                value = received((gy_a, gy_b), which, end_y, c * 32 + part * 8)
+                put_every(rim_y, start + (part * 8 * STRIP + c), STRIP, value)
+    rim_x[8 * CY : 24 * CY, :] = jnp.concatenate([pres[0 : 8 * CY, :], pres[24 * CY : 32 * CY, :]], axis=0)
+    for x in range(CX):
+        rim_y[x * STRIP + 8 : x * STRIP + 16, :] = pres[x * CY : x * CY + 8, :]
+        at = (CX + x) * STRIP
+        rim_y[at : at + 8, :] = pres[x * CY + 24 : x * CY + 32, :]
     wide_x[8 * CY : 32 * CY, :] = in_x[8 * CY : 32 * CY, :]
     for x in range(CX):
         wide_y[x * WIDE + 8 : x * WIDE + 32, :] = in_y[x * WIDE + 8 : x * WIDE + 32, :]
-    s, g, h = place()
-    end_x = (g == 0) | (g == 3)
-    end_y = (h == 0) | (h == 7)
-    x_pair, y_pair = (gx_a, gx_b), (gy_a, gy_b)
-    low_x[8 * CY : 16 * CY, :] = pres[0 : 8 * CY, :]
-    high_x[0 : 8 * CY, :] = pres[24 * CY : 32 * CY, :]
-    for x in range(CX):
-        low_y[x * STRIP + 8 : x * STRIP + 16, :] = pres[x * CY : x * CY + 8, :]
-        high_y[x * STRIP : x * STRIP + 8, :] = pres[x * CY + 24 : x * CY + 32, :]
-
-    def place_x(which, ref, start):
-        for i in range(HALO):
-            for part in range(4):
-                at = (start + i) * CY + part * 8
-                ref[at : at + 8, :] = received(x_pair, which, end_x, i * 32 + part * 8)
-
-    def place_y(which, ref, start):
-        for c in range(HALO):
-            for part in range(4):
-                value = received(y_pair, which, end_y, c * 32 + part * 8)
-                put_every(ref, part * 8 * STRIP + start + c, STRIP, value)
-
-    for where, put, low, high in ((g, place_x, low_x, high_x), (h, place_y, low_y, high_y)):
-
-        @pl.when(odd(where))
-        def _():
-            put(0, low, 1)
-            put(1, high, 8)
-
-        @pl.when(jnp.logical_not(odd(where)))
-        def _():
-            put(1, low, 1)
-            put(0, high, 8)
-
-    for strip, first in ((low_x, -4), (high_x, 28)):
+    for rim, first in ((0, -4), (16, 28)):
         for half in range(2):
             for n in range(4):
-                taps = [
-                    strip[(half * 4 + 4 + d) * CY + n * 8 : (half * 4 + 4 + d) * CY + n * 8 + 8, :]
-                    for d in range(-3, 8)
-                ]
+                mid = (rim + half * 4 + 4) * CY + n * 8
+                taps = [rim_x[mid + d * CY : mid + d * CY + 8, :] for d in range(-3, 8)]
                 for i in range(4):
                     x = first + half * 4 + i
                     at = (x + 4) * CY + n * 8
@@ -519,44 +488,36 @@
 
     if last:
         push(wide_x.at[pl.ds(4 * CY, CX * CY)], x_to, pl.ds(0, CX * CY))
-
-    def rows(x0, with_x):
-        part_x = {}
-        if with_x:
-            for n in range(4):
-                taps = [
-                    wide_x[pl.ds(pl.multiple_of((x0 + d + 4) * CY + n * 8, 8), 8), :]
-                    for d in range(-4, 7)
-                ]
-                for i in range(4):
-                    part_x[i, n] = backward(taps, i)
-        for i in range(4):
-            x = x0 + i
-            for strip, col in ((low_y, 0), (high_y, 32)):
-                taps = [strip[pl.ds(x * STRIP + 4 + d, 8), :] for d in range(-3, 5)]
-                at = pl.multiple_of(x * WIDE + col, 8)
-                wide_y[pl.ds(at, 8), :] = in_y[pl.ds(at, 8), :] - buoy_at(
-                    buoy, x, col - 4
-                ) * forward(taps, 0)
-            for n in range(4):
-                at = pl.multiple_of(x * CY + n * 8, 8)
-                total = spread[pl.ds(at, 8), :]
-                if n in (0, 3):
-                    taps = [wide_y[pl.ds(x * WIDE + 4 + n * 8 + d, 8), :] for d in range(-4, 4)]
-                    total = total + backward(taps, 0)
-                if with_x:
-                    total = total + part_x[i, n]
-                new_p[pl.ds(at, 8), :] = pres[pl.ds(at, 8), :] - modu[pl.ds(at, 8), :] * total
-
-    for first, count, with_x in ((0, 2, True), (8, 4, False), (24, 2, True)):
-
-        def some(chunk, carry):
-            rows(first + chunk * 4, with_x)
-            return carry
-
-        lax.fori_loop(0, count, some, 0)
+    for x in range(CX):
+        for rim, col in ((0, 0), (CX, 32)):
+            mid = (rim + x) * STRIP + 4
+            taps = [rim_y[mid + d : mid + d + 8, :] for d in range(-3, 5)]
+            at = x * WIDE + col
+            wide_y[at : at + 8, :] = in_y[at : at + 8, :] - buoy_at(buoy, x, col - 4) * forward(taps, 0)
+
+    for first, count in ((0, 2), (8, 4), (24, 2)):
+        for x0 in range(first, first + count * 4, 4):
+            part_x = {}
+            if count == 2:
+                for n in range(4):
+                    taps = [
+                        wide_x[(x0 + d + 4) * CY + n * 8 : (x0 + d + 4) * CY + n * 8 + 8, :]
+                        for d in range(-4, 7)
+                    ]
+                    for i in range(4):
+                        part_x[i, n] = backward(taps, i)
+            for i in range(4):
+                for n in range(4):
+                    at = (x0 + i) * CY + n * 8
+                    total = spread[at : at + 8, :]
+                    if n in (0, 3):
+                        mid = (x0 + i) * WIDE + 4 + n * 8
+                        taps = [wide_y[mid + d : mid + d + 8, :] for d in range(-4, 4)]
+                        total = total + backward(taps, 0)
+                    if count == 2:
+                        total = total + part_x[i, n]
+                    new_p[at : at + 8, :] = kicked[at : at + 8, :] - modu[at : at + 8, :] * total
         if last:
-            kick_source(step, cells, amps, new_p, first, first + count * 4)
             for x in range(first, first + count * 4):
                 out_y[x * CY : (x + 1) * CY, :] = wide_y[x * WIDE + 4 : x * WIDE + 36, :]
             part = pl.ds(first * CY, count * 4 * CY)
@@ -566,7 +527,6 @@
         for copy in pushes:
             copy.wait()
     else:
-        kick_source(step, cells, amps, new_p)
         send_faces(new_p, (to_a, to_b), (to_c, to_d), 0, HALO)
 
 
@@ -685,48 +645,49 @@
         to_hbm=True,
     )
     window = lax.all_to_all(cut, DEVICES, 0, 0, tiled=True)
-    grad_x, grad_y, flow_x, flow_y = call(
+    grad_x, grad_y, flow_x, flow_y, pres = call(
         grad0_kernel,
-        [wide, wide, wide, wide],
-        [pres, *faces, flow_x, flow_y],
-        [vmem(WIDE * CY)] * 4
-        + [vmem(PAD * PAD)] + [vmem(CX * CY)] * 3 + [dma((3,)), dma((4,))],
+        [wide, wide, wide, wide, block],
+        [source_cells, wavelet, pres, *faces, flow_x, flow_y],
+        [vmem(WIDE * CY)] * 4 + [vmem(CX * CY)]
+        + [vmem(PAD * PAD)] + [vmem(CX * CY)] * 2 + [dma((3,)), dma((5,))],
         "step0_gradients",
-        hbm=(0, 5, 6),
+        smem=2,
+        hbm=(2, 7, 8),
         to_hbm=True,
         cost=long,
     )
     pres, flow_x, flow_y, flow_z, buoy, modu, *faces = call(
         step0_kernel,
         [block, wide, wide, block, shape(WIDE * WIDE), block] + [face] * 4,
-        [offsets, source_cells, wavelet, mat_b, window]
+        [offsets, mat_b, window]
         + [pres, flow_x, flow_y, flow_z, grad_x, grad_y, grad_z],
         [vmem(CX * CY), vmem(WIDE * CY), vmem(WIDE * CY), vmem(CX * CY)]
         + [vmem(WIDE * CY), vmem(WIDE * CY), vmem(CX * CY)]
         + [vmem(WIDE * WIDE), vmem(CX * CY), dma((7,))],
         "step0",
-        smem=3,
-        hbm=range(5, 12),
+        smem=1,
+        hbm=range(3, 10),
     )
     for step in range(1, STEPS):
         last = step == STEPS - 1
         faces = exchange(faces)
-        flow_x, flow_y, flow_z, spread = call(
-            inner_kernel,
-            [wide, wide, block, block],
-            [mat_f, mat_b, pres, flow_x, flow_y, flow_z, buoy],
+        flow_x, flow_y, flow_z, spread, kicked = call(
+            functools.partial(inner_kernel, step),
+            [wide, wide, block, block, block],
+            [source_cells, wavelet, mat_f, mat_b, pres, flow_x, flow_y, flow_z, buoy],
             [],
             f"inner{step}",
+            smem=2,
             cost=cost,
         )
         pres, flow_x, flow_y, *faces = call(
             functools.partial(edge_kernel, step),
             [block, block, block] if last else [block, wide, wide] + [face] * 4,
-            [source_cells, wavelet, pres, *faces, flow_x, flow_y, buoy, modu, spread],
-            [vmem(16 * CY), vmem(16 * CY), vmem(CX * STRIP), vmem(CX * STRIP)]
+            [pres, *faces, flow_x, flow_y, buoy, modu, spread, kicked],
+            [vmem(32 * CY), vmem(2 * CX * STRIP)]
             + ([vmem(WIDE * CY)] * 2 + [vmem(CX * CY)] * 2 + [dma((7,))] if last else []),
             f"edge{step}",
-            smem=2,
             to_hbm=last or (),
         )
     return tuple(a.reshape(1, CX, CY, 128) for a in (pres, flow_x, flow_y, flow_z))

time: 98.3 us -> 95.9 us (0.976)
  waiting for transfers between devices: 32.7 us -> 30.1 us
    ppermute x16, waiting for transfers between devices: 7.9 us -> 6.09 us  [exchange(): lax.ppermute(face, plane, pairs)]
  transfers between devices with their start and end apart: 18 -> 18, of which waited for: 6 -> 6; matrix products, arithmetic and copies ran while one was open for 0% -> 0% of each run, Pallas kernels for 15% -> 19%
where the time goes in v7:
time: 95.9 us; the launch traced here: 95.5 us
  starting transfers between devices  37.5 us (39%)
  waiting for transfers between devices  30.1 us (31%)
  Pallas kernels  26.9 us (28%)
    pallas_call x12, Pallas kernels, call(): pl.pallas_call(kernel, out_shape=outs, in_specs=specs, out_specs=[pl.Bloc...  26.9 us
    ppermute x16, starting transfers between devices, exchange(): lax.ppermute(face, plane, pairs)  20.6 us
    all_to_all x1, waiting for transfers between devices, shards(): window = lax.all_to_all(cut, DEVICES, 0, 0, tiled=True)  16.5 us
    all_to_all x1, starting transfers between devices, shards(): lax.all_to_all(deal.reshape(128, 16, 128), DEVICES, 0, 0, tiled=True)  10.3 us
    all_to_all x1, waiting for transfers between devices, shards(): lax.all_to_all(deal.reshape(128, 16, 128), DEVICES, 0, 0, tiled=True)  7.57 us
    all_to_all x1, starting transfers between devices, shards(): window = lax.all_to_all(cut, DEVICES, 0, 0, tiled=True)  6.61 us
    ppermute x16, waiting for transfers between devices, exchange(): lax.ppermute(face, plane, pairs)  6.09 us
  transfers between devices with their start and end apart: 18, of which 6 were waited for; matrix products, arithmetic and copies ran while one was open for 0% of the time, Pallas kernels for 19%

profile of v7, /device:TPU:16, one launch (start us, length us, event | category | flops | bytes accessed | tf_op | source)
XLA Modules:
  0.0 95.5 jit_solution(17279687606657792638)
XLA Ops:
  0.6 2.2 %pack.1._ = f32[2048,128]{1,0:T(8,128)} custom-call(f32[1024,128]{1,0:T(8,128)} %bitcast.21, f32[1024,128]{1,0:T(8,128)} %bitcast.22), custom_call_target="tpu_custom_call" | custom-call | tf_op jit(solution)/shard_map/pack/pallas_call | solution.py:554
  2.8 10.3 %all-to-all-start = ((f32[128,16,128]{2,1,0:T(8,128)}), f32[128,16,128]{2,1,0:T(8,128)S(1)}, u32[]{:S(2)}, u32[]{:S(2)}) async-start(f32[128,16,128]{2,1,0:T(8,128)} %bitcast.13), calls=%async_computation | async-start | bytes 2097152 | tf_op jit(solution)/shard_map/all_to_all | solution.py:616
  13.2 1.7 %first_faces.1 = (f32[352,128]{1,0:T(8,128)S(1)}, f32[352,128]{1,0:T(8,128)S(1)}, f32[352,128]{1,0:T(8,128)S(1)}, f32[352,128]{1,0:T(8,128)S(1)}) custom-call(f32[1024,128]{1,0:T(8,128)} %bitcast.14, f32[1024,128]{1,0:T(8,128)} %bitcast.17, f32[1024,128]{1,0:T(8,128)} %bitcast.19, f32[2048,128]{1,0:T(8,128)} %pack.1._), custom_call_target="tpu_custom_call" | custom-call | flops 20000000 | bytes 8000000 | tf_op jit(solution)/shard_map/first_faces/pallas_call | solution.py:554
  14.8 3.4 %collective-permute-start = (f32[352,128]{1,0:T(8,128)S(1)}, f32[352,128]{1,0:T(8,128)S(1)}, u32[]{:S(2)}, u32[]{:S(2)}) collective-permute-start(f32[352,128]{1,0:T(8,128)S(1)} %get-tuple-element.55), channel_id=1, source_target_pairs={{0,8},{1,2},{2,1},{3,4},{4,3},{5,6},{6,5},{7,15},{8,0},{9,10},{10,... | collective-permute-start | bytes 540680 | tf_op jit(solution)/shard_map/ppermute | solution.py:587
  18.4 1.9 %collective-permute-start.2 = (f32[352,128]{1,0:T(8,128)S(1)}, f32[352,128]{1,0:T(8,128)S(1)}, u32[]{:S(2)}, u32[]{:S(2)}) collective-permute-start(f32[352,128]{1,0:T(8,128)S(1)} %get-tuple-element.57), channel_id=1, source_target_pairs={{0,1},{1,0},{2,3},{3,2},{4,5},{5,4},{6,7},{7,6},{8,16},{9,17},{10,... | collective-permute-start | bytes 540680 | tf_op jit(solution)/shard_map/ppermute | solution.py:587
  20.5 2.2 %step0_depth.1._.refs_6_ = f32[1024,128]{1,0:T(8,128)} custom-call(bf16[384,128]{1,0:T(8,128)(2,1)S(1)} %copy-done.1, f32[1024,128]{1,0:T(8,128)} %bitcast.15), custom_call_target="tpu_custom_call" | custom-call | flops 30000001024 | bytes 8000000 | tf_op jit(solution)/shard_map/step0_depth/pallas_call | solution.py:554
  22.8 7.6 %all-to-all-done = f32[128,16,128]{2,1,0:T(8,128)S(1)} async-done(((f32[128,16,128]{2,1,0:T(8,128)}), f32[128,16,128]{2,1,0:T(8,128)S(1)}, u32[]{:S(2)}, u32[]{:S(2)}) %all-to-all-start) | async-done | bytes 1048608 | tf_op jit(solution)/shard_map/all_to_all | solution.py:616
  30.4 1.9 %cut.1 = f32[128,11,2,128]{3,2,1,0:T(2,128)} custom-call(s32[4,2]{1,0:T(4,128)S(1)} %copy.16.corners, f32[2048,128]{1,0:T(8,128)S(1)} %bitcast.12, f32[1024,128]{1,0:T(8,128)} %step0_depth.1._.refs_6_), custom_call_target="tpu_custom_call" | custom-call | tf_op jit(solution)/shard_map/cut/pallas_call | solution.py:554
  32.3 6.6 %all-to-all-start.1 = ((f32[128,11,2,128]{3,2,1,0:T(2,128)}), f32[128,11,2,128]{3,2,1,0:T(2,128)S(1)}, u32[]{:S(2)}, u32[]{:S(2)}) async-start(f32[128,11,2,128]{3,2,1,0:T(2,128)} %cut.1), calls=%async_computation.1 | async-start | bytes 2883584 | tf_op jit(solution)/shard_map/all_to_all | solution.py:647
  39.0 4.7 %step0_gradients.1 = (f32[1280,128]{1,0:T(8,128)}, f32[1280,128]{1,0:T(8,128)}, f32[1280,128]{1,0:T(8,128)}, f32[1280,128]{1,0:T(8,128)}, f32[1024,128]{1,0:T(8,128)}) custom-call(s32[4,3]{1,0:T(4,128)S(1)} %copy-done.2, f32[4,4]{1,0:T(4,128)S(1)} %copy-done.3, f32[1024,128]{1,0:T(8,128)} %bitcast.16, f32[352,128]{1,0:T(8,128)S(1)} %collective-permute-done.gy_b, ...), custom_call_target="tpu_custom_call" | custom-call | flops 30000001024 | bytes 8000000 | tf_op jit(solution)/shard_map/step0_gradients/pallas_call | solution.py:554
  43.7 16.5 %all-to-all-done.1.window = f32[128,11,2,128]{3,2,1,0:T(2,128)S(1)} async-done(((f32[128,11,2,128]{3,2,1,0:T(2,128)}), f32[128,11,2,128]{3,2,1,0:T(2,128)S(1)}, u32[]{:S(2)}, u32[]{:S(2)}) %all-to-all-start.1) | async-done | bytes 1441824 | tf_op jit(solution)/shard_map/all_to_all | solution.py:647
  60.2 3.6 %step0.1 = (f32[1024,128]{1,0:T(8,128)S(1)}, f32[1280,128]{1,0:T(8,128)S(1)}, f32[1280,128]{1,0:T(8,128)S(1)}, f32[1024,128]{1,0:T(8,128)S(1)}, f32[1600,128]{1,...) custom-call(s32[4,2]{1,0:T(4,128)S(1)} %copy.16.corners, ...), custom_call_target="tpu_custom_call" | custom-call | tf_op jit(solution)/shard_map/step0/pallas_call | solution.py:554
  63.8 2.9 %collective-permute-start.4 = (f32[224,128]{1,0:T(8,128)S(1)}, f32[224,128]{1,0:T(8,128)S(1)}, u32[]{:S(2)}, u32[]{:S(2)}) collective-permute-start(f32[224,128]{1,0:T(8,128)S(1)} %get-tuple-element.65), channel_id=1, source_target_pairs={{0,8},{1,2},{2,1},{3,4},{4,3},{5,6},{6,5},{7,15},{8,0},{9,10},{10,... | collective-permute-start | bytes 344072 | tf_op jit(solution)/shard_map/ppermute | solution.py:587
  66.7 2.0 %collective-permute-start.6 = (f32[224,128]{1,0:T(8,128)S(1)}, f32[224,128]{1,0:T(8,128)S(1)}, u32[]{:S(2)}, u32[]{:S(2)}) collective-permute-start(f32[224,128]{1,0:T(8,128)S(1)} %get-tuple-element.67), channel_id=1, source_target_pairs={{0,1},{1,0},{2,3},{3,2},{4,5},{5,4},{6,7},{7,6},{8,16},{9,17},{10,... | collective-permute-start | bytes 344072 | tf_op jit(solution)/shard_map/ppermute | solution.py:587
  68.7 2.1 %inner1.1 = (f32[1280,128]{1,0:T(8,128)S(1)}, f32[1280,128]{1,0:T(8,128)S(1)}, f32[1024,128]{1,0:T(8,128)S(1)}, f32[1024,128]{1,0:T(8,128)S(1)}, f32[1024,128]{1,0:T(8,128)S(1)}) custom-call(s32[4,3]{1,0:T(4,128)S(1)} %copy-done.2, f32[4,4]{1,0:T(4,128)S(1)} %copy-done.3, bf16[384,128]{1,0:T(8,128)(2,1)S(1)} %copy-done.1, bf16[384,128]{1,0:T(8,128)(2,1)S(1)} %copy-done, ...), custom_call_target="tpu_custom_call" | custom-call | flops 20000000 | bytes 8000000 | tf_op jit(solution)/shard_map/inner1/pallas_call | solution.py:554
  70.8 2.6 %collective-permute-done.4.refs_1_ = f32[224,128]{1,0:T(8,128)S(1)} collective-permute-done((f32[224,128]{1,0:T(8,128)S(1)}, f32[224,128]{1,0:T(8,128)S(1)}, u32[]{:S(2)}, u32[]{:S(2)}) %collective-permute-start.4) | collective-permute-done | bytes 114720 | tf_op jit(solution)/shard_map/ppermute | solution.py:587
  74.3 2.9 %collective-permute-start.8 = (f32[224,128]{1,0:T(8,128)S(1)}, f32[224,128]{1,0:T(8,128)S(1)}, u32[]{:S(2)}, u32[]{:S(2)}) collective-permute-start(f32[224,128]{1,0:T(8,128)S(1)} %get-tuple-element.79), channel_id=1, source_target_pairs={{0,8},{1,2},{2,1},{3,4},{4,3},{5,6},{6,5},{7,15},{8,0},{9,10},{10,... | collective-permute-start | bytes 344072 | tf_op jit(solution)/shard_map/ppermute | solution.py:587
  77.2 2.0 %collective-permute-start.10 = (f32[224,128]{1,0:T(8,128)S(1)}, f32[224,128]{1,0:T(8,128)S(1)}, u32[]{:S(2)}, u32[]{:S(2)}) collective-permute-start(f32[224,128]{1,0:T(8,128)S(1)} %get-tuple-element.81), channel_id=1, source_target_pairs={{0,1},{1,0},{2,3},{3,2},{4,5},{5,4},{6,7},{7,6},{8,16},{9,17},{10,... | collective-permute-start | bytes 344072 | tf_op jit(solution)/shard_map/ppermute | solution.py:587
  79.3 2.1 %inner2.1 = (f32[1280,128]{1,0:T(8,128)S(1)}, f32[1280,128]{1,0:T(8,128)S(1)}, f32[1024,128]{1,0:T(8,128)S(1)}, f32[1024,128]{1,0:T(8,128)S(1)}, f32[1024,128]{1,0:T(8,128)S(1)}) custom-call(s32[4,3]{1,0:T(4,128)S(1)} %copy-done.2, f32[4,4]{1,0:T(4,128)S(1)} %copy-done.3, bf16[384,128]{1,0:T(8,128)(2,1)S(1)} %copy-done.1, bf16[384,128]{1,0:T(8,128)(2,1)S(1)} %copy-done, ...), custom_call_target="tpu_custom_call" | custom-call | flops 20000000 | bytes 8000000 | tf_op jit(solution)/shard_map/inner2/pallas_call | solution.py:554
  81.4 2.4 %collective-permute-done.8.refs_1_ = f32[224,128]{1,0:T(8,128)S(1)} collective-permute-done((f32[224,128]{1,0:T(8,128)S(1)}, f32[224,128]{1,0:T(8,128)S(1)}, u32[]{:S(2)}, u32[]{:S(2)}) %collective-permute-start.8) | collective-permute-done | bytes 114720 | tf_op jit(solution)/shard_map/ppermute | solution.py:587
  84.8 3.0 %collective-permute-start.12 = (f32[224,128]{1,0:T(8,128)S(1)}, f32[224,128]{1,0:T(8,128)S(1)}, u32[]{:S(2)}, u32[]{:S(2)}) collective-permute-start(f32[224,128]{1,0:T(8,128)S(1)} %get-tuple-element.91), channel_id=1, source_target_pairs={{0,8},{1,2},{2,1},{3,4},{4,3},{5,6},{6,5},{7,15},{8,0},{9,10},{10,... | collective-permute-start | bytes 344072 | tf_op jit(solution)/shard_map/ppermute | solution.py:587
  87.8 2.0 %collective-permute-start.14 = (f32[224,128]{1,0:T(8,128)S(1)}, f32[224,128]{1,0:T(8,128)S(1)}, u32[]{:S(2)}, u32[]{:S(2)}) collective-permute-start(f32[224,128]{1,0:T(8,128)S(1)} %get-tuple-element.93), channel_id=1, source_target_pairs={{0,1},{1,0},{2,3},{3,2},{4,5},{5,4},{6,7},{7,6},{8,16},{9,17},{10,... | collective-permute-start | bytes 344072 | tf_op jit(solution)/shard_map/ppermute | solution.py:587
  89.8 2.9 %inner3.1 = (f32[1280,128]{1,0:T(8,128)S(1)}, f32[1280,128]{1,0:T(8,128)S(1)}, f32[1024,128]{1,0:T(8,128)}, f32[1024,128]{1,0:T(8,128)S(1)}, f32[1024,128]{1,0:T(8,128)S(1)}) custom-call(s32[4,3]{1,0:T(4,128)S(1)} %copy-done.2, f32[4,4]{1,0:T(4,128)S(1)} %copy-done.3, bf16[384,128]{1,0:T(8,128)(2,1)S(1)} %copy-done.1, bf16[384,128]{1,0:T(8,128)(2,1)S(1)} %copy-done, ...), custom_call_target="tpu_custom_call" | custom-call | flops 20000000 | bytes 8000000 | tf_op jit(solution)/shard_map/inner3/pallas_call | solution.py:554
  93.8 1.6 %edge3.1 = (f32[1024,128]{1,0:T(8,128)}, f32[1024,128]{1,0:T(8,128)}, f32[1024,128]{1,0:T(8,128)}) custom-call(f32[1024,128]{1,0:T(8,128)S(1)} %get-tuple-element.90.pres.refs_0_, f32[224,128]{1,0:T(8,128)S(1)} %collective-permute-done.12.refs_1_, f32[224,128]{1,0:T(8,128)S(1)} %collective-permute-done.13.refs_2_, ...), custom_call_target="tpu_custom_call" | custom-call | tf_op jit(solution)/shard_map/edge3/pallas_call | solution.py:554
  (35 shorter events, 3.3 us)
Async XLA Ops:
  2.8 27.6 %all-to-all-start = ((f32[128,16,128]{2,1,0:T(8,128)}), f32[128,16,128]{2,1,0:T(8,128)S(1)}, u32[]{:S(2)}, u32[]{:S(2)}) async-start(f32[128,16,128]{2,1,0:T(8,128)} %bitcast.13), calls=%async_computation | async-start | bytes 2097152 | tf_op jit(solution)/shard_map/all_to_all | solution.py:616
  13.2 7.3 %copy-start.1 = (bf16[384,128]{1,0:T(8,128)(2,1)S(1)}, bf16[384,128]{1,0:T(8,128)(2,1)}, u32[]{:S(2)}) copy-start(bf16[384,128]{1,0:T(8,128)(2,1)} %constant.4.clone.mat_f) | copy-start | bytes 294916
  14.8 24.1 %collective-permute-start = (f32[352,128]{1,0:T(8,128)S(1)}, f32[352,128]{1,0:T(8,128)S(1)}, u32[]{:S(2)}, u32[]{:S(2)}) collective-permute-start(f32[352,128]{1,0:T(8,128)S(1)} %get-tuple-element.55), channel_id=1, source_target_pairs={{0,8},{1,2},{2,1},{3,4},{4,3},{5,6},{6,5},{7,15},{8,0},{9,10},{10,... | collective-permute-start | bytes 540680 | tf_op jit(solution)/shard_map/ppermute | solution.py:587
  18.2 20.7 %collective-permute-start.1 = (f32[352,128]{1,0:T(8,128)S(1)}, f32[352,128]{1,0:T(8,128)S(1)}, u32[]{:S(2)}, u32[]{:S(2)}) collective-permute-start(f32[352,128]{1,0:T(8,128)S(1)} %get-tuple-element.56), channel_id=1, source_target_pairs={{0,1},{1,0},{2,3},{3,2},{4,5},{5,4},{6,7},{7,6},{8,9},{9,8},{10,11... | collective-permute-start | bytes 540680 | tf_op jit(solution)/shard_map/ppermute | solution.py:587
  18.4 20.6 %collective-permute-start.2 = (f32[352,128]{1,0:T(8,128)S(1)}, f32[352,128]{1,0:T(8,128)S(1)}, u32[]{:S(2)}, u32[]{:S(2)}) collective-permute-start(f32[352,128]{1,0:T(8,128)S(1)} %get-tuple-element.57), channel_id=1, source_target_pairs={{0,1},{1,0},{2,3},{3,2},{4,5},{5,4},{6,7},{7,6},{8,16},{9,17},{10,... | collective-permute-start | bytes 540680 | tf_op jit(solution)/shard_map/ppermute | solution.py:587
  20.3 2.5 %copy-start.4 = (s32[4,2]{0,1:T(2,128)S(1)}, s32[4,2]{0,1:T(2,128)}, u32[]{:S(2)}) copy-start(s32[4,2]{0,1:T(2,128)} %param.13) | copy-start | bytes 100
  20.3 18.7 %collective-permute-start.3 = (f32[352,128]{1,0:T(8,128)S(1)}, f32[352,128]{1,0:T(8,128)S(1)}, u32[]{:S(2)}, u32[]{:S(2)}) collective-permute-start(f32[352,128]{1,0:T(8,128)S(1)} %get-tuple-element.58), channel_id=1, source_target_pairs={{0,8},{1,9},{2,10},{3,11},{4,12},{5,13},{6,14},{7,15},{8,0},{9,1},... | collective-permute-start | bytes 540680 | tf_op jit(solution)/shard_map/ppermute | solution.py:587
  32.3 6.7 %copy-start.2 = (s32[4,3]{1,0:T(4,128)S(1)}, s32[4,3]{1,0:T(4,128)}, u32[]{:S(2)}) copy-start(s32[4,3]{1,0:T(4,128)} %cells.7) | copy-start | bytes 148
  32.3 6.7 %copy-start.3 = (f32[4,4]{1,0:T(4,128)S(1)}, f32[4,4]{1,0:T(4,128)}, u32[]{:S(2)}) copy-start(f32[4,4]{1,0:T(4,128)} %amps.7) | copy-start | bytes 196
  32.3 27.9 %all-to-all-start.1 = ((f32[128,11,2,128]{3,2,1,0:T(2,128)}), f32[128,11,2,128]{3,2,1,0:T(2,128)S(1)}, u32[]{:S(2)}, u32[]{:S(2)}) async-start(f32[128,11,2,128]{3,2,1,0:T(2,128)} %cut.1), calls=%async_computation.1 | async-start | bytes 2883584 | tf_op jit(solution)/shard_map/all_to_all | solution.py:647
  39.0 21.2 %copy-start = (bf16[384,128]{1,0:T(8,128)(2,1)S(1)}, bf16[384,128]{1,0:T(8,128)(2,1)}, u32[]{:S(2)}) copy-start(bf16[384,128]{1,0:T(8,128)(2,1)} %constant.5.clone.mat_b) | copy-start | bytes 294916
  63.8 9.6 %collective-permute-start.4 = (f32[224,128]{1,0:T(8,128)S(1)}, f32[224,128]{1,0:T(8,128)S(1)}, u32[]{:S(2)}, u32[]{:S(2)}) collective-permute-start(f32[224,128]{1,0:T(8,128)S(1)} %get-tuple-element.65), channel_id=1, source_target_pairs={{0,8},{1,2},{2,1},{3,4},{4,3},{5,6},{6,5},{7,15},{8,0},{9,10},{10,... | collective-permute-start | bytes 344072 | tf_op jit(solution)/shard_map/ppermute | solution.py:587
  66.7 6.8 %collective-permute-start.5 = (f32[224,128]{1,0:T(8,128)S(1)}, f32[224,128]{1,0:T(8,128)S(1)}, u32[]{:S(2)}, u32[]{:S(2)}) collective-permute-start(f32[224,128]{1,0:T(8,128)S(1)} %get-tuple-element.66), channel_id=1, source_target_pairs={{0,1},{1,0},{2,3},{3,2},{4,5},{5,4},{6,7},{7,6},{8,9},{9,8},{10,11... | collective-permute-start | bytes 344072 | tf_op jit(solution)/shard_map/ppermute | solution.py:587
  66.7 6.8 %collective-permute-start.6 = (f32[224,128]{1,0:T(8,128)S(1)}, f32[224,128]{1,0:T(8,128)S(1)}, u32[]{:S(2)}, u32[]{:S(2)}) collective-permute-start(f32[224,128]{1,0:T(8,128)S(1)} %get-tuple-element.67), channel_id=1, source_target_pairs={{0,1},{1,0},{2,3},{3,2},{4,5},{5,4},{6,7},{7,6},{8,16},{9,17},{10,... | collective-permute-start | bytes 344072 | tf_op jit(solution)/shard_map/ppermute | solution.py:587
  68.7 4.7 %collective-permute-start.7 = (f32[224,128]{1,0:T(8,128)S(1)}, f32[224,128]{1,0:T(8,128)S(1)}, u32[]{:S(2)}, u32[]{:S(2)}) collective-permute-start(f32[224,128]{1,0:T(8,128)S(1)} %get-tuple-element.68), channel_id=1, source_target_pairs={{0,8},{1,9},{2,10},{3,11},{4,12},{5,13},{6,14},{7,15},{8,0},{9,1},... | collective-permute-start | bytes 344072 | tf_op jit(solution)/shard_map/ppermute | solution.py:587
  74.3 9.5 %collective-permute-start.8 = (f32[224,128]{1,0:T(8,128)S(1)}, f32[224,128]{1,0:T(8,128)S(1)}, u32[]{:S(2)}, u32[]{:S(2)}) collective-permute-start(f32[224,128]{1,0:T(8,128)S(1)} %get-tuple-element.79), channel_id=1, source_target_pairs={{0,8},{1,2},{2,1},{3,4},{4,3},{5,6},{6,5},{7,15},{8,0},{9,10},{10,... | collective-permute-start | bytes 344072 | tf_op jit(solution)/shard_map/ppermute | solution.py:587
  77.2 6.6 %collective-permute-start.9 = (f32[224,128]{1,0:T(8,128)S(1)}, f32[224,128]{1,0:T(8,128)S(1)}, u32[]{:S(2)}, u32[]{:S(2)}) collective-permute-start(f32[224,128]{1,0:T(8,128)S(1)} %get-tuple-element.80), channel_id=1, source_target_pairs={{0,1},{1,0},{2,3},{3,2},{4,5},{5,4},{6,7},{7,6},{8,9},{9,8},{10,11... | collective-permute-start | bytes 344072 | tf_op jit(solution)/shard_map/ppermute | solution.py:587
  77.2 6.6 %collective-permute-start.10 = (f32[224,128]{1,0:T(8,128)S(1)}, f32[224,128]{1,0:T(8,128)S(1)}, u32[]{:S(2)}, u32[]{:S(2)}) collective-permute-start(f32[224,128]{1,0:T(8,128)S(1)} %get-tuple-element.81), channel_id=1, source_target_pairs={{0,1},{1,0},{2,3},{3,2},{4,5},{5,4},{6,7},{7,6},{8,16},{9,17},{10,... | collective-permute-start | bytes 344072 | tf_op jit(solution)/shard_map/ppermute | solution.py:587
  79.3 4.6 %collective-permute-start.11 = (f32[224,128]{1,0:T(8,128)S(1)}, f32[224,128]{1,0:T(8,128)S(1)}, u32[]{:S(2)}, u32[]{:S(2)}) collective-permute-start(f32[224,128]{1,0:T(8,128)S(1)} %get-tuple-element.82), channel_id=1, source_target_pairs={{0,8},{1,9},{2,10},{3,11},{4,12},{5,13},{6,14},{7,15},{8,0},{9,1},... | collective-permute-start | bytes 344072 | tf_op jit(solution)/shard_map/ppermute | solution.py:587
  84.8 8.6 %collective-permute-start.12 = (f32[224,128]{1,0:T(8,128)S(1)}, f32[224,128]{1,0:T(8,128)S(1)}, u32[]{:S(2)}, u32[]{:S(2)}) collective-permute-start(f32[224,128]{1,0:T(8,128)S(1)} %get-tuple-element.91), channel_id=1, source_target_pairs={{0,8},{1,2},{2,1},{3,4},{4,3},{5,6},{6,5},{7,15},{8,0},{9,10},{10,... | collective-permute-start | bytes 344072 | tf_op jit(solution)/shard_map/ppermute | solution.py:587
  87.8 5.6 %collective-permute-start.13 = (f32[224,128]{1,0:T(8,128)S(1)}, f32[224,128]{1,0:T(8,128)S(1)}, u32[]{:S(2)}, u32[]{:S(2)}) collective-permute-start(f32[224,128]{1,0:T(8,128)S(1)} %get-tuple-element.92), channel_id=1, source_target_pairs={{0,1},{1,0},{2,3},{3,2},{4,5},{5,4},{6,7},{7,6},{8,9},{9,8},{10,11... | collective-permute-start | bytes 344072 | tf_op jit(solution)/shard_map/ppermute | solution.py:587
  87.8 6.0 %collective-permute-start.14 = (f32[224,128]{1,0:T(8,128)S(1)}, f32[224,128]{1,0:T(8,128)S(1)}, u32[]{:S(2)}, u32[]{:S(2)}) collective-permute-start(f32[224,128]{1,0:T(8,128)S(1)} %get-tuple-element.93), channel_id=1, source_target_pairs={{0,1},{1,0},{2,3},{3,2},{4,5},{5,4},{6,7},{7,6},{8,16},{9,17},{10,... | collective-permute-start | bytes 344072 | tf_op jit(solution)/shard_map/ppermute | solution.py:587
  89.8 4.0 %collective-permute-start.15 = (f32[224,128]{1,0:T(8,128)S(1)}, f32[224,128]{1,0:T(8,128)S(1)}, u32[]{:S(2)}, u32[]{:S(2)}) collective-permute-start(f32[224,128]{1,0:T(8,128)S(1)} %get-tuple-element.94), channel_id=1, source_target_pairs={{0,8},{1,9},{2,10},{3,11},{4,12},{5,13},{6,14},{7,15},{8,0},{9,1},... | collective-permute-start | bytes 344072 | tf_op jit(solution)/shard_map/ppermute | solution.py:587

commit v8 on v7

--- a/solution.py
+++ b/solution.py
@@ -148,7 +148,9 @@
     send_faces(y_in, (), (gy_a, gy_b), HALO, 4)
 
 
-def cut_kernel(corners, dealt, _, out, rho_lines, vel_lines, cuts, sem):
+def cut_kernel(dealt, corners_from, _, out, rho_lines, vel_lines, cuts, sem, corners, corner_sem):
+    pull = pltpu.make_async_copy(corners_from, corners, corner_sem.at[0])
+    pull.start()
     s, g, col_class = place()
     row_class = s * 4 + g
     for t in range(16):
@@ -158,6 +160,7 @@
             vel_lines[dst : dst + 8, :] = dealt[src : src + 8, :]
             rho_lines[dst : dst + 8, :] = dealt[src + 8 : src + 16, :]
     flat = out.reshape(128 * MESSAGE, 128)
+    pull.wait()
     pushes = []
     for shot in range(4):
         col = lax.shift_right_arithmetic(corners[shot, 1] - col_class + 7, 3)
@@ -322,12 +325,15 @@
         field[pl.ds(at, 1), :] = field[pl.ds(at, 1), :] + jnp.where(lane == cells[s, 2], kick, 0.0)
 
 
-def step0_kernel(corners, mat_b, window, *refs):
+def step0_kernel(corners_from, mat_b, window, *refs):
     sources, outs, scratch = refs[:7], refs[7:17], refs[17:]
     new_p, wide_x, wide_y, new_z, buoy, modu, gy_b, gy_a, gx_b, gx_a = outs
-    pres, in_x, in_y, in_z, grad_x, grad_y, grad_z, rho, spread, sem = scratch
+    pres, in_x, in_y, in_z, grad_x, grad_y, grad_z, rho, spread, sem, corners, corner_sem = scratch
+    pull = pltpu.make_async_copy(corners_from, corners, corner_sem.at[0])
+    pull.start()
     order = (6, 3, 4, 1, 0, 5, 2)
     pulls = pull_all([(sources[i], scratch[i]) for i in order], sem)
+    pull.wait()
     unpack_model(corners, window, buoy, modu, rho)
 
     def wait(*which):
@@ -348,23 +354,24 @@
         wide_x[at : at + 8, :] = (
             in_x[at : at + 8, :] - buoy_at(buoy, x - 4, n * 8) * grad_x[at : at + 8, :]
         )
+    for x0 in range(0, CX, 4):
+        for n in range(4):
+            mid = (x0 + 4) * CY + n * 8
+            taps = [wide_x[mid + d * CY : mid + d * CY + 8, :] for d in range(-4, 7)]
+            for i in range(4):
+                at = (x0 + i) * CY + n * 8
+                spread[at : at + 8, :] = spread[at : at + 8, :] + backward(taps, i)
     wait(4, 5, 6)
     for x, n, at in tiles(CX, 5):
         wide_y[at : at + 8, :] = (
             in_y[at : at + 8, :] - buoy_at(buoy, x, n * 8 - 4) * grad_y[at : at + 8, :]
         )
-    for x0 in range(0, CX, 4):
-        part_x = {}
+    for x in range(CX):
+        taps = [every(wide_y, x * WIDE + 4 + d, 4) for d in range(-4, 7)]
         for j in range(4):
-            taps = [every(wide_x, (x0 + d + 4) * CY + j, 4) for d in range(-4, 7)]
-            for i in range(4):
-                part_x[i, j] = backward(taps, i)
-        for i in range(4):
-            taps = [every(wide_y, (x0 + i) * WIDE + 4 + d, 4) for d in range(-4, 7)]
-            for j in range(4):
-                at = (x0 + i) * CY + j
-                total = part_x[i, j] + backward(taps, j) + every(spread, at, 4)
-                put_every(new_p, at, 4, every(pres, at, 4) - every(modu, at, 4) * total)
+            at = x * CY + j
+            total = every(spread, at, 4) + backward(taps, j)
+            put_every(new_p, at, 4, every(pres, at, 4) - every(modu, at, 4) * total)
     send_faces(new_p, (gx_a, gx_b), (gy_a, gy_b), 0, HALO)
 
 
@@ -604,6 +611,7 @@
     long = pl.CostEstimate(flops=3 * 10**10, bytes_accessed=8_000_000, transcendentals=0)
 
     dma = pltpu.SemaphoreType.DMA
+    corner_scratch = [pltpu.SMEM((4, 2), jnp.int32), dma((1,))]
     (deal,) = call(
         pack_kernel,
         [shape(128 * 16)],
@@ -637,11 +645,10 @@
     (cut,) = call(
         cut_kernel,
         [jax.ShapeDtypeStruct((128, MESSAGE // 2, 2, 128), f32)],
-        [offsets, dealt.reshape(128 * 16, 128), grad_z],
-        [vmem(16 * LINE), vmem(16 * LINE), vmem(128 * MESSAGE), dma((4,))],
+        [dealt.reshape(128 * 16, 128), offsets, grad_z],
+        [vmem(16 * LINE), vmem(16 * LINE), vmem(128 * MESSAGE), dma((4,))] + corner_scratch,
         "cut",
-        smem=1,
-        hbm=(2,),
+        hbm=(1, 2),
         to_hbm=True,
     )
     window = lax.all_to_all(cut, DEVICES, 0, 0, tiled=True)
@@ -664,10 +671,9 @@
         + [pres, flow_x, flow_y, flow_z, grad_x, grad_y, grad_z],
         [vmem(CX * CY), vmem(WIDE * CY), vmem(WIDE * CY), vmem(CX * CY)]
         + [vmem(WIDE * CY), vmem(WIDE * CY), vmem(CX * CY)]
-        + [vmem(WIDE * WIDE), vmem(CX * CY), dma((7,))],
+        + [vmem(WIDE * WIDE), vmem(CX * CY), dma((7,))] + corner_scratch,
         "step0",
-        smem=1,
-        hbm=range(3, 10),
+        hbm=[0, *range(3, 10)],
     )
     for step in range(1, STEPS):
         last = step == STEPS - 1

time: 95.9 us -> 95.2 us (level)
  transfers between devices with their start and end apart: 18 -> 18, of which waited for: 6 -> 6; matrix products, arithmetic and copies ran while one was open for 0% -> 1% of each run, Pallas kernels for 19% -> 19%
where the time goes in v8:
time: 95.2 us; the launch traced here: 94.8 us
  starting transfers between devices  37.5 us (39%)
  waiting for transfers between devices  29.5 us (31%)
  Pallas kernels  26.2 us (28%)
    pallas_call x12, Pallas kernels, call(): pl.pallas_call(kernel, out_shape=outs, in_specs=specs, out_specs=[pl.Bloc...  26.2 us
    ppermute x16, starting transfers between devices, exchange(): lax.ppermute(face, plane, pairs)  20.6 us
    all_to_all x1, waiting for transfers between devices, shards(): window = lax.all_to_all(cut, DEVICES, 0, 0, tiled=True)  16.5 us
    all_to_all x1, starting transfers between devices, shards(): lax.all_to_all(deal.reshape(128, 16, 128), DEVICES, 0, 0, tiled=True)  10.3 us
    all_to_all x1, waiting for transfers between devices, shards(): lax.all_to_all(deal.reshape(128, 16, 128), DEVICES, 0, 0, tiled=True)  7 us
    all_to_all x1, starting transfers between devices, shards(): window = lax.all_to_all(cut, DEVICES, 0, 0, tiled=True)  6.61 us
    ppermute x16, waiting for transfers between devices, exchange(): lax.ppermute(face, plane, pairs)  6.07 us
  transfers between devices with their start and end apart: 18, of which 6 were waited for; matrix products, arithmetic and copies ran while one was open for 1% of the time, Pallas kernels for 19%

profile of v8, /device:TPU:16, one launch (start us, length us, event | category | flops | bytes accessed | tf_op | source)
XLA Modules:
  0.0 94.8 jit_solution(2733496757467785555)
XLA Ops:
  0.6 2.2 %pack.1._ = f32[2048,128]{1,0:T(8,128)} custom-call(f32[1024,128]{1,0:T(8,128)} %bitcast.21, f32[1024,128]{1,0:T(8,128)} %bitcast.22), custom_call_target="tpu_custom_call" | custom-call | tf_op jit(solution)/shard_map/pack/pallas_call | solution.py:561
  2.8 10.3 %all-to-all-start = ((f32[128,16,128]{2,1,0:T(8,128)}), f32[128,16,128]{2,1,0:T(8,128)S(1)}, u32[]{:S(2)}, u32[]{:S(2)}) async-start(f32[128,16,128]{2,1,0:T(8,128)} %bitcast.13), calls=%async_computation | async-start | bytes 2097152 | tf_op jit(solution)/shard_map/all_to_all | solution.py:624
  13.2 1.7 %first_faces.1 = (f32[352,128]{1,0:T(8,128)S(1)}, f32[352,128]{1,0:T(8,128)S(1)}, f32[352,128]{1,0:T(8,128)S(1)}, f32[352,128]{1,0:T(8,128)S(1)}) custom-call(f32[1024,128]{1,0:T(8,128)} %bitcast.14, f32[1024,128]{1,0:T(8,128)} %bitcast.17, f32[1024,128]{1,0:T(8,128)} %bitcast.19, f32[2048,128]{1,0:T(8,128)} %pack.1._), custom_call_target="tpu_custom_call" | custom-call | flops 20000000 | bytes 8000000 | tf_op jit(solution)/shard_map/first_faces/pallas_call | solution.py:561
  14.8 3.4 %collective-permute-start = (f32[352,128]{1,0:T(8,128)S(1)}, f32[352,128]{1,0:T(8,128)S(1)}, u32[]{:S(2)}, u32[]{:S(2)}) collective-permute-start(f32[352,128]{1,0:T(8,128)S(1)} %get-tuple-element.55), channel_id=1, source_target_pairs={{0,8},{1,2},{2,1},{3,4},{4,3},{5,6},{6,5},{7,15},{8,0},{9,10},{10,... | collective-permute-start | bytes 540680 | tf_op jit(solution)/shard_map/ppermute | solution.py:594
  18.4 1.9 %collective-permute-start.2 = (f32[352,128]{1,0:T(8,128)S(1)}, f32[352,128]{1,0:T(8,128)S(1)}, u32[]{:S(2)}, u32[]{:S(2)}) collective-permute-start(f32[352,128]{1,0:T(8,128)S(1)} %get-tuple-element.57), channel_id=1, source_target_pairs={{0,1},{1,0},{2,3},{3,2},{4,5},{5,4},{6,7},{7,6},{8,16},{9,17},{10,... | collective-permute-start | bytes 540680 | tf_op jit(solution)/shard_map/ppermute | solution.py:594
  20.5 2.2 %step0_depth.1._.refs_6_ = f32[1024,128]{1,0:T(8,128)} custom-call(bf16[384,128]{1,0:T(8,128)(2,1)S(1)} %copy-done.1, f32[1024,128]{1,0:T(8,128)} %bitcast.15), custom_call_target="tpu_custom_call" | custom-call | flops 30000001024 | bytes 8000000 | tf_op jit(solution)/shard_map/step0_depth/pallas_call | solution.py:561
  23.4 7.0 %all-to-all-done = f32[128,16,128]{2,1,0:T(8,128)S(1)} async-done(((f32[128,16,128]{2,1,0:T(8,128)}), f32[128,16,128]{2,1,0:T(8,128)S(1)}, u32[]{:S(2)}, u32[]{:S(2)}) %all-to-all-start) | async-done | bytes 1048608 | tf_op jit(solution)/shard_map/all_to_all | solution.py:624
  30.4 2.0 %cut.1 = f32[128,11,2,128]{3,2,1,0:T(2,128)} custom-call(f32[2048,128]{1,0:T(8,128)S(1)} %bitcast.12, s32[4,2]{1,0:T(4,128)} %copy.16.corners_from, f32[1024,128]{1,0:T(8,128)} %step0_depth.1._.refs_6_), custom_call_target="tpu_custom_call" | custom-call | tf_op jit(solution)/shard_map/cut/pallas_call | solution.py:561
  32.4 6.6 %all-to-all-start.1 = ((f32[128,11,2,128]{3,2,1,0:T(2,128)}), f32[128,11,2,128]{3,2,1,0:T(2,128)S(1)}, u32[]{:S(2)}, u32[]{:S(2)}) async-start(f32[128,11,2,128]{3,2,1,0:T(2,128)} %cut.1), calls=%async_computation.1 | async-start | bytes 2883584 | tf_op jit(solution)/shard_map/all_to_all | solution.py:654
  39.1 4.7 %step0_gradients.1 = (f32[1280,128]{1,0:T(8,128)}, f32[1280,128]{1,0:T(8,128)}, f32[1280,128]{1,0:T(8,128)}, f32[1280,128]{1,0:T(8,128)}, f32[1024,128]{1,0:T(8,128)}) custom-call(s32[4,3]{1,0:T(4,128)S(1)} %copy-done.2, f32[4,4]{1,0:T(4,128)S(1)} %copy-done.3, f32[1024,128]{1,0:T(8,128)} %bitcast.16, f32[352,128]{1,0:T(8,128)S(1)} %collective-permute-done.gy_b, ...), custom_call_target="tpu_custom_call" | custom-call | flops 30000001024 | bytes 8000000 | tf_op jit(solution)/shard_map/step0_gradients/pallas_call | solution.py:561
  43.8 16.5 %all-to-all-done.1.window = f32[128,11,2,128]{3,2,1,0:T(2,128)S(1)} async-done(((f32[128,11,2,128]{3,2,1,0:T(2,128)}), f32[128,11,2,128]{3,2,1,0:T(2,128)S(1)}, u32[]{:S(2)}, u32[]{:S(2)}) %all-to-all-start.1) | async-done | bytes 1441824 | tf_op jit(solution)/shard_map/all_to_all | solution.py:654
  60.3 2.8 %step0.1 = (f32[1024,128]{1,0:T(8,128)S(1)}, f32[1280,128]{1,0:T(8,128)S(1)}, f32[1280,128]{1,0:T(8,128)S(1)}, f32[1024,128]{1,0:T(8,128)S(1)}, f32[1600,128]{1,...) custom-call(s32[4,2]{1,0:T(4,128)} %copy.16.corners_from, ...), custom_call_target="tpu_custom_call" | custom-call | tf_op jit(solution)/shard_map/step0/pallas_call | solution.py:561
  63.1 2.9 %collective-permute-start.4 = (f32[224,128]{1,0:T(8,128)S(1)}, f32[224,128]{1,0:T(8,128)S(1)}, u32[]{:S(2)}, u32[]{:S(2)}) collective-permute-start(f32[224,128]{1,0:T(8,128)S(1)} %get-tuple-element.65), channel_id=1, source_target_pairs={{0,8},{1,2},{2,1},{3,4},{4,3},{5,6},{6,5},{7,15},{8,0},{9,10},{10,... | collective-permute-start | bytes 344072 | tf_op jit(solution)/shard_map/ppermute | solution.py:594
  66.0 2.0 %collective-permute-start.6 = (f32[224,128]{1,0:T(8,128)S(1)}, f32[224,128]{1,0:T(8,128)S(1)}, u32[]{:S(2)}, u32[]{:S(2)}) collective-permute-start(f32[224,128]{1,0:T(8,128)S(1)} %get-tuple-element.67), channel_id=1, source_target_pairs={{0,1},{1,0},{2,3},{3,2},{4,5},{5,4},{6,7},{7,6},{8,16},{9,17},{10,... | collective-permute-start | bytes 344072 | tf_op jit(solution)/shard_map/ppermute | solution.py:594
  68.0 2.2 %inner1.1 = (f32[1280,128]{1,0:T(8,128)S(1)}, f32[1280,128]{1,0:T(8,128)S(1)}, f32[1024,128]{1,0:T(8,128)S(1)}, f32[1024,128]{1,0:T(8,128)S(1)}, f32[1024,128]{1,0:T(8,128)S(1)}) custom-call(s32[4,3]{1,0:T(4,128)S(1)} %copy-done.2, f32[4,4]{1,0:T(4,128)S(1)} %copy-done.3, bf16[384,128]{1,0:T(8,128)(2,1)S(1)} %copy-done.1, bf16[384,128]{1,0:T(8,128)(2,1)S(1)} %copy-done, ...), custom_call_target="tpu_custom_call" | custom-call | flops 20000000 | bytes 8000000 | tf_op jit(solution)/shard_map/inner1/pallas_call | solution.py:561
  70.2 2.6 %collective-permute-done.4.refs_1_ = f32[224,128]{1,0:T(8,128)S(1)} collective-permute-done((f32[224,128]{1,0:T(8,128)S(1)}, f32[224,128]{1,0:T(8,128)S(1)}, u32[]{:S(2)}, u32[]{:S(2)}) %collective-permute-start.4) | collective-permute-done | bytes 114720 | tf_op jit(solution)/shard_map/ppermute | solution.py:594
  73.6 2.9 %collective-permute-start.8 = (f32[224,128]{1,0:T(8,128)S(1)}, f32[224,128]{1,0:T(8,128)S(1)}, u32[]{:S(2)}, u32[]{:S(2)}) collective-permute-start(f32[224,128]{1,0:T(8,128)S(1)} %get-tuple-element.79), channel_id=1, source_target_pairs={{0,8},{1,2},{2,1},{3,4},{4,3},{5,6},{6,5},{7,15},{8,0},{9,10},{10,... | collective-permute-start | bytes 344072 | tf_op jit(solution)/shard_map/ppermute | solution.py:594
  76.5 2.0 %collective-permute-start.10 = (f32[224,128]{1,0:T(8,128)S(1)}, f32[224,128]{1,0:T(8,128)S(1)}, u32[]{:S(2)}, u32[]{:S(2)}) collective-permute-start(f32[224,128]{1,0:T(8,128)S(1)} %get-tuple-element.81), channel_id=1, source_target_pairs={{0,1},{1,0},{2,3},{3,2},{4,5},{5,4},{6,7},{7,6},{8,16},{9,17},{10,... | collective-permute-start | bytes 344072 | tf_op jit(solution)/shard_map/ppermute | solution.py:594
  78.6 2.2 %inner2.1 = (f32[1280,128]{1,0:T(8,128)S(1)}, f32[1280,128]{1,0:T(8,128)S(1)}, f32[1024,128]{1,0:T(8,128)S(1)}, f32[1024,128]{1,0:T(8,128)S(1)}, f32[1024,128]{1,0:T(8,128)S(1)}) custom-call(s32[4,3]{1,0:T(4,128)S(1)} %copy-done.2, f32[4,4]{1,0:T(4,128)S(1)} %copy-done.3, bf16[384,128]{1,0:T(8,128)(2,1)S(1)} %copy-done.1, bf16[384,128]{1,0:T(8,128)(2,1)S(1)} %copy-done, ...), custom_call_target="tpu_custom_call" | custom-call | flops 20000000 | bytes 8000000 | tf_op jit(solution)/shard_map/inner2/pallas_call | solution.py:561
  80.7 2.4 %collective-permute-done.8.refs_1_ = f32[224,128]{1,0:T(8,128)S(1)} collective-permute-done((f32[224,128]{1,0:T(8,128)S(1)}, f32[224,128]{1,0:T(8,128)S(1)}, u32[]{:S(2)}, u32[]{:S(2)}) %collective-permute-start.8) | collective-permute-done | bytes 114720 | tf_op jit(solution)/shard_map/ppermute | solution.py:594
  84.1 3.0 %collective-permute-start.12 = (f32[224,128]{1,0:T(8,128)S(1)}, f32[224,128]{1,0:T(8,128)S(1)}, u32[]{:S(2)}, u32[]{:S(2)}) collective-permute-start(f32[224,128]{1,0:T(8,128)S(1)} %get-tuple-element.91), channel_id=1, source_target_pairs={{0,8},{1,2},{2,1},{3,4},{4,3},{5,6},{6,5},{7,15},{8,0},{9,10},{10,... | collective-permute-start | bytes 344072 | tf_op jit(solution)/shard_map/ppermute | solution.py:594
  87.1 2.0 %collective-permute-start.14 = (f32[224,128]{1,0:T(8,128)S(1)}, f32[224,128]{1,0:T(8,128)S(1)}, u32[]{:S(2)}, u32[]{:S(2)}) collective-permute-start(f32[224,128]{1,0:T(8,128)S(1)} %get-tuple-element.93), channel_id=1, source_target_pairs={{0,1},{1,0},{2,3},{3,2},{4,5},{5,4},{6,7},{7,6},{8,16},{9,17},{10,... | collective-permute-start | bytes 344072 | tf_op jit(solution)/shard_map/ppermute | solution.py:594
  89.2 2.9 %inner3.1 = (f32[1280,128]{1,0:T(8,128)S(1)}, f32[1280,128]{1,0:T(8,128)S(1)}, f32[1024,128]{1,0:T(8,128)}, f32[1024,128]{1,0:T(8,128)S(1)}, f32[1024,128]{1,0:T(8,128)S(1)}) custom-call(s32[4,3]{1,0:T(4,128)S(1)} %copy-done.2, f32[4,4]{1,0:T(4,128)S(1)} %copy-done.3, bf16[384,128]{1,0:T(8,128)(2,1)S(1)} %copy-done.1, bf16[384,128]{1,0:T(8,128)(2,1)S(1)} %copy-done, ...), custom_call_target="tpu_custom_call" | custom-call | flops 20000000 | bytes 8000000 | tf_op jit(solution)/shard_map/inner3/pallas_call | solution.py:561
  93.2 1.6 %edge3.1 = (f32[1024,128]{1,0:T(8,128)}, f32[1024,128]{1,0:T(8,128)}, f32[1024,128]{1,0:T(8,128)}) custom-call(f32[1024,128]{1,0:T(8,128)S(1)} %get-tuple-element.90.pres.refs_0_, f32[224,128]{1,0:T(8,128)S(1)} %collective-permute-done.12.refs_1_, f32[224,128]{1,0:T(8,128)S(1)} %collective-permute-done.13.refs_2_, ...), custom_call_target="tpu_custom_call" | custom-call | tf_op jit(solution)/shard_map/edge3/pallas_call | solution.py:561
  (35 shorter events, 3.9 us)
Async XLA Ops:
  2.8 27.6 %all-to-all-start = ((f32[128,16,128]{2,1,0:T(8,128)}), f32[128,16,128]{2,1,0:T(8,128)S(1)}, u32[]{:S(2)}, u32[]{:S(2)}) async-start(f32[128,16,128]{2,1,0:T(8,128)} %bitcast.13), calls=%async_computation | async-start | bytes 2097152 | tf_op jit(solution)/shard_map/all_to_all | solution.py:624
  13.2 7.3 %copy-start.1 = (bf16[384,128]{1,0:T(8,128)(2,1)S(1)}, bf16[384,128]{1,0:T(8,128)(2,1)}, u32[]{:S(2)}) copy-start(bf16[384,128]{1,0:T(8,128)(2,1)} %constant.4.clone.mat_f) | copy-start | bytes 294916
  14.8 24.2 %collective-permute-start = (f32[352,128]{1,0:T(8,128)S(1)}, f32[352,128]{1,0:T(8,128)S(1)}, u32[]{:S(2)}, u32[]{:S(2)}) collective-permute-start(f32[352,128]{1,0:T(8,128)S(1)} %get-tuple-element.55), channel_id=1, source_target_pairs={{0,8},{1,2},{2,1},{3,4},{4,3},{5,6},{6,5},{7,15},{8,0},{9,10},{10,... | collective-permute-start | bytes 540680 | tf_op jit(solution)/shard_map/ppermute | solution.py:594
  18.2 20.8 %collective-permute-start.1 = (f32[352,128]{1,0:T(8,128)S(1)}, f32[352,128]{1,0:T(8,128)S(1)}, u32[]{:S(2)}, u32[]{:S(2)}) collective-permute-start(f32[352,128]{1,0:T(8,128)S(1)} %get-tuple-element.56), channel_id=1, source_target_pairs={{0,1},{1,0},{2,3},{3,2},{4,5},{5,4},{6,7},{7,6},{8,9},{9,8},{10,11... | collective-permute-start | bytes 540680 | tf_op jit(solution)/shard_map/ppermute | solution.py:594
  18.4 20.7 %collective-permute-start.2 = (f32[352,128]{1,0:T(8,128)S(1)}, f32[352,128]{1,0:T(8,128)S(1)}, u32[]{:S(2)}, u32[]{:S(2)}) collective-permute-start(f32[352,128]{1,0:T(8,128)S(1)} %get-tuple-element.57), channel_id=1, source_target_pairs={{0,1},{1,0},{2,3},{3,2},{4,5},{5,4},{6,7},{7,6},{8,16},{9,17},{10,... | collective-permute-start | bytes 540680 | tf_op jit(solution)/shard_map/ppermute | solution.py:594
  20.3 2.5 %copy-start.4 = (s32[4,2]{0,1:T(2,128)S(1)}, s32[4,2]{0,1:T(2,128)}, u32[]{:S(2)}) copy-start(s32[4,2]{0,1:T(2,128)} %param.13) | copy-start | bytes 100
  20.3 18.8 %collective-permute-start.3 = (f32[352,128]{1,0:T(8,128)S(1)}, f32[352,128]{1,0:T(8,128)S(1)}, u32[]{:S(2)}, u32[]{:S(2)}) collective-permute-start(f32[352,128]{1,0:T(8,128)S(1)} %get-tuple-element.58), channel_id=1, source_target_pairs={{0,8},{1,9},{2,10},{3,11},{4,12},{5,13},{6,14},{7,15},{8,0},{9,1},... | collective-permute-start | bytes 540680 | tf_op jit(solution)/shard_map/ppermute | solution.py:594
  32.4 6.7 %copy-start.2 = (s32[4,3]{1,0:T(4,128)S(1)}, s32[4,3]{1,0:T(4,128)}, u32[]{:S(2)}) copy-start(s32[4,3]{1,0:T(4,128)} %cells.7) | copy-start | bytes 148
  32.4 6.7 %copy-start.3 = (f32[4,4]{1,0:T(4,128)S(1)}, f32[4,4]{1,0:T(4,128)}, u32[]{:S(2)}) copy-start(f32[4,4]{1,0:T(4,128)} %amps.7) | copy-start | bytes 196
  32.4 27.9 %all-to-all-start.1 = ((f32[128,11,2,128]{3,2,1,0:T(2,128)}), f32[128,11,2,128]{3,2,1,0:T(2,128)S(1)}, u32[]{:S(2)}, u32[]{:S(2)}) async-start(f32[128,11,2,128]{3,2,1,0:T(2,128)} %cut.1), calls=%async_computation.1 | async-start | bytes 2883584 | tf_op jit(solution)/shard_map/all_to_all | solution.py:654
  39.0 21.2 %copy-start = (bf16[384,128]{1,0:T(8,128)(2,1)S(1)}, bf16[384,128]{1,0:T(8,128)(2,1)}, u32[]{:S(2)}) copy-start(bf16[384,128]{1,0:T(8,128)(2,1)} %constant.5.clone.mat_b) | copy-start | bytes 294916
  63.1 9.6 %collective-permute-start.4 = (f32[224,128]{1,0:T(8,128)S(1)}, f32[224,128]{1,0:T(8,128)S(1)}, u32[]{:S(2)}, u32[]{:S(2)}) collective-permute-start(f32[224,128]{1,0:T(8,128)S(1)} %get-tuple-element.65), channel_id=1, source_target_pairs={{0,8},{1,2},{2,1},{3,4},{4,3},{5,6},{6,5},{7,15},{8,0},{9,10},{10,... | collective-permute-start | bytes 344072 | tf_op jit(solution)/shard_map/ppermute | solution.py:594
  66.0 6.8 %collective-permute-start.5 = (f32[224,128]{1,0:T(8,128)S(1)}, f32[224,128]{1,0:T(8,128)S(1)}, u32[]{:S(2)}, u32[]{:S(2)}) collective-permute-start(f32[224,128]{1,0:T(8,128)S(1)} %get-tuple-element.66), channel_id=1, source_target_pairs={{0,1},{1,0},{2,3},{3,2},{4,5},{5,4},{6,7},{7,6},{8,9},{9,8},{10,11... | collective-permute-start | bytes 344072 | tf_op jit(solution)/shard_map/ppermute | solution.py:594
  66.0 6.8 %collective-permute-start.6 = (f32[224,128]{1,0:T(8,128)S(1)}, f32[224,128]{1,0:T(8,128)S(1)}, u32[]{:S(2)}, u32[]{:S(2)}) collective-permute-start(f32[224,128]{1,0:T(8,128)S(1)} %get-tuple-element.67), channel_id=1, source_target_pairs={{0,1},{1,0},{2,3},{3,2},{4,5},{5,4},{6,7},{7,6},{8,16},{9,17},{10,... | collective-permute-start | bytes 344072 | tf_op jit(solution)/shard_map/ppermute | solution.py:594
  68.0 4.7 %collective-permute-start.7 = (f32[224,128]{1,0:T(8,128)S(1)}, f32[224,128]{1,0:T(8,128)S(1)}, u32[]{:S(2)}, u32[]{:S(2)}) collective-permute-start(f32[224,128]{1,0:T(8,128)S(1)} %get-tuple-element.68), channel_id=1, source_target_pairs={{0,8},{1,9},{2,10},{3,11},{4,12},{5,13},{6,14},{7,15},{8,0},{9,1},... | collective-permute-start | bytes 344072 | tf_op jit(solution)/shard_map/ppermute | solution.py:594
  73.6 9.5 %collective-permute-start.8 = (f32[224,128]{1,0:T(8,128)S(1)}, f32[224,128]{1,0:T(8,128)S(1)}, u32[]{:S(2)}, u32[]{:S(2)}) collective-permute-start(f32[224,128]{1,0:T(8,128)S(1)} %get-tuple-element.79), channel_id=1, source_target_pairs={{0,8},{1,2},{2,1},{3,4},{4,3},{5,6},{6,5},{7,15},{8,0},{9,10},{10,... | collective-permute-start | bytes 344072 | tf_op jit(solution)/shard_map/ppermute | solution.py:594
  76.5 6.6 %collective-permute-start.9 = (f32[224,128]{1,0:T(8,128)S(1)}, f32[224,128]{1,0:T(8,128)S(1)}, u32[]{:S(2)}, u32[]{:S(2)}) collective-permute-start(f32[224,128]{1,0:T(8,128)S(1)} %get-tuple-element.80), channel_id=1, source_target_pairs={{0,1},{1,0},{2,3},{3,2},{4,5},{5,4},{6,7},{7,6},{8,9},{9,8},{10,11... | collective-permute-start | bytes 344072 | tf_op jit(solution)/shard_map/ppermute | solution.py:594
  76.5 6.6 %collective-permute-start.10 = (f32[224,128]{1,0:T(8,128)S(1)}, f32[224,128]{1,0:T(8,128)S(1)}, u32[]{:S(2)}, u32[]{:S(2)}) collective-permute-start(f32[224,128]{1,0:T(8,128)S(1)} %get-tuple-element.81), channel_id=1, source_target_pairs={{0,1},{1,0},{2,3},{3,2},{4,5},{5,4},{6,7},{7,6},{8,16},{9,17},{10,... | collective-permute-start | bytes 344072 | tf_op jit(solution)/shard_map/ppermute | solution.py:594
  78.6 4.6 %collective-permute-start.11 = (f32[224,128]{1,0:T(8,128)S(1)}, f32[224,128]{1,0:T(8,128)S(1)}, u32[]{:S(2)}, u32[]{:S(2)}) collective-permute-start(f32[224,128]{1,0:T(8,128)S(1)} %get-tuple-element.82), channel_id=1, source_target_pairs={{0,8},{1,9},{2,10},{3,11},{4,12},{5,13},{6,14},{7,15},{8,0},{9,1},... | collective-permute-start | bytes 344072 | tf_op jit(solution)/shard_map/ppermute | solution.py:594
  84.1 8.6 %collective-permute-start.12 = (f32[224,128]{1,0:T(8,128)S(1)}, f32[224,128]{1,0:T(8,128)S(1)}, u32[]{:S(2)}, u32[]{:S(2)}) collective-permute-start(f32[224,128]{1,0:T(8,128)S(1)} %get-tuple-element.91), channel_id=1, source_target_pairs={{0,8},{1,2},{2,1},{3,4},{4,3},{5,6},{6,5},{7,15},{8,0},{9,10},{10,... | collective-permute-start | bytes 344072 | tf_op jit(solution)/shard_map/ppermute | solution.py:594
  87.1 5.6 %collective-permute-start.13 = (f32[224,128]{1,0:T(8,128)S(1)}, f32[224,128]{1,0:T(8,128)S(1)}, u32[]{:S(2)}, u32[]{:S(2)}) collective-permute-start(f32[224,128]{1,0:T(8,128)S(1)} %get-tuple-element.92), channel_id=1, source_target_pairs={{0,1},{1,0},{2,3},{3,2},{4,5},{5,4},{6,7},{7,6},{8,9},{9,8},{10,11... | collective-permute-start | bytes 344072 | tf_op jit(solution)/shard_map/ppermute | solution.py:594
  87.1 6.0 %collective-permute-start.14 = (f32[224,128]{1,0:T(8,128)S(1)}, f32[224,128]{1,0:T(8,128)S(1)}, u32[]{:S(2)}, u32[]{:S(2)}) collective-permute-start(f32[224,128]{1,0:T(8,128)S(1)} %get-tuple-element.93), channel_id=1, source_target_pairs={{0,1},{1,0},{2,3},{3,2},{4,5},{5,4},{6,7},{7,6},{8,16},{9,17},{10,... | collective-permute-start | bytes 344072 | tf_op jit(solution)/shard_map/ppermute | solution.py:594
  89.2 4.0 %collective-permute-start.15 = (f32[224,128]{1,0:T(8,128)S(1)}, f32[224,128]{1,0:T(8,128)S(1)}, u32[]{:S(2)}, u32[]{:S(2)}) collective-permute-start(f32[224,128]{1,0:T(8,128)S(1)} %get-tuple-element.94), channel_id=1, source_target_pairs={{0,8},{1,9},{2,10},{3,11},{4,12},{5,13},{6,14},{7,15},{8,0},{9,1},... | collective-permute-start | bytes 344072 | tf_op jit(solution)/shard_map/ppermute | solution.py:594

commit v9 on v8

--- a/solution.py
+++ b/solution.py
@@ -148,9 +148,11 @@
     send_faces(y_in, (), (gy_a, gy_b), HALO, 4)
 
 
-def cut_kernel(dealt, corners_from, _, out, rho_lines, vel_lines, cuts, sem, corners, corner_sem):
-    pull = pltpu.make_async_copy(corners_from, corners, corner_sem.at[0])
-    pull.start()
+def corner(corners, shot, which):
+    return jnp.max(corners[pl.ds(shot, 1), which : which + 1])
+
+
+def cut_kernel(dealt, corners, _, out, rho_lines, vel_lines, cuts, sem):
     s, g, col_class = place()
     row_class = s * 4 + g
     for t in range(16):
@@ -160,14 +162,14 @@
             vel_lines[dst : dst + 8, :] = dealt[src : src + 8, :]
             rho_lines[dst : dst + 8, :] = dealt[src + 8 : src + 16, :]
     flat = out.reshape(128 * MESSAGE, 128)
-    pull.wait()
     pushes = []
     for shot in range(4):
-        col = lax.shift_right_arithmetic(corners[shot, 1] - col_class + 7, 3)
-        wide_col = lax.shift_right_arithmetic(corners[shot, 1] - 4 - col_class + 7, 3)
+        shot_x, shot_y = corner(corners, shot, 0), corner(corners, shot, 1)
+        col = lax.shift_right_arithmetic(shot_y - col_class + 7, 3)
+        wide_col = lax.shift_right_arithmetic(shot_y - 4 - col_class + 7, 3)
 
         def block(part, carry):
-            corner_x = corners[shot, 0] + part * CX
+            corner_x = shot_x + part * CX
             row = lax.shift_right_arithmetic(corner_x - row_class + 15, 4)
             low = lax.rem(row_class - corner_x + 4 + 1024, 16) < 4
             rim = jnp.clip(jnp.where(low, row - 1, row + 2), 0, 15)
@@ -196,8 +198,8 @@
 
 def unpack_model(corners, window, buoy, modu, rho):
     s, g, h = place()
-    corner_x = corners[s, 0] + g * CX
-    corner_y = corners[s, 1] + h * CY
+    corner_x = corner(corners, s, 0) + g * CX
+    corner_y = corner(corners, s, 1) + h * CY
     wide_turn = lax.rem(8 - lax.rem(corner_y + 4, 8), 8)
     turn = lax.rem(8 - lax.rem(corner_y, 8), 8)
     sub = lax.broadcasted_iota(jnp.int32, (8, 128), 0)
@@ -325,15 +327,12 @@
         field[pl.ds(at, 1), :] = field[pl.ds(at, 1), :] + jnp.where(lane == cells[s, 2], kick, 0.0)
 
 
-def step0_kernel(corners_from, mat_b, window, *refs):
+def step0_kernel(corners, mat_b, window, *refs):
     sources, outs, scratch = refs[:7], refs[7:17], refs[17:]
     new_p, wide_x, wide_y, new_z, buoy, modu, gy_b, gy_a, gx_b, gx_a = outs
-    pres, in_x, in_y, in_z, grad_x, grad_y, grad_z, rho, spread, sem, corners, corner_sem = scratch
-    pull = pltpu.make_async_copy(corners_from, corners, corner_sem.at[0])
-    pull.start()
+    pres, in_x, in_y, in_z, grad_x, grad_y, grad_z, rho, spread, sem = scratch
     order = (6, 3, 4, 1, 0, 5, 2)
     pulls = pull_all([(sources[i], scratch[i]) for i in order], sem)
-    pull.wait()
     unpack_model(corners, window, buoy, modu, rho)
 
     def wait(*which):
@@ -575,25 +574,28 @@
 
 def partners(match):
     out = []
-    for g in range(GX):
-        for h in range(GY):
-            to_g, to_h = match(g, h)
-            out.append((g * GY + h, to_g * GY + to_h))
+    for s in range(4):
+        for g in range(GX):
+            for h in range(GY):
+                to_s, to_g, to_h = match(s, g, h)
+                out.append(((s * GX + g) * GY + h, (to_s * GX + to_g) * GY + to_h))
     return out
 
 
-gx_near = partners(lambda g, h: (g ^ 1, h))
-gx_far = partners(lambda g, h: (g, h ^ 1) if g in (0, GX - 1) else (3 - g, h))
-gy_near = partners(lambda g, h: (g, h ^ 1))
-gy_far = partners(lambda g, h: (g ^ 1, h) if h in (0, GY - 1) else (g, ((h + 1) ^ 1) - 1))
+gx_near = partners(lambda s, g, h: (s, g ^ 1, h))
+gx_far = partners(lambda s, g, h: (s ^ 1, g, h) if g in (0, GX - 1) else (s, 3 - g, h))
+gy_near = partners(lambda s, g, h: (s, g, h ^ 1))
+gy_far = partners(
+    lambda s, g, h: (s ^ 1, g, h) if h in (0, GY - 1) else (s, g, ((h + 1) ^ 1) - 1)
+)
 
 
 def exchange(faces):
-    plane = ("gx", "gy")
-    return [
-        lax.ppermute(face, plane, pairs)
-        for face, pairs in zip(faces, (gy_far, gy_near, gx_far, gx_near))
-    ]
+    gy_b = lax.ppermute(faces[0], DEVICES, gy_far)
+    gx_b = lax.ppermute(faces[2], DEVICES, gx_far)
+    gy_a = lax.ppermute(faces[1], DEVICES, gy_near)
+    gx_a = lax.ppermute(faces[3], DEVICES, gx_near)
+    return [gy_b, gy_a, gx_b, gx_a]
 
 
 def shards(velocity, density, offsets, pressure, vel_x, vel_y, vel_z, source_cells, wavelet):
@@ -611,7 +613,6 @@
     long = pl.CostEstimate(flops=3 * 10**10, bytes_accessed=8_000_000, transcendentals=0)
 
     dma = pltpu.SemaphoreType.DMA
-    corner_scratch = [pltpu.SMEM((4, 2), jnp.int32), dma((1,))]
     (deal,) = call(
         pack_kernel,
         [shape(128 * 16)],
@@ -646,9 +647,9 @@
         cut_kernel,
         [jax.ShapeDtypeStruct((128, MESSAGE // 2, 2, 128), f32)],
         [dealt.reshape(128 * 16, 128), offsets, grad_z],
-        [vmem(16 * LINE), vmem(16 * LINE), vmem(128 * MESSAGE), dma((4,))] + corner_scratch,
+        [vmem(16 * LINE), vmem(16 * LINE), vmem(128 * MESSAGE), dma((4,))],
         "cut",
-        hbm=(1, 2),
+        hbm=(2,),
         to_hbm=True,
     )
     window = lax.all_to_all(cut, DEVICES, 0, 0, tiled=True)
@@ -671,9 +672,9 @@
         + [pres, flow_x, flow_y, flow_z, grad_x, grad_y, grad_z],
         [vmem(CX * CY), vmem(WIDE * CY), vmem(WIDE * CY), vmem(CX * CY)]
         + [vmem(WIDE * CY), vmem(WIDE * CY), vmem(CX * CY)]
-        + [vmem(WIDE * WIDE), vmem(CX * CY), dma((7,))] + corner_scratch,
+        + [vmem(WIDE * WIDE), vmem(CX * CY), dma((7,))],
         "step0",
-        hbm=[0, *range(3, 10)],
+        hbm=range(3, 10),
     )
     for step in range(1, STEPS):
         last = step == STEPS - 1

time: 95.2 us -> 94.6 us (level)
  waiting for transfers between devices: 29.5 us -> 33.4 us
  starting transfers between devices: 37.5 us -> 34.1 us
    ppermute x16, starting transfers between devices: 20.6 us -> 16.8 us  [the longest x4 12.3 us: exchange(): gy_b = lax.ppermute(faces[0], DEVICES, gy_far)]
    ppermute x16, waiting for transfers between devices: 6.07 us -> 9.39 us  [the longest x4 9.36 us: exchange(): gy_b = lax.ppermute(faces[0], DEVICES, gy_far)]
  transfers between devices with their start and end apart: 18 -> 18, of which waited for: 6 -> 5; matrix products, arithmetic and copies ran while one was open for 1% -> 0% of each run, Pallas kernels for 19% -> 18%
where the time goes in v9:
time: 94.6 us; the launch traced here: 94.2 us
  starting transfers between devices  34.1 us (36%)
  waiting for transfers between devices  33.4 us (35%)
  Pallas kernels  25.7 us (27%)
    pallas_call x12, Pallas kernels, call(): pl.pallas_call(kernel, out_shape=outs, in_specs=specs, out_specs=[pl.Bloc...  25.7 us
    all_to_all x1, waiting for transfers between devices, shards(): window = lax.all_to_all(cut, DEVICES, 0, 0, tiled=True)  16.5 us
    ppermute x4, starting transfers between devices, exchange(): gy_b = lax.ppermute(faces[0], DEVICES, gy_far)  12.3 us
    all_to_all x1, starting transfers between devices, shards(): lax.all_to_all(deal.reshape(128, 16, 128), DEVICES, 0, 0, tiled=True)  10.3 us
    ppermute x4, waiting for transfers between devices, exchange(): gy_b = lax.ppermute(faces[0], DEVICES, gy_far)  9.36 us
    all_to_all x1, waiting for transfers between devices, shards(): lax.all_to_all(deal.reshape(128, 16, 128), DEVICES, 0, 0, tiled=True)  7.57 us
    all_to_all x1, starting transfers between devices, shards(): window = lax.all_to_all(cut, DEVICES, 0, 0, tiled=True)  7.03 us
    ppermute x4, starting transfers between devices, exchange(): gx_b = lax.ppermute(faces[2], DEVICES, gx_far)  2.26 us
  transfers between devices with their start and end apart: 18, of which 5 were waited for; matrix products, arithmetic and copies ran while one was open for 0% of the time, Pallas kernels for 18%

profile of v9, /device:TPU:16, one launch (start us, length us, event | category | flops | bytes accessed | tf_op | source)
XLA Modules:
  0.0 94.2 jit_solution(4889282285841360610)
XLA Ops:
  0.6 2.2 %pack.1._ = f32[2048,128]{1,0:T(8,128)} custom-call(f32[1024,128]{1,0:T(8,128)} %bitcast.21, f32[1024,128]{1,0:T(8,128)} %bitcast.22), custom_call_target="tpu_custom_call" | custom-call | tf_op jit(solution)/shard_map/pack/pallas_call | solution.py:560
  2.8 10.3 %all-to-all-start = ((f32[128,16,128]{2,1,0:T(8,128)}), f32[128,16,128]{2,1,0:T(8,128)S(1)}, u32[]{:S(2)}, u32[]{:S(2)}) async-start(f32[128,16,128]{2,1,0:T(8,128)} %bitcast.13), calls=%async_computation | async-start | bytes 2097152 | tf_op jit(solution)/shard_map/all_to_all | solution.py:625
  13.2 1.7 %first_faces.1 = (f32[352,128]{1,0:T(8,128)S(1)}, f32[352,128]{1,0:T(8,128)S(1)}, f32[352,128]{1,0:T(8,128)S(1)}, f32[352,128]{1,0:T(8,128)S(1)}) custom-call(f32[1024,128]{1,0:T(8,128)} %bitcast.14, f32[1024,128]{1,0:T(8,128)} %bitcast.17, f32[1024,128]{1,0:T(8,128)} %bitcast.19, f32[2048,128]{1,0:T(8,128)} %pack.1._), custom_call_target="tpu_custom_call" | custom-call | flops 20000000 | bytes 8000000 | tf_op jit(solution)/shard_map/first_faces/pallas_call | solution.py:560
  14.8 3.4 %collective-permute-start = (f32[352,128]{1,0:T(8,128)S(1)}, f32[352,128]{1,0:T(8,128)S(1)}, u32[]{:S(2)}, u32[]{:S(2)}) collective-permute-start(f32[352,128]{1,0:T(8,128)S(1)} %get-tuple-element.55), channel_id=1, source_target_pairs={{0,32},{1,2},{2,1},{3,4},{4,3},{5,6},{6,5},{7,39},{8,40},{9,10},{1... | collective-permute-start | bytes 540680 | tf_op jit(solution)/shard_map/ppermute | solution.py:594
  18.4 1.5 %collective-permute-start.2 = (f32[352,128]{1,0:T(8,128)S(1)}, f32[352,128]{1,0:T(8,128)S(1)}, u32[]{:S(2)}, u32[]{:S(2)}) collective-permute-start(f32[352,128]{1,0:T(8,128)S(1)} %get-tuple-element.57), channel_id=1, source_target_pairs={{0,32},{1,33},{2,34},{3,35},{4,36},{5,37},{6,38},{7,39},{8,16},{9,... | collective-permute-start | bytes 540680 | tf_op jit(solution)/shard_map/ppermute | solution.py:595
  20.5 2.2 %step0_depth.1._.refs_6_ = f32[1024,128]{1,0:T(8,128)} custom-call(bf16[384,128]{1,0:T(8,128)(2,1)S(1)} %copy-done.1, f32[1024,128]{1,0:T(8,128)} %bitcast.15), custom_call_target="tpu_custom_call" | custom-call | flops 30000001024 | bytes 8000000 | tf_op jit(solution)/shard_map/step0_depth/pallas_call | solution.py:560
  22.8 7.6 %all-to-all-done = f32[128,16,128]{2,1,0:T(8,128)S(1)} async-done(((f32[128,16,128]{2,1,0:T(8,128)}), f32[128,16,128]{2,1,0:T(8,128)S(1)}, u32[]{:S(2)}, u32[]{:S(2)}) %all-to-all-start) | async-done | bytes 1048608 | tf_op jit(solution)/shard_map/all_to_all | solution.py:625
  30.4 1.5 %cut.1 = f32[128,11,2,128]{3,2,1,0:T(2,128)} custom-call(f32[2048,128]{1,0:T(8,128)S(1)} %bitcast.12, s32[4,2]{1,0:T(4,128)S(1)} %copy.16.corners, f32[1024,128]{1,0:T(8,128)} %step0_depth.1._.refs_6_), custom_call_target="tpu_custom_call" | custom-call | tf_op jit(solution)/shard_map/cut/pallas_call | solution.py:560
  32.0 7.0 %all-to-all-start.1 = ((f32[128,11,2,128]{3,2,1,0:T(2,128)}), f32[128,11,2,128]{3,2,1,0:T(2,128)S(1)}, u32[]{:S(2)}, u32[]{:S(2)}) async-start(f32[128,11,2,128]{3,2,1,0:T(2,128)} %cut.1), calls=%async_computation.1 | async-start | bytes 2883584 | tf_op jit(solution)/shard_map/all_to_all | solution.py:655
  39.1 4.7 %step0_gradients.1 = (f32[1280,128]{1,0:T(8,128)}, f32[1280,128]{1,0:T(8,128)}, f32[1280,128]{1,0:T(8,128)}, f32[1280,128]{1,0:T(8,128)}, f32[1024,128]{1,0:T(8,128)}) custom-call(s32[4,3]{1,0:T(4,128)S(1)} %copy-done.2, f32[4,4]{1,0:T(4,128)S(1)} %copy-done.3, f32[1024,128]{1,0:T(8,128)} %bitcast.16, f32[352,128]{1,0:T(8,128)S(1)} %collective-permute-done.gy_b, ...), custom_call_target="tpu_custom_call" | custom-call | flops 30000001024 | bytes 8000000 | tf_op jit(solution)/shard_map/step0_gradients/pallas_call | solution.py:560
  43.8 16.5 %all-to-all-done.1.window = f32[128,11,2,128]{3,2,1,0:T(2,128)S(1)} async-done(((f32[128,11,2,128]{3,2,1,0:T(2,128)}), f32[128,11,2,128]{3,2,1,0:T(2,128)S(1)}, u32[]{:S(2)}, u32[]{:S(2)}) %all-to-all-start.1) | async-done | bytes 1441824 | tf_op jit(solution)/shard_map/all_to_all | solution.py:655
  60.2 2.8 %step0.1 = (f32[1024,128]{1,0:T(8,128)S(1)}, f32[1280,128]{1,0:T(8,128)S(1)}, f32[1280,128]{1,0:T(8,128)S(1)}, f32[1024,128]{1,0:T(8,128)S(1)}, f32[1600,128]{1,...) custom-call(s32[4,2]{1,0:T(4,128)S(1)} %copy.16.corners, ...), custom_call_target="tpu_custom_call" | custom-call | tf_op jit(solution)/shard_map/step0/pallas_call | solution.py:560
  63.0 2.9 %collective-permute-start.4 = (f32[224,128]{1,0:T(8,128)S(1)}, f32[224,128]{1,0:T(8,128)S(1)}, u32[]{:S(2)}, u32[]{:S(2)}) collective-permute-start(f32[224,128]{1,0:T(8,128)S(1)} %get-tuple-element.65), channel_id=1, source_target_pairs={{0,32},{1,2},{2,1},{3,4},{4,3},{5,6},{6,5},{7,39},{8,40},{9,10},{1... | collective-permute-start | bytes 344072 | tf_op jit(solution)/shard_map/ppermute | solution.py:594
  66.3 1.1 %collective-permute-start.7 = (f32[224,128]{1,0:T(8,128)S(1)}, f32[224,128]{1,0:T(8,128)S(1)}, u32[]{:S(2)}, u32[]{:S(2)}) collective-permute-start(f32[224,128]{1,0:T(8,128)S(1)} %get-tuple-element.68), channel_id=1, source_target_pairs={{0,8},{1,9},{2,10},{3,11},{4,12},{5,13},{6,14},{7,15},{8,0},{9,1},... | collective-permute-start | bytes 344072 | tf_op jit(solution)/shard_map/ppermute | solution.py:597
  67.4 2.1 %inner1.1 = (f32[1280,128]{1,0:T(8,128)S(1)}, f32[1280,128]{1,0:T(8,128)S(1)}, f32[1024,128]{1,0:T(8,128)S(1)}, f32[1024,128]{1,0:T(8,128)S(1)}, f32[1024,128]{1,0:T(8,128)S(1)}) custom-call(s32[4,3]{1,0:T(4,128)S(1)} %copy-done.2, f32[4,4]{1,0:T(4,128)S(1)} %copy-done.3, bf16[384,128]{1,0:T(8,128)(2,1)S(1)} %copy-done.1, bf16[384,128]{1,0:T(8,128)(2,1)S(1)} %copy-done, ...), custom_call_target="tpu_custom_call" | custom-call | flops 20000000 | bytes 8000000 | tf_op jit(solution)/shard_map/inner1/pallas_call | solution.py:560
  69.5 3.2 %collective-permute-done.4.refs_1_ = f32[224,128]{1,0:T(8,128)S(1)} collective-permute-done((f32[224,128]{1,0:T(8,128)S(1)}, f32[224,128]{1,0:T(8,128)S(1)}, u32[]{:S(2)}, u32[]{:S(2)}) %collective-permute-start.4) | collective-permute-done | bytes 114720 | tf_op jit(solution)/shard_map/ppermute | solution.py:594
  72.7 0.9 edge1.1
  73.6 2.9 %collective-permute-start.8 = (f32[224,128]{1,0:T(8,128)S(1)}, f32[224,128]{1,0:T(8,128)S(1)}, u32[]{:S(2)}, u32[]{:S(2)}) collective-permute-start(f32[224,128]{1,0:T(8,128)S(1)} %get-tuple-element.79), channel_id=1, source_target_pairs={{0,32},{1,2},{2,1},{3,4},{4,3},{5,6},{6,5},{7,39},{8,40},{9,10},{1... | collective-permute-start | bytes 344072 | tf_op jit(solution)/shard_map/ppermute | solution.py:594
  77.2 2.1 %inner2.1 = (f32[1280,128]{1,0:T(8,128)S(1)}, f32[1280,128]{1,0:T(8,128)S(1)}, f32[1024,128]{1,0:T(8,128)S(1)}, f32[1024,128]{1,0:T(8,128)S(1)}, f32[1024,128]{1,0:T(8,128)S(1)}) custom-call(s32[4,3]{1,0:T(4,128)S(1)} %copy-done.2, f32[4,4]{1,0:T(4,128)S(1)} %copy-done.3, bf16[384,128]{1,0:T(8,128)(2,1)S(1)} %copy-done.1, bf16[384,128]{1,0:T(8,128)(2,1)S(1)} %copy-done, ...), custom_call_target="tpu_custom_call" | custom-call | flops 20000000 | bytes 8000000 | tf_op jit(solution)/shard_map/inner2/pallas_call | solution.py:560
  79.4 3.8 %collective-permute-done.8.refs_1_ = f32[224,128]{1,0:T(8,128)S(1)} collective-permute-done((f32[224,128]{1,0:T(8,128)S(1)}, f32[224,128]{1,0:T(8,128)S(1)}, u32[]{:S(2)}, u32[]{:S(2)}) %collective-permute-start.8) | collective-permute-done | bytes 114720 | tf_op jit(solution)/shard_map/ppermute | solution.py:594
  84.1 3.1 %collective-permute-start.12 = (f32[224,128]{1,0:T(8,128)S(1)}, f32[224,128]{1,0:T(8,128)S(1)}, u32[]{:S(2)}, u32[]{:S(2)}) collective-permute-start(f32[224,128]{1,0:T(8,128)S(1)} %get-tuple-element.91), channel_id=1, source_target_pairs={{0,32},{1,2},{2,1},{3,4},{4,3},{5,6},{6,5},{7,39},{8,40},{9,10},{1... | collective-permute-start | bytes 344072 | tf_op jit(solution)/shard_map/ppermute | solution.py:594
  87.2 2.9 %inner3.1 = (f32[1280,128]{1,0:T(8,128)S(1)}, f32[1280,128]{1,0:T(8,128)S(1)}, f32[1024,128]{1,0:T(8,128)}, f32[1024,128]{1,0:T(8,128)S(1)}, f32[1024,128]{1,0:T(8,128)S(1)}) custom-call(s32[4,3]{1,0:T(4,128)S(1)} %copy-done.2, f32[4,4]{1,0:T(4,128)S(1)} %copy-done.3, bf16[384,128]{1,0:T(8,128)(2,1)S(1)} %copy-done.1, bf16[384,128]{1,0:T(8,128)(2,1)S(1)} %copy-done, ...), custom_call_target="tpu_custom_call" | custom-call | flops 20000000 | bytes 8000000 | tf_op jit(solution)/shard_map/inner3/pallas_call | solution.py:560
  90.2 2.4 %collective-permute-done.12.refs_1_ = f32[224,128]{1,0:T(8,128)S(1)} collective-permute-done((f32[224,128]{1,0:T(8,128)S(1)}, f32[224,128]{1,0:T(8,128)S(1)}, u32[]{:S(2)}, u32[]{:S(2)}) %collective-permute-start.12) | collective-permute-done | bytes 114720 | tf_op jit(solution)/shard_map/ppermute | solution.py:594
  92.6 1.7 %edge3.1 = (f32[1024,128]{1,0:T(8,128)}, f32[1024,128]{1,0:T(8,128)}, f32[1024,128]{1,0:T(8,128)}) custom-call(f32[1024,128]{1,0:T(8,128)S(1)} %get-tuple-element.90.pres.refs_0_, f32[224,128]{1,0:T(8,128)S(1)} %collective-permute-done.12.refs_1_, f32[224,128]{1,0:T(8,128)S(1)} %collective-permute-done.13.refs_2_, ...), custom_call_target="tpu_custom_call" | custom-call | tf_op jit(solution)/shard_map/edge3/pallas_call | solution.py:560
  (35 shorter events, 3.0 us)
Async XLA Ops:
  2.8 27.6 %all-to-all-start = ((f32[128,16,128]{2,1,0:T(8,128)}), f32[128,16,128]{2,1,0:T(8,128)S(1)}, u32[]{:S(2)}, u32[]{:S(2)}) async-start(f32[128,16,128]{2,1,0:T(8,128)} %bitcast.13), calls=%async_computation | async-start | bytes 2097152 | tf_op jit(solution)/shard_map/all_to_all | solution.py:625
  13.2 7.3 %copy-start.1 = (bf16[384,128]{1,0:T(8,128)(2,1)S(1)}, bf16[384,128]{1,0:T(8,128)(2,1)}, u32[]{:S(2)}) copy-start(bf16[384,128]{1,0:T(8,128)(2,1)} %constant.4.clone.mat_f) | copy-start | bytes 294916
  14.8 24.2 %collective-permute-start = (f32[352,128]{1,0:T(8,128)S(1)}, f32[352,128]{1,0:T(8,128)S(1)}, u32[]{:S(2)}, u32[]{:S(2)}) collective-permute-start(f32[352,128]{1,0:T(8,128)S(1)} %get-tuple-element.55), channel_id=1, source_target_pairs={{0,32},{1,2},{2,1},{3,4},{4,3},{5,6},{6,5},{7,39},{8,40},{9,10},{1... | collective-permute-start | bytes 540680 | tf_op jit(solution)/shard_map/ppermute | solution.py:594
  18.2 20.8 %collective-permute-start.1 = (f32[352,128]{1,0:T(8,128)S(1)}, f32[352,128]{1,0:T(8,128)S(1)}, u32[]{:S(2)}, u32[]{:S(2)}) collective-permute-start(f32[352,128]{1,0:T(8,128)S(1)} %get-tuple-element.56), channel_id=1, source_target_pairs={{0,1},{1,0},{2,3},{3,2},{4,5},{5,4},{6,7},{7,6},{8,9},{9,8},{10,11... | collective-permute-start | bytes 540680 | tf_op jit(solution)/shard_map/ppermute | solution.py:596
  18.4 20.7 %collective-permute-start.2 = (f32[352,128]{1,0:T(8,128)S(1)}, f32[352,128]{1,0:T(8,128)S(1)}, u32[]{:S(2)}, u32[]{:S(2)}) collective-permute-start(f32[352,128]{1,0:T(8,128)S(1)} %get-tuple-element.57), channel_id=1, source_target_pairs={{0,32},{1,33},{2,34},{3,35},{4,36},{5,37},{6,38},{7,39},{8,16},{9,... | collective-permute-start | bytes 540680 | tf_op jit(solution)/shard_map/ppermute | solution.py:595
  19.8 2.9 %copy-start.4 = (s32[4,2]{0,1:T(2,128)S(1)}, s32[4,2]{0,1:T(2,128)}, u32[]{:S(2)}) copy-start(s32[4,2]{0,1:T(2,128)} %param.13) | copy-start | bytes 100
  19.8 19.2 %collective-permute-start.3 = (f32[352,128]{1,0:T(8,128)S(1)}, f32[352,128]{1,0:T(8,128)S(1)}, u32[]{:S(2)}, u32[]{:S(2)}) collective-permute-start(f32[352,128]{1,0:T(8,128)S(1)} %get-tuple-element.58), channel_id=1, source_target_pairs={{0,8},{1,9},{2,10},{3,11},{4,12},{5,13},{6,14},{7,15},{8,0},{9,1},... | collective-permute-start | bytes 540680 | tf_op jit(solution)/shard_map/ppermute | solution.py:597
  31.9 7.1 %copy-start.2 = (s32[4,3]{1,0:T(4,128)S(1)}, s32[4,3]{1,0:T(4,128)}, u32[]{:S(2)}) copy-start(s32[4,3]{1,0:T(4,128)} %cells.7) | copy-start | bytes 148
  31.9 7.1 %copy-start.3 = (f32[4,4]{1,0:T(4,128)S(1)}, f32[4,4]{1,0:T(4,128)}, u32[]{:S(2)}) copy-start(f32[4,4]{1,0:T(4,128)} %amps.7) | copy-start | bytes 196
  32.0 28.3 %all-to-all-start.1 = ((f32[128,11,2,128]{3,2,1,0:T(2,128)}), f32[128,11,2,128]{3,2,1,0:T(2,128)S(1)}, u32[]{:S(2)}, u32[]{:S(2)}) async-start(f32[128,11,2,128]{3,2,1,0:T(2,128)} %cut.1), calls=%async_computation.1 | async-start | bytes 2883584 | tf_op jit(solution)/shard_map/all_to_all | solution.py:655
  39.0 21.2 %copy-start = (bf16[384,128]{1,0:T(8,128)(2,1)S(1)}, bf16[384,128]{1,0:T(8,128)(2,1)}, u32[]{:S(2)}) copy-start(bf16[384,128]{1,0:T(8,128)(2,1)} %constant.5.clone.mat_b) | copy-start | bytes 294916
  63.0 9.6 %collective-permute-start.4 = (f32[224,128]{1,0:T(8,128)S(1)}, f32[224,128]{1,0:T(8,128)S(1)}, u32[]{:S(2)}, u32[]{:S(2)}) collective-permute-start(f32[224,128]{1,0:T(8,128)S(1)} %get-tuple-element.65), channel_id=1, source_target_pairs={{0,32},{1,2},{2,1},{3,4},{4,3},{5,6},{6,5},{7,39},{8,40},{9,10},{1... | collective-permute-start | bytes 344072 | tf_op jit(solution)/shard_map/ppermute | solution.py:594
  65.9 6.8 %collective-permute-start.5 = (f32[224,128]{1,0:T(8,128)S(1)}, f32[224,128]{1,0:T(8,128)S(1)}, u32[]{:S(2)}, u32[]{:S(2)}) collective-permute-start(f32[224,128]{1,0:T(8,128)S(1)} %get-tuple-element.66), channel_id=1, source_target_pairs={{0,1},{1,0},{2,3},{3,2},{4,5},{5,4},{6,7},{7,6},{8,9},{9,8},{10,11... | collective-permute-start | bytes 344072 | tf_op jit(solution)/shard_map/ppermute | solution.py:596
  65.9 6.8 %collective-permute-start.6 = (f32[224,128]{1,0:T(8,128)S(1)}, f32[224,128]{1,0:T(8,128)S(1)}, u32[]{:S(2)}, u32[]{:S(2)}) collective-permute-start(f32[224,128]{1,0:T(8,128)S(1)} %get-tuple-element.67), channel_id=1, source_target_pairs={{0,32},{1,33},{2,34},{3,35},{4,36},{5,37},{6,38},{7,39},{8,16},{9,... | collective-permute-start | bytes 344072 | tf_op jit(solution)/shard_map/ppermute | solution.py:595
  66.3 6.4 %collective-permute-start.7 = (f32[224,128]{1,0:T(8,128)S(1)}, f32[224,128]{1,0:T(8,128)S(1)}, u32[]{:S(2)}, u32[]{:S(2)}) collective-permute-start(f32[224,128]{1,0:T(8,128)S(1)} %get-tuple-element.68), channel_id=1, source_target_pairs={{0,8},{1,9},{2,10},{3,11},{4,12},{5,13},{6,14},{7,15},{8,0},{9,1},... | collective-permute-start | bytes 344072 | tf_op jit(solution)/shard_map/ppermute | solution.py:597
  73.6 9.5 %collective-permute-start.8 = (f32[224,128]{1,0:T(8,128)S(1)}, f32[224,128]{1,0:T(8,128)S(1)}, u32[]{:S(2)}, u32[]{:S(2)}) collective-permute-start(f32[224,128]{1,0:T(8,128)S(1)} %get-tuple-element.79), channel_id=1, source_target_pairs={{0,32},{1,2},{2,1},{3,4},{4,3},{5,6},{6,5},{7,39},{8,40},{9,10},{1... | collective-permute-start | bytes 344072 | tf_op jit(solution)/shard_map/ppermute | solution.py:594
  76.5 6.6 %collective-permute-start.9 = (f32[224,128]{1,0:T(8,128)S(1)}, f32[224,128]{1,0:T(8,128)S(1)}, u32[]{:S(2)}, u32[]{:S(2)}) collective-permute-start(f32[224,128]{1,0:T(8,128)S(1)} %get-tuple-element.80), channel_id=1, source_target_pairs={{0,1},{1,0},{2,3},{3,2},{4,5},{5,4},{6,7},{7,6},{8,9},{9,8},{10,11... | collective-permute-start | bytes 344072 | tf_op jit(solution)/shard_map/ppermute | solution.py:596
  76.5 6.6 %collective-permute-start.10 = (f32[224,128]{1,0:T(8,128)S(1)}, f32[224,128]{1,0:T(8,128)S(1)}, u32[]{:S(2)}, u32[]{:S(2)}) collective-permute-start(f32[224,128]{1,0:T(8,128)S(1)} %get-tuple-element.81), channel_id=1, source_target_pairs={{0,32},{1,33},{2,34},{3,35},{4,36},{5,37},{6,38},{7,39},{8,16},{9,... | collective-permute-start | bytes 344072 | tf_op jit(solution)/shard_map/ppermute | solution.py:595
  76.9 6.3 %collective-permute-start.11 = (f32[224,128]{1,0:T(8,128)S(1)}, f32[224,128]{1,0:T(8,128)S(1)}, u32[]{:S(2)}, u32[]{:S(2)}) collective-permute-start(f32[224,128]{1,0:T(8,128)S(1)} %get-tuple-element.82), channel_id=1, source_target_pairs={{0,8},{1,9},{2,10},{3,11},{4,12},{5,13},{6,14},{7,15},{8,0},{9,1},... | collective-permute-start | bytes 344072 | tf_op jit(solution)/shard_map/ppermute | solution.py:597
  84.1 8.5 %collective-permute-start.12 = (f32[224,128]{1,0:T(8,128)S(1)}, f32[224,128]{1,0:T(8,128)S(1)}, u32[]{:S(2)}, u32[]{:S(2)}) collective-permute-start(f32[224,128]{1,0:T(8,128)S(1)} %get-tuple-element.91), channel_id=1, source_target_pairs={{0,32},{1,2},{2,1},{3,4},{4,3},{5,6},{6,5},{7,39},{8,40},{9,10},{1... | collective-permute-start | bytes 344072 | tf_op jit(solution)/shard_map/ppermute | solution.py:594
  87.1 5.5 %collective-permute-start.13 = (f32[224,128]{1,0:T(8,128)S(1)}, f32[224,128]{1,0:T(8,128)S(1)}, u32[]{:S(2)}, u32[]{:S(2)}) collective-permute-start(f32[224,128]{1,0:T(8,128)S(1)} %get-tuple-element.92), channel_id=1, source_target_pairs={{0,1},{1,0},{2,3},{3,2},{4,5},{5,4},{6,7},{7,6},{8,9},{9,8},{10,11... | collective-permute-start | bytes 344072 | tf_op jit(solution)/shard_map/ppermute | solution.py:596
  87.1 5.5 %collective-permute-start.14 = (f32[224,128]{1,0:T(8,128)S(1)}, f32[224,128]{1,0:T(8,128)S(1)}, u32[]{:S(2)}, u32[]{:S(2)}) collective-permute-start(f32[224,128]{1,0:T(8,128)S(1)} %get-tuple-element.93), channel_id=1, source_target_pairs={{0,32},{1,33},{2,34},{3,35},{4,36},{5,37},{6,38},{7,39},{8,16},{9,... | collective-permute-start | bytes 344072 | tf_op jit(solution)/shard_map/ppermute | solution.py:595
  87.2 5.4 %collective-permute-start.15 = (f32[224,128]{1,0:T(8,128)S(1)}, f32[224,128]{1,0:T(8,128)S(1)}, u32[]{:S(2)}, u32[]{:S(2)}) collective-permute-start(f32[224,128]{1,0:T(8,128)S(1)} %get-tuple-element.94), channel_id=1, source_target_pairs={{0,8},{1,9},{2,10},{3,11},{4,12},{5,13},{6,14},{7,15},{8,0},{9,1},... | collective-permute-start | bytes 344072 | tf_op jit(solution)/shard_map/ppermute | solution.py:597

commit v10 on v9

--- a/solution.py
+++ b/solution.py
@@ -188,7 +188,8 @@
                 cuts[pl.ds(to + 10, 4), :] = rho_lines[pl.ds(rim_line + 4 * h, 4), :]
             return carry
 
-        lax.fori_loop(0, 4, block, 0)
+        for part in range(4):
+            block(part, 0)
         rows = pl.ds(shot * 32 * MESSAGE, 32 * MESSAGE)
         pushes.append(pltpu.make_async_copy(cuts.at[rows], flat.at[rows], sem.at[shot]))
         pushes[-1].start()
@@ -501,10 +502,10 @@
             at = x * WIDE + col
             wide_y[at : at + 8, :] = in_y[at : at + 8, :] - buoy_at(buoy, x, col - 4) * forward(taps, 0)
 
-    for first, count in ((0, 2), (8, 4), (24, 2)):
+    for first, count in ((0, 2), (24, 2), (8, 4)) if not last else ((0, 2), (24, 2), (8, 3), (20, 1)):
         for x0 in range(first, first + count * 4, 4):
             part_x = {}
-            if count == 2:
+            if first in (0, 24):
                 for n in range(4):
                     taps = [
                         wide_x[(x0 + d + 4) * CY + n * 8 : (x0 + d + 4) * CY + n * 8 + 8, :]
@@ -520,7 +521,7 @@
                         mid = (x0 + i) * WIDE + 4 + n * 8
                         taps = [wide_y[mid + d : mid + d + 8, :] for d in range(-4, 4)]
                         total = total + backward(taps, 0)
-                    if count == 2:
+                    if first in (0, 24):
                         total = total + part_x[i, n]
                     new_p[at : at + 8, :] = kicked[at : at + 8, :] - modu[at : at + 8, :] * total
         if last:
@@ -693,7 +694,7 @@
             [block, block, block] if last else [block, wide, wide] + [face] * 4,
             [pres, *faces, flow_x, flow_y, buoy, modu, spread, kicked],
             [vmem(32 * CY), vmem(2 * CX * STRIP)]
-            + ([vmem(WIDE * CY)] * 2 + [vmem(CX * CY)] * 2 + [dma((7,))] if last else []),
+            + ([vmem(WIDE * CY)] * 2 + [vmem(CX * CY)] * 2 + [dma((9,))] if last else []),
             f"edge{step}",
             to_hbm=last or (),
         )

time: 94.6 us -> 94.4 us (level)
  no operation moved by 1% of the time
where the time goes in v10:
time: 94.4 us; the launch traced here: 94.1 us
  starting transfers between devices  34.1 us (36%)
  waiting for transfers between devices  33.4 us (35%)
  Pallas kernels  25.6 us (27%)
    pallas_call x12, Pallas kernels, call(): pl.pallas_call(kernel, out_shape=outs, in_specs=specs, out_specs=[pl.Bloc...  25.6 us
    all_to_all x1, waiting for transfers between devices, shards(): window = lax.all_to_all(cut, DEVICES, 0, 0, tiled=True)  16.5 us
    ppermute x4, starting transfers between devices, exchange(): gy_b = lax.ppermute(faces[0], DEVICES, gy_far)  12.3 us
    all_to_all x1, starting transfers between devices, shards(): lax.all_to_all(deal.reshape(128, 16, 128), DEVICES, 0, 0, tiled=True)  10.3 us
    ppermute x4, waiting for transfers between devices, exchange(): gy_b = lax.ppermute(faces[0], DEVICES, gy_far)  9.34 us
    all_to_all x1, waiting for transfers between devices, shards(): lax.all_to_all(deal.reshape(128, 16, 128), DEVICES, 0, 0, tiled=True)  7.57 us
    all_to_all x1, starting transfers between devices, shards(): window = lax.all_to_all(cut, DEVICES, 0, 0, tiled=True)  7.03 us
    ppermute x4, starting transfers between devices, exchange(): gx_b = lax.ppermute(faces[2], DEVICES, gx_far)  2.26 us
  transfers between devices with their start and end apart: 18, of which 5 were waited for; matrix products, arithmetic and copies ran while one was open for 0% of the time, Pallas kernels for 18%

profile of v10, /device:TPU:16, one launch (start us, length us, event | category | flops | bytes accessed | tf_op | source)
XLA Modules:
  0.0 94.1 jit_solution(912831133374287983)
XLA Ops:
  0.6 2.2 %pack.1._ = f32[2048,128]{1,0:T(8,128)} custom-call(f32[1024,128]{1,0:T(8,128)} %bitcast.21, f32[1024,128]{1,0:T(8,128)} %bitcast.22), custom_call_target="tpu_custom_call" | custom-call | tf_op jit(solution)/shard_map/pack/pallas_call | solution.py:561
  2.8 10.3 %all-to-all-start = ((f32[128,16,128]{2,1,0:T(8,128)}), f32[128,16,128]{2,1,0:T(8,128)S(1)}, u32[]{:S(2)}, u32[]{:S(2)}) async-start(f32[128,16,128]{2,1,0:T(8,128)} %bitcast.13), calls=%async_computation | async-start | bytes 2097152 | tf_op jit(solution)/shard_map/all_to_all | solution.py:626
  13.2 1.7 %first_faces.1 = (f32[352,128]{1,0:T(8,128)S(1)}, f32[352,128]{1,0:T(8,128)S(1)}, f32[352,128]{1,0:T(8,128)S(1)}, f32[352,128]{1,0:T(8,128)S(1)}) custom-call(f32[1024,128]{1,0:T(8,128)} %bitcast.14, f32[1024,128]{1,0:T(8,128)} %bitcast.17, f32[1024,128]{1,0:T(8,128)} %bitcast.19, f32[2048,128]{1,0:T(8,128)} %pack.1._), custom_call_target="tpu_custom_call" | custom-call | flops 20000000 | bytes 8000000 | tf_op jit(solution)/shard_map/first_faces/pallas_call | solution.py:561
  14.8 3.4 %collective-permute-start = (f32[352,128]{1,0:T(8,128)S(1)}, f32[352,128]{1,0:T(8,128)S(1)}, u32[]{:S(2)}, u32[]{:S(2)}) collective-permute-start(f32[352,128]{1,0:T(8,128)S(1)} %get-tuple-element.55), channel_id=1, source_target_pairs={{0,32},{1,2},{2,1},{3,4},{4,3},{5,6},{6,5},{7,39},{8,40},{9,10},{1... | collective-permute-start | bytes 540680 | tf_op jit(solution)/shard_map/ppermute | solution.py:595
  18.4 1.5 %collective-permute-start.2 = (f32[352,128]{1,0:T(8,128)S(1)}, f32[352,128]{1,0:T(8,128)S(1)}, u32[]{:S(2)}, u32[]{:S(2)}) collective-permute-start(f32[352,128]{1,0:T(8,128)S(1)} %get-tuple-element.57), channel_id=1, source_target_pairs={{0,32},{1,33},{2,34},{3,35},{4,36},{5,37},{6,38},{7,39},{8,16},{9,... | collective-permute-start | bytes 540680 | tf_op jit(solution)/shard_map/ppermute | solution.py:596
  20.5 2.2 %step0_depth.1._.refs_6_ = f32[1024,128]{1,0:T(8,128)} custom-call(bf16[384,128]{1,0:T(8,128)(2,1)S(1)} %copy-done.1, f32[1024,128]{1,0:T(8,128)} %bitcast.15), custom_call_target="tpu_custom_call" | custom-call | flops 30000001024 | bytes 8000000 | tf_op jit(solution)/shard_map/step0_depth/pallas_call | solution.py:561
  22.8 7.6 %all-to-all-done = f32[128,16,128]{2,1,0:T(8,128)S(1)} async-done(((f32[128,16,128]{2,1,0:T(8,128)}), f32[128,16,128]{2,1,0:T(8,128)S(1)}, u32[]{:S(2)}, u32[]{:S(2)}) %all-to-all-start) | async-done | bytes 1048608 | tf_op jit(solution)/shard_map/all_to_all | solution.py:626
  30.4 1.3 %cut.1 = f32[128,11,2,128]{3,2,1,0:T(2,128)} custom-call(f32[2048,128]{1,0:T(8,128)S(1)} %bitcast.12, s32[4,2]{1,0:T(4,128)S(1)} %copy.16.corners, f32[1024,128]{1,0:T(8,128)} %step0_depth.1._.refs_6_), custom_call_target="tpu_custom_call" | custom-call | tf_op jit(solution)/shard_map/cut/pallas_call | solution.py:561
  31.8 7.0 %all-to-all-start.1 = ((f32[128,11,2,128]{3,2,1,0:T(2,128)}), f32[128,11,2,128]{3,2,1,0:T(2,128)S(1)}, u32[]{:S(2)}, u32[]{:S(2)}) async-start(f32[128,11,2,128]{3,2,1,0:T(2,128)} %cut.1), calls=%async_computation.1 | async-start | bytes 2883584 | tf_op jit(solution)/shard_map/all_to_all | solution.py:656
  38.9 4.7 %step0_gradients.1 = (f32[1280,128]{1,0:T(8,128)}, f32[1280,128]{1,0:T(8,128)}, f32[1280,128]{1,0:T(8,128)}, f32[1280,128]{1,0:T(8,128)}, f32[1024,128]{1,0:T(8,128)}) custom-call(s32[4,3]{1,0:T(4,128)S(1)} %copy-done.2, f32[4,4]{1,0:T(4,128)S(1)} %copy-done.3, f32[1024,128]{1,0:T(8,128)} %bitcast.16, f32[352,128]{1,0:T(8,128)S(1)} %collective-permute-done.gy_b, ...), custom_call_target="tpu_custom_call" | custom-call | flops 30000001024 | bytes 8000000 | tf_op jit(solution)/shard_map/step0_gradients/pallas_call | solution.py:561
  43.6 16.5 %all-to-all-done.1.window = f32[128,11,2,128]{3,2,1,0:T(2,128)S(1)} async-done(((f32[128,11,2,128]{3,2,1,0:T(2,128)}), f32[128,11,2,128]{3,2,1,0:T(2,128)S(1)}, u32[]{:S(2)}, u32[]{:S(2)}) %all-to-all-start.1) | async-done | bytes 1441824 | tf_op jit(solution)/shard_map/all_to_all | solution.py:656
  60.1 2.8 %step0.1 = (f32[1024,128]{1,0:T(8,128)S(1)}, f32[1280,128]{1,0:T(8,128)S(1)}, f32[1280,128]{1,0:T(8,128)S(1)}, f32[1024,128]{1,0:T(8,128)S(1)}, f32[1600,128]{1,...) custom-call(s32[4,2]{1,0:T(4,128)S(1)} %copy.16.corners, ...), custom_call_target="tpu_custom_call" | custom-call | tf_op jit(solution)/shard_map/step0/pallas_call | solution.py:561
  62.9 2.9 %collective-permute-start.4 = (f32[224,128]{1,0:T(8,128)S(1)}, f32[224,128]{1,0:T(8,128)S(1)}, u32[]{:S(2)}, u32[]{:S(2)}) collective-permute-start(f32[224,128]{1,0:T(8,128)S(1)} %get-tuple-element.65), channel_id=1, source_target_pairs={{0,32},{1,2},{2,1},{3,4},{4,3},{5,6},{6,5},{7,39},{8,40},{9,10},{1... | collective-permute-start | bytes 344072 | tf_op jit(solution)/shard_map/ppermute | solution.py:595
  66.1 1.1 %collective-permute-start.7 = (f32[224,128]{1,0:T(8,128)S(1)}, f32[224,128]{1,0:T(8,128)S(1)}, u32[]{:S(2)}, u32[]{:S(2)}) collective-permute-start(f32[224,128]{1,0:T(8,128)S(1)} %get-tuple-element.68), channel_id=1, source_target_pairs={{0,8},{1,9},{2,10},{3,11},{4,12},{5,13},{6,14},{7,15},{8,0},{9,1},... | collective-permute-start | bytes 344072 | tf_op jit(solution)/shard_map/ppermute | solution.py:598
  67.2 2.1 %inner1.1 = (f32[1280,128]{1,0:T(8,128)S(1)}, f32[1280,128]{1,0:T(8,128)S(1)}, f32[1024,128]{1,0:T(8,128)S(1)}, f32[1024,128]{1,0:T(8,128)S(1)}, f32[1024,128]{1,0:T(8,128)S(1)}) custom-call(s32[4,3]{1,0:T(4,128)S(1)} %copy-done.2, f32[4,4]{1,0:T(4,128)S(1)} %copy-done.3, bf16[384,128]{1,0:T(8,128)(2,1)S(1)} %copy-done.1, bf16[384,128]{1,0:T(8,128)(2,1)S(1)} %copy-done, ...), custom_call_target="tpu_custom_call" | custom-call | flops 20000000 | bytes 8000000 | tf_op jit(solution)/shard_map/inner1/pallas_call | solution.py:561
  69.4 3.2 %collective-permute-done.4.refs_1_ = f32[224,128]{1,0:T(8,128)S(1)} collective-permute-done((f32[224,128]{1,0:T(8,128)S(1)}, f32[224,128]{1,0:T(8,128)S(1)}, u32[]{:S(2)}, u32[]{:S(2)}) %collective-permute-start.4) | collective-permute-done | bytes 114720 | tf_op jit(solution)/shard_map/ppermute | solution.py:595
  72.5 0.9 edge1.1
  73.4 2.9 %collective-permute-start.8 = (f32[224,128]{1,0:T(8,128)S(1)}, f32[224,128]{1,0:T(8,128)S(1)}, u32[]{:S(2)}, u32[]{:S(2)}) collective-permute-start(f32[224,128]{1,0:T(8,128)S(1)} %get-tuple-element.79), channel_id=1, source_target_pairs={{0,32},{1,2},{2,1},{3,4},{4,3},{5,6},{6,5},{7,39},{8,40},{9,10},{1... | collective-permute-start | bytes 344072 | tf_op jit(solution)/shard_map/ppermute | solution.py:595
  77.0 2.2 %inner2.1 = (f32[1280,128]{1,0:T(8,128)S(1)}, f32[1280,128]{1,0:T(8,128)S(1)}, f32[1024,128]{1,0:T(8,128)S(1)}, f32[1024,128]{1,0:T(8,128)S(1)}, f32[1024,128]{1,0:T(8,128)S(1)}) custom-call(s32[4,3]{1,0:T(4,128)S(1)} %copy-done.2, f32[4,4]{1,0:T(4,128)S(1)} %copy-done.3, bf16[384,128]{1,0:T(8,128)(2,1)S(1)} %copy-done.1, bf16[384,128]{1,0:T(8,128)(2,1)S(1)} %copy-done, ...), custom_call_target="tpu_custom_call" | custom-call | flops 20000000 | bytes 8000000 | tf_op jit(solution)/shard_map/inner2/pallas_call | solution.py:561
  79.2 3.8 %collective-permute-done.8.refs_1_ = f32[224,128]{1,0:T(8,128)S(1)} collective-permute-done((f32[224,128]{1,0:T(8,128)S(1)}, f32[224,128]{1,0:T(8,128)S(1)}, u32[]{:S(2)}, u32[]{:S(2)}) %collective-permute-start.8) | collective-permute-done | bytes 114720 | tf_op jit(solution)/shard_map/ppermute | solution.py:595
  83.9 3.1 %collective-permute-start.12 = (f32[224,128]{1,0:T(8,128)S(1)}, f32[224,128]{1,0:T(8,128)S(1)}, u32[]{:S(2)}, u32[]{:S(2)}) collective-permute-start(f32[224,128]{1,0:T(8,128)S(1)} %get-tuple-element.91), channel_id=1, source_target_pairs={{0,32},{1,2},{2,1},{3,4},{4,3},{5,6},{6,5},{7,39},{8,40},{9,10},{1... | collective-permute-start | bytes 344072 | tf_op jit(solution)/shard_map/ppermute | solution.py:595
  87.0 2.9 %inner3.1 = (f32[1280,128]{1,0:T(8,128)S(1)}, f32[1280,128]{1,0:T(8,128)S(1)}, f32[1024,128]{1,0:T(8,128)}, f32[1024,128]{1,0:T(8,128)S(1)}, f32[1024,128]{1,0:T(8,128)S(1)}) custom-call(s32[4,3]{1,0:T(4,128)S(1)} %copy-done.2, f32[4,4]{1,0:T(4,128)S(1)} %copy-done.3, bf16[384,128]{1,0:T(8,128)(2,1)S(1)} %copy-done.1, bf16[384,128]{1,0:T(8,128)(2,1)S(1)} %copy-done, ...), custom_call_target="tpu_custom_call" | custom-call | flops 20000000 | bytes 8000000 | tf_op jit(solution)/shard_map/inner3/pallas_call | solution.py:561
  90.0 2.4 %collective-permute-done.12.refs_1_ = f32[224,128]{1,0:T(8,128)S(1)} collective-permute-done((f32[224,128]{1,0:T(8,128)S(1)}, f32[224,128]{1,0:T(8,128)S(1)}, u32[]{:S(2)}, u32[]{:S(2)}) %collective-permute-start.12) | collective-permute-done | bytes 114720 | tf_op jit(solution)/shard_map/ppermute | solution.py:595
  92.4 1.7 %edge3.1 = (f32[1024,128]{1,0:T(8,128)}, f32[1024,128]{1,0:T(8,128)}, f32[1024,128]{1,0:T(8,128)}) custom-call(f32[1024,128]{1,0:T(8,128)S(1)} %get-tuple-element.90.pres.refs_0_, f32[224,128]{1,0:T(8,128)S(1)} %collective-permute-done.12.refs_1_, f32[224,128]{1,0:T(8,128)S(1)} %collective-permute-done.13.refs_2_, ...), custom_call_target="tpu_custom_call" | custom-call | tf_op jit(solution)/shard_map/edge3/pallas_call | solution.py:561
  (35 shorter events, 3.0 us)
Async XLA Ops:
  2.8 27.6 %all-to-all-start = ((f32[128,16,128]{2,1,0:T(8,128)}), f32[128,16,128]{2,1,0:T(8,128)S(1)}, u32[]{:S(2)}, u32[]{:S(2)}) async-start(f32[128,16,128]{2,1,0:T(8,128)} %bitcast.13), calls=%async_computation | async-start | bytes 2097152 | tf_op jit(solution)/shard_map/all_to_all | solution.py:626
  13.2 7.3 %copy-start.1 = (bf16[384,128]{1,0:T(8,128)(2,1)S(1)}, bf16[384,128]{1,0:T(8,128)(2,1)}, u32[]{:S(2)}) copy-start(bf16[384,128]{1,0:T(8,128)(2,1)} %constant.4.clone.mat_f) | copy-start | bytes 294916
  14.8 24.0 %collective-permute-start = (f32[352,128]{1,0:T(8,128)S(1)}, f32[352,128]{1,0:T(8,128)S(1)}, u32[]{:S(2)}, u32[]{:S(2)}) collective-permute-start(f32[352,128]{1,0:T(8,128)S(1)} %get-tuple-element.55), channel_id=1, source_target_pairs={{0,32},{1,2},{2,1},{3,4},{4,3},{5,6},{6,5},{7,39},{8,40},{9,10},{1... | collective-permute-start | bytes 540680 | tf_op jit(solution)/shard_map/ppermute | solution.py:595
  18.2 20.6 %collective-permute-start.1 = (f32[352,128]{1,0:T(8,128)S(1)}, f32[352,128]{1,0:T(8,128)S(1)}, u32[]{:S(2)}, u32[]{:S(2)}) collective-permute-start(f32[352,128]{1,0:T(8,128)S(1)} %get-tuple-element.56), channel_id=1, source_target_pairs={{0,1},{1,0},{2,3},{3,2},{4,5},{5,4},{6,7},{7,6},{8,9},{9,8},{10,11... | collective-permute-start | bytes 540680 | tf_op jit(solution)/shard_map/ppermute | solution.py:597
  18.4 20.5 %collective-permute-start.2 = (f32[352,128]{1,0:T(8,128)S(1)}, f32[352,128]{1,0:T(8,128)S(1)}, u32[]{:S(2)}, u32[]{:S(2)}) collective-permute-start(f32[352,128]{1,0:T(8,128)S(1)} %get-tuple-element.57), channel_id=1, source_target_pairs={{0,32},{1,33},{2,34},{3,35},{4,36},{5,37},{6,38},{7,39},{8,16},{9,... | collective-permute-start | bytes 540680 | tf_op jit(solution)/shard_map/ppermute | solution.py:596
  19.8 2.9 %copy-start.4 = (s32[4,2]{0,1:T(2,128)S(1)}, s32[4,2]{0,1:T(2,128)}, u32[]{:S(2)}) copy-start(s32[4,2]{0,1:T(2,128)} %param.13) | copy-start | bytes 100
  19.8 19.0 %collective-permute-start.3 = (f32[352,128]{1,0:T(8,128)S(1)}, f32[352,128]{1,0:T(8,128)S(1)}, u32[]{:S(2)}, u32[]{:S(2)}) collective-permute-start(f32[352,128]{1,0:T(8,128)S(1)} %get-tuple-element.58), channel_id=1, source_target_pairs={{0,8},{1,9},{2,10},{3,11},{4,12},{5,13},{6,14},{7,15},{8,0},{9,1},... | collective-permute-start | bytes 540680 | tf_op jit(solution)/shard_map/ppermute | solution.py:598
  31.8 7.1 %copy-start.2 = (s32[4,3]{1,0:T(4,128)S(1)}, s32[4,3]{1,0:T(4,128)}, u32[]{:S(2)}) copy-start(s32[4,3]{1,0:T(4,128)} %cells.7) | copy-start | bytes 148
  31.8 7.1 %copy-start.3 = (f32[4,4]{1,0:T(4,128)S(1)}, f32[4,4]{1,0:T(4,128)}, u32[]{:S(2)}) copy-start(f32[4,4]{1,0:T(4,128)} %amps.7) | copy-start | bytes 196
  31.8 28.3 %all-to-all-start.1 = ((f32[128,11,2,128]{3,2,1,0:T(2,128)}), f32[128,11,2,128]{3,2,1,0:T(2,128)S(1)}, u32[]{:S(2)}, u32[]{:S(2)}) async-start(f32[128,11,2,128]{3,2,1,0:T(2,128)} %cut.1), calls=%async_computation.1 | async-start | bytes 2883584 | tf_op jit(solution)/shard_map/all_to_all | solution.py:656
  38.8 21.2 %copy-start = (bf16[384,128]{1,0:T(8,128)(2,1)S(1)}, bf16[384,128]{1,0:T(8,128)(2,1)}, u32[]{:S(2)}) copy-start(bf16[384,128]{1,0:T(8,128)(2,1)} %constant.5.clone.mat_b) | copy-start | bytes 294916
  62.9 9.6 %collective-permute-start.4 = (f32[224,128]{1,0:T(8,128)S(1)}, f32[224,128]{1,0:T(8,128)S(1)}, u32[]{:S(2)}, u32[]{:S(2)}) collective-permute-start(f32[224,128]{1,0:T(8,128)S(1)} %get-tuple-element.65), channel_id=1, source_target_pairs={{0,32},{1,2},{2,1},{3,4},{4,3},{5,6},{6,5},{7,39},{8,40},{9,10},{1... | collective-permute-start | bytes 344072 | tf_op jit(solution)/shard_map/ppermute | solution.py:595
  65.8 6.8 %collective-permute-start.5 = (f32[224,128]{1,0:T(8,128)S(1)}, f32[224,128]{1,0:T(8,128)S(1)}, u32[]{:S(2)}, u32[]{:S(2)}) collective-permute-start(f32[224,128]{1,0:T(8,128)S(1)} %get-tuple-element.66), channel_id=1, source_target_pairs={{0,1},{1,0},{2,3},{3,2},{4,5},{5,4},{6,7},{7,6},{8,9},{9,8},{10,11... | collective-permute-start | bytes 344072 | tf_op jit(solution)/shard_map/ppermute | solution.py:597
  65.8 6.8 %collective-permute-start.6 = (f32[224,128]{1,0:T(8,128)S(1)}, f32[224,128]{1,0:T(8,128)S(1)}, u32[]{:S(2)}, u32[]{:S(2)}) collective-permute-start(f32[224,128]{1,0:T(8,128)S(1)} %get-tuple-element.67), channel_id=1, source_target_pairs={{0,32},{1,33},{2,34},{3,35},{4,36},{5,37},{6,38},{7,39},{8,16},{9,... | collective-permute-start | bytes 344072 | tf_op jit(solution)/shard_map/ppermute | solution.py:596
  66.1 6.4 %collective-permute-start.7 = (f32[224,128]{1,0:T(8,128)S(1)}, f32[224,128]{1,0:T(8,128)S(1)}, u32[]{:S(2)}, u32[]{:S(2)}) collective-permute-start(f32[224,128]{1,0:T(8,128)S(1)} %get-tuple-element.68), channel_id=1, source_target_pairs={{0,8},{1,9},{2,10},{3,11},{4,12},{5,13},{6,14},{7,15},{8,0},{9,1},... | collective-permute-start | bytes 344072 | tf_op jit(solution)/shard_map/ppermute | solution.py:598
  73.4 9.5 %collective-permute-start.8 = (f32[224,128]{1,0:T(8,128)S(1)}, f32[224,128]{1,0:T(8,128)S(1)}, u32[]{:S(2)}, u32[]{:S(2)}) collective-permute-start(f32[224,128]{1,0:T(8,128)S(1)} %get-tuple-element.79), channel_id=1, source_target_pairs={{0,32},{1,2},{2,1},{3,4},{4,3},{5,6},{6,5},{7,39},{8,40},{9,10},{1... | collective-permute-start | bytes 344072 | tf_op jit(solution)/shard_map/ppermute | solution.py:595
  76.3 6.6 %collective-permute-start.9 = (f32[224,128]{1,0:T(8,128)S(1)}, f32[224,128]{1,0:T(8,128)S(1)}, u32[]{:S(2)}, u32[]{:S(2)}) collective-permute-start(f32[224,128]{1,0:T(8,128)S(1)} %get-tuple-element.80), channel_id=1, source_target_pairs={{0,1},{1,0},{2,3},{3,2},{4,5},{5,4},{6,7},{7,6},{8,9},{9,8},{10,11... | collective-permute-start | bytes 344072 | tf_op jit(solution)/shard_map/ppermute | solution.py:597
  76.3 6.6 %collective-permute-start.10 = (f32[224,128]{1,0:T(8,128)S(1)}, f32[224,128]{1,0:T(8,128)S(1)}, u32[]{:S(2)}, u32[]{:S(2)}) collective-permute-start(f32[224,128]{1,0:T(8,128)S(1)} %get-tuple-element.81), channel_id=1, source_target_pairs={{0,32},{1,33},{2,34},{3,35},{4,36},{5,37},{6,38},{7,39},{8,16},{9,... | collective-permute-start | bytes 344072 | tf_op jit(solution)/shard_map/ppermute | solution.py:596
  76.7 6.3 %collective-permute-start.11 = (f32[224,128]{1,0:T(8,128)S(1)}, f32[224,128]{1,0:T(8,128)S(1)}, u32[]{:S(2)}, u32[]{:S(2)}) collective-permute-start(f32[224,128]{1,0:T(8,128)S(1)} %get-tuple-element.82), channel_id=1, source_target_pairs={{0,8},{1,9},{2,10},{3,11},{4,12},{5,13},{6,14},{7,15},{8,0},{9,1},... | collective-permute-start | bytes 344072 | tf_op jit(solution)/shard_map/ppermute | solution.py:598
  83.9 8.5 %collective-permute-start.12 = (f32[224,128]{1,0:T(8,128)S(1)}, f32[224,128]{1,0:T(8,128)S(1)}, u32[]{:S(2)}, u32[]{:S(2)}) collective-permute-start(f32[224,128]{1,0:T(8,128)S(1)} %get-tuple-element.91), channel_id=1, source_target_pairs={{0,32},{1,2},{2,1},{3,4},{4,3},{5,6},{6,5},{7,39},{8,40},{9,10},{1... | collective-permute-start | bytes 344072 | tf_op jit(solution)/shard_map/ppermute | solution.py:595
  86.9 5.5 %collective-permute-start.13 = (f32[224,128]{1,0:T(8,128)S(1)}, f32[224,128]{1,0:T(8,128)S(1)}, u32[]{:S(2)}, u32[]{:S(2)}) collective-permute-start(f32[224,128]{1,0:T(8,128)S(1)} %get-tuple-element.92), channel_id=1, source_target_pairs={{0,1},{1,0},{2,3},{3,2},{4,5},{5,4},{6,7},{7,6},{8,9},{9,8},{10,11... | collective-permute-start | bytes 344072 | tf_op jit(solution)/shard_map/ppermute | solution.py:597
  86.9 5.5 %collective-permute-start.14 = (f32[224,128]{1,0:T(8,128)S(1)}, f32[224,128]{1,0:T(8,128)S(1)}, u32[]{:S(2)}, u32[]{:S(2)}) collective-permute-start(f32[224,128]{1,0:T(8,128)S(1)} %get-tuple-element.93), channel_id=1, source_target_pairs={{0,32},{1,33},{2,34},{3,35},{4,36},{5,37},{6,38},{7,39},{8,16},{9,... | collective-permute-start | bytes 344072 | tf_op jit(solution)/shard_map/ppermute | solution.py:596
  87.0 5.4 %collective-permute-start.15 = (f32[224,128]{1,0:T(8,128)S(1)}, f32[224,128]{1,0:T(8,128)S(1)}, u32[]{:S(2)}, u32[]{:S(2)}) collective-permute-start(f32[224,128]{1,0:T(8,128)S(1)} %get-tuple-element.94), channel_id=1, source_target_pairs={{0,8},{1,9},{2,10},{3,11},{4,12},{5,13},{6,14},{7,15},{8,0},{9,1},... | collective-permute-start | bytes 344072 | tf_op jit(solution)/shard_map/ppermute | solution.py:598
